TPU v7x, 32 devices: a whole 2x2x4 slice. The times are simulated.
32 devices in a mesh: grp: 2 (over y), layer: 16 (over z, x, core).
Axes of the slice: x: 2, y: 2, z: 4, core: 2. Of those that a mesh axis runs over, the one named last changes fastest.
Arguments:
- residual: bfloat16 [2, 4096, 3584], P(None, ('grp', 'layer')), parts along dimension 1, may hold values from -6 to 6
- mlp_target: bfloat16 [2, 4096, 3584], P(None, ('grp', 'layer')), parts along dimension 1, may hold values from -6 to 6
- pre_acts: bfloat16 [2, 4096, 1, 128], P(None, ('grp', 'layer')), parts along dimension 1, may hold values from -6 to 6
- blocks: int32 [2, 4096, 1], P(None, ('grp', 'layer')), parts along dimension 1, may hold values from 0 to 15; in each aligned block of 128 rows (0 to 127, 128 to 255, ..., all dimensions but the last counted through in order) at most 16 rows name the same one
- decoder: bfloat16 [3, 2048, 3584], P(None, 'layer'), may hold values from -0.5 to 0.5
- decoder_bias: float32 [2, 3584], replicated, may hold values from -3 to 3
Outputs:
- decoder_gradient: bfloat16 [6, 2048, 3584], P('grp', 'layer'), parts along dimension 0
- encoder_gradient: bfloat16 [4, 3584, 2048], P('grp', None, 'layer'), parts along dimension 0
- encoder_bias_gradient: float32 [4, 2048], P('grp', 'layer'), parts along dimension 0
- decoder_bias_gradient: float32 [4, 3584], P('grp'), parts along dimension 0
There are 2 independent parts, one for each index of `grp`. A program takes and returns all parts, laid end to end along the dimension named above; an argument that names none is the same for every part. Nothing has to cross between parts.
Inputs may be any that keep to these rules, and one draw needn't show every extreme that they name: Each row names 1 different blocks. Among the rows of one device in one layer (aligned blocks of 128 rows over the first two dimensions taken together) no block is named more than 16 times.
All inputs are finite; a program needn't handle non-finite values.
Results may differ from a plain program's by a relative error of at most 0.0051.
Values may be sent and summed in bfloat16 or wider, within the bound.
No kernel may reach another device: no remote copies, remote signals or barrier semaphores. Data moves between devices by JAX's collectives and lax.ppermute only.
A program may use at most 128 MiB of HBM per device.

v0:
```python
import math

import jax
import jax.numpy as jnp
from jax import lax
from jax.sharding import PartitionSpec as P


def pair_index(source, output_layer, layers):
    return source * layers - source * (source - 1) // 2 + (output_layer - source)


def row_pick(table, chosen):
    return jax.vmap(lambda rows_of, picked: rows_of[picked])(table, chosen)


def decode(latent_act, weights):
    return jnp.dot(latent_act, weights, preferred_element_type=jnp.float32).astype(jnp.bfloat16)


def per_device(residual, mlp_target, pre_acts, blocks, decoder, decoder_bias):
    devices = lax.axis_size("layer")
    layers, tokens_here, model_width = residual.shape
    per_token = pre_acts.shape[2]
    block_width = pre_acts.shape[3]
    route_count = tokens_here * per_token
    capacity = max(2, 2 * route_count // devices)
    slot_count = devices * capacity
    err_scale = 1.0 / math.sqrt(route_count)
    routes = blocks.reshape(layers, route_count)
    matches = (routes[:, :, None] == jnp.arange(devices, dtype=jnp.int32)).astype(jnp.int32)
    ordinal = jnp.sum((jnp.cumsum(matches, axis=1) - 1) * matches, axis=2)
    slot_of = routes * capacity + ordinal
    layer_ids = jnp.broadcast_to(jnp.arange(layers, dtype=jnp.int32)[:, None], routes.shape)
    route_ids = jnp.broadcast_to(jnp.arange(route_count, dtype=jnp.int32)[None, :], routes.shape)
    slot_route = (
        jnp.full((layers, slot_count), route_count, jnp.int32).at[layer_ids, slot_of].set(route_ids)
    )
    slot_token = slot_route // per_token
    pre_rows = jnp.concatenate(
        [
            pre_acts.reshape(layers, route_count, block_width),
            jnp.zeros((layers, 1, block_width), pre_acts.dtype),
        ],
        axis=1,
    )
    resid_rows = jnp.concatenate(
        [residual, jnp.zeros((layers, 1, model_width), residual.dtype)], axis=1
    )
    send_pre = row_pick(pre_rows, slot_route)
    send_resid = row_pick(resid_rows, slot_token)
    recv_pre, recv_resid = (
        lax.all_to_all(send_pre, "layer", split_axis=1, concat_axis=1, tiled=True),
        lax.all_to_all(send_resid, "layer", split_axis=1, concat_axis=1, tiled=True),
    )
    latent_act = jnp.maximum(recv_pre, 0)
    back_rows = {}
    for source in range(layers):
        stacked = jnp.stack(
            [
                decode(latent_act[source], decoder[pair_index(source, output_layer, layers)])
                for output_layer in range(source, layers)
            ]
        )
        returned = lax.all_to_all(stacked, "layer", split_axis=1, concat_axis=1, tiled=True)
        for offset in range(layers - source):
            back_rows[source, source + offset] = returned[offset]
    error_list = []
    for output_layer in range(layers):
        summed = jnp.broadcast_to(decoder_bias[output_layer][None, :], (tokens_here, model_width))
        for source in range(output_layer + 1):
            picked = back_rows[source, output_layer][slot_of[source]]
            summed = summed + picked.astype(jnp.float32).reshape(
                tokens_here, per_token, model_width
            ).sum(axis=1)
        error_list.append(((summed - mlp_target[output_layer]) * err_scale).astype(jnp.bfloat16))
    errors = jnp.stack(error_list)
    decoder_bias_gradient = lax.psum(jnp.sum(errors.astype(jnp.float32), axis=1), "layer")
    error_rows = jnp.concatenate(
        [errors, jnp.zeros((layers, 1, model_width), jnp.bfloat16)], axis=1
    )
    error_in = {}
    for source in range(layers):
        stacked = jnp.stack(
            [error_rows[output_layer][slot_token[source]] for output_layer in range(source, layers)]
        )
        arrived = lax.all_to_all(stacked, "layer", split_axis=1, concat_axis=1, tiled=True)
        for offset in range(layers - source):
            error_in[source, source + offset] = arrived[offset]
    dec_grads = [None] * (layers * (layers + 1) // 2)
    enc_grads = []
    bias_grads = []
    for source in range(layers):
        latent_grad = jnp.zeros((slot_count, block_width), jnp.float32)
        for output_layer in range(source, layers):
            pair_slot = pair_index(source, output_layer, layers)
            error_local = error_in[source, output_layer]
            latent_grad = latent_grad + lax.dot_general(
                error_local,
                decoder[pair_slot],
                (((1,), (1,)), ((), ())),
                preferred_element_type=jnp.float32,
            )
            dec_grads[pair_slot] = lax.dot_general(
                latent_act[source],
                error_local,
                (((0,), (0,)), ((), ())),
                preferred_element_type=jnp.float32,
            ).astype(jnp.bfloat16)
        pre_grad = jnp.where(recv_pre[source] > 0, latent_grad, 0.0)
        bias_grads.append(jnp.sum(pre_grad, axis=0))
        enc_grads.append(
            lax.dot_general(
                recv_resid[source],
                pre_grad.astype(jnp.bfloat16),
                (((0,), (0,)), ((), ())),
                preferred_element_type=jnp.float32,
            ).astype(jnp.bfloat16)
        )
    return (
        jnp.stack(dec_grads),
        jnp.stack(enc_grads),
        jnp.stack(bias_grads),
        decoder_bias_gradient,
    )


def solution(mesh):
    return jax.shard_map(
        per_device,
        mesh=mesh,
        in_specs=(
            P(None, ("grp", "layer"), None),
            P(None, ("grp", "layer"), None),
            P(None, ("grp", "layer"), None, None),
            P(None, ("grp", "layer"), None),
            P(None, "layer", None),
            P(),
        ),
        out_specs=(
            P("grp", "layer", None),
            P("grp", None, "layer"),
            P("grp", "layer"),
            P("grp", None),
        ),
        check_vma=False,
    )
```

profile of v0, /device:TPU:0, one launch (start us, length us, event | category | flops | bytes accessed | tf_op | source)
XLA Modules:
  0.0 481.0 jit_solution(3131709928751300624)
XLA Ops:
  0.6 0.9 copy.87
  1.6 0.8 fusion.38
  2.5 0.9 select_reduce_fusion
  3.4 0.7 fusion.48
  4.1 12.5 %scatter_fusion = s32[2,256]{1,0:T(2,128)S(1)} fusion(s32[2,256]{1,0:T(2,128)S(1)} %broadcast_in_dim.20, s32[256]{0:T(256)S(1)} %fusion.48, s32[256]{0:T(256)S(1)} %iota_bitcast_fusion), kind=kCustom, calls=%fused_computation.8 | custom fusion | bytes 5120 | tf_op jit(solution)/shard_map/scatter | solution.py:37
  16.7 2.7 gather_fusion.6
  19.5 15.1 %all_to_all.30 = bf16[2,256,128]{2,0,1:T(2,128)(2,1)S(1)} all-to-all(bf16[2,256,128]{2,0,1:T(2,128)(2,1)S(1)} %copy.31), channel_id=1, replica_groups=mesh['grp'=2,'layer'=16] {'layer'}, dimensions={1} | all-to-all | bytes 262144 | tf_op jit(solution)/shard_map/all_to_all | solution.py:53
  34.6 1.8 fusion.2
  36.4 4.6 copy.89
  41.0 0.5 broadcast.268
  41.6 11.9 %reduce.4 = bf16[256,3584]{1,0:T(8,128)(2,1)S(1)} reduce(bf16[256,1,3584]{2,1,0:T(2,128)(2,1)} %bitcast.156, bf16[]{:T(256)} %broadcast.268), dimensions={1}, to_apply=%bitcast.151.reduce_sub_computation | reduce | bytes 3670018
  53.4 2.3 reshape.311
  55.7 4.0 all-to-all-start.2
  59.7 1.8 fusion.1
  61.5 1.8 fusion
  63.3 0.3 pad_maximum_fusion
  63.7 5.6 %copy.33 = bf16[2,256,3584]{2,0,1:T(2,128)(2,1)} copy(bf16[2,256,3584]{2,1,0:T(8,128)(2,1)S(1)} %pad_maximum_fusion) | data formatting | bytes 7340032 | tf_op jit(solution)/shard_map/stack | solution.py:59
  69.3 26.9 %all-to-all-done.2 = bf16[16,2,28672]{2,1,0:T(2,128)(2,1)S(1)} async-done(((bf16[16,2,28672]{2,1,0:T(2,128)(2,1)}), bf16[16,2,28672]{2,1,0:T(2,128)(2,1)S(1)}, u32[]{:S(2)}, u32[]{:S(2)}) %all-to-all-start.2) | async-done | bytes 1835040 | tf_op jit(solution)/shard_map/all_to_all | solution.py:65
  96.2 1.2 copy-done.4
  97.4 10.7 %all-to-all-start.1 = ((bf16[2,256,3584]{2,0,1:T(2,128)(2,1)}), bf16[2,256,3584]{2,0,1:T(2,128)(2,1)}, u32[]{:S(2)}, u32[]{:S(2)}) async-start(bf16[2,256,3584]{2,0,1:T(2,128)(2,1)} %copy.33), calls=%async_computation.1 | async-start | bytes 7340032 | tf_op jit(solution)/shard_map/all_to_all | solution.py:65
  108.1 3.4 copy.41
  111.5 1.4 concatenate.15
  113.0 11.6 %gather_fusion.7 = bf16[512,3584]{1,0:T(8,128)(2,1)} fusion(bf16[2,129,3584]{2,0,1:T(2,128)(2,1)S(1)} %concatenate.15, s32[512]{0:T(512)S(1)} %bitcast.154), kind=kCustom, calls=%fused_computation.7 | custom fusion | bytes 7344128 | tf_op jit(solution)/shard_map/vmap()/gather | solution.py:14
  124.6 7.6 %copy.42 = bf16[2,256,3584]{2,0,1:T(2,128)(2,1)} copy(bf16[2,256,3584]{2,1,0:T(8,128)(2,1)} %bitcast.159) | data formatting | bytes 7340032 | tf_op jit(solution)/shard_map/vmap()/gather | solution.py:14
  132.3 44.4 %all-to-all-done.1 = bf16[2,256,3584]{2,0,1:T(2,128)(2,1)} async-done(((bf16[2,256,3584]{2,0,1:T(2,128)(2,1)}), bf16[2,256,3584]{2,0,1:T(2,128)(2,1)}, u32[]{:S(2)}, u32[]{:S(2)}) %all-to-all-start.1) | async-done | bytes 3670048 | tf_op jit(solution)/shard_map/all_to_all | solution.py:65
  176.7 17.8 %all-to-all-start.5 = ((bf16[2,256,3584]{2,0,1:T(2,128)(2,1)}), bf16[2,256,3584]{2,0,1:T(2,128)(2,1)}, u32[]{:S(2)}, u32[]{:S(2)}) async-start(bf16[2,256,3584]{2,0,1:T(2,128)(2,1)} %copy.42), calls=%async_computation.5 | async-start | bytes 7340032 | tf_op jit(solution)/shard_map/all_to_all | solution.py:54
  194.6 6.5 %reshape.312 = bf16[256,1,3584]{2,1,0:T(2,128)(2,1)} reshape(bf16[16,2,28672]{2,1,0:T(2,128)(2,1)S(1)} %copy-done.5) | data formatting | bytes 3670016
  201.2 2.3 copy.86
  203.4 2.0 gather_fusion.2
  205.5 7.8 %fusion.53 = (bf16[1,256,3584]{2,0,1:T(2,128)(2,1)S(1)}, bf16[1,256,3584]{2,0,1:T(2,128)(2,1)S(1)}) fusion(bf16[2,256,3584]{2,0,1:T(2,128)(2,1)} %all-to-all-done.1), kind=kLoop, calls=%fused_computation.114 | loop fusion | bytes 7340032 | tf_op jit(solution)/shard_map/slice | solution.py:67
  213.3 2.0 copy_bitcast_fusion.6
  215.3 4.7 gather_fusion.1
  220.0 2.0 gather_fusion
  222.0 3.1 fusion.16
  225.3 0.8 copy-done
  226.2 3.0 gather_fusion.5
  229.1 6.2 %copy.88 = bf16[1,256,3584]{2,0,1:T(2,128)(2,1)} copy(bf16[1,256,3584]{2,1,0:T(8,128)(2,1)} %bitcast.164) | data formatting | bytes 3670016 | tf_op jit(solution)/shard_map/stack | solution.py:84
  235.4 13.3 %reduce.5 = bf16[256,3584]{1,0:T(8,128)(2,1)} reduce(bf16[256,1,3584]{2,1,0:T(2,128)(2,1)} %bitcast.157, bf16[]{:T(256)} %broadcast.268), dimensions={1}, to_apply=%bitcast.150.reduce_sub_computation | reduce | bytes 3670018
  248.7 5.4 %reshape.313 = bf16[16,2,28672]{2,1,0:T(2,128)(2,1)} reshape(bf16[256,3584]{1,0:T(8,128)(2,1)} %reduce.5) | data formatting | bytes 3670016
  254.1 8.9 %all-to-all-done.5 = bf16[2,256,3584]{2,0,1:T(2,128)(2,1)} async-done(((bf16[2,256,3584]{2,0,1:T(2,128)(2,1)}), bf16[2,256,3584]{2,0,1:T(2,128)(2,1)}, u32[]{:S(2)}, u32[]{:S(2)}) %all-to-all-start.5) | async-done | bytes 3670048 | tf_op jit(solution)/shard_map/all_to_all | solution.py:54
  263.0 17.6 %all-to-all-start.4 = ((bf16[16,2,28672]{2,1,0:T(2,128)(2,1)}), bf16[16,2,28672]{2,1,0:T(2,128)(2,1)}, u32[]{:S(2)}, u32[]{:S(2)}) async-start(bf16[16,2,28672]{2,1,0:T(2,128)(2,1)} %reshape.313), calls=%async_computation.4 | async-start | bytes 3670016 | tf_op jit(solution)/shard_map/all_to_all | solution.py:87
  280.6 3.0 gather_fusion.4
  283.5 3.0 gather_fusion.3
  286.5 2.4 pad_maximum_fusion.1
  288.9 5.7 %copy.37 = bf16[2,256,3584]{2,0,1:T(2,128)(2,1)} copy(bf16[2,256,3584]{2,1,0:T(8,128)(2,1)S(1)} %pad_maximum_fusion.1) | data formatting | bytes 7340032 | tf_op jit(solution)/shard_map/stack | solution.py:84
  294.5 22.6 %all-to-all-done.4 = bf16[16,2,28672]{2,1,0:T(2,128)(2,1)} async-done(((bf16[16,2,28672]{2,1,0:T(2,128)(2,1)}), bf16[16,2,28672]{2,1,0:T(2,128)(2,1)}, u32[]{:S(2)}, u32[]{:S(2)}) %all-to-all-start.4) | async-done | bytes 1835040 | tf_op jit(solution)/shard_map/all_to_all | solution.py:87
  317.2 10.2 %all-to-all-start.3 = ((bf16[2,256,3584]{2,0,1:T(2,128)(2,1)}), bf16[2,256,3584]{2,0,1:T(2,128)(2,1)}, u32[]{:S(2)}, u32[]{:S(2)}) async-start(bf16[2,256,3584]{2,0,1:T(2,128)(2,1)} %copy.37), calls=%async_computation.3 | async-start | bytes 7340032 | tf_op jit(solution)/shard_map/all_to_all | solution.py:87
  327.4 9.1 %fusion.51 = (bf16[1,256,3584]{2,0,1:T(2,128)(2,1)}, bf16[1,256,3584]{2,0,1:T(2,128)(2,1)}) fusion(bf16[2,256,3584]{2,0,1:T(2,128)(2,1)} %all-to-all-done.5), kind=kLoop, calls=%fused_computation.112 | loop fusion | bytes 7340032 | tf_op jit(solution)/shard_map/slice | solution.py:114
  336.8 110.9 %psum.7 = f32[2,3584]{1,0:T(2,128)} all-reduce(f32[2,3584]{1,0:T(2,128)S(1)} %convert_reduce_fusion), channel_id=1, replica_groups=mesh['grp'=2,'layer'=16] {'layer'}, use_global_device_ids=true, to_apply=%region_6.7 | all-reduce | flops 7168 | bytes 57344 | tf_op jit(solution)/shard_map/psum | solution.py:78
  447.7 10.3 %reshape.314 = bf16[256,1,3584]{2,1,0:T(2,128)(2,1)} reshape(bf16[16,2,28672]{2,1,0:T(2,128)(2,1)} %all-to-all-done.4) | data formatting | bytes 3670016
  457.9 2.5 fusion.5
  460.4 3.1 fusion.55
  463.5 0.3 copy-done.3
  463.8 0.7 fusion.7
  464.5 8.0 %fusion.52 = (bf16[1,256,3584]{2,0,1:T(2,128)(2,1)S(1)}, bf16[1,256,3584]{2,0,1:T(2,128)(2,1)S(1)}) fusion(bf16[2,256,3584]{2,0,1:T(2,128)(2,1)} %all-to-all-done.3), kind=kLoop, calls=%fused_computation.113 | loop fusion | bytes 7340032 | tf_op jit(solution)/shard_map/slice | solution.py:89
  472.5 0.6 fusion.27
  473.2 0.4 fusion.3
  473.6 0.4 fusion.4
  474.1 0.7 fusion.56
  474.7 1.4 copy-done.2
  476.1 0.7 fusion.6
  476.8 0.6 pad_maximum_fusion.5
  477.4 1.4 pad_maximum_fusion.4
  478.7 1.8 pad_maximum_fusion.2
  (33 shorter events, 1.2 us)
Async XLA Ops:
  55.7 40.5 %all-to-all-start.2 = ((bf16[16,2,28672]{2,1,0:T(2,128)(2,1)}), bf16[16,2,28672]{2,1,0:T(2,128)(2,1)S(1)}, u32[]{:S(2)}, u32[]{:S(2)}) async-start(bf16[16,2,28672]{2,1,0:T(2,128)(2,1)} %reshape.311), calls=%async_computation.2 | async-start | bytes 3670016 | tf_op jit(solution)/shard_map/all_to_all | solution.py:65
  96.2 1.2 copy-start.4
  97.4 79.3 %all-to-all-start.1 = ((bf16[2,256,3584]{2,0,1:T(2,128)(2,1)}), bf16[2,256,3584]{2,0,1:T(2,128)(2,1)}, u32[]{:S(2)}, u32[]{:S(2)}) async-start(bf16[2,256,3584]{2,0,1:T(2,128)(2,1)} %copy.33), calls=%async_computation.1 | async-start | bytes 7340032 | tf_op jit(solution)/shard_map/all_to_all | solution.py:65
  132.3 62.2 %copy-start.8 = (s32[2,128,1]{1,2,0:T(1,128)S(1)}, s32[2,128,1]{1,2,0:T(1,128)}, u32[]{:S(2)}) copy-start(s32[2,128,1]{1,2,0:T(1,128)} %param.9) | copy-start | bytes 3076
  132.3 62.3 %copy-start.7 = (f32[2,3584]{1,0:T(2,128)S(1)}, f32[2,3584]{1,0:T(2,128)}, u32[]{:S(2)}) copy-start(f32[2,3584]{1,0:T(2,128)} %param.11) | copy-start | bytes 86020
  132.3 62.4 %copy-start.5 = (bf16[16,2,28672]{2,1,0:T(2,128)(2,1)S(1)}, bf16[16,2,28672]{2,1,0:T(2,128)(2,1)}, u32[]{:S(2)}) copy-start(bf16[16,2,28672]{2,1,0:T(2,128)(2,1)} %copy-done.4) | copy-start | bytes 5505028
  176.7 86.3 %all-to-all-start.5 = ((bf16[2,256,3584]{2,0,1:T(2,128)(2,1)}), bf16[2,256,3584]{2,0,1:T(2,128)(2,1)}, u32[]{:S(2)}, u32[]{:S(2)}) async-start(bf16[2,256,3584]{2,0,1:T(2,128)(2,1)} %copy.42), calls=%async_computation.5 | async-start | bytes 7340032 | tf_op jit(solution)/shard_map/all_to_all | solution.py:54
  225.1 0.9 copy-start
  263.0 54.2 %all-to-all-start.4 = ((bf16[16,2,28672]{2,1,0:T(2,128)(2,1)}), bf16[16,2,28672]{2,1,0:T(2,128)(2,1)}, u32[]{:S(2)}, u32[]{:S(2)}) async-start(bf16[16,2,28672]{2,1,0:T(2,128)(2,1)} %reshape.313), calls=%async_computation.4 | async-start | bytes 3670016 | tf_op jit(solution)/shard_map/all_to_all | solution.py:87
  317.2 147.4 %all-to-all-start.3 = ((bf16[2,256,3584]{2,0,1:T(2,128)(2,1)}), bf16[2,256,3584]{2,0,1:T(2,128)(2,1)}, u32[]{:S(2)}, u32[]{:S(2)}) async-start(bf16[2,256,3584]{2,0,1:T(2,128)(2,1)} %copy.37), calls=%async_computation.3 | async-start | bytes 7340032 | tf_op jit(solution)/shard_map/all_to_all | solution.py:87
  327.4 9.1 %copy-start.1 = (bf16[1,128,3584]{2,1,0:T(8,128)(2,1)S(1)}, bf16[1,128,3584]{2,1,0:T(8,128)(2,1)}, u32[]{:S(2)}) copy-start(bf16[1,128,3584]{2,1,0:T(8,128)(2,1)} %copy-done) | copy-start | bytes 2752516
  460.4 3.4 copy-start.3
  464.5 8.0 %copy-start.6 = (bf16[3,128,3584]{2,1,0:T(8,128)(2,1)S(1)}, bf16[3,128,3584]{2,1,0:T(8,128)(2,1)}, u32[]{:S(2)}) copy-start(bf16[3,128,3584]{2,1,0:T(8,128)(2,1)} %param.10) | copy-start | bytes 8257540
  474.1 2.0 copy-start.2
where the time goes:
time: 488 us; the launch traced here: 481 us
  local copies, waits for them, and re-layouts  138 us (28%)
  blocking collectives  126 us (26%)
  waiting for transfers between devices  103 us (21%)
  starting transfers between devices  60.2 us (12%)
  other arithmetic  37.8 us (8%)
  matrix products  14.5 us (3%)
    psum x1, blocking collectives, per_device(): lax.psum(jnp.sum(errors.astype(jnp.float32), axis=1), 'layer')  111 us
    all_to_all x4, waiting for transfers between devices, per_device(): lax.all_to_all(stacked, 'layer', split_axis=1, concat_axis=1, tiled=True)  94 us
    all_to_all x4, starting transfers between devices, per_device(): lax.all_to_all(stacked, 'layer', split_axis=1, concat_axis=1, tiled=True)  42.5 us
    unnamed x27, local copies, waits for them, and re-layouts  35.2 us
    unnamed x3, other arithmetic  25.2 us
    gather x4, local copies, waits for them, and re-layouts, row_pick(): return jax.vmap(lambda rows_of, picked: rows_of[picked])(table, chosen)  22.1 us
    all_to_all x1, starting transfers between devices, per_device(): lax.all_to_all(send_resid, 'layer', split_axis=1, concat_axis=1, tiled=True)  17.8 us
    all_to_all x1, blocking collectives, per_device(): lax.all_to_all(send_pre, 'layer', split_axis=1, concat_axis=1, tiled=True)  15.1 us
  transfers between devices with their start and end apart: 5, of which 4 were waited for; matrix products, arithmetic and copies ran while one was open for 27% of the time, Pallas kernels for 0%

commit v1 on v0

v1 whole, which is shorter than its diff:
```python
import math

import jax
import jax.numpy as jnp
from jax import lax
from jax.sharding import PartitionSpec as P

BF = jnp.bfloat16
F32 = jnp.float32


def mm(a, b, dims=((1,), (0,))):
    return lax.dot_general(a, b, (dims, ((), ())), preferred_element_type=F32)


def per_device(residual, mlp_target, pre_acts, blocks, decoder, decoder_bias):
    devices = lax.axis_size("layer")
    layers, tokens, width = residual.shape
    latents = pre_acts.shape[3]
    cap = max(2, 2 * tokens // devices)
    slots = devices * cap
    scale = 1.0 / math.sqrt(tokens)

    def exchange(x):
        return lax.all_to_all(x, "layer", split_axis=0, concat_axis=0, tiled=True)

    routes = blocks.reshape(layers, tokens)
    earlier = jnp.arange(tokens)[:, None] > jnp.arange(tokens)[None, :]
    same = routes[:, :, None] == routes[:, None, :]
    ordinal = jnp.sum((same & earlier).astype(jnp.int32), axis=2)
    slot_of = routes * cap + ordinal
    place = (slot_of[:, None, :] == jnp.arange(slots, dtype=jnp.int32)[None, :, None]).astype(BF)
    place0, place1 = place[0], place[1]
    pre = pre_acts.reshape(layers, tokens, latents)

    first = jnp.concatenate(
        [
            mm(place0, mlp_target[0]).astype(BF),
            mm(place0, pre[0]).astype(BF),
            mm(place1, pre[1]).astype(BF),
        ],
        axis=1,
    )
    first = exchange(first.reshape(devices, cap, width + 2 * latents)).reshape(slots, -1)
    target_in, pre0, pre1 = (
        first[:, :width],
        first[:, width : width + latents],
        first[:, width + latents :],
    )
    act0, act1 = jnp.maximum(pre0, 0), jnp.maximum(pre1, 0)

    def pair_up(a, b):
        return jnp.concatenate(
            [a.reshape(devices, cap, width), b.reshape(devices, cap, width)], axis=1
        )

    def split_up(x):
        return x[:, :cap].reshape(slots, width), x[:, cap:].reshape(slots, width)

    pieces = exchange(
        pair_up(mm(act0, decoder[1]).astype(BF), mm(act1, decoder[2]).astype(BF))
    )
    resid_in = exchange(
        pair_up(mm(place0, residual[0]).astype(BF), mm(place1, residual[1]).astype(BF))
    )

    piece00 = mm(act0, decoder[0]).astype(BF).astype(F32)
    error0 = ((piece00 + decoder_bias[0] - target_in.astype(F32)) * scale).astype(BF)
    empty0 = (decoder_bias[0] * scale).astype(BF).astype(F32)
    empties = float(slots * devices - tokens * devices)

    back0, back1 = split_up(pieces)
    rebuilt = mm(place0, back0, ((0,), (0,))) + mm(place1, back1, ((0,), (0,))) + decoder_bias[1]
    error1 = ((rebuilt - mlp_target[1].astype(F32)) * scale).astype(BF)
    sums = jnp.stack(
        [jnp.sum(error0.astype(F32), axis=0), jnp.sum(error1.astype(F32), axis=0)]
    )
    sums = jnp.sum(lax.all_gather(sums, "layer"), axis=0)
    bias_grad = sums - jnp.stack([empties * empty0, jnp.zeros_like(empty0)])

    errors_in = exchange(
        pair_up(mm(place0, error1).astype(BF), mm(place1, error1).astype(BF))
    )
    error01, error11 = split_up(errors_in)
    resid0, resid1 = split_up(resid_in)

    grad0 = mm(error0, decoder[0], ((1,), (1,))) + mm(error01, decoder[1], ((1,), (1,)))
    grad1 = mm(error11, decoder[2], ((1,), (1,)))
    grad0 = jnp.where(pre0 > 0, grad0, 0.0)
    grad1 = jnp.where(pre1 > 0, grad1, 0.0)
    rows = ((0,), (0,))
    dec = jnp.stack(
        [
            mm(act0, error0, rows).astype(BF),
            mm(act0, error01, rows).astype(BF),
            mm(act1, error11, rows).astype(BF),
        ]
    )
    enc = jnp.stack(
        [
            mm(resid0, grad0.astype(BF), rows).astype(BF),
            mm(resid1, grad1.astype(BF), rows).astype(BF),
        ]
    )
    return dec, enc, jnp.stack([jnp.sum(grad0, axis=0), jnp.sum(grad1, axis=0)]), bias_grad


def solution(mesh):
    return jax.shard_map(
        per_device,
        mesh=mesh,
        in_specs=(
            P(None, ("grp", "layer"), None),
            P(None, ("grp", "layer"), None),
            P(None, ("grp", "layer"), None, None),
            P(None, ("grp", "layer"), None),
            P(None, "layer", None),
            P(),
        ),
        out_specs=(
            P("grp", "layer", None),
            P("grp", None, "layer"),
            P("grp", "layer"),
            P("grp", None),
        ),
        check_vma=False,
    )
```

time: 488 us -> 346 us (0.71)
  the two profiles are of different devices: /device:TPU:0 before, /device:TPU:9 now
where the time goes in v1:
time: 346 us
  waiting for transfers between devices  145 us (42%)
  blocking collectives  137 us (40%)
  matrix products  21.2 us (6%)
  starting transfers between devices  18.6 us (5%)
  other arithmetic  12.7 us (4%)
  local copies, waits for them, and re-layouts  9.78 us (3%)
    all_to_all x3, waiting for transfers between devices, exchange(): return lax.all_to_all(x, 'layer', split_axis=0, concat_axis=0, tiled=True)  145 us
    all_gather x1, blocking collectives, per_device(): sums = jnp.sum(lax.all_gather(sums, 'layer'), axis=0)  85.2 us
    all_to_all x1, blocking collectives, exchange(): return lax.all_to_all(x, 'layer', split_axis=0, concat_axis=0, tiled=True)  51.8 us
    dot_general x20, matrix products, mm(): return lax.dot_general(a, b, (dims, ((), ())), preferred_element_type=F32)  21.2 us
    all_to_all x3, starting transfers between devices, exchange(): return lax.all_to_all(x, 'layer', split_axis=0, concat_axis=0, tiled=True)  18.6 us
    slice x3, local copies, waits for them, and re-layouts, split_up(): return (x[:, :cap].reshape(slots, width), x[:, cap:].reshape(slots, width))  8.27 us
  transfers between devices with their start and end apart: 3, of which 2 were waited for; matrix products, arithmetic and copies ran while one was open for 6% of the time, Pallas kernels for 0%

profile of v1, /device:TPU:9, one launch (start us, length us, event | category | flops | bytes accessed | tf_op | source)
XLA Modules:
  0.0 345.6 jit_solution(8242741920131213639)
XLA Ops:
  0.7 0.9 convert_reduce_fusion.2
  1.6 0.7 multiply_add_fusion
  2.3 0.9 convolution_convert_fusion.14
  3.2 0.9 convolution_convert_fusion.13
  4.2 1.8 convolution_convert_fusion.7
  6.0 0.1 pad_maximum_fusion.4
  6.1 0.0 copy-start.4
  6.1 51.8 %all_to_all.20 = bf16[16,16,3840]{2,1,0:T(8,128)(2,1)S(1)} all-to-all(bf16[16,16,3840]{2,1,0:T(8,128)(2,1)S(1)} %bitcast.97), channel_id=1, replica_groups=mesh['grp'=2,'layer'=16] {'layer'}, dimensions={0} | all-to-all | bytes 3932160 | tf_op jit(solution)/shard_map/all_to_all | solution.py:25
  57.9 0.0 copy-start.1
  57.9 0.0 copy-done.4
  57.9 0.6 convolution_convert_fusion.5
  58.5 0.6 convolution_convert_fusion.4
  59.2 2.0 pad_maximum_fusion
  61.2 4.4 %all-to-all-start.1 = ((bf16[16,32,3584]{2,1,0:T(8,128)(2,1)}), bf16[16,32,3584]{2,1,0:T(8,128)(2,1)}, u32[]{:S(2)}, u32[]{:S(2)}) async-start(bf16[16,32,3584]{2,1,0:T(8,128)(2,1)} %pad_maximum_fusion), calls=%async_computation.1 | async-start | bytes 7340032 | tf_op jit(solution)/shard_map/all_to_all | solution.py:25
  65.6 0.0 copy-start.2
  65.6 1.9 convolution_convert_fusion.1
  67.6 0.0 copy-done.2
  67.6 0.6 convolution_convert_fusion
  68.2 2.1 pad_maximum_fusion.2
  70.3 0.0 copy-start.6
  70.3 74.4 %all-to-all-done.1 = bf16[16,32,3584]{2,1,0:T(8,128)(2,1)} async-done(((bf16[16,32,3584]{2,1,0:T(8,128)(2,1)}), bf16[16,32,3584]{2,1,0:T(8,128)(2,1)}, u32[]{:S(2)}, u32[]{:S(2)}) %all-to-all-start.1) | async-done | bytes 3670048 | tf_op jit(solution)/shard_map/all_to_all | solution.py:25
  144.7 7.1 %all-to-all-start.3 = ((bf16[16,32,3584]{2,1,0:T(8,128)(2,1)}), bf16[16,32,3584]{2,1,0:T(8,128)(2,1)}, u32[]{:S(2)}, u32[]{:S(2)}) async-start(bf16[16,32,3584]{2,1,0:T(8,128)(2,1)} %pad_maximum_fusion.2), calls=%async_computation.3 | async-start | bytes 7340032 | tf_op jit(solution)/shard_map/all_to_all | solution.py:25
  151.8 0.0 copy-done.6
  151.8 0.1 slice_reduce_fusion.1
  151.9 2.3 fusion.51
  154.2 0.0 copy-start.3
  154.2 0.5 fusion.42
  154.6 1.0 copy-done.3
  155.7 0.7 convert_reduce_fusion.1
  156.4 0.6 convolution_convert_fusion.2
  157.0 0.6 convolution_convert_fusion.3
  157.7 2.1 pad_maximum_fusion.1
  159.8 71.0 %all-to-all-done.3 = bf16[16,32,3584]{2,1,0:T(8,128)(2,1)} async-done(((bf16[16,32,3584]{2,1,0:T(8,128)(2,1)}), bf16[16,32,3584]{2,1,0:T(8,128)(2,1)}, u32[]{:S(2)}, u32[]{:S(2)}) %all-to-all-start.3) | async-done | bytes 3670048 | tf_op jit(solution)/shard_map/all_to_all | solution.py:25
  230.8 7.1 %all-to-all-start.2 = ((bf16[16,32,3584]{2,1,0:T(8,128)(2,1)}), bf16[16,32,3584]{2,1,0:T(8,128)(2,1)}, u32[]{:S(2)}, u32[]{:S(2)}) async-start(bf16[16,32,3584]{2,1,0:T(8,128)(2,1)} %pad_maximum_fusion.1), calls=%async_computation.2 | async-start | bytes 7340032 | tf_op jit(solution)/shard_map/all_to_all | solution.py:25
  237.9 2.0 convert_reduce_fusion
  240.0 0.0 copy-done.1
  240.0 0.4 fusion.9
  240.4 1.8 fusion.21
  242.2 3.5 %fusion.49 = (bf16[16,16,3584]{2,1,0:T(8,128)(2,1)S(1)}, bf16[16,16,3584]{2,1,0:T(8,128)(2,1)}) fusion(bf16[16,32,3584]{2,1,0:T(8,128)(2,1)} %all-to-all-done.3), kind=kLoop, calls=%fused_computation.89 | loop fusion | bytes 7340032 | tf_op jit(solution)/shard_map/slice | solution.py:58
  245.8 85.2 %all-gather.1 = f32[16,2,3584]{2,1,0:T(2,128)S(1)} all-gather(f32[1,2,3584]{2,1,0:T(2,128)S(1)} %maximum_bitcast_fusion), channel_id=2, replica_groups=mesh['grp'=2,'layer'=16] {'layer'}, dimensions={0}, use_global_device_ids=true | all-gather | bytes 487424 | tf_op jit(solution)/shard_map/all_gather | solution.py:78
  331.1 0.1 reduce_sum.59
  331.2 0.6 pad_subtract_fusion
  331.8 0.0 all-to-all-done.2
  331.8 0.0 copy-start.5
  331.8 2.4 fusion.50
  334.3 0.4 copy-done.5
  334.7 1.5 fusion.52
  336.2 1.3 fusion.11
  337.5 1.3 fusion.10
  338.7 0.0 copy-start
  338.8 1.6 fusion.53
  340.4 0.0 copy-done
  340.4 0.7 fusion.13
  341.1 0.7 fusion.12
  341.8 0.6 pad_maximum_fusion.6
  342.4 1.4 pad_maximum_fusion.5
  343.8 1.8 pad_maximum_fusion.3
  (5 shorter events, 0.1 us)
Async XLA Ops:
  6.1 51.8 %copy-start.4 = (bf16[3,128,3584]{2,1,0:T(8,128)(2,1)S(1)}, bf16[3,128,3584]{2,1,0:T(8,128)(2,1)}, u32[]{:S(2)}) copy-start(bf16[3,128,3584]{2,1,0:T(8,128)(2,1)} %param.10) | copy-start | bytes 8257540
  57.9 182.1 %copy-start.1 = (bf16[16,16,3840]{2,1,0:T(8,128)(2,1)}, bf16[16,16,3840]{2,1,0:T(8,128)(2,1)S(1)}, u32[]{:S(2)}) copy-start(bf16[16,16,3840]{2,1,0:T(8,128)(2,1)S(1)} %all_to_all.20) | copy-start | bytes 5898244
  61.2 83.5 %all-to-all-start.1 = ((bf16[16,32,3584]{2,1,0:T(8,128)(2,1)}), bf16[16,32,3584]{2,1,0:T(8,128)(2,1)}, u32[]{:S(2)}, u32[]{:S(2)}) async-start(bf16[16,32,3584]{2,1,0:T(8,128)(2,1)} %pad_maximum_fusion), calls=%async_computation.1 | async-start | bytes 7340032 | tf_op jit(solution)/shard_map/all_to_all | solution.py:25
  65.6 1.9 copy-start.2
  70.3 81.5 %copy-start.6 = (f32[2,3584]{1,0:T(2,128)S(1)}, f32[2,3584]{1,0:T(2,128)}, u32[]{:S(2)}) copy-start(f32[2,3584]{1,0:T(2,128)} %param.11) | copy-start | bytes 86020
  144.7 86.1 %all-to-all-start.3 = ((bf16[16,32,3584]{2,1,0:T(8,128)(2,1)}), bf16[16,32,3584]{2,1,0:T(8,128)(2,1)}, u32[]{:S(2)}, u32[]{:S(2)}) async-start(bf16[16,32,3584]{2,1,0:T(8,128)(2,1)} %pad_maximum_fusion.2), calls=%async_computation.3 | async-start | bytes 7340032 | tf_op jit(solution)/shard_map/all_to_all | solution.py:25
  154.2 1.5 copy-start.3
  230.8 101.0 %all-to-all-start.2 = ((bf16[16,32,3584]{2,1,0:T(8,128)(2,1)}), bf16[16,32,3584]{2,1,0:T(8,128)(2,1)}, u32[]{:S(2)}, u32[]{:S(2)}) async-start(bf16[16,32,3584]{2,1,0:T(8,128)(2,1)} %pad_maximum_fusion.1), calls=%async_computation.2 | async-start | bytes 7340032 | tf_op jit(solution)/shard_map/all_to_all | solution.py:25
  331.8 2.9 copy-start.5
  338.7 1.6 copy-start

commit v2 on v1

v2 whole, which is shorter than its diff:
```python
import math

import jax
import jax.numpy as jnp
from jax import lax
from jax.sharding import PartitionSpec as P

BF = jnp.bfloat16
F32 = jnp.float32
ROWS = ((0,), (0,))
LAST = ((1,), (1,))


def mm(a, b, dims=((1,), (0,))):
    return lax.dot_general(a, b, (dims, ((), ())), preferred_element_type=F32)


def per_device(residual, mlp_target, pre_acts, blocks, decoder, decoder_bias):
    devices = lax.axis_size("layer")
    layers, tokens, width = residual.shape
    latents = pre_acts.shape[3]
    cap = max(2, 2 * tokens // devices)
    slots = devices * cap
    half = devices // 2
    scale = 1.0 / math.sqrt(tokens)
    me = lax.axis_index("layer")
    upper = me >= half
    mirror = [(i, (i + half) % devices) for i in range(devices)]
    halves = [list(range(half)), list(range(half, devices))]

    def everyone(x):
        return lax.all_to_all(x, "layer", split_axis=0, concat_axis=0, tiled=True)

    def within(x):
        return lax.all_to_all(
            x, "layer", split_axis=0, concat_axis=0, tiled=True, axis_index_groups=halves
        )

    def across(x):
        return lax.ppermute(x, "layer", mirror)

    def turn(x):
        first, second = x[: x.shape[0] // 2], x[x.shape[0] // 2 :]
        return jnp.concatenate(
            [jnp.where(upper, second, first), jnp.where(upper, first, second)], axis=0
        )

    routes = blocks.reshape(layers, tokens)
    earlier = jnp.arange(tokens)[:, None] > jnp.arange(tokens)[None, :]

    def ordinals(named):
        same = named[:, :, None] == named[:, None, :]
        return jnp.sum((same & earlier).astype(jnp.int32), axis=2)

    routes_m = across(routes)
    pre = pre_acts.reshape(layers, tokens, latents)
    resid1_m = across(residual[1])

    order = ordinals(routes)
    slot_of = routes * cap + order
    place = (slot_of[:, None, :] == jnp.arange(slots, dtype=jnp.int32)[None, :, None]).astype(BF)

    def pair_places(named, order, base):
        block = base + jnp.arange(half, dtype=jnp.int32)[:, None, None, None]
        slot = jnp.arange(cap, dtype=jnp.int32)[None, None, :, None]
        hit = (named[None, :, None, :] == block) & (order[None, :, None, :] == slot)
        return hit.astype(BF).reshape(half, layers, cap, tokens)

    base = jnp.where(upper, half, 0).astype(jnp.int32)
    place_o = pair_places(routes, order, base)
    place_m = pair_places(routes_m, ordinals(routes_m), base)

    def flat(p):
        return p.reshape(-1, p.shape[-1])

    sent_pre = jnp.stack(
        [mm(place[l], pre[l]).astype(BF).reshape(devices, cap, latents) for l in range(layers)],
        axis=1,
    )
    got_pre = everyone(sent_pre.reshape(devices, layers * cap, latents))
    got_pre = got_pre.reshape(devices, layers, cap, latents)
    pre0 = got_pre[:, 0].reshape(slots, latents)
    pre1 = got_pre[:, 1].reshape(slots, latents)
    act0 = jnp.maximum(pre0, 0)

    acts = turn(jnp.maximum(got_pre, 0))
    nothing = jnp.zeros((devices, 1, cap, latents), BF)
    wide = jnp.concatenate(
        [
            jnp.concatenate([acts[:, 0:1], nothing], axis=3),
            jnp.concatenate([nothing, acts[:, 1:2]], axis=3),
        ],
        axis=1,
    ).reshape(devices, layers * cap, 2 * latents)
    dec1 = decoder[1:3].reshape(2 * latents, width)

    def decode(rows):
        return mm(rows.reshape(-1, 2 * latents), dec1).astype(BF).reshape(half, -1, width)

    pieces_m = within(decode(wide[half:])).reshape(-1, width)
    sum_m = mm(flat(place_m), pieces_m, ROWS)
    sum_low = across(sum_m.astype(BF))
    pieces_o = within(decode(wide[:half])).reshape(-1, width)
    sum_o = mm(flat(place_o), pieces_o, ROWS) + decoder_bias[1] - mlp_target[1].astype(F32)
    sum_high = across(sum_o.astype(BF))

    error1 = ((sum_o + sum_low.astype(F32)) * scale).astype(BF)
    error1_m = ((sum_m + sum_high.astype(F32)) * scale).astype(BF)

    def send_errors(p, error):
        return within(mm(flat(p), error).astype(BF).reshape(half, layers * cap, width))

    resid1_in = within(
        jnp.concatenate(
            [
                mm(flat(place_o[:, 1]), residual[1]).astype(BF).reshape(half, cap, width),
                mm(flat(place_m[:, 1]), resid1_m).astype(BF).reshape(half, cap, width),
            ],
            axis=1,
        )
    )
    errors_o = send_errors(place_o, error1)
    errors_m = send_errors(place_m, error1_m)

    layer0 = everyone(
        jnp.concatenate(
            [
                mm(place[0], mlp_target[0]).astype(BF).reshape(devices, cap, width),
                mm(place[0], residual[0]).astype(BF).reshape(devices, cap, width),
            ],
            axis=1,
        )
    )
    target0 = layer0[:, :cap].reshape(slots, width)
    resid0 = layer0[:, cap:].reshape(slots, width)
    piece00 = mm(act0, decoder[0]).astype(BF).astype(F32)
    error0 = ((piece00 + decoder_bias[0] - target0.astype(F32)) * scale).astype(BF)
    empty0 = (decoder_bias[0] * scale).astype(BF).astype(F32)
    empties = float(slots * devices - tokens * devices)

    def total(x):
        step = 1
        while step < devices:
            x = x + lax.ppermute(x, "layer", [(i, i ^ step) for i in range(devices)])
            step *= 2
        return x

    bias_grad = jnp.stack(
        [
            total(jnp.sum(error0.astype(F32), axis=0)[None])[0] - empties * empty0,
            total(jnp.sum(error1.astype(F32), axis=0)[None])[0],
        ]
    )

    wide_o = wide[:half].reshape(-1, 2 * latents)
    wide_m = wide[half:].reshape(-1, 2 * latents)
    errors_o = errors_o.reshape(-1, width)
    errors_m = errors_m.reshape(-1, width)
    dec_later = mm(wide_o, errors_o, ROWS) + mm(wide_m, errors_m, ROWS)
    back = jnp.concatenate([mm(errors_o, dec1, LAST), mm(errors_m, dec1, LAST)], axis=0)
    back = back.reshape(devices, layers, cap, 2 * latents)
    pres = turn(got_pre)
    grad1 = jnp.where(pres[:, 1] > 0, back[:, 1, :, latents:], 0.0)
    grad0 = turn(back[:, 0, :, :latents]).reshape(slots, latents) + mm(error0, decoder[0], LAST)
    grad0 = jnp.where(pre0 > 0, grad0, 0.0)
    low1 = grad1.astype(BF).reshape(2, half, cap, latents).swapaxes(0, 1).reshape(slots, latents)
    dec = jnp.concatenate(
        [mm(act0, error0, ROWS).astype(BF)[None], dec_later.astype(BF).reshape(2, latents, width)]
    )
    enc = jnp.stack(
        [
            mm(resid0, grad0.astype(BF), ROWS).astype(BF),
            mm(resid1_in.reshape(slots, width), low1, ROWS).astype(BF),
        ]
    )
    enc_bias = jnp.stack([jnp.sum(grad0, axis=0), jnp.sum(grad1, axis=(0, 1))])
    return dec, enc, enc_bias, bias_grad


def solution(mesh):
    return jax.shard_map(
        per_device,
        mesh=mesh,
        in_specs=(
            P(None, ("grp", "layer"), None),
            P(None, ("grp", "layer"), None),
            P(None, ("grp", "layer"), None, None),
            P(None, ("grp", "layer"), None),
            P(None, "layer", None),
            P(),
        ),
        out_specs=(
            P("grp", "layer", None),
            P("grp", None, "layer"),
            P("grp", "layer"),
            P("grp", None),
        ),
        check_vma=False,
    )
```

time: 346 us -> 379 us (1.095)
  the two profiles are of different devices: /device:TPU:9 before, /device:TPU:0 now
where the time goes in v2:
time: 379 us; the launch traced here: 378 us
  waiting for transfers between devices  266 us (70%)
  starting transfers between devices  51.7 us (14%)
  matrix products  38.9 us (10%)
  other arithmetic  10.8 us (3%)
  local copies, waits for them, and re-layouts  9.56 us (3%)
    ppermute x4, waiting for transfers between devices, across(): return lax.ppermute(x, 'layer', mirror)  194 us
    all_to_all x5, waiting for transfers between devices, within(): lax.all_to_all(x, 'layer', split_axis=0, concat_axis=0, tiled=True, axis_...  48 us
    dot_general x21, matrix products, mm(): return lax.dot_general(a, b, (dims, ((), ())), preferred_element_type=F32)  38.9 us
    all_to_all x5, starting transfers between devices, within(): lax.all_to_all(x, 'layer', split_axis=0, concat_axis=0, tiled=True, axis_...  21.8 us
    ppermute x8, waiting for transfers between devices, total(): x = x + lax.ppermute(x, 'layer', [(i, i ^ step) for i in range(devices)])  18.1 us
    all_to_all x2, starting transfers between devices, everyone(): return lax.all_to_all(x, 'layer', split_axis=0, concat_axis=0, tiled=True)  10.7 us
    ppermute x8, starting transfers between devices, total(): x = x + lax.ppermute(x, 'layer', [(i, i ^ step) for i in range(devices)])  9.75 us
    ppermute x4, starting transfers between devices, across(): return lax.ppermute(x, 'layer', mirror)  9.46 us
  transfers between devices with their start and end apart: 19, of which 10 were waited for; matrix products, arithmetic and copies ran while one was open for 12% of the time, Pallas kernels for 0%

profile of v2, /device:TPU:0, one launch (start us, length us, event | category | flops | bytes accessed | tf_op | source)
XLA Modules:
  0.0 378.0 jit_solution(6610917469549316457)
XLA Ops:
  0.6 4.1 %collective-permute-start = (s32[2,128]{1,0:T(2,128)}, s32[2,128]{1,0:T(2,128)S(1)}, u32[]{:S(2)}, u32[]{:S(2)}) collective-permute-start(s32[2,128]{1,0:T(2,128)} %bitcast.193), channel_id=1, source_target_pairs={{0,8},{1,9},{2,10},{3,11},{4,12},{5,13},{6,14},{7,15},{8,0},{9,1},... | collective-permute-start | bytes 3080 | tf_op jit(solution)/shard_map/ppermute | solution.py:40
  4.8 1.7 collective-permute-done
  6.5 1.0 convert_reduce_fusion.2
  7.5 0.7 multiply_add_fusion
  8.2 0.9 convolution_convert_fusion.13
  9.1 0.9 convolution_convert_fusion.12
  10.1 0.7 pad_maximum_fusion.5
  10.7 6.2 %all-to-all-start = ((bf16[16,32,128]{2,1,0:T(8,128)(2,1)}), bf16[16,32,128]{2,1,0:T(8,128)(2,1)S(1)}, u32[]{:S(2)}, u32[]{:S(2)}) async-start(bf16[16,32,128]{2,1,0:T(8,128)(2,1)} %bitcast.9), calls=%async_computation | async-start | bytes 262144 | tf_op jit(solution)/shard_map/all_to_all | solution.py:32
  17.0 1.6 slice.120
  18.6 6.3 %all-to-all-done = bf16[16,32,128]{2,1,0:T(8,128)(2,1)S(1)} async-done(((bf16[16,32,128]{2,1,0:T(8,128)(2,1)}), bf16[16,32,128]{2,1,0:T(8,128)(2,1)S(1)}, u32[]{:S(2)}, u32[]{:S(2)}) %all-to-all-start) | async-done | bytes 131104 | tf_op jit(solution)/shard_map/all_to_all | solution.py:32
  25.0 1.9 convolution_convert_fusion.5
  26.9 4.3 %all-to-all-start.3 = ((bf16[8,32,3584]{2,1,0:T(8,128)(2,1)}), bf16[8,32,3584]{2,1,0:T(8,128)(2,1)}, u32[]{:S(2)}, u32[]{:S(2)}) async-start(bf16[8,32,3584]{2,1,0:T(8,128)(2,1)} %bitcast.159), calls=%async_computation.3 | async-start | bytes 3670016 | tf_op jit(solution)/shard_map/all_to_all | solution.py:35
  31.2 1.9 convolution_convert_fusion.6
  33.1 21.0 %all-to-all-done.3 = bf16[8,32,3584]{2,1,0:T(8,128)(2,1)} async-done(((bf16[8,32,3584]{2,1,0:T(8,128)(2,1)}), bf16[8,32,3584]{2,1,0:T(8,128)(2,1)}, u32[]{:S(2)}, u32[]{:S(2)}) %all-to-all-start.3) | async-done | bytes 1835040 | tf_op jit(solution)/shard_map/all_to_all | solution.py:35
  54.1 4.3 %all-to-all-start.2 = ((bf16[8,32,3584]{2,1,0:T(8,128)(2,1)}), bf16[8,32,3584]{2,1,0:T(8,128)(2,1)}, u32[]{:S(2)}, u32[]{:S(2)}) async-start(bf16[8,32,3584]{2,1,0:T(8,128)(2,1)} %bitcast.158), calls=%async_computation.2 | async-start | bytes 3670016 | tf_op jit(solution)/shard_map/all_to_all | solution.py:35
  58.5 1.9 convolution_convert_fusion.3
  60.4 0.6 convolution_convert_fusion.2
  61.0 2.1 pad_maximum_fusion
  63.1 18.2 %all-to-all-done.2 = bf16[8,32,3584]{2,1,0:T(8,128)(2,1)} async-done(((bf16[8,32,3584]{2,1,0:T(8,128)(2,1)}), bf16[8,32,3584]{2,1,0:T(8,128)(2,1)}, u32[]{:S(2)}, u32[]{:S(2)}) %all-to-all-start.2) | async-done | bytes 1835040 | tf_op jit(solution)/shard_map/all_to_all | solution.py:35
  81.3 4.5 %all-to-all-start.1 = ((bf16[16,32,3584]{2,1,0:T(8,128)(2,1)}), bf16[16,32,3584]{2,1,0:T(8,128)(2,1)}, u32[]{:S(2)}, u32[]{:S(2)}) async-start(bf16[16,32,3584]{2,1,0:T(8,128)(2,1)} %pad_maximum_fusion), calls=%async_computation.1 | async-start | bytes 7340032 | tf_op jit(solution)/shard_map/all_to_all | solution.py:32
  85.9 0.1 broadcast_compare_fusion
  86.0 3.3 fusion.41
  89.4 2.7 collective-permute-start.1
  92.0 0.1 slice_reduce_fusion.1
  92.1 115.7 %collective-permute-done.1 = bf16[128,3584]{1,0:T(8,128)(2,1)S(1)} collective-permute-done((bf16[128,3584]{1,0:T(8,128)(2,1)S(1)}, bf16[128,3584]{1,0:T(8,128)(2,1)S(1)}, u32[]{:S(2)}, u32[]{:S(2)}) %collective-permute-start.1) | collective-permute-done | bytes 917536 | tf_op jit(solution)/shard_map/ppermute | solution.py:40
  207.9 3.2 convert_reduce_fusion.1
  211.0 1.9 convolution_convert_fusion.1
  212.9 4.3 %all-to-all-start.4 = ((bf16[8,32,3584]{2,1,0:T(8,128)(2,1)}), bf16[8,32,3584]{2,1,0:T(8,128)(2,1)}, u32[]{:S(2)}, u32[]{:S(2)}) async-start(bf16[8,32,3584]{2,1,0:T(8,128)(2,1)} %bitcast.155), calls=%async_computation.4 | async-start | bytes 3670016 | tf_op jit(solution)/shard_map/all_to_all | solution.py:35
  217.3 2.3 slice_bitcast_fusion
  219.6 1.6 convolution_convert_fusion.9
  221.2 0.4 collective-permute-start.8
  221.6 2.7 collective-permute-start.2
  224.3 1.9 collective-permute-start.9
  226.3 76.1 %collective-permute-done.2 = bf16[128,3584]{1,0:T(8,128)(2,1)S(1)} collective-permute-done((bf16[128,3584]{1,0:T(8,128)(2,1)S(1)}, bf16[128,3584]{1,0:T(8,128)(2,1)S(1)}, u32[]{:S(2)}, u32[]{:S(2)}) %collective-permute-start.2) | collective-permute-done | bytes 917536 | tf_op jit(solution)/shard_map/ppermute | solution.py:40
  302.3 1.9 convolution_convert_fusion
  304.2 4.2 %fusion.39 = (bf16[16,16,3584]{2,1,0:T(8,128)(2,1)}, bf16[16,16,3584]{2,1,0:T(8,128)(2,1)}) fusion(bf16[16,32,3584]{2,1,0:T(8,128)(2,1)} %all-to-all-done.1), kind=kLoop, calls=%fused_computation.101 | loop fusion | bytes 7340032 | tf_op jit(solution)/shard_map/slice | solution.py:135
  308.4 4.3 %all-to-all-start.5 = ((bf16[8,32,3584]{2,1,0:T(8,128)(2,1)}), bf16[8,32,3584]{2,1,0:T(8,128)(2,1)}, u32[]{:S(2)}, u32[]{:S(2)}) async-start(bf16[8,32,3584]{2,1,0:T(8,128)(2,1)} %bitcast.154), calls=%async_computation.5 | async-start | bytes 3670016 | tf_op jit(solution)/shard_map/all_to_all | solution.py:35
  312.7 2.7 convert_reduce_fusion
  315.4 0.4 collective-permute-start.4
  315.9 1.8 collective-permute-start.10
  317.7 1.5 collective-permute-start.5
  319.2 1.6 convolution_convert_fusion.8
  320.8 15.0 %collective-permute-done.10 = f32[1,3584]{1,0:T(1,128)S(1)} collective-permute-done((f32[1,3584]{1,0:T(1,128)S(1)}, f32[1,3584]{1,0:T(1,128)S(1)}, u32[]{:S(2)}, u32[]{:S(2)}) %collective-permute-start.10) | collective-permute-done | bytes 14368 | tf_op jit(solution)/shard_map/ppermute | solution.py:144
  335.8 0.1 collective-permute-start.11
  335.9 1.4 collective-permute-start.6
  337.4 1.4 pad_maximum_fusion.2
  338.7 1.8 collective-permute-done.11
  340.6 2.1 collective-permute-start.7
  342.7 1.4 fusion.7
  344.1 1.3 collective-permute-done.7
  345.4 4.5 %all-to-all-start.6 = ((bf16[8,32,3584]{2,1,0:T(8,128)(2,1)}), bf16[8,32,3584]{2,1,0:T(8,128)(2,1)}, u32[]{:S(2)}, u32[]{:S(2)}) async-start(bf16[8,32,3584]{2,1,0:T(8,128)(2,1)} %pad_maximum_fusion.2), calls=%async_computation.6 | async-start | bytes 3670016 | tf_op jit(solution)/shard_map/all_to_all | solution.py:35
  349.9 0.6 pad_maximum_fusion.8
  350.6 2.2 fusion.44
  352.7 2.2 fusion.43
  354.9 2.2 fusion.45
  357.3 1.3 copy-done.6
  358.6 1.8 fusion.42
  360.4 0.6 pad_maximum_fusion.9
  361.0 0.7 fusion.8
  361.7 2.2 fusion.5
  363.9 8.8 %all-to-all-done.6 = bf16[8,32,3584]{2,1,0:T(8,128)(2,1)} async-done(((bf16[8,32,3584]{2,1,0:T(8,128)(2,1)}), bf16[8,32,3584]{2,1,0:T(8,128)(2,1)}, u32[]{:S(2)}, u32[]{:S(2)}) %all-to-all-start.6) | async-done | bytes 1835040 | tf_op jit(solution)/shard_map/all_to_all | solution.py:35
  372.6 2.2 fusion.9
  374.8 1.4 pad_maximum_fusion.3
  376.2 1.8 pad_maximum_fusion.1
  (63 shorter events, 0.7 us)
Async XLA Ops:
  0.6 5.9 %collective-permute-start = (s32[2,128]{1,0:T(2,128)}, s32[2,128]{1,0:T(2,128)S(1)}, u32[]{:S(2)}, u32[]{:S(2)}) collective-permute-start(s32[2,128]{1,0:T(2,128)} %bitcast.193), channel_id=1, source_target_pairs={{0,8},{1,9},{2,10},{3,11},{4,12},{5,13},{6,14},{7,15},{8,0},{9,1},... | collective-permute-start | bytes 3080 | tf_op jit(solution)/shard_map/ppermute | solution.py:40
  10.7 14.2 %all-to-all-start = ((bf16[16,32,128]{2,1,0:T(8,128)(2,1)}), bf16[16,32,128]{2,1,0:T(8,128)(2,1)S(1)}, u32[]{:S(2)}, u32[]{:S(2)}) async-start(bf16[16,32,128]{2,1,0:T(8,128)(2,1)} %bitcast.9), calls=%async_computation | async-start | bytes 262144 | tf_op jit(solution)/shard_map/all_to_all | solution.py:32
  26.9 27.2 %all-to-all-start.3 = ((bf16[8,32,3584]{2,1,0:T(8,128)(2,1)}), bf16[8,32,3584]{2,1,0:T(8,128)(2,1)}, u32[]{:S(2)}, u32[]{:S(2)}) async-start(bf16[8,32,3584]{2,1,0:T(8,128)(2,1)} %bitcast.159), calls=%async_computation.3 | async-start | bytes 3670016 | tf_op jit(solution)/shard_map/all_to_all | solution.py:35
  54.1 27.2 %all-to-all-start.2 = ((bf16[8,32,3584]{2,1,0:T(8,128)(2,1)}), bf16[8,32,3584]{2,1,0:T(8,128)(2,1)}, u32[]{:S(2)}, u32[]{:S(2)}) async-start(bf16[8,32,3584]{2,1,0:T(8,128)(2,1)} %bitcast.158), calls=%async_computation.2 | async-start | bytes 3670016 | tf_op jit(solution)/shard_map/all_to_all | solution.py:35
  58.4 2.0 copy-start.2
  63.1 22.8 %copy-start.9 = (s32[2,128,1]{1,2,0:T(1,128)S(1)}, s32[2,128,1]{1,2,0:T(1,128)}, u32[]{:S(2)}) copy-start(s32[2,128,1]{1,2,0:T(1,128)} %param.9) | copy-start | bytes 3076
  81.3 131.6 %all-to-all-start.1 = ((bf16[16,32,3584]{2,1,0:T(8,128)(2,1)}), bf16[16,32,3584]{2,1,0:T(8,128)(2,1)}, u32[]{:S(2)}, u32[]{:S(2)}) async-start(bf16[16,32,3584]{2,1,0:T(8,128)(2,1)} %pad_maximum_fusion), calls=%async_computation.1 | async-start | bytes 7340032 | tf_op jit(solution)/shard_map/all_to_all | solution.py:32
  86.0 6.0 %copy-start.8 = (f32[2,3584]{1,0:T(2,128)S(1)}, f32[2,3584]{1,0:T(2,128)}, u32[]{:S(2)}) copy-start(f32[2,3584]{1,0:T(2,128)} %param.11) | copy-start | bytes 86020
  86.0 121.8 %copy-start.4 = (bf16[2,128,3584]{2,1,0:T(8,128)(2,1)S(1)}, bf16[2,128,3584]{2,1,0:T(8,128)(2,1)}, u32[]{:S(2)}) copy-start(bf16[2,128,3584]{2,1,0:T(8,128)(2,1)} %param.7) | copy-start | bytes 5505028
  89.4 118.5 %collective-permute-start.1 = (bf16[128,3584]{1,0:T(8,128)(2,1)S(1)}, bf16[128,3584]{1,0:T(8,128)(2,1)S(1)}, u32[]{:S(2)}, u32[]{:S(2)}) collective-permute-start(bf16[128,3584]{1,0:T(8,128)(2,1)S(1)} %get-tuple-element.20), channel_id=1, source_target_pairs={{0,8},{1,9},{2,10},{3,11},{4,12},{5,13},{6,14},{7,15},{8,0},{9,1},... | collective-permute-start | bytes 2752520 | tf_op jit(solution)/shard_map/ppermute | solution.py:40
  212.9 95.5 %all-to-all-start.4 = ((bf16[8,32,3584]{2,1,0:T(8,128)(2,1)}), bf16[8,32,3584]{2,1,0:T(8,128)(2,1)}, u32[]{:S(2)}, u32[]{:S(2)}) async-start(bf16[8,32,3584]{2,1,0:T(8,128)(2,1)} %bitcast.155), calls=%async_computation.4 | async-start | bytes 3670016 | tf_op jit(solution)/shard_map/all_to_all | solution.py:35
  217.2 4.4 %copy-start.7 = (bf16[128,3584]{1,0:T(8,128)(2,1)S(1)}, bf16[128,3584]{1,0:T(8,128)(2,1)}, u32[]{:S(2)}) copy-start(bf16[128,3584]{1,0:T(8,128)(2,1)} %get-tuple-element.11) | copy-start | bytes 2752516
  217.2 85.1 %copy-start.1 = (f32[128,3584]{1,0:T(8,128)S(1)}, f32[128,3584]{1,0:T(8,128)}, u32[]{:S(2)}) copy-start(f32[128,3584]{1,0:T(8,128)} %get-tuple-element.21) | copy-start | bytes 5505028
  219.6 99.7 %collective-permute-start.3 = (bf16[128,3584]{1,0:T(8,128)(2,1)}, bf16[128,3584]{1,0:T(8,128)(2,1)}, u32[]{:S(2)}, u32[]{:S(2)}) collective-permute-start(bf16[128,3584]{1,0:T(8,128)(2,1)} %slice_bitcast_fusion), channel_id=1, source_target_pairs={{0,8},{1,9},{2,10},{3,11},{4,12},{5,13},{6,14},{7,15},{8,0},{9,1},... | collective-permute-start | bytes 2752520 | tf_op jit(solution)/shard_map/ppermute | solution.py:40
  221.2 3.1 collective-permute-start.8
  221.6 80.7 %collective-permute-start.2 = (bf16[128,3584]{1,0:T(8,128)(2,1)S(1)}, bf16[128,3584]{1,0:T(8,128)(2,1)S(1)}, u32[]{:S(2)}, u32[]{:S(2)}) collective-permute-start(bf16[128,3584]{1,0:T(8,128)(2,1)S(1)} %copy-done.7), channel_id=1, source_target_pairs={{0,8},{1,9},{2,10},{3,11},{4,12},{5,13},{6,14},{7,15},{8,0},{9,1},... | collective-permute-start | bytes 2752520 | tf_op jit(solution)/shard_map/ppermute | solution.py:40
  224.3 91.5 %collective-permute-start.9 = (f32[1,3584]{1,0:T(1,128)S(1)}, f32[1,3584]{1,0:T(1,128)S(1)}, u32[]{:S(2)}, u32[]{:S(2)}) collective-permute-start(f32[1,3584]{1,0:T(1,128)S(1)} %reshape_add_fusion.1), channel_id=1, source_target_pairs={{0,2},{1,3},{2,0},{3,1},{4,6},{5,7},{6,4},{7,5},{8,10},{9,11},{10,... | collective-permute-start | bytes 43016 | tf_op jit(solution)/shard_map/ppermute | solution.py:144
  308.4 37.0 %all-to-all-start.5 = ((bf16[8,32,3584]{2,1,0:T(8,128)(2,1)}), bf16[8,32,3584]{2,1,0:T(8,128)(2,1)}, u32[]{:S(2)}, u32[]{:S(2)}) async-start(bf16[8,32,3584]{2,1,0:T(8,128)(2,1)} %bitcast.154), calls=%async_computation.5 | async-start | bytes 3670016 | tf_op jit(solution)/shard_map/all_to_all | solution.py:35
  315.4 27.3 %copy-start.5 = (bf16[256,3584]{1,0:T(8,128)(2,1)}, bf16[256,3584]{1,0:T(8,128)(2,1)S(1)}, u32[]{:S(2)}) copy-start(bf16[256,3584]{1,0:T(8,128)(2,1)S(1)} %get-tuple-element.26) | copy-start | bytes 5505028
  315.4 2.3 collective-permute-start.4
  315.9 19.9 %collective-permute-start.10 = (f32[1,3584]{1,0:T(1,128)S(1)}, f32[1,3584]{1,0:T(1,128)S(1)}, u32[]{:S(2)}, u32[]{:S(2)}) collective-permute-start(f32[1,3584]{1,0:T(1,128)S(1)} %add.98), channel_id=1, source_target_pairs={{0,4},{1,5},{2,6},{3,7},{4,0},{5,1},{6,2},{7,3},{8,12},{9,13},{10,... | collective-permute-start | bytes 43016 | tf_op jit(solution)/shard_map/ppermute | solution.py:144
  317.7 18.2 %collective-permute-start.5 = (f32[1,3584]{1,0:T(1,128)S(1)}, f32[1,3584]{1,0:T(1,128)S(1)}, u32[]{:S(2)}, u32[]{:S(2)}) collective-permute-start(f32[1,3584]{1,0:T(1,128)S(1)} %reshape_add_fusion), channel_id=1, source_target_pairs={{0,2},{1,3},{2,0},{3,1},{4,6},{5,7},{6,4},{7,5},{8,10},{9,11},{10,... | collective-permute-start | bytes 43016 | tf_op jit(solution)/shard_map/ppermute | solution.py:144
  335.8 4.7 %collective-permute-start.11 = (f32[1,3584]{1,0:T(1,128)S(1)}, f32[1,3584]{1,0:T(1,128)S(1)}, u32[]{:S(2)}, u32[]{:S(2)}) collective-permute-start(f32[1,3584]{1,0:T(1,128)S(1)} %add.99), channel_id=1, source_target_pairs={{0,8},{1,9},{2,10},{3,11},{4,12},{5,13},{6,14},{7,15},{8,0},{9,1},... | collective-permute-start | bytes 43016 | tf_op jit(solution)/shard_map/ppermute | solution.py:144
  335.9 4.6 %collective-permute-start.6 = (f32[1,3584]{1,0:T(1,128)S(1)}, f32[1,3584]{1,0:T(1,128)S(1)}, u32[]{:S(2)}, u32[]{:S(2)}) collective-permute-start(f32[1,3584]{1,0:T(1,128)S(1)} %add.94), channel_id=1, source_target_pairs={{0,4},{1,5},{2,6},{3,7},{4,0},{5,1},{6,2},{7,3},{8,12},{9,13},{10,... | collective-permute-start | bytes 43016 | tf_op jit(solution)/shard_map/ppermute | solution.py:144
  340.6 4.8 %collective-permute-start.7 = (f32[1,3584]{1,0:T(1,128)S(1)}, f32[1,3584]{1,0:T(1,128)S(1)}, u32[]{:S(2)}, u32[]{:S(2)}) collective-permute-start(f32[1,3584]{1,0:T(1,128)S(1)} %add.95), channel_id=1, source_target_pairs={{0,8},{1,9},{2,10},{3,11},{4,12},{5,13},{6,14},{7,15},{8,0},{9,1},... | collective-permute-start | bytes 43016 | tf_op jit(solution)/shard_map/ppermute | solution.py:144
  345.4 27.2 %all-to-all-start.6 = ((bf16[8,32,3584]{2,1,0:T(8,128)(2,1)}), bf16[8,32,3584]{2,1,0:T(8,128)(2,1)}, u32[]{:S(2)}, u32[]{:S(2)}) async-start(bf16[8,32,3584]{2,1,0:T(8,128)(2,1)} %pad_maximum_fusion.2), calls=%async_computation.6 | async-start | bytes 3670016 | tf_op jit(solution)/shard_map/all_to_all | solution.py:35
  357.1 1.5 copy-start.6
  357.2 3.8 copy-start
  374.8 1.4 copy-start.3

commit v3 on v2

--- a/solution.py
+++ b/solution.py
@@ -36,6 +36,9 @@
             x, "layer", split_axis=0, concat_axis=0, tiled=True, axis_index_groups=halves
         )
 
+    def after(x, done):
+        return lax.optimization_barrier((x, done))[0]
+
     def across(x):
         return lax.ppermute(x, "layer", mirror)
 
@@ -52,11 +55,11 @@
         same = named[:, :, None] == named[:, None, :]
         return jnp.sum((same & earlier).astype(jnp.int32), axis=2)
 
-    routes_m = across(routes)
     pre = pre_acts.reshape(layers, tokens, latents)
     resid1_m = across(residual[1])
 
     order = ordinals(routes)
+    routes_m, order_m = across(jnp.stack([routes, order]))
     slot_of = routes * cap + order
     place = (slot_of[:, None, :] == jnp.arange(slots, dtype=jnp.int32)[None, :, None]).astype(BF)
 
@@ -68,7 +71,7 @@
 
     base = jnp.where(upper, half, 0).astype(jnp.int32)
     place_o = pair_places(routes, order, base)
-    place_m = pair_places(routes_m, ordinals(routes_m), base)
+    place_m = pair_places(routes_m, order_m, base)
 
     def flat(p):
         return p.reshape(-1, p.shape[-1])
@@ -99,10 +102,12 @@
 
     pieces_m = within(decode(wide[half:])).reshape(-1, width)
     sum_m = mm(flat(place_m), pieces_m, ROWS)
-    sum_low = across(sum_m.astype(BF))
-    pieces_o = within(decode(wide[:half])).reshape(-1, width)
+    sum_low_sent = sum_m.astype(BF)
+    sum_low = across(sum_low_sent)
+    pieces_o = within(decode(after(wide[:half], sum_low_sent))).reshape(-1, width)
     sum_o = mm(flat(place_o), pieces_o, ROWS) + decoder_bias[1] - mlp_target[1].astype(F32)
-    sum_high = across(sum_o.astype(BF))
+    sum_high_sent = sum_o.astype(BF)
+    sum_high = across(sum_high_sent)
 
     error1 = ((sum_o + sum_low.astype(F32)) * scale).astype(BF)
     error1_m = ((sum_m + sum_high.astype(F32)) * scale).astype(BF)
@@ -110,29 +115,24 @@
     def send_errors(p, error):
         return within(mm(flat(p), error).astype(BF).reshape(half, layers * cap, width))
 
+    residual1 = after(residual[1], sum_high_sent)
     resid1_in = within(
         jnp.concatenate(
             [
-                mm(flat(place_o[:, 1]), residual[1]).astype(BF).reshape(half, cap, width),
+                mm(flat(place_o[:, 1]), residual1).astype(BF).reshape(half, cap, width),
                 mm(flat(place_m[:, 1]), resid1_m).astype(BF).reshape(half, cap, width),
             ],
             axis=1,
         )
     )
-    errors_o = send_errors(place_o, error1)
-    errors_m = send_errors(place_m, error1_m)
+    errors_o = send_errors(place_o, after(error1, resid1_in))
+    errors_m = send_errors(place_m, after(error1_m, errors_o))
 
-    layer0 = everyone(
-        jnp.concatenate(
-            [
-                mm(place[0], mlp_target[0]).astype(BF).reshape(devices, cap, width),
-                mm(place[0], residual[0]).astype(BF).reshape(devices, cap, width),
-            ],
-            axis=1,
-        )
-    )
-    target0 = layer0[:, :cap].reshape(slots, width)
-    resid0 = layer0[:, cap:].reshape(slots, width)
+    target_last = after(mlp_target[0], errors_m)
+    target0 = everyone(mm(place[0], target_last).astype(BF).reshape(devices, cap, width))
+    residual_last = after(residual[0], target0)
+    resid0 = everyone(mm(place[0], residual_last).astype(BF).reshape(devices, cap, width))
+    target0, resid0 = target0.reshape(slots, width), resid0.reshape(slots, width)
     piece00 = mm(act0, decoder[0]).astype(BF).astype(F32)
     error0 = ((piece00 + decoder_bias[0] - target0.astype(F32)) * scale).astype(BF)
     empty0 = (decoder_bias[0] * scale).astype(BF).astype(F32)
@@ -145,12 +145,10 @@
             step *= 2
         return x
 
-    bias_grad = jnp.stack(
-        [
-            total(jnp.sum(error0.astype(F32), axis=0)[None])[0] - empties * empty0,
-            total(jnp.sum(error1.astype(F32), axis=0)[None])[0],
-        ]
+    sums = total(
+        jnp.stack([jnp.sum(error0.astype(F32), axis=0), jnp.sum(error1.astype(F32), axis=0)])
     )
+    bias_grad = sums - jnp.stack([empties * empty0, jnp.zeros_like(empty0)])
 
     wide_o = wide[:half].reshape(-1, 2 * latents)
     wide_m = wide[half:].reshape(-1, 2 * latents)

time: 379 us -> 359 us (0.947)
  waiting for transfers between devices: 266 us -> 222 us
  blocking collectives: 0 us -> 26.3 us
    ppermute x4, waiting for transfers between devices: 194 us -> 137 us  [across(): return lax.ppermute(x, 'layer', mirror)]
    all_to_all x0 -> x1, blocking collectives: none -> 26.3 us  [within(): lax.all_to_all(x, 'layer', split_axis=0, concat_axis=0, tiled=True, axis_...]
    all_to_all x2 -> x3, waiting for transfers between devices: 6.3 us -> 30.6 us  [everyone(): return lax.all_to_all(x, 'layer', split_axis=0, concat_axis=0, tiled=True)]
    all_to_all x5 -> x4, waiting for transfers between devices: 48 us -> 24.2 us  [within(): lax.all_to_all(x, 'layer', split_axis=0, concat_axis=0, tiled=True, axis_...]
    ppermute x8 -> x4, waiting for transfers between devices: 18.1 us -> 30 us  [total(): x = x + lax.ppermute(x, 'layer', [(i, i ^ step) for i in range(devices)])]
    all_to_all x2 -> x3, starting transfers between devices: 10.7 us -> 22.3 us  [everyone(): return lax.all_to_all(x, 'layer', split_axis=0, concat_axis=0, tiled=True)]
    slice x2 -> x0, local copies, waits for them, and re-layouts: 4.23 us -> none  [the longest x1 4.16 us: per_device(): resid0 = layer0[:, cap:].reshape(slots, width)]
    ppermute x4, starting transfers between devices: 9.46 us -> 5.45 us  [across(): return lax.ppermute(x, 'layer', mirror)]
  transfers between devices with their start and end apart: 19 -> 15, of which waited for: 10 -> 13; matrix products, arithmetic and copies ran while one was open for 12% -> 8% of each run, Pallas kernels for 0% -> 0%
where the time goes in v3:
time: 359 us; the launch traced here: 358 us
  waiting for transfers between devices  222 us (62%)
  starting transfers between devices  54 us (15%)
  matrix products  38.1 us (11%)
  blocking collectives  26.3 us (7%)
  other arithmetic  9.21 us (3%)
  local copies, waits for them, and re-layouts  7.64 us (2%)
    ppermute x4, waiting for transfers between devices, across(): return lax.ppermute(x, 'layer', mirror)  137 us
    dot_general x21, matrix products, mm(): return lax.dot_general(a, b, (dims, ((), ())), preferred_element_type=F32)  38.1 us
    all_to_all x3, waiting for transfers between devices, everyone(): return lax.all_to_all(x, 'layer', split_axis=0, concat_axis=0, tiled=True)  30.6 us
    ppermute x4, waiting for transfers between devices, total(): x = x + lax.ppermute(x, 'layer', [(i, i ^ step) for i in range(devices)])  30 us
    all_to_all x1, blocking collectives, within(): lax.all_to_all(x, 'layer', split_axis=0, concat_axis=0, tiled=True, axis_...  26.3 us
    all_to_all x4, waiting for transfers between devices, within(): lax.all_to_all(x, 'layer', split_axis=0, concat_axis=0, tiled=True, axis_...  24.2 us
    all_to_all x3, starting transfers between devices, everyone(): return lax.all_to_all(x, 'layer', split_axis=0, concat_axis=0, tiled=True)  22.3 us
    all_to_all x4, starting transfers between devices, within(): lax.all_to_all(x, 'layer', split_axis=0, concat_axis=0, tiled=True, axis_...  19 us
  transfers between devices with their start and end apart: 15, of which 13 were waited for; matrix products, arithmetic and copies ran while one was open for 8% of the time, Pallas kernels for 0%

profile of v3, /device:TPU:0, one launch (start us, length us, event | category | flops | bytes accessed | tf_op | source)
XLA Modules:
  0.0 358.0 jit_solution(14362415131603042830)
XLA Ops:
  0.7 0.9 convert_reduce_fusion.2
  1.6 0.7 multiply_add_fusion
  2.3 0.9 convolution_convert_fusion.12
  3.2 0.9 convolution_convert_fusion.13
  4.2 0.7 pad_maximum_fusion.4
  4.8 7.4 %all-to-all-start = ((bf16[16,32,128]{2,1,0:T(8,128)(2,1)}), bf16[16,32,128]{2,1,0:T(8,128)(2,1)S(1)}, u32[]{:S(2)}, u32[]{:S(2)}) async-start(bf16[16,32,128]{2,1,0:T(8,128)(2,1)} %bitcast.9), calls=%async_computation | async-start | bytes 262144 | tf_op jit(solution)/shard_map/all_to_all | solution.py:32
  12.2 1.6 slice.114
  13.8 6.3 %all-to-all-done = bf16[16,32,128]{2,1,0:T(8,128)(2,1)S(1)} async-done(((bf16[16,32,128]{2,1,0:T(8,128)(2,1)}), bf16[16,32,128]{2,1,0:T(8,128)(2,1)S(1)}, u32[]{:S(2)}, u32[]{:S(2)}) %all-to-all-start) | async-done | bytes 131104 | tf_op jit(solution)/shard_map/all_to_all | solution.py:32
  20.3 1.9 convolution_convert_fusion.6
  22.1 4.4 %all-to-all-start.1 = ((bf16[8,32,3584]{2,1,0:T(8,128)(2,1)}), bf16[8,32,3584]{2,1,0:T(8,128)(2,1)}, u32[]{:S(2)}, u32[]{:S(2)}) async-start(bf16[8,32,3584]{2,1,0:T(8,128)(2,1)} %bitcast.168), calls=%async_computation.1 | async-start | bytes 3670016 | tf_op jit(solution)/shard_map/all_to_all | solution.py:35
  26.6 0.5 collective-permute-start
  27.1 20.3 %collective-permute-done = s32[2,2,128]{2,1,0:T(2,128)S(1)} collective-permute-done((s32[2,2,128]{2,1,0:T(2,128)S(1)}, s32[2,2,128]{2,1,0:T(2,128)S(1)}, u32[]{:S(2)}, u32[]{:S(2)}) %collective-permute-start) | collective-permute-done | bytes 2080 | tf_op jit(solution)/shard_map/ppermute | solution.py:43
  47.5 2.0 all-to-all-done.1
  49.5 3.5 fusion.35
  53.0 1.9 convolution_convert_fusion.5
  54.9 4.3 %all-to-all-start.2 = ((bf16[8,32,3584]{2,1,0:T(8,128)(2,1)}), bf16[8,32,3584]{2,1,0:T(8,128)(2,1)}, u32[]{:S(2)}, u32[]{:S(2)}) async-start(bf16[8,32,3584]{2,1,0:T(8,128)(2,1)} %bitcast.167), calls=%async_computation.2 | async-start | bytes 3670016 | tf_op jit(solution)/shard_map/all_to_all | solution.py:35
  59.2 2.6 slice_bitcast_fusion
  61.9 1.3 collective-permute-start.3
  63.2 1.6 collective-permute-start.2
  65.0 60.3 %collective-permute-done.3 = bf16[128,3584]{1,0:T(8,128)(2,1)S(1)} collective-permute-done((bf16[128,3584]{1,0:T(8,128)(2,1)S(1)}, bf16[128,3584]{1,0:T(8,128)(2,1)S(1)}, u32[]{:S(2)}, u32[]{:S(2)}) %collective-permute-start.3) | collective-permute-done | bytes 917536 | tf_op jit(solution)/shard_map/ppermute | solution.py:43
  125.3 1.3 convolution_convert_fusion.10
  126.6 17.9 %collective-permute-done.2 = bf16[128,3584]{1,0:T(8,128)(2,1)} collective-permute-done((bf16[128,3584]{1,0:T(8,128)(2,1)S(1)}, bf16[128,3584]{1,0:T(8,128)(2,1)}, u32[]{:S(2)}, u32[]{:S(2)}) %collective-permute-start.2) | collective-permute-done | bytes 917536 | tf_op jit(solution)/shard_map/ppermute | solution.py:43
  144.5 3.7 %convert_reduce_fusion.1 = (f32[3584]{0:T(1024)S(1)}, bf16[128,3584]{1,0:T(8,128)(2,1)S(1)}, bf16[128,3584]{1,0:T(8,128)(2,1)}) fusion(bf16[128,3584]{1,0:T(8,128)(2,1)} %collective-permute-done.2, bf16[2,128,3584]{2,1,0:T(8,128)(2,1)} %param.7, f32[3584]{0:T(1024)S(1)} %get-tuple-element.17, pred[256,128]{1,0:T(8,128)(4,1)S(1)} %bitcast.191, ...), kind=kOutput, calls=%fused_computation.28 | convolution fusion | flops 239464960 | bytes 5566464 | tf_op jit(solution)/shard_map/dot_general | solution.py:15
  148.2 0.4 convolution_convert_fusion.11
  148.6 0.8 copy-done.2
  149.4 0.1 pad_maximum_fusion.1
  149.5 26.3 %all_to_all.40 = bf16[8,32,3584]{2,1,0:T(8,128)(2,1)} all-to-all(bf16[8,32,3584]{2,1,0:T(8,128)(2,1)S(1)} %pad_maximum_fusion.1), channel_id=1, replica_groups={{0,1,2,3,4,5,6,7},{8,9,10,11,12,13,14,15},{16,17,18,19,20,21,22,23},{24..., dimensions={0} | all-to-all | bytes 3670016 | tf_op jit(solution)/shard_map/all_to_all | solution.py:35
  175.8 1.9 convolution_convert_fusion.3
  177.7 4.5 %all-to-all-start.4 = ((bf16[8,32,3584]{2,1,0:T(8,128)(2,1)}), bf16[8,32,3584]{2,1,0:T(8,128)(2,1)}, u32[]{:S(2)}, u32[]{:S(2)}) async-start(bf16[8,32,3584]{2,1,0:T(8,128)(2,1)} %bitcast.169), calls=%async_computation.4 | async-start | bytes 3670016 | tf_op jit(solution)/shard_map/all_to_all | solution.py:35
  182.1 2.0 collective-permute-start.1
  184.1 38.4 %collective-permute-done.1 = bf16[128,3584]{1,0:T(8,128)(2,1)S(1)} collective-permute-done((bf16[128,3584]{1,0:T(8,128)(2,1)S(1)}, bf16[128,3584]{1,0:T(8,128)(2,1)S(1)}, u32[]{:S(2)}, u32[]{:S(2)}) %collective-permute-start.1) | collective-permute-done | bytes 917536 | tf_op jit(solution)/shard_map/ppermute | solution.py:43
  222.5 1.7 multiply_convert_fusion.1
  224.3 0.4 all-to-all-done.4
  224.7 1.9 convolution_convert_fusion.2
  226.5 5.8 %all-to-all-start.5 = ((bf16[8,32,3584]{2,1,0:T(8,128)(2,1)}), bf16[8,32,3584]{2,1,0:T(8,128)(2,1)}, u32[]{:S(2)}, u32[]{:S(2)}) async-start(bf16[8,32,3584]{2,1,0:T(8,128)(2,1)} %bitcast.170), calls=%async_computation.5 | async-start | bytes 3670016 | tf_op jit(solution)/shard_map/all_to_all | solution.py:35
  232.3 1.2 slice_bitcast_fusion.2
  233.5 21.8 %all-to-all-done.5 = bf16[8,32,3584]{2,1,0:T(8,128)(2,1)} async-done(((bf16[8,32,3584]{2,1,0:T(8,128)(2,1)}), bf16[8,32,3584]{2,1,0:T(8,128)(2,1)}, u32[]{:S(2)}, u32[]{:S(2)}) %all-to-all-start.5) | async-done | bytes 1835040 | tf_op jit(solution)/shard_map/all_to_all | solution.py:35
  255.3 1.9 convolution_convert_fusion.1
  257.1 4.8 %all-to-all-start.6 = ((bf16[16,16,3584]{2,1,0:T(8,128)(2,1)}), bf16[16,16,3584]{2,1,0:T(8,128)(2,1)}, u32[]{:S(2)}, u32[]{:S(2)}) async-start(bf16[16,16,3584]{2,1,0:T(8,128)(2,1)} %bitcast.166), calls=%async_computation.6 | async-start | bytes 3670016 | tf_op jit(solution)/shard_map/all_to_all | solution.py:32
  262.1 2.2 fusion.38
  264.2 2.2 fusion.37
  266.4 2.2 fusion.39
  268.8 1.3 copy-done
  270.1 0.7 fusion.9
  270.8 3.5 fusion.5
  274.3 24.3 %all-to-all-done.6 = bf16[16,16,3584]{2,1,0:T(8,128)(2,1)} async-done(((bf16[16,16,3584]{2,1,0:T(8,128)(2,1)}), bf16[16,16,3584]{2,1,0:T(8,128)(2,1)}, u32[]{:S(2)}, u32[]{:S(2)}) %all-to-all-start.6) | async-done | bytes 1835040 | tf_op jit(solution)/shard_map/all_to_all | solution.py:32
  298.6 1.8 convolution_convert_fusion
  300.4 10.2 %all-to-all-start.7 = ((bf16[16,16,3584]{2,1,0:T(8,128)(2,1)}), bf16[16,16,3584]{2,1,0:T(8,128)(2,1)S(1)}, u32[]{:S(2)}, u32[]{:S(2)}) async-start(bf16[16,16,3584]{2,1,0:T(8,128)(2,1)} %bitcast.165), calls=%async_computation.7 | async-start | bytes 3670016 | tf_op jit(solution)/shard_map/all_to_all | solution.py:32
  310.6 2.6 convert_reduce_fusion
  313.3 0.5 collective-permute-start.4
  313.8 0.4 fusion.7
  314.2 0.4 collective-permute-done.4
  314.7 1.9 collective-permute-start.5
  316.6 1.8 pad_maximum_fusion
  318.4 4.5 %collective-permute-done.5 = f32[2,3584]{1,0:T(2,128)S(1)} collective-permute-done((f32[2,3584]{1,0:T(2,128)S(1)}, f32[2,3584]{1,0:T(2,128)S(1)}, u32[]{:S(2)}, u32[]{:S(2)}) %collective-permute-start.5) | collective-permute-done | bytes 28704 | tf_op jit(solution)/shard_map/ppermute | solution.py:144
  322.9 0.3 collective-permute-start.6
  323.3 1.8 fusion.36
  325.1 16.8 %collective-permute-done.6 = f32[2,3584]{1,0:T(2,128)S(1)} collective-permute-done((f32[2,3584]{1,0:T(2,128)S(1)}, f32[2,3584]{1,0:T(2,128)S(1)}, u32[]{:S(2)}, u32[]{:S(2)}) %collective-permute-start.6) | collective-permute-done | bytes 28704 | tf_op jit(solution)/shard_map/ppermute | solution.py:144
  341.9 4.5 %collective-permute-start.7 = (f32[2,3584]{1,0:T(2,128)S(1)}, f32[2,3584]{1,0:T(2,128)S(1)}, u32[]{:S(2)}, u32[]{:S(2)}) collective-permute-start(f32[2,3584]{1,0:T(2,128)S(1)} %add.85), channel_id=1, source_target_pairs={{0,8},{1,9},{2,10},{3,11},{4,12},{5,13},{6,14},{7,15},{8,0},{9,1},... | collective-permute-start | bytes 86024 | tf_op jit(solution)/shard_map/ppermute | solution.py:144
  346.4 0.6 pad_maximum_fusion.8
  347.0 8.3 %collective-permute-done.7 = f32[2,3584]{1,0:T(2,128)S(1)} collective-permute-done((f32[2,3584]{1,0:T(2,128)S(1)}, f32[2,3584]{1,0:T(2,128)S(1)}, u32[]{:S(2)}, u32[]{:S(2)}) %collective-permute-start.7) | collective-permute-done | bytes 28704 | tf_op jit(solution)/shard_map/ppermute | solution.py:144
  355.3 0.6 pad_subtract_fusion
  355.9 0.7 fusion.8
  356.6 1.4 pad_maximum_fusion.2
  (51 shorter events, 0.8 us)
Async XLA Ops:
  4.8 15.3 %all-to-all-start = ((bf16[16,32,128]{2,1,0:T(8,128)(2,1)}), bf16[16,32,128]{2,1,0:T(8,128)(2,1)S(1)}, u32[]{:S(2)}, u32[]{:S(2)}) async-start(bf16[16,32,128]{2,1,0:T(8,128)(2,1)} %bitcast.9), calls=%async_computation | async-start | bytes 262144 | tf_op jit(solution)/shard_map/all_to_all | solution.py:32
  22.1 4.5 %copy-start.7 = (s32[2,128,1]{1,2,0:T(1,128)S(1)}, s32[2,128,1]{1,2,0:T(1,128)}, u32[]{:S(2)}) copy-start(s32[2,128,1]{1,2,0:T(1,128)} %param.9) | copy-start | bytes 3076
  22.1 27.4 %all-to-all-start.1 = ((bf16[8,32,3584]{2,1,0:T(8,128)(2,1)}), bf16[8,32,3584]{2,1,0:T(8,128)(2,1)}, u32[]{:S(2)}, u32[]{:S(2)}) async-start(bf16[8,32,3584]{2,1,0:T(8,128)(2,1)} %bitcast.168), calls=%async_computation.1 | async-start | bytes 3670016 | tf_op jit(solution)/shard_map/all_to_all | solution.py:35
  26.6 20.8 %collective-permute-start = (s32[2,2,128]{2,1,0:T(2,128)S(1)}, s32[2,2,128]{2,1,0:T(2,128)S(1)}, u32[]{:S(2)}, u32[]{:S(2)}) collective-permute-start(s32[2,2,128]{2,1,0:T(2,128)S(1)} %pad_add_fusion), channel_id=1, source_target_pairs={{0,8},{1,9},{2,10},{3,11},{4,12},{5,13},{6,14},{7,15},{8,0},{9,1},... | collective-permute-start | bytes 6152 | tf_op jit(solution)/shard_map/ppermute | solution.py:43
  54.9 89.6 %all-to-all-start.2 = ((bf16[8,32,3584]{2,1,0:T(8,128)(2,1)}), bf16[8,32,3584]{2,1,0:T(8,128)(2,1)}, u32[]{:S(2)}, u32[]{:S(2)}) async-start(bf16[8,32,3584]{2,1,0:T(8,128)(2,1)} %bitcast.167), calls=%async_computation.2 | async-start | bytes 3670016 | tf_op jit(solution)/shard_map/all_to_all | solution.py:35
  59.2 4.0 %copy-start.4 = (bf16[128,3584]{1,0:T(8,128)(2,1)S(1)}, bf16[128,3584]{1,0:T(8,128)(2,1)}, u32[]{:S(2)}) copy-start(bf16[128,3584]{1,0:T(8,128)(2,1)} %get-tuple-element.34) | copy-start | bytes 2752516
  59.2 5.6 %copy-start.6 = (f32[2,3584]{1,0:T(2,128)S(1)}, f32[2,3584]{1,0:T(2,128)}, u32[]{:S(2)}) copy-start(f32[2,3584]{1,0:T(2,128)} %param.11) | copy-start | bytes 86020
  61.9 63.4 %collective-permute-start.3 = (bf16[128,3584]{1,0:T(8,128)(2,1)S(1)}, bf16[128,3584]{1,0:T(8,128)(2,1)S(1)}, u32[]{:S(2)}, u32[]{:S(2)}) collective-permute-start(bf16[128,3584]{1,0:T(8,128)(2,1)S(1)} %get-tuple-element.11), channel_id=1, source_target_pairs={{0,8},{1,9},{2,10},{3,11},{4,12},{5,13},{6,14},{7,15},{8,0},{9,1},... | collective-permute-start | bytes 2752520 | tf_op jit(solution)/shard_map/ppermute | solution.py:43
  63.2 81.3 %collective-permute-start.2 = (bf16[128,3584]{1,0:T(8,128)(2,1)S(1)}, bf16[128,3584]{1,0:T(8,128)(2,1)}, u32[]{:S(2)}, u32[]{:S(2)}) collective-permute-start(bf16[128,3584]{1,0:T(8,128)(2,1)S(1)} %copy-done.4), channel_id=1, source_target_pairs={{0,8},{1,9},{2,10},{3,11},{4,12},{5,13},{6,14},{7,15},{8,0},{9,1},... | collective-permute-start | bytes 2752520 | tf_op jit(solution)/shard_map/ppermute | solution.py:43
  148.2 1.2 copy-start.2
  177.7 4.5 %copy-start.5 = (bf16[128,3584]{1,0:T(8,128)(2,1)S(1)}, bf16[128,3584]{1,0:T(8,128)(2,1)}, u32[]{:S(2)}) copy-start(bf16[128,3584]{1,0:T(8,128)(2,1)} %get-tuple-element.22) | copy-start | bytes 2752516
  177.7 47.0 %all-to-all-start.4 = ((bf16[8,32,3584]{2,1,0:T(8,128)(2,1)}), bf16[8,32,3584]{2,1,0:T(8,128)(2,1)}, u32[]{:S(2)}, u32[]{:S(2)}) async-start(bf16[8,32,3584]{2,1,0:T(8,128)(2,1)} %bitcast.169), calls=%async_computation.4 | async-start | bytes 3670016 | tf_op jit(solution)/shard_map/all_to_all | solution.py:35
  182.1 40.4 %collective-permute-start.1 = (bf16[128,3584]{1,0:T(8,128)(2,1)S(1)}, bf16[128,3584]{1,0:T(8,128)(2,1)S(1)}, u32[]{:S(2)}, u32[]{:S(2)}) collective-permute-start(bf16[128,3584]{1,0:T(8,128)(2,1)S(1)} %copy-done.5), channel_id=1, source_target_pairs={{0,8},{1,9},{2,10},{3,11},{4,12},{5,13},{6,14},{7,15},{8,0},{9,1},... | collective-permute-start | bytes 2752520 | tf_op jit(solution)/shard_map/ppermute | solution.py:43
  226.5 28.8 %all-to-all-start.5 = ((bf16[8,32,3584]{2,1,0:T(8,128)(2,1)}), bf16[8,32,3584]{2,1,0:T(8,128)(2,1)}, u32[]{:S(2)}, u32[]{:S(2)}) async-start(bf16[8,32,3584]{2,1,0:T(8,128)(2,1)} %bitcast.170), calls=%async_computation.5 | async-start | bytes 3670016 | tf_op jit(solution)/shard_map/all_to_all | solution.py:35
  257.1 41.4 %all-to-all-start.6 = ((bf16[16,16,3584]{2,1,0:T(8,128)(2,1)}), bf16[16,16,3584]{2,1,0:T(8,128)(2,1)}, u32[]{:S(2)}, u32[]{:S(2)}) async-start(bf16[16,16,3584]{2,1,0:T(8,128)(2,1)} %bitcast.166), calls=%async_computation.6 | async-start | bytes 3670016 | tf_op jit(solution)/shard_map/all_to_all | solution.py:32
  268.6 1.5 copy-start
  270.8 27.8 %copy-start.3 = (bf16[128,3584]{1,0:T(8,128)(2,1)S(1)}, bf16[128,3584]{1,0:T(8,128)(2,1)}, u32[]{:S(2)}) copy-start(bf16[128,3584]{1,0:T(8,128)(2,1)} %get-tuple-element.15) | copy-start | bytes 2752516
  300.4 55.5 %all-to-all-start.7 = ((bf16[16,16,3584]{2,1,0:T(8,128)(2,1)}), bf16[16,16,3584]{2,1,0:T(8,128)(2,1)S(1)}, u32[]{:S(2)}, u32[]{:S(2)}) async-start(bf16[16,16,3584]{2,1,0:T(8,128)(2,1)} %bitcast.165), calls=%async_computation.7 | async-start | bytes 3670016 | tf_op jit(solution)/shard_map/all_to_all | solution.py:32
  313.3 3.4 copy-start.1
  313.3 1.3 collective-permute-start.4
  314.7 8.2 %collective-permute-start.5 = (f32[2,3584]{1,0:T(2,128)S(1)}, f32[2,3584]{1,0:T(2,128)S(1)}, u32[]{:S(2)}, u32[]{:S(2)}) collective-permute-start(f32[2,3584]{1,0:T(2,128)S(1)} %fusion.33), channel_id=1, source_target_pairs={{0,2},{1,3},{2,0},{3,1},{4,6},{5,7},{6,4},{7,5},{8,10},{9,11},{10,... | collective-permute-start | bytes 86024 | tf_op jit(solution)/shard_map/ppermute | solution.py:144
  322.9 19.0 %collective-permute-start.6 = (f32[2,3584]{1,0:T(2,128)S(1)}, f32[2,3584]{1,0:T(2,128)S(1)}, u32[]{:S(2)}, u32[]{:S(2)}) collective-permute-start(f32[2,3584]{1,0:T(2,128)S(1)} %fusion.74), channel_id=1, source_target_pairs={{0,4},{1,5},{2,6},{3,7},{4,0},{5,1},{6,2},{7,3},{8,12},{9,13},{10,... | collective-permute-start | bytes 86024 | tf_op jit(solution)/shard_map/ppermute | solution.py:144
  341.9 13.3 %collective-permute-start.7 = (f32[2,3584]{1,0:T(2,128)S(1)}, f32[2,3584]{1,0:T(2,128)S(1)}, u32[]{:S(2)}, u32[]{:S(2)}) collective-permute-start(f32[2,3584]{1,0:T(2,128)S(1)} %add.85), channel_id=1, source_target_pairs={{0,8},{1,9},{2,10},{3,11},{4,12},{5,13},{6,14},{7,15},{8,0},{9,1},... | collective-permute-start | bytes 86024 | tf_op jit(solution)/shard_map/ppermute | solution.py:144

commit v4 on v3

--- a/solution.py
+++ b/solution.py
@@ -3,6 +3,8 @@
 import jax
 import jax.numpy as jnp
 from jax import lax
+from jax.experimental import pallas as pl
+from jax.experimental.pallas import tpu as pltpu
 from jax.sharding import PartitionSpec as P
 
 BF = jnp.bfloat16
@@ -13,6 +15,70 @@
 
 def mm(a, b, dims=((1,), (0,))):
     return lax.dot_general(a, b, (dims, ((), ())), preferred_element_type=F32)
+
+
+def column_block(width):
+    return next((b for b in (512, 256, 128) if width % b == 0), width)
+
+
+def pack_rows(keys, rows, groups, cap):
+    layers, tokens, width = rows.shape
+    step = column_block(width)
+
+    def kernel(keys_ref, rows_ref, *outs):
+        slot = lax.broadcasted_iota(jnp.int32, (groups * cap, tokens), 0)
+        for l in range(layers):
+            hot = (keys_ref[l : l + 1, :] == slot).astype(F32).astype(BF)
+            placed = mm(hot, rows_ref[l]).astype(BF)
+            for k in range(groups):
+                outs[k][l * cap : (l + 1) * cap, :] = placed[k * cap : (k + 1) * cap]
+
+    return pl.pallas_call(
+        kernel,
+        grid=(width // step,),
+        in_specs=[
+            pl.BlockSpec((layers, tokens), lambda i: (0, 0)),
+            pl.BlockSpec((layers, tokens, step), lambda i: (0, 0, i)),
+        ],
+        out_specs=[pl.BlockSpec((layers * cap, step), lambda i: (0, i))] * groups,
+        out_shape=[jax.ShapeDtypeStruct((layers * cap, width), BF)] * groups,
+        compiler_params=pltpu.CompilerParams(vmem_limit_bytes=32 * 2**20),
+        cost_estimate=pl.CostEstimate(
+            flops=2 * layers * groups * cap * tokens * width,
+            bytes_accessed=2 * layers * (tokens + groups * cap) * width,
+            transcendentals=0,
+        ),
+    )(keys, rows)
+
+
+def encoder_products(rows, low, cap):
+    layers, slots, latents = low.shape
+    groups = len(rows)
+    width = rows[0].shape[1]
+    step = column_block(width)
+
+    def kernel(low_ref, *refs):
+        ins, out_ref, all_rows = refs[:groups], refs[groups], refs[groups + 1]
+        for l in range(layers):
+            for k in range(groups):
+                all_rows[k * cap : (k + 1) * cap, :] = ins[k][l * cap : (l + 1) * cap, :]
+            out_ref[l] = mm(all_rows[...], low_ref[l], ROWS).astype(BF)
+
+    return pl.pallas_call(
+        kernel,
+        grid=(width // step,),
+        in_specs=[pl.BlockSpec((layers, slots, latents), lambda i: (0, 0, 0))]
+        + [pl.BlockSpec((layers * cap, step), lambda i: (0, i))] * groups,
+        out_specs=pl.BlockSpec((layers, step, latents), lambda i: (0, i, 0)),
+        out_shape=jax.ShapeDtypeStruct((layers, width, latents), BF),
+        scratch_shapes=[pltpu.VMEM((slots, step), BF)],
+        compiler_params=pltpu.CompilerParams(vmem_limit_bytes=32 * 2**20),
+        cost_estimate=pl.CostEstimate(
+            flops=2 * layers * slots * latents * width,
+            bytes_accessed=2 * layers * (slots + latents) * width,
+            transcendentals=0,
+        ),
+    )(low, *rows)
 
 
 def per_device(residual, mlp_target, pre_acts, blocks, decoder, decoder_bias):
@@ -56,7 +122,6 @@
         return jnp.sum((same & earlier).astype(jnp.int32), axis=2)
 
     pre = pre_acts.reshape(layers, tokens, latents)
-    resid1_m = across(residual[1])
 
     order = ordinals(routes)
     routes_m, order_m = across(jnp.stack([routes, order]))
@@ -85,6 +150,31 @@
     pre0 = got_pre[:, 0].reshape(slots, latents)
     pre1 = got_pre[:, 1].reshape(slots, latents)
     act0 = jnp.maximum(pre0, 0)
+
+    direct = devices <= 16 and cap % 16 == 0
+    if direct:
+        packed = pack_rows((routes ^ me) * cap + order, residual, devices, cap)
+        resid_in = [packed[0]] + [
+            lax.ppermute(packed[k], "layer", [(i, i ^ k) for i in range(devices)])
+            for k in range(1, devices)
+        ]
+        early = [k for k in range(half, devices) if 8 * (k - half) < 3 * half]
+        within_half = list(range(1, half))
+        arrived = (me ^ jnp.arange(devices, dtype=jnp.int32)).astype(jnp.int32)
+    else:
+        resid_in = everyone(
+            jnp.stack(
+                [
+                    mm(place[l], residual[l]).astype(BF).reshape(devices, cap, width)
+                    for l in range(layers)
+                ],
+                axis=1,
+            ).reshape(devices, layers * cap, width)
+        )
+        early, within_half = [], []
+
+    def received(ks):
+        return [resid_in[k] for k in ks]
 
     acts = turn(jnp.maximum(got_pre, 0))
     nothing = jnp.zeros((devices, 1, cap, latents), BF)
@@ -104,7 +194,7 @@
     sum_m = mm(flat(place_m), pieces_m, ROWS)
     sum_low_sent = sum_m.astype(BF)
     sum_low = across(sum_low_sent)
-    pieces_o = within(decode(after(wide[:half], sum_low_sent))).reshape(-1, width)
+    pieces_o = within(decode(after(wide[:half], (sum_low_sent, received(early))))).reshape(-1, width)
     sum_o = mm(flat(place_o), pieces_o, ROWS) + decoder_bias[1] - mlp_target[1].astype(F32)
     sum_high_sent = sum_o.astype(BF)
     sum_high = across(sum_high_sent)
@@ -115,24 +205,13 @@
     def send_errors(p, error):
         return within(mm(flat(p), error).astype(BF).reshape(half, layers * cap, width))
 
-    residual1 = after(residual[1], sum_high_sent)
-    resid1_in = within(
-        jnp.concatenate(
-            [
-                mm(flat(place_o[:, 1]), residual1).astype(BF).reshape(half, cap, width),
-                mm(flat(place_m[:, 1]), resid1_m).astype(BF).reshape(half, cap, width),
-            ],
-            axis=1,
-        )
-    )
-    errors_o = send_errors(place_o, after(error1, resid1_in))
-    errors_m = send_errors(place_m, after(error1_m, errors_o))
-
-    target_last = after(mlp_target[0], errors_m)
+    error1 = after(error1, received(within_half[: half // 2]))
+    errors_o = send_errors(place_o, error1)
+
+    target_last = after(mlp_target[0], (errors_o, sum_high, received(within_half[half // 2 :])))
     target0 = everyone(mm(place[0], target_last).astype(BF).reshape(devices, cap, width))
-    residual_last = after(residual[0], target0)
-    resid0 = everyone(mm(place[0], residual_last).astype(BF).reshape(devices, cap, width))
-    target0, resid0 = target0.reshape(slots, width), resid0.reshape(slots, width)
+    target0 = target0.reshape(slots, width)
+    errors_m = send_errors(place_m, after(error1_m, target0))
     piece00 = mm(act0, decoder[0]).astype(BF).astype(F32)
     error0 = ((piece00 + decoder_bias[0] - target0.astype(F32)) * scale).astype(BF)
     empty0 = (decoder_bias[0] * scale).astype(BF).astype(F32)
@@ -157,21 +236,24 @@
     dec_later = mm(wide_o, errors_o, ROWS) + mm(wide_m, errors_m, ROWS)
     back = jnp.concatenate([mm(errors_o, dec1, LAST), mm(errors_m, dec1, LAST)], axis=0)
     back = back.reshape(devices, layers, cap, 2 * latents)
-    pres = turn(got_pre)
-    grad1 = jnp.where(pres[:, 1] > 0, back[:, 1, :, latents:], 0.0)
-    grad0 = turn(back[:, 0, :, :latents]).reshape(slots, latents) + mm(error0, decoder[0], LAST)
-    grad0 = jnp.where(pre0 > 0, grad0, 0.0)
-    low1 = grad1.astype(BF).reshape(2, half, cap, latents).swapaxes(0, 1).reshape(slots, latents)
+    back = turn(back)
+    own = mm(error0, decoder[0], LAST).reshape(devices, cap, latents)
+    grads = jnp.stack([back[:, 0, :, :latents] + own, back[:, 1, :, latents:]], axis=1)
+    grads = jnp.where(got_pre > 0, grads, 0.0)
+    enc_bias = jnp.sum(grads, axis=(0, 2))
+    low = grads.astype(BF)
+    if direct:
+        low = jnp.take(low, arrived, axis=0)
+        low = jnp.swapaxes(low, 0, 1).reshape(layers, slots, latents)
+        enc = encoder_products(resid_in, low, cap)
+    else:
+        low = jnp.swapaxes(low, 0, 1).reshape(layers, slots, latents)
+        resid = resid_in.reshape(devices, layers, cap, width)
+        resid = jnp.swapaxes(resid, 0, 1).reshape(layers, slots, width)
+        enc = jnp.stack([mm(resid[l], low[l], ROWS).astype(BF) for l in range(layers)])
     dec = jnp.concatenate(
         [mm(act0, error0, ROWS).astype(BF)[None], dec_later.astype(BF).reshape(2, latents, width)]
     )
-    enc = jnp.stack(
-        [
-            mm(resid0, grad0.astype(BF), ROWS).astype(BF),
-            mm(resid1_in.reshape(slots, width), low1, ROWS).astype(BF),
-        ]
-    )
-    enc_bias = jnp.stack([jnp.sum(grad0, axis=0), jnp.sum(grad1, axis=(0, 1))])
     return dec, enc, enc_bias, bias_grad
 
 

time: 359 us -> 330 us (0.919)
  waiting for transfers between devices: 222 us -> 177 us
  blocking collectives: 26.3 us -> 0 us
  starting transfers between devices: 54 us -> 72.4 us
  Pallas kernels: 0 us -> 10.1 us
  other arithmetic: 9.21 us -> 17 us
  matrix products: 38.1 us -> 41.8 us
    ppermute x4 -> x3, waiting for transfers between devices: 137 us -> 44.9 us  [across(): return lax.ppermute(x, 'layer', mirror)]
    ppermute x0 -> x15, waiting for transfers between devices: none -> 50.6 us  [per_device(): lax.ppermute(packed[k], 'layer', [(i, i ^ k) for i in range(devices)])]
    all_to_all x1 -> x0, blocking collectives: 26.3 us -> none  [within(): lax.all_to_all(x, 'layer', split_axis=0, concat_axis=0, tiled=True, axis_...]
    ppermute x0 -> x15, starting transfers between devices: none -> 24.2 us  [per_device(): lax.ppermute(packed[k], 'layer', [(i, i ^ k) for i in range(devices)])]
    all_to_all x3 -> x2, waiting for transfers between devices: 30.6 us -> 48 us  [everyone(): return lax.all_to_all(x, 'layer', split_axis=0, concat_axis=0, tiled=True)]
    ppermute x4, waiting for transfers between devices: 30 us -> 18.1 us  [total(): x = x + lax.ppermute(x, 'layer', [(i, i ^ step) for i in range(devices)])]
    all_to_all x3 -> x2, starting transfers between devices: 22.3 us -> 11.8 us  [everyone(): return lax.all_to_all(x, 'layer', split_axis=0, concat_axis=0, tiled=True)]
    pallas_call x0 -> x2, Pallas kernels: none -> 10.1 us  [the longest x1 5.75 us: encoder_products(): pl.pallas_call(kernel, grid=(width // step,), in_specs=[pl.BlockSpec((lay...]
  transfers between devices with their start and end apart: 15 -> 28, of which waited for: 13 -> 13; matrix products, arithmetic and copies ran while one was open for 8% -> 15% of each run, Pallas kernels for 0% -> 1%
where the time goes in v4:
time: 330 us; the launch traced here: 327 us
  waiting for transfers between devices  177 us (54%)
  starting transfers between devices  72.4 us (22%)
  matrix products  41.8 us (13%)
  other arithmetic  17 us (5%)
  Pallas kernels  10.1 us (3%)
  local copies, waits for them, and re-layouts  7.5 us (2%)
    ppermute x15, waiting for transfers between devices, per_device(): lax.ppermute(packed[k], 'layer', [(i, i ^ k) for i in range(devices)])  50.6 us
    all_to_all x2, waiting for transfers between devices, everyone(): return lax.all_to_all(x, 'layer', split_axis=0, concat_axis=0, tiled=True)  48 us
    ppermute x3, waiting for transfers between devices, across(): return lax.ppermute(x, 'layer', mirror)  44.9 us
    dot_general x16, matrix products, mm(): return lax.dot_general(a, b, (dims, ((), ())), preferred_element_type=F32)  41.8 us
    ppermute x15, starting transfers between devices, per_device(): lax.ppermute(packed[k], 'layer', [(i, i ^ k) for i in range(devices)])  24.2 us
    all_to_all x4, starting transfers between devices, within(): lax.all_to_all(x, 'layer', split_axis=0, concat_axis=0, tiled=True, axis_...  22.6 us
    ppermute x4, waiting for transfers between devices, total(): x = x + lax.ppermute(x, 'layer', [(i, i ^ step) for i in range(devices)])  18.1 us
    all_to_all x4, waiting for transfers between devices, within(): lax.all_to_all(x, 'layer', split_axis=0, concat_axis=0, tiled=True, axis_...  15.7 us
  transfers between devices with their start and end apart: 28, of which 13 were waited for; matrix products, arithmetic and copies ran while one was open for 15% of the time, Pallas kernels for 1%

profile of v4, /device:TPU:0, one launch (start us, length us, event | category | flops | bytes accessed | tf_op | source)
XLA Modules:
  0.0 327.0 jit_solution(3691074939943941746)
XLA Ops:
  0.7 0.9 convert_reduce_fusion.2
  2.3 0.9 convolution_convert_fusion.7
  3.2 0.9 convolution_convert_fusion.8
  4.8 7.4 %all-to-all-start = ((bf16[16,32,128]{2,1,0:T(8,128)(2,1)}), bf16[16,32,128]{2,1,0:T(8,128)(2,1)S(1)}, u32[]{:S(2)}, u32[]{:S(2)}) async-start(bf16[16,32,128]{2,1,0:T(8,128)(2,1)} %bitcast.9), calls=%async_computation | async-start | bytes 262144 | tf_op jit(solution)/shard_map/all_to_all | solution.py:98
  12.2 1.6 slice.87
  13.8 6.3 %all-to-all-done = bf16[16,32,128]{2,1,0:T(8,128)(2,1)S(1)} async-done(((bf16[16,32,128]{2,1,0:T(8,128)(2,1)}), bf16[16,32,128]{2,1,0:T(8,128)(2,1)S(1)}, u32[]{:S(2)}, u32[]{:S(2)}) %all-to-all-start) | async-done | bytes 131104 | tf_op jit(solution)/shard_map/all_to_all | solution.py:98
  20.3 1.9 convolution_convert_fusion.5
  22.2 4.5 %all-to-all-start.1 = ((bf16[8,32,3584]{2,1,0:T(8,128)(2,1)}), bf16[8,32,3584]{2,1,0:T(8,128)(2,1)}, u32[]{:S(2)}, u32[]{:S(2)}) async-start(bf16[8,32,3584]{2,1,0:T(8,128)(2,1)} %bitcast.118), calls=%async_computation.1 | async-start | bytes 3670016 | tf_op jit(solution)/shard_map/all_to_all | solution.py:101
  27.2 4.3 %shard_map.93 = (bf16[32,3584]{1,0:T(8,128)(2,1)S(1)}, bf16[32,3584]{1,0:T(8,128)(2,1)}, bf16[32,3584]{1,0:T(8,128)(2,1)S(1)}, bf16[32,3584]{1,0:T(8,128)(2,1)S(...) custom-call(s32[2,128]{1,0:T(2,128)S(1)} %get-tuple-element.57.keys_, ...), custom_call_target="tpu_custom_call" | custom-call | flops 469762048 | bytes 5505024 | tf_op jit(solution)/shard_map/pallas_call | solution.py:36
  32.2 2.5 collective-permute-start.1
  34.7 3.4 %collective-permute-start.3 = (bf16[32,3584]{1,0:T(8,128)(2,1)}, bf16[32,3584]{1,0:T(8,128)(2,1)S(1)}, u32[]{:S(2)}, u32[]{:S(2)}) collective-permute-start(bf16[32,3584]{1,0:T(8,128)(2,1)} %get-tuple-element.26), channel_id=1, source_target_pairs={{0,10},{1,11},{2,8},{3,9},{4,14},{5,15},{6,12},{7,13},{8,2},{9,3},... | collective-permute-start | bytes 688136 | tf_op jit(solution)/shard_map/ppermute | solution.py:158
  38.2 9.5 %collective-permute-done = s32[2,2,128]{2,1,0:T(2,128)S(1)} collective-permute-done((s32[2,2,128]{2,1,0:T(2,128)S(1)}, s32[2,2,128]{2,1,0:T(2,128)S(1)}, u32[]{:S(2)}, u32[]{:S(2)}) %collective-permute-start) | collective-permute-done | bytes 2080 | tf_op jit(solution)/shard_map/ppermute | solution.py:109
  47.8 15.1 %all-to-all-done.1 = bf16[8,32,3584]{2,1,0:T(8,128)(2,1)} async-done(((bf16[8,32,3584]{2,1,0:T(8,128)(2,1)}), bf16[8,32,3584]{2,1,0:T(8,128)(2,1)}, u32[]{:S(2)}, u32[]{:S(2)}) %all-to-all-start.1) | async-done | bytes 1835040 | tf_op jit(solution)/shard_map/all_to_all | solution.py:101
  63.0 3.6 %fusion.30 = (bf16[128,3584]{1,0:T(8,128)(2,1)}, f32[128,3584]{1,0:T(8,128)}) fusion(pred[256,128]{1,0:T(8,128)(4,1)S(1)} %bitcast.132, bf16[256,3584]{1,0:T(8,128)(2,1)} %bitcast.24), kind=kOutput, calls=%fused_computation.92 | convolution fusion | flops 235339776 | bytes 4620288 | tf_op jit(solution)/shard_map/dot_general | solution.py:17
  66.7 1.9 convolution_convert_fusion.4
  68.6 4.5 %all-to-all-start.2 = ((bf16[8,32,3584]{2,1,0:T(8,128)(2,1)}), bf16[8,32,3584]{2,1,0:T(8,128)(2,1)}, u32[]{:S(2)}, u32[]{:S(2)}) async-start(bf16[8,32,3584]{2,1,0:T(8,128)(2,1)} %bitcast.121), calls=%async_computation.2 | async-start | bytes 3670016 | tf_op jit(solution)/shard_map/all_to_all | solution.py:101
  73.1 0.9 collective-permute-start.4
  74.2 1.8 collective-permute-start.6
  76.2 2.8 collective-permute-start.8
  78.9 1.2 slice_reduce_fusion.1
  80.2 35.4 %collective-permute-done.4 = bf16[128,3584]{1,0:T(8,128)(2,1)} collective-permute-done((bf16[128,3584]{1,0:T(8,128)(2,1)}, bf16[128,3584]{1,0:T(8,128)(2,1)}, u32[]{:S(2)}, u32[]{:S(2)}) %collective-permute-start.4) | collective-permute-done | bytes 917536 | tf_op jit(solution)/shard_map/ppermute | solution.py:109
  116.1 3.9 %fusion.28 = (bf16[128,3584]{1,0:T(8,128)(2,1)}, bf16[128,3584]{1,0:T(8,128)(2,1)}) fusion(bf16[128,3584]{1,0:T(8,128)(2,1)} %collective-permute-done.4, bf16[2,128,3584]{2,1,0:T(8,128)(2,1)} %param.7, f32[3584]{0:T(1024)S(1)} %get-tuple-element.45, pred[256,128]{1,0:T(8,128)(4,1)S(1)} %bitcast.134, bf16[256,3584]{1,0:T(8,128)(2,1)} %bitcast.27), kind=kOutput, calls=%fused_computation.90 | convolution fusion | flops 238551040 | bytes 5552128 | tf_op jit(solution)/shard_map/dot_general | solution.py:17
  120.4 3.1 convolution_convert_fusion.2
  123.5 4.3 %all-to-all-start.3 = ((bf16[8,32,3584]{2,1,0:T(8,128)(2,1)}), bf16[8,32,3584]{2,1,0:T(8,128)(2,1)}, u32[]{:S(2)}, u32[]{:S(2)}) async-start(bf16[8,32,3584]{2,1,0:T(8,128)(2,1)} %bitcast.120), calls=%async_computation.3 | async-start | bytes 3670016 | tf_op jit(solution)/shard_map/all_to_all | solution.py:101
  127.9 1.7 collective-permute-start.10
  129.5 1.5 collective-permute-start.11
  131.0 1.1 collective-permute-start.12
  132.1 1.1 collective-permute-start.9
  133.3 2.2 slice_bitcast_fusion
  135.4 39.3 %collective-permute-done.10.refs_5_ = bf16[32,3584]{1,0:T(8,128)(2,1)S(1)} collective-permute-done((bf16[32,3584]{1,0:T(8,128)(2,1)S(1)}, bf16[32,3584]{1,0:T(8,128)(2,1)S(1)}, u32[]{:S(2)}, u32[]{:S(2)}) %collective-permute-start.10) | collective-permute-done | bytes 229408 | tf_op jit(solution)/shard_map/ppermute | solution.py:158
  174.7 6.8 %collective-permute-done.11.refs_6_ = bf16[32,3584]{1,0:T(8,128)(2,1)S(1)} collective-permute-done((bf16[32,3584]{1,0:T(8,128)(2,1)S(1)}, bf16[32,3584]{1,0:T(8,128)(2,1)S(1)}, u32[]{:S(2)}, u32[]{:S(2)}) %collective-permute-start.11) | collective-permute-done | bytes 229408 | tf_op jit(solution)/shard_map/ppermute | solution.py:158
  181.5 4.0 %collective-permute-done.12.refs_7_ = bf16[32,3584]{1,0:T(8,128)(2,1)S(1)} collective-permute-done((bf16[32,3584]{1,0:T(8,128)(2,1)S(1)}, bf16[32,3584]{1,0:T(8,128)(2,1)S(1)}, u32[]{:S(2)}, u32[]{:S(2)}) %collective-permute-start.12) | collective-permute-done | bytes 229408 | tf_op jit(solution)/shard_map/ppermute | solution.py:158
  185.5 3.1 convolution_convert_fusion.1
  188.6 4.4 %all-to-all-start.4 = ((bf16[16,16,3584]{2,1,0:T(8,128)(2,1)}), bf16[16,16,3584]{2,1,0:T(8,128)(2,1)}, u32[]{:S(2)}, u32[]{:S(2)}) async-start(bf16[16,16,3584]{2,1,0:T(8,128)(2,1)} %bitcast.122), calls=%async_computation.4 | async-start | bytes 3670016 | tf_op jit(solution)/shard_map/all_to_all | solution.py:98
  193.0 3.4 %collective-permute-start.13 = (bf16[32,3584]{1,0:T(8,128)(2,1)}, bf16[32,3584]{1,0:T(8,128)(2,1)S(1)}, u32[]{:S(2)}, u32[]{:S(2)}) collective-permute-start(bf16[32,3584]{1,0:T(8,128)(2,1)} %get-tuple-element.39), channel_id=1, source_target_pairs={{0,11},{1,10},{2,9},{3,8},{4,15},{5,14},{6,13},{7,12},{8,3},{9,2},... | collective-permute-start | bytes 688136 | tf_op jit(solution)/shard_map/ppermute | solution.py:158
  196.4 1.4 collective-permute-start.14
  197.8 2.1 collective-permute-start.15
  199.9 1.4 collective-permute-start.16
  202.4 0.8 slice_maximum_fusion
  203.3 1.3 convert_reduce_fusion.1
  204.6 2.9 multiply_convert_fusion
  207.5 41.7 %all-to-all-done.4 = bf16[16,16,3584]{2,1,0:T(8,128)(2,1)} async-done(((bf16[16,16,3584]{2,1,0:T(8,128)(2,1)}), bf16[16,16,3584]{2,1,0:T(8,128)(2,1)}, u32[]{:S(2)}, u32[]{:S(2)}) %all-to-all-start.4) | async-done | bytes 1835040 | tf_op jit(solution)/shard_map/all_to_all | solution.py:98
  249.2 4.0 %convert_reduce_fusion = (f32[3584]{0:T(1024)S(1)}, bf16[256,3584]{1,0:T(8,128)(2,1)}) fusion(bf16[256,3584]{1,0:T(8,128)(2,1)} %bitcast.31, f32[3584]{0:T(1024)} %get-tuple-element.44, bf16[256,128]{1,0:T(8,128)(2,1)S(1)} %bitcast.136, bf16[3,128,3584]{2,1,0:T(8,128)(2,1)} %param.10), kind=kOutput, calls=%fused_computation.18 | convolution fusion | flops 243134976 | bytes 4683776 | tf_op jit(solution)/shard_map/dot_general | solution.py:17
  255.2 1.9 convolution_convert_fusion
  257.0 9.3 %all-to-all-start.5 = ((bf16[8,32,3584]{2,1,0:T(8,128)(2,1)}), bf16[8,32,3584]{2,1,0:T(8,128)(2,1)}, u32[]{:S(2)}, u32[]{:S(2)}) async-start(bf16[8,32,3584]{2,1,0:T(8,128)(2,1)} %bitcast.119), calls=%async_computation.5 | async-start | bytes 3670016 | tf_op jit(solution)/shard_map/all_to_all | solution.py:101
  266.4 0.8 fusion.26
  267.2 2.1 collective-permute-start.19
  269.3 4.2 %fusion.31 = f32[256,3584]{1,0:T(8,128)} fusion(bf16[256,256]{1,0:T(8,128)(2,1)} %bitcast.131, bf16[256,3584]{1,0:T(8,128)(2,1)} %bitcast.34), kind=kOutput, calls=%fused_computation.93 | convolution fusion | flops 469762048 | bytes 5636096 | tf_op jit(solution)/shard_map/dot_general | solution.py:17
  273.4 16.4 %collective-permute-done.19 = f32[2,3584]{1,0:T(2,128)S(1)} collective-permute-done((f32[2,3584]{1,0:T(2,128)S(1)}, f32[2,3584]{1,0:T(2,128)S(1)}, u32[]{:S(2)}, u32[]{:S(2)}) %collective-permute-start.19) | collective-permute-done | bytes 28704 | tf_op jit(solution)/shard_map/ppermute | solution.py:223
  289.9 0.8 fusion.58
  290.7 6.5 %collective-permute-start.20 = (f32[2,3584]{1,0:T(2,128)S(1)}, f32[2,3584]{1,0:T(2,128)S(1)}, u32[]{:S(2)}, u32[]{:S(2)}) collective-permute-start(f32[2,3584]{1,0:T(2,128)S(1)} %fusion.58), channel_id=1, source_target_pairs={{0,4},{1,5},{2,6},{3,7},{4,0},{5,1},{6,2},{7,3},{8,12},{9,13},{10,... | collective-permute-start | bytes 86024 | tf_op jit(solution)/shard_map/ppermute | solution.py:223
  297.2 3.0 fusion.32
  300.2 1.9 collective-permute-start.21
  302.1 1.4 fusion.7
  303.5 1.6 collective-permute-done.21
  305.1 0.8 collective-permute-start.17
  306.5 2.9 broadcast_select_fusion.1
  309.4 1.9 fusion.8
  311.3 0.8 select_convert_fusion
  312.1 2.3 gather_fusion
  314.4 1.0 select_bitcast_fusion
  315.4 3.4 %fusion.5 = bf16[256,3584]{1,0:T(8,128)(2,1)S(1)} fusion(f32[256,3584]{1,0:T(8,128)} %fusion.31, bf16[256,256]{1,0:T(8,128)(2,1)} %bitcast.129, bf16[256,3584]{1,0:T(8,128)(2,1)} %bitcast.36), kind=kOutput, calls=%fused_computation.11 | convolution fusion | flops 471597056 | bytes 7471104 | tf_op jit(solution)/shard_map/dot_general | solution.py:17
  318.8 1.8 pad_maximum_fusion
  321.2 5.8 %shard_map.94 = bf16[2,3584,128]{2,1,0:T(8,128)(2,1)} custom-call(bf16[2,256,128]{2,1,0:T(8,128)(2,1)S(1)} %bitcast.113, bf16[32,3584]{1,0:T(8,128)(2,1)S(1)} %get-tuple-element.38.refs_0_, bf16[32,3584]{1,0:T(8,128)(2,1)S(1)} %collective-permute-done.5.refs_1_, bf16[32,3584]{1,0:T(8,128)(2,1)S(1)} %collective-permute-done.6.refs_2_, ...), custom_call_target="tpu_custom_call" | custom-call | flops 469762048 | bytes 5505024 | tf_op jit(solution)/shard_map/pallas_call | solution.py:67
  (98 shorter events, 8.8 us)
Async XLA Ops:
  4.8 15.3 %all-to-all-start = ((bf16[16,32,128]{2,1,0:T(8,128)(2,1)}), bf16[16,32,128]{2,1,0:T(8,128)(2,1)S(1)}, u32[]{:S(2)}, u32[]{:S(2)}) async-start(bf16[16,32,128]{2,1,0:T(8,128)(2,1)} %bitcast.9), calls=%async_computation | async-start | bytes 262144 | tf_op jit(solution)/shard_map/all_to_all | solution.py:98
  13.8 8.3 %copy-start.4 = (bf16[2,128,3584]{2,1,0:T(8,128)(2,1)}, bf16[2,128,3584]{2,1,0:T(8,128)(2,1)S(1)}, u32[]{:S(2)}) copy-start(bf16[2,128,3584]{2,1,0:T(8,128)(2,1)S(1)} %slice.87) | copy-start | bytes 5505028
  20.1 2.0 copy-start.11
  20.3 1.9 copy-start.14
  20.3 46.4 %copy-start.15 = (bf16[8,2,16,256]{3,2,1,0:T(8,128)(2,1)}, bf16[8,2,16,256]{3,2,1,0:T(8,128)(2,1)S(1)}, u32[]{:S(2)}) copy-start(bf16[8,2,16,256]{3,2,1,0:T(8,128)(2,1)S(1)} %get-tuple-element.53) | copy-start | bytes 393220
  22.2 4.5 %copy-start.21 = (s32[2,128,1]{1,2,0:T(1,128)S(1)}, s32[2,128,1]{1,2,0:T(1,128)}, u32[]{:S(2)}) copy-start(s32[2,128,1]{1,2,0:T(1,128)} %param.9) | copy-start | bytes 3076
  22.2 5.0 %copy-start = (bf16[2,128,3584]{2,1,0:T(8,128)(2,1)S(1)}, bf16[2,128,3584]{2,1,0:T(8,128)(2,1)}, u32[]{:S(2)}) copy-start(bf16[2,128,3584]{2,1,0:T(8,128)(2,1)} %rows_ref.1) | copy-start | bytes 5505028
  22.2 40.8 %all-to-all-start.1 = ((bf16[8,32,3584]{2,1,0:T(8,128)(2,1)}), bf16[8,32,3584]{2,1,0:T(8,128)(2,1)}, u32[]{:S(2)}, u32[]{:S(2)}) async-start(bf16[8,32,3584]{2,1,0:T(8,128)(2,1)} %bitcast.118), calls=%async_computation.1 | async-start | bytes 3670016 | tf_op jit(solution)/shard_map/all_to_all | solution.py:101
  26.7 21.0 %collective-permute-start = (s32[2,2,128]{2,1,0:T(2,128)S(1)}, s32[2,2,128]{2,1,0:T(2,128)S(1)}, u32[]{:S(2)}, u32[]{:S(2)}) collective-permute-start(s32[2,2,128]{2,1,0:T(2,128)S(1)} %pad_add_fusion), channel_id=1, source_target_pairs={{0,8},{1,9},{2,10},{3,11},{4,12},{5,13},{6,14},{7,15},{8,0},{9,1},... | collective-permute-start | bytes 6152 | tf_op jit(solution)/shard_map/ppermute | solution.py:109
  31.5 0.7 copy-start.2
  32.2 2.5 copy-start.1
  32.2 34.4 %collective-permute-start.1 = (bf16[32,3584]{1,0:T(8,128)(2,1)}, bf16[32,3584]{1,0:T(8,128)(2,1)S(1)}, u32[]{:S(2)}, u32[]{:S(2)}) collective-permute-start(bf16[32,3584]{1,0:T(8,128)(2,1)} %get-tuple-element.24), channel_id=1, source_target_pairs={{0,8},{1,9},{2,10},{3,11},{4,12},{5,13},{6,14},{7,15},{8,0},{9,1},... | collective-permute-start | bytes 688136 | tf_op jit(solution)/shard_map/ppermute | solution.py:158
  34.7 31.9 %collective-permute-start.2 = (bf16[32,3584]{1,0:T(8,128)(2,1)}, bf16[32,3584]{1,0:T(8,128)(2,1)S(1)}, u32[]{:S(2)}, u32[]{:S(2)}) collective-permute-start(bf16[32,3584]{1,0:T(8,128)(2,1)} %get-tuple-element.25), channel_id=1, source_target_pairs={{0,9},{1,8},{2,11},{3,10},{4,13},{5,12},{6,15},{7,14},{8,1},{9,0},... | collective-permute-start | bytes 688136 | tf_op jit(solution)/shard_map/ppermute | solution.py:158
  34.7 32.0 %collective-permute-start.3 = (bf16[32,3584]{1,0:T(8,128)(2,1)}, bf16[32,3584]{1,0:T(8,128)(2,1)S(1)}, u32[]{:S(2)}, u32[]{:S(2)}) collective-permute-start(bf16[32,3584]{1,0:T(8,128)(2,1)} %get-tuple-element.26), channel_id=1, source_target_pairs={{0,10},{1,11},{2,8},{3,9},{4,14},{5,15},{6,12},{7,13},{8,2},{9,3},... | collective-permute-start | bytes 688136 | tf_op jit(solution)/shard_map/ppermute | solution.py:158
  63.0 3.7 %copy-start.5 = (bf16[2,128,3584]{2,1,0:T(8,128)(2,1)S(1)}, bf16[2,128,3584]{2,1,0:T(8,128)(2,1)}, u32[]{:S(2)}) copy-start(bf16[2,128,3584]{2,1,0:T(8,128)(2,1)} %copy-done.4) | copy-start | bytes 5505028
  68.6 5.6 %copy-start.3 = (bf16[32,3584]{1,0:T(8,128)(2,1)S(1)}, bf16[32,3584]{1,0:T(8,128)(2,1)}, u32[]{:S(2)}) copy-start(bf16[32,3584]{1,0:T(8,128)(2,1)} %copy-done.2) | copy-start | bytes 688132
  68.6 10.3 %copy-start.20 = (f32[2,3584]{1,0:T(2,128)S(1)}, f32[2,3584]{1,0:T(2,128)}, u32[]{:S(2)}) copy-start(f32[2,3584]{1,0:T(2,128)} %param.11) | copy-start | bytes 86020
  68.6 47.5 %all-to-all-start.2 = ((bf16[8,32,3584]{2,1,0:T(8,128)(2,1)}), bf16[8,32,3584]{2,1,0:T(8,128)(2,1)}, u32[]{:S(2)}, u32[]{:S(2)}) async-start(bf16[8,32,3584]{2,1,0:T(8,128)(2,1)} %bitcast.121), calls=%async_computation.2 | async-start | bytes 3670016 | tf_op jit(solution)/shard_map/all_to_all | solution.py:101
  73.1 42.5 %collective-permute-start.4 = (bf16[128,3584]{1,0:T(8,128)(2,1)}, bf16[128,3584]{1,0:T(8,128)(2,1)}, u32[]{:S(2)}, u32[]{:S(2)}) collective-permute-start(bf16[128,3584]{1,0:T(8,128)(2,1)} %get-tuple-element.63), channel_id=1, source_target_pairs={{0,8},{1,9},{2,10},{3,11},{4,12},{5,13},{6,14},{7,15},{8,0},{9,1},... | collective-permute-start | bytes 2752520 | tf_op jit(solution)/shard_map/ppermute | solution.py:109
  74.0 46.0 %collective-permute-start.5 = (bf16[32,3584]{1,0:T(8,128)(2,1)}, bf16[32,3584]{1,0:T(8,128)(2,1)S(1)}, u32[]{:S(2)}, u32[]{:S(2)}) collective-permute-start(bf16[32,3584]{1,0:T(8,128)(2,1)} %get-tuple-element.28), channel_id=1, source_target_pairs={{0,1},{1,0},{2,3},{3,2},{4,5},{5,4},{6,7},{7,6},{8,9},{9,8},{10,11... | collective-permute-start | bytes 688136 | tf_op jit(solution)/shard_map/ppermute | solution.py:158
  74.2 45.8 %collective-permute-start.6 = (bf16[32,3584]{1,0:T(8,128)(2,1)S(1)}, bf16[32,3584]{1,0:T(8,128)(2,1)S(1)}, u32[]{:S(2)}, u32[]{:S(2)}) collective-permute-start(bf16[32,3584]{1,0:T(8,128)(2,1)S(1)} %copy-done.3), channel_id=1, source_target_pairs={{0,2},{1,3},{2,0},{3,1},{4,6},{5,7},{6,4},{7,5},{8,10},{9,11},{10,... | collective-permute-start | bytes 688136 | tf_op jit(solution)/shard_map/ppermute | solution.py:158
  76.0 44.0 %collective-permute-start.7 = (bf16[32,3584]{1,0:T(8,128)(2,1)S(1)}, bf16[32,3584]{1,0:T(8,128)(2,1)S(1)}, u32[]{:S(2)}, u32[]{:S(2)}) collective-permute-start(bf16[32,3584]{1,0:T(8,128)(2,1)S(1)} %get-tuple-element.30), channel_id=1, source_target_pairs={{0,3},{1,2},{2,1},{3,0},{4,7},{5,6},{6,5},{7,4},{8,11},{9,10},{10,... | collective-permute-start | bytes 688136 | tf_op jit(solution)/shard_map/ppermute | solution.py:158
  76.2 44.3 %collective-permute-start.8 = (bf16[32,3584]{1,0:T(8,128)(2,1)S(1)}, bf16[32,3584]{1,0:T(8,128)(2,1)S(1)}, u32[]{:S(2)}, u32[]{:S(2)}) collective-permute-start(bf16[32,3584]{1,0:T(8,128)(2,1)S(1)} %get-tuple-element.31), channel_id=1, source_target_pairs={{0,4},{1,5},{2,6},{3,7},{4,0},{5,1},{6,2},{7,3},{8,12},{9,13},{10,... | collective-permute-start | bytes 688136 | tf_op jit(solution)/shard_map/ppermute | solution.py:158
  123.5 62.0 %all-to-all-start.3 = ((bf16[8,32,3584]{2,1,0:T(8,128)(2,1)}), bf16[8,32,3584]{2,1,0:T(8,128)(2,1)}, u32[]{:S(2)}, u32[]{:S(2)}) async-start(bf16[8,32,3584]{2,1,0:T(8,128)(2,1)} %bitcast.120), calls=%async_computation.3 | async-start | bytes 3670016 | tf_op jit(solution)/shard_map/all_to_all | solution.py:101
  127.9 46.9 %collective-permute-start.10 = (bf16[32,3584]{1,0:T(8,128)(2,1)S(1)}, bf16[32,3584]{1,0:T(8,128)(2,1)S(1)}, u32[]{:S(2)}, u32[]{:S(2)}) collective-permute-start(bf16[32,3584]{1,0:T(8,128)(2,1)S(1)} %get-tuple-element.33), channel_id=1, source_target_pairs={{0,5},{1,4},{2,7},{3,6},{4,1},{5,0},{6,3},{7,2},{8,13},{9,12},{10,... | collective-permute-start | bytes 688136 | tf_op jit(solution)/shard_map/ppermute | solution.py:158
  129.5 52.0 %collective-permute-start.11 = (bf16[32,3584]{1,0:T(8,128)(2,1)S(1)}, bf16[32,3584]{1,0:T(8,128)(2,1)S(1)}, u32[]{:S(2)}, u32[]{:S(2)}) collective-permute-start(bf16[32,3584]{1,0:T(8,128)(2,1)S(1)} %get-tuple-element.34), channel_id=1, source_target_pairs={{0,6},{1,7},{2,4},{3,5},{4,2},{5,3},{6,0},{7,1},{8,14},{9,15},{10,... | collective-permute-start | bytes 688136 | tf_op jit(solution)/shard_map/ppermute | solution.py:158
  131.0 54.5 %collective-permute-start.12 = (bf16[32,3584]{1,0:T(8,128)(2,1)S(1)}, bf16[32,3584]{1,0:T(8,128)(2,1)S(1)}, u32[]{:S(2)}, u32[]{:S(2)}) collective-permute-start(bf16[32,3584]{1,0:T(8,128)(2,1)S(1)} %get-tuple-element.35), channel_id=1, source_target_pairs={{0,7},{1,6},{2,5},{3,4},{4,3},{5,2},{6,1},{7,0},{8,15},{9,14},{10,... | collective-permute-start | bytes 688136 | tf_op jit(solution)/shard_map/ppermute | solution.py:158
  132.1 53.3 %collective-permute-start.9 = (bf16[128,3584]{1,0:T(8,128)(2,1)}, bf16[128,3584]{1,0:T(8,128)(2,1)}, u32[]{:S(2)}, u32[]{:S(2)}) collective-permute-start(bf16[128,3584]{1,0:T(8,128)(2,1)} %get-tuple-element.48), channel_id=1, source_target_pairs={{0,8},{1,9},{2,10},{3,11},{4,12},{5,13},{6,14},{7,15},{8,0},{9,1},... | collective-permute-start | bytes 2752520 | tf_op jit(solution)/shard_map/ppermute | solution.py:109
  188.6 60.6 %all-to-all-start.4 = ((bf16[16,16,3584]{2,1,0:T(8,128)(2,1)}), bf16[16,16,3584]{2,1,0:T(8,128)(2,1)}, u32[]{:S(2)}, u32[]{:S(2)}) async-start(bf16[16,16,3584]{2,1,0:T(8,128)(2,1)} %bitcast.122), calls=%async_computation.4 | async-start | bytes 3670016 | tf_op jit(solution)/shard_map/all_to_all | solution.py:98
  193.0 128.2 %collective-permute-start.13 = (bf16[32,3584]{1,0:T(8,128)(2,1)}, bf16[32,3584]{1,0:T(8,128)(2,1)S(1)}, u32[]{:S(2)}, u32[]{:S(2)}) collective-permute-start(bf16[32,3584]{1,0:T(8,128)(2,1)} %get-tuple-element.39), channel_id=1, source_target_pairs={{0,11},{1,10},{2,9},{3,8},{4,15},{5,14},{6,13},{7,12},{8,3},{9,2},... | collective-permute-start | bytes 688136 | tf_op jit(solution)/shard_map/ppermute | solution.py:158
  196.4 124.8 %collective-permute-start.14 = (bf16[32,3584]{1,0:T(8,128)(2,1)}, bf16[32,3584]{1,0:T(8,128)(2,1)S(1)}, u32[]{:S(2)}, u32[]{:S(2)}) collective-permute-start(bf16[32,3584]{1,0:T(8,128)(2,1)} %get-tuple-element.40), channel_id=1, source_target_pairs={{0,12},{1,13},{2,14},{3,15},{4,8},{5,9},{6,10},{7,11},{8,4},{9,5},... | collective-permute-start | bytes 688136 | tf_op jit(solution)/shard_map/ppermute | solution.py:158
  197.8 123.4 %collective-permute-start.15 = (bf16[32,3584]{1,0:T(8,128)(2,1)}, bf16[32,3584]{1,0:T(8,128)(2,1)S(1)}, u32[]{:S(2)}, u32[]{:S(2)}) collective-permute-start(bf16[32,3584]{1,0:T(8,128)(2,1)} %get-tuple-element.41), channel_id=1, source_target_pairs={{0,13},{1,12},{2,15},{3,14},{4,9},{5,8},{6,11},{7,10},{8,5},{9,4},... | collective-permute-start | bytes 688136 | tf_op jit(solution)/shard_map/ppermute | solution.py:158
  199.9 121.3 %collective-permute-start.16 = (bf16[32,3584]{1,0:T(8,128)(2,1)}, bf16[32,3584]{1,0:T(8,128)(2,1)S(1)}, u32[]{:S(2)}, u32[]{:S(2)}) collective-permute-start(bf16[32,3584]{1,0:T(8,128)(2,1)} %copy-done.1), channel_id=1, source_target_pairs={{0,14},{1,15},{2,12},{3,13},{4,10},{5,11},{6,8},{7,9},{8,6},{9,7},... | collective-permute-start | bytes 688136 | tf_op jit(solution)/shard_map/ppermute | solution.py:158
  249.2 6.0 %copy-start.9 = (bf16[128,3584]{1,0:T(8,128)(2,1)S(1)}, bf16[128,3584]{1,0:T(8,128)(2,1)}, u32[]{:S(2)}) copy-start(bf16[128,3584]{1,0:T(8,128)(2,1)} %multiply_convert_fusion) | copy-start | bytes 2752516
  253.2 0.6 copy-start.17
  254.4 12.0 %collective-permute-start.18 = (f32[2,3584]{1,0:T(2,128)}, f32[2,3584]{1,0:T(2,128)}, u32[]{:S(2)}, u32[]{:S(2)}) collective-permute-start(f32[2,3584]{1,0:T(2,128)} %pad_maximum_fusion.2), channel_id=1, source_target_pairs={{0,1},{1,0},{2,3},{3,2},{4,5},{5,4},{6,7},{7,6},{8,9},{9,8},{10,11... | collective-permute-start | bytes 86024 | tf_op jit(solution)/shard_map/ppermute | solution.py:223
  257.0 9.4 %copy-start.18 = (f32[1,3584]{1,0:T(1,128)S(1)}, f32[1,3584]{1,0:T(1,128)}, u32[]{:S(2)}) copy-start(f32[1,3584]{1,0:T(1,128)} %copy-done.17) | copy-start | bytes 43012
  257.0 49.5 %all-to-all-start.5 = ((bf16[8,32,3584]{2,1,0:T(8,128)(2,1)}), bf16[8,32,3584]{2,1,0:T(8,128)(2,1)}, u32[]{:S(2)}, u32[]{:S(2)}) async-start(bf16[8,32,3584]{2,1,0:T(8,128)(2,1)} %bitcast.119), calls=%async_computation.5 | async-start | bytes 3670016 | tf_op jit(solution)/shard_map/all_to_all | solution.py:101
  267.2 22.7 %collective-permute-start.19 = (f32[2,3584]{1,0:T(2,128)S(1)}, f32[2,3584]{1,0:T(2,128)S(1)}, u32[]{:S(2)}, u32[]{:S(2)}) collective-permute-start(f32[2,3584]{1,0:T(2,128)S(1)} %fusion.26), channel_id=1, source_target_pairs={{0,2},{1,3},{2,0},{3,1},{4,6},{5,7},{6,4},{7,5},{8,10},{9,11},{10,... | collective-permute-start | bytes 86024 | tf_op jit(solution)/shard_map/ppermute | solution.py:223
  269.3 27.9 %copy-start.6 = (bf16[2,128,3584]{2,1,0:T(8,128)(2,1)S(1)}, bf16[2,128,3584]{2,1,0:T(8,128)(2,1)}, u32[]{:S(2)}) copy-start(bf16[2,128,3584]{2,1,0:T(8,128)(2,1)} %copy-done.4) | copy-start | bytes 5505028
  290.7 9.5 %collective-permute-start.20 = (f32[2,3584]{1,0:T(2,128)S(1)}, f32[2,3584]{1,0:T(2,128)S(1)}, u32[]{:S(2)}, u32[]{:S(2)}) collective-permute-start(f32[2,3584]{1,0:T(2,128)S(1)} %fusion.58), channel_id=1, source_target_pairs={{0,4},{1,5},{2,6},{3,7},{4,0},{5,1},{6,2},{7,3},{8,12},{9,13},{10,... | collective-permute-start | bytes 86024 | tf_op jit(solution)/shard_map/ppermute | solution.py:223
  297.2 4.9 %copy-start.7 = (bf16[256,3584]{1,0:T(8,128)(2,1)S(1)}, bf16[256,3584]{1,0:T(8,128)(2,1)}, u32[]{:S(2)}) copy-start(bf16[256,3584]{1,0:T(8,128)(2,1)} %get-tuple-element.66) | copy-start | bytes 5505028
  300.2 5.7 %copy-start.19 = (f32[1,3584]{1,0:T(1,128)S(1)}, f32[1,3584]{1,0:T(1,128)}, u32[]{:S(2)}) copy-start(f32[1,3584]{1,0:T(1,128)} %get-tuple-element.56) | copy-start | bytes 43012
  300.2 4.8 %collective-permute-start.21 = (f32[2,3584]{1,0:T(2,128)S(1)}, f32[2,3584]{1,0:T(2,128)S(1)}, u32[]{:S(2)}, u32[]{:S(2)}) collective-permute-start(f32[2,3584]{1,0:T(2,128)S(1)} %add.106), channel_id=1, source_target_pairs={{0,8},{1,9},{2,10},{3,11},{4,12},{5,13},{6,14},{7,15},{8,0},{9,1},... | collective-permute-start | bytes 86024 | tf_op jit(solution)/shard_map/ppermute | solution.py:223
  305.1 16.1 %collective-permute-start.17 = (bf16[32,3584]{1,0:T(8,128)(2,1)}, bf16[32,3584]{1,0:T(8,128)(2,1)}, u32[]{:S(2)}, u32[]{:S(2)}) collective-permute-start(bf16[32,3584]{1,0:T(8,128)(2,1)} %get-tuple-element.43), channel_id=1, source_target_pairs={{0,15},{1,14},{2,13},{3,12},{4,11},{5,10},{6,9},{7,8},{8,7},{9,6},... | collective-permute-start | bytes 688136 | tf_op jit(solution)/shard_map/ppermute | solution.py:158
  306.5 2.9 copy-start.8
  309.4 1.9 copy-start.12
  309.4 5.0 %copy-start.22 = (pred[16]{0:T(512)(128)(4,1)S(1)}, pred[16]{0:T(512)(128)(4,1)}, u32[]{:S(2)}) copy-start(pred[16]{0:T(512)(128)(4,1)} %compare_and_fusion) | copy-start | bytes 52
  315.4 3.4 %copy-start.10 = (bf16[1,128,3584]{2,1,0:T(8,128)(2,1)S(1)}, bf16[1,128,3584]{2,1,0:T(8,128)(2,1)}, u32[]{:S(2)}) copy-start(bf16[1,128,3584]{2,1,0:T(8,128)(2,1)} %fusion.7) | copy-start | bytes 2752516
  318.8 1.8 copy-start.13
  318.8 1.8 copy-start.16

commit v5 on v3

--- a/solution.py
+++ b/solution.py
@@ -3,6 +3,8 @@
 import jax
 import jax.numpy as jnp
 from jax import lax
+from jax.experimental import pallas as pl
+from jax.experimental.pallas import tpu as pltpu
 from jax.sharding import PartitionSpec as P
 
 BF = jnp.bfloat16
@@ -13,6 +15,38 @@
 
 def mm(a, b, dims=((1,), (0,))):
     return lax.dot_general(a, b, (dims, ((), ())), preferred_element_type=F32)
+
+
+def column_block(width):
+    return next((b for b in (512, 256, 128) if width % b == 0), width)
+
+
+def pack_rows(key, first, second, groups, cap):
+    _, tokens, width = first.shape
+    step = column_block(width)
+
+    def kernel(key_ref, first_ref, second_ref, *outs):
+        slot = lax.broadcasted_iota(jnp.int32, (groups * cap, tokens), 0)
+        hot = (key_ref[...] == slot).astype(F32).astype(BF)
+        for at, rows_ref in enumerate((first_ref, second_ref)):
+            placed = mm(hot, rows_ref[0]).astype(BF)
+            for k in range(groups):
+                outs[k][at * cap : (at + 1) * cap, :] = placed[k * cap : (k + 1) * cap]
+
+    rows_spec = pl.BlockSpec((1, tokens, step), lambda i: (0, 0, i))
+    return pl.pallas_call(
+        kernel,
+        grid=(width // step,),
+        in_specs=[pl.BlockSpec((1, tokens), lambda i: (0, 0)), rows_spec, rows_spec],
+        out_specs=[pl.BlockSpec((2 * cap, step), lambda i: (0, i))] * groups,
+        out_shape=[jax.ShapeDtypeStruct((2 * cap, width), BF)] * groups,
+        compiler_params=pltpu.CompilerParams(vmem_limit_bytes=32 * 2**20),
+        cost_estimate=pl.CostEstimate(
+            flops=4 * groups * cap * tokens * width,
+            bytes_accessed=4 * (tokens + groups * cap) * width,
+            transcendentals=0,
+        ),
+    )(key, first, second)
 
 
 def per_device(residual, mlp_target, pre_acts, blocks, decoder, decoder_bias):
@@ -56,7 +90,6 @@
         return jnp.sum((same & earlier).astype(jnp.int32), axis=2)
 
     pre = pre_acts.reshape(layers, tokens, latents)
-    resid1_m = across(residual[1])
 
     order = ordinals(routes)
     routes_m, order_m = across(jnp.stack([routes, order]))
@@ -82,9 +115,33 @@
     )
     got_pre = everyone(sent_pre.reshape(devices, layers * cap, latents))
     got_pre = got_pre.reshape(devices, layers, cap, latents)
-    pre0 = got_pre[:, 0].reshape(slots, latents)
-    pre1 = got_pre[:, 1].reshape(slots, latents)
-    act0 = jnp.maximum(pre0, 0)
+    direct = devices <= 16 and cap % 16 == 0
+    if direct:
+        key = ((routes[:1] ^ me) * cap + order[:1]).astype(jnp.int32)
+        packed = pack_rows(key, mlp_target, residual, devices, cap)
+        arrivals = [packed[0]] + [
+            lax.ppermute(packed[k], "layer", [(i, i ^ k) for i in range(devices)])
+            for k in range(1, devices)
+        ]
+        windows = [[8, 9, 10], [1, 4, 5], [2, 6], [3, 7, 11, 12, 13, 14, 15]]
+        windows = [[k for k in ks if k < devices] for ks in windows]
+        sender = (me ^ jnp.arange(devices, dtype=jnp.int32)).astype(jnp.int32)
+    else:
+        arrivals = [
+            everyone(
+                jnp.concatenate(
+                    [
+                        mm(place[0], rows[0]).astype(BF).reshape(devices, cap, width)
+                        for rows in (mlp_target, residual)
+                    ],
+                    axis=1,
+                )
+            )
+        ]
+        windows = [[], [], [], [0]]
+
+    def received(window):
+        return [arrivals[k] for k in windows[window]]
 
     acts = turn(jnp.maximum(got_pre, 0))
     nothing = jnp.zeros((devices, 1, cap, latents), BF)
@@ -104,7 +161,7 @@
     sum_m = mm(flat(place_m), pieces_m, ROWS)
     sum_low_sent = sum_m.astype(BF)
     sum_low = across(sum_low_sent)
-    pieces_o = within(decode(after(wide[:half], sum_low_sent))).reshape(-1, width)
+    pieces_o = within(decode(after(wide[:half], (sum_low_sent, received(0))))).reshape(-1, width)
     sum_o = mm(flat(place_o), pieces_o, ROWS) + decoder_bias[1] - mlp_target[1].astype(F32)
     sum_high_sent = sum_o.astype(BF)
     sum_high = across(sum_high_sent)
@@ -115,24 +172,23 @@
     def send_errors(p, error):
         return within(mm(flat(p), error).astype(BF).reshape(half, layers * cap, width))
 
-    residual1 = after(residual[1], sum_high_sent)
-    resid1_in = within(
-        jnp.concatenate(
-            [
-                mm(flat(place_o[:, 1]), residual1).astype(BF).reshape(half, cap, width),
-                mm(flat(place_m[:, 1]), resid1_m).astype(BF).reshape(half, cap, width),
-            ],
-            axis=1,
-        )
-    )
-    errors_o = send_errors(place_o, after(error1, resid1_in))
-    errors_m = send_errors(place_m, after(error1_m, errors_o))
-
-    target_last = after(mlp_target[0], errors_m)
-    target0 = everyone(mm(place[0], target_last).astype(BF).reshape(devices, cap, width))
-    residual_last = after(residual[0], target0)
-    resid0 = everyone(mm(place[0], residual_last).astype(BF).reshape(devices, cap, width))
-    target0, resid0 = target0.reshape(slots, width), resid0.reshape(slots, width)
+    error1 = after(error1, received(1))
+    errors_o = send_errors(place_o, error1)
+
+    errors_m = send_errors(place_m, after(error1_m, (errors_o, received(2))))
+    residual1 = after(residual[1], (errors_m, received(3)))
+    resid1 = everyone(mm(place[1], residual1).astype(BF).reshape(devices, cap, width))
+    resid1 = resid1.reshape(slots, width)
+
+    if direct:
+        layer0 = jnp.stack(arrivals)
+        pre0 = jnp.take(got_pre[:, 0], sender, axis=0).reshape(slots, latents)
+    else:
+        layer0 = arrivals[0]
+        pre0 = got_pre[:, 0].reshape(slots, latents)
+    target0 = layer0[:, :cap].reshape(slots, width)
+    resid0 = layer0[:, cap:].reshape(slots, width)
+    act0 = jnp.maximum(pre0, 0)
     piece00 = mm(act0, decoder[0]).astype(BF).astype(F32)
     error0 = ((piece00 + decoder_bias[0] - target0.astype(F32)) * scale).astype(BF)
     empty0 = (decoder_bias[0] * scale).astype(BF).astype(F32)
@@ -157,21 +213,23 @@
     dec_later = mm(wide_o, errors_o, ROWS) + mm(wide_m, errors_m, ROWS)
     back = jnp.concatenate([mm(errors_o, dec1, LAST), mm(errors_m, dec1, LAST)], axis=0)
     back = back.reshape(devices, layers, cap, 2 * latents)
-    pres = turn(got_pre)
-    grad1 = jnp.where(pres[:, 1] > 0, back[:, 1, :, latents:], 0.0)
-    grad0 = turn(back[:, 0, :, :latents]).reshape(slots, latents) + mm(error0, decoder[0], LAST)
+    back = turn(back)
+    back0 = back[:, 0, :, :latents]
+    if direct:
+        back0 = jnp.take(back0, sender, axis=0)
+    grad0 = back0.reshape(slots, latents) + mm(error0, decoder[0], LAST)
     grad0 = jnp.where(pre0 > 0, grad0, 0.0)
-    low1 = grad1.astype(BF).reshape(2, half, cap, latents).swapaxes(0, 1).reshape(slots, latents)
+    grad1 = jnp.where(got_pre[:, 1] > 0, back[:, 1, :, latents:], 0.0).reshape(slots, latents)
+    enc_bias = jnp.stack([jnp.sum(grad0, axis=0), jnp.sum(grad1, axis=0)])
     dec = jnp.concatenate(
         [mm(act0, error0, ROWS).astype(BF)[None], dec_later.astype(BF).reshape(2, latents, width)]
     )
     enc = jnp.stack(
         [
             mm(resid0, grad0.astype(BF), ROWS).astype(BF),
-            mm(resid1_in.reshape(slots, width), low1, ROWS).astype(BF),
+            mm(resid1, grad1.astype(BF), ROWS).astype(BF),
         ]
     )
-    enc_bias = jnp.stack([jnp.sum(grad0, axis=0), jnp.sum(grad1, axis=(0, 1))])
     return dec, enc, enc_bias, bias_grad
 
 

time: 359 us -> 320 us (0.89); the launches traced: 358 us -> 314 us
  waiting for transfers between devices: 222 us -> 173 us
  blocking collectives: 26.3 us -> 0 us
  local copies, waits for them, and re-layouts: 7.64 us -> 32.5 us
  Pallas kernels: 0 us -> 3.71 us
    ppermute x4 -> x3, waiting for transfers between devices: 137 us -> 78.4 us  [across(): return lax.ppermute(x, 'layer', mirror)]
    all_to_all x1 -> x0, blocking collectives: 26.3 us -> none  [within(): lax.all_to_all(x, 'layer', split_axis=0, concat_axis=0, tiled=True, axis_...]
    unnamed x16 -> x63, local copies, waits for them, and re-layouts: 2.1 us -> 21.2 us
    ppermute x0 -> x15, starting transfers between devices: none -> 18.2 us  [per_device(): lax.ppermute(packed[k], 'layer', [(i, i ^ k) for i in range(devices)])]
    ppermute x0 -> x15, waiting for transfers between devices: none -> 15.6 us  [per_device(): lax.ppermute(packed[k], 'layer', [(i, i ^ k) for i in range(devices)])]
    all_to_all x4, waiting for transfers between devices: 24.2 us -> 39.5 us  [within(): lax.all_to_all(x, 'layer', split_axis=0, concat_axis=0, tiled=True, axis_...]
    all_to_all x3 -> x2, starting transfers between devices: 22.3 us -> 9.72 us  [everyone(): return lax.all_to_all(x, 'layer', split_axis=0, concat_axis=0, tiled=True)]
    all_to_all x3 -> x2, waiting for transfers between devices: 30.6 us -> 19.1 us  [everyone(): return lax.all_to_all(x, 'layer', split_axis=0, concat_axis=0, tiled=True)]
  transfers between devices with their start and end apart: 15 -> 28, of which waited for: 13 -> 9; matrix products, arithmetic and copies ran while one was open for 8% -> 23% of each run, Pallas kernels for 0% -> 0%
where the time goes in v5:
time: 320 us; the launch traced here: 314 us
  waiting for transfers between devices  173 us (54%)
  starting transfers between devices  52.6 us (16%)
  matrix products  38.5 us (12%)
  local copies, waits for them, and re-layouts  32.5 us (10%)
  other arithmetic  12.6 us (4%)
  Pallas kernels  3.71 us (1%)
    ppermute x3, waiting for transfers between devices, across(): return lax.ppermute(x, 'layer', mirror)  78.4 us
    all_to_all x4, waiting for transfers between devices, within(): lax.all_to_all(x, 'layer', split_axis=0, concat_axis=0, tiled=True, axis_...  39.5 us
    dot_general x18, matrix products, mm(): return lax.dot_general(a, b, (dims, ((), ())), preferred_element_type=F32)  38.5 us
    unnamed x63, local copies, waits for them, and re-layouts  21.2 us
    ppermute x4, waiting for transfers between devices, total(): x = x + lax.ppermute(x, 'layer', [(i, i ^ step) for i in range(devices)])  20.7 us
    all_to_all x2, waiting for transfers between devices, everyone(): return lax.all_to_all(x, 'layer', split_axis=0, concat_axis=0, tiled=True)  19.1 us
    ppermute x15, starting transfers between devices, per_device(): lax.ppermute(packed[k], 'layer', [(i, i ^ k) for i in range(devices)])  18.2 us
    all_to_all x4, starting transfers between devices, within(): lax.all_to_all(x, 'layer', split_axis=0, concat_axis=0, tiled=True, axis_...  17.1 us
  transfers between devices with their start and end apart: 28, of which 9 were waited for; matrix products, arithmetic and copies ran while one was open for 23% of the time, Pallas kernels for 0%

profile of v5, /device:TPU:0, one launch (start us, length us, event | category | flops | bytes accessed | tf_op | source)
XLA Modules:
  0.0 314.3 jit_solution(9881584705176949071)
XLA Ops:
  0.7 0.9 convert_reduce_fusion.2
  2.3 1.5 copy-done
  3.8 1.5 copy-done.2
  5.3 3.7 %shard_map.93 = (bf16[32,3584]{1,0:T(8,128)(2,1)S(1)}, bf16[32,3584]{1,0:T(8,128)(2,1)}, bf16[32,3584]{1,0:T(8,128)(2,1)S(1)}, bf16[32,3584]{1,0:T(8,128)(2,1)S(...) custom-call(s32[1,128]{1,0:T(1,128)S(1)} %bitcast_add_fusion.key_ref, ...), custom_call_target="tpu_custom_call" | custom-call | flops 469762048 | bytes 5505024 | tf_op jit(solution)/shard_map/pallas_call | solution.py:37
  9.4 2.5 collective-permute-start.1
  12.1 1.8 collective-permute-start.3
  15.4 4.9 %all-to-all-start = ((bf16[16,32,128]{2,1,0:T(8,128)(2,1)}), bf16[16,32,128]{2,1,0:T(8,128)(2,1)}, u32[]{:S(2)}, u32[]{:S(2)}) async-start(bf16[16,32,128]{2,1,0:T(8,128)(2,1)} %bitcast.169), calls=%async_computation | async-start | bytes 262144 | tf_op jit(solution)/shard_map/all_to_all | solution.py:66
  20.3 2.8 collective-permute-start.15
  25.7 2.9 slice.105
  28.6 0.9 collective-permute-start.4
  29.7 1.5 collective-permute-start.5
  31.2 1.7 bitcast_dynamic-update-slice_fusion.14
  32.9 1.4 collective-permute-start.6
  34.3 1.7 bitcast_dynamic-update-slice_fusion.13
  36.5 1.6 bitcast_dynamic-update-slice_fusion.12
  38.2 1.9 collective-permute-start.8
  40.0 1.6 bitcast_dynamic-update-slice_fusion.11
  41.6 1.5 collective-permute-start.9
  43.8 5.3 %collective-permute-done.5 = bf16[32,3584]{1,0:T(8,128)(2,1)S(1)} collective-permute-done((bf16[32,3584]{1,0:T(8,128)(2,1)S(1)}, bf16[32,3584]{1,0:T(8,128)(2,1)S(1)}, u32[]{:S(2)}, u32[]{:S(2)}) %collective-permute-start.5) | collective-permute-done | bytes 229408 | tf_op jit(solution)/shard_map/ppermute | solution.py:123
  49.1 1.9 collective-permute-start.10
  51.7 1.0 broadcast_maximum_fusion
  53.2 1.9 convolution_convert_fusion.5
  55.1 4.7 %all-to-all-start.1 = ((bf16[8,32,3584]{2,1,0:T(8,128)(2,1)}), bf16[8,32,3584]{2,1,0:T(8,128)(2,1)}, u32[]{:S(2)}, u32[]{:S(2)}) async-start(bf16[8,32,3584]{2,1,0:T(8,128)(2,1)} %bitcast.162), calls=%async_computation.1 | async-start | bytes 3670016 | tf_op jit(solution)/shard_map/all_to_all | solution.py:69
  59.8 1.9 collective-permute-start.11
  62.5 1.7 collective-permute-start.12
  64.9 3.5 %collective-permute-done.8 = bf16[32,3584]{1,0:T(8,128)(2,1)S(1)} collective-permute-done((bf16[32,3584]{1,0:T(8,128)(2,1)S(1)}, bf16[32,3584]{1,0:T(8,128)(2,1)S(1)}, u32[]{:S(2)}, u32[]{:S(2)}) %collective-permute-start.8) | collective-permute-done | bytes 229408 | tf_op jit(solution)/shard_map/ppermute | solution.py:123
  69.2 6.8 %collective-permute-done.9 = bf16[32,3584]{1,0:T(8,128)(2,1)S(1)} collective-permute-done((bf16[32,3584]{1,0:T(8,128)(2,1)S(1)}, bf16[32,3584]{1,0:T(8,128)(2,1)S(1)}, u32[]{:S(2)}, u32[]{:S(2)}) %collective-permute-start.9) | collective-permute-done | bytes 229408 | tf_op jit(solution)/shard_map/ppermute | solution.py:123
  75.9 0.7 bitcast_dynamic-update-slice_fusion.5
  76.7 39.5 %all-to-all-done.1 = bf16[8,32,3584]{2,1,0:T(8,128)(2,1)} async-done(((bf16[8,32,3584]{2,1,0:T(8,128)(2,1)}), bf16[8,32,3584]{2,1,0:T(8,128)(2,1)}, u32[]{:S(2)}, u32[]{:S(2)}) %all-to-all-start.1) | async-done | bytes 1835040 | tf_op jit(solution)/shard_map/all_to_all | solution.py:69
  116.2 3.7 %fusion.36 = (bf16[128,3584]{1,0:T(8,128)(2,1)}, f32[128,3584]{1,0:T(8,128)}) fusion(pred[256,128]{1,0:T(8,128)(4,1)S(1)} %bitcast.170, bf16[256,3584]{1,0:T(8,128)(2,1)} %bitcast.46), kind=kOutput, calls=%fused_computation.118 | convolution fusion | flops 235339776 | bytes 4620288 | tf_op jit(solution)/shard_map/dot_general | solution.py:17
  119.9 1.9 convolution_convert_fusion.4
  121.8 4.3 %all-to-all-start.2 = ((bf16[8,32,3584]{2,1,0:T(8,128)(2,1)}), bf16[8,32,3584]{2,1,0:T(8,128)(2,1)}, u32[]{:S(2)}, u32[]{:S(2)}) async-start(bf16[8,32,3584]{2,1,0:T(8,128)(2,1)} %bitcast.48), calls=%async_computation.2 | async-start | bytes 3670016 | tf_op jit(solution)/shard_map/all_to_all | solution.py:69
  126.1 1.8 bitcast_dynamic-update-slice_fusion.4
  127.9 1.6 bitcast_dynamic-update-slice_fusion.3
  129.5 1.6 bitcast_dynamic-update-slice_fusion.2
  131.9 41.2 %collective-permute-done.16 = bf16[128,3584]{1,0:T(8,128)(2,1)} collective-permute-done((bf16[128,3584]{1,0:T(8,128)(2,1)}, bf16[128,3584]{1,0:T(8,128)(2,1)}, u32[]{:S(2)}, u32[]{:S(2)}) %collective-permute-start.16) | collective-permute-done | bytes 917536 | tf_op jit(solution)/shard_map/ppermute | solution.py:77
  173.1 3.3 %fusion.34 = (bf16[128,3584]{1,0:T(8,128)(2,1)}, bf16[128,3584]{1,0:T(8,128)(2,1)S(1)}) fusion(bf16[128,3584]{1,0:T(8,128)(2,1)} %collective-permute-done.16, bf16[2,128,3584]{2,1,0:T(8,128)(2,1)S(1)} %copy-done.3, f32[3584]{0:T(1024)S(1)} %get-tuple-element.45, pred[256,128]{1,0:T(8,128)(4,1)S(1)} %bitcast.172, bf16[256,3584]{1,0:T(8,128)(2,1)} %bitcast.49), kind=kOutput, calls=%fused_computation.116 | convolution fusion | flops 238551040 | bytes 5552128 | tf_op jit(solution)/shard_map/dot_general | solution.py:17
  176.4 2.0 convolution_convert_fusion.2
  178.4 3.6 %all-to-all-start.3 = ((bf16[8,32,3584]{2,1,0:T(8,128)(2,1)}), bf16[8,32,3584]{2,1,0:T(8,128)(2,1)S(1)}, u32[]{:S(2)}, u32[]{:S(2)}) async-start(bf16[8,32,3584]{2,1,0:T(8,128)(2,1)} %bitcast.163), calls=%async_computation.3 | async-start | bytes 3670016 | tf_op jit(solution)/shard_map/all_to_all | solution.py:69
  182.0 1.6 bitcast_dynamic-update-slice_fusion
  183.6 4.2 %fusion.33 = (bf16[16,16,3584]{2,1,0:T(8,128)(2,1)}, bf16[16,16,3584]{2,1,0:T(8,128)(2,1)}) fusion(bf16[16,32,3584]{2,1,0:T(8,128)(2,1)} %bitcast_dynamic-update-slice_fusion), kind=kLoop, calls=%fused_computation.115 | loop fusion | bytes 7340032 | tf_op jit(solution)/shard_map/slice | solution.py:190
  188.3 0.8 slice_bitcast_fusion.6
  190.0 4.0 %convert_reduce_fusion = (f32[3584]{0:T(1024)S(1)}, bf16[256,3584]{1,0:T(8,128)(2,1)}) fusion(bf16[16,16,3584]{2,1,0:T(8,128)(2,1)} %get-tuple-element.49, f32[3584]{0:T(1024)S(1)} %get-tuple-element.44, bf16[256,128]{1,0:T(8,128)(2,1)S(1)} %bitcast.175, bf16[3,128,3584]{2,1,0:T(8,128)(2,1)} %param.10), kind=kOutput, calls=%fused_computation.23 | convolution fusion | flops 243134976 | bytes 4681728 | tf_op jit(solution)/shard_map/dot_general | solution.py:17
  194.2 37.2 %collective-permute-done.17 = bf16[128,3584]{1,0:T(8,128)(2,1)} collective-permute-done((bf16[128,3584]{1,0:T(8,128)(2,1)}, bf16[128,3584]{1,0:T(8,128)(2,1)}, u32[]{:S(2)}, u32[]{:S(2)}) %collective-permute-start.17) | collective-permute-done | bytes 917536 | tf_op jit(solution)/shard_map/ppermute | solution.py:77
  231.4 1.4 multiply_convert_fusion
  232.9 1.9 convolution_convert_fusion.1
  234.8 4.5 %all-to-all-start.4 = ((bf16[8,32,3584]{2,1,0:T(8,128)(2,1)}), bf16[8,32,3584]{2,1,0:T(8,128)(2,1)}, u32[]{:S(2)}, u32[]{:S(2)}) async-start(bf16[8,32,3584]{2,1,0:T(8,128)(2,1)} %bitcast.161), calls=%async_computation.4 | async-start | bytes 3670016 | tf_op jit(solution)/shard_map/all_to_all | solution.py:69
  240.7 1.9 collective-permute-start.19
  242.7 20.0 %collective-permute-done.19 = f32[2,3584]{1,0:T(2,128)S(1)} collective-permute-done((f32[2,3584]{1,0:T(2,128)S(1)}, f32[2,3584]{1,0:T(2,128)S(1)}, u32[]{:S(2)}, u32[]{:S(2)}) %collective-permute-start.19) | collective-permute-done | bytes 28704 | tf_op jit(solution)/shard_map/ppermute | solution.py:200
  262.7 1.6 collective-permute-start.20
  264.2 2.9 fusion.4
  267.4 2.0 convolution_convert_fusion
  269.4 4.8 %all-to-all-start.5 = ((bf16[16,16,3584]{2,1,0:T(8,128)(2,1)}), bf16[16,16,3584]{2,1,0:T(8,128)(2,1)}, u32[]{:S(2)}, u32[]{:S(2)}) async-start(bf16[16,16,3584]{2,1,0:T(8,128)(2,1)} %bitcast.160), calls=%async_computation.5 | async-start | bytes 3670016 | tf_op jit(solution)/shard_map/all_to_all | solution.py:66
  274.8 2.3 fusion.39
  277.1 2.5 fusion.38
  279.6 2.3 broadcast_select_fusion.1
  281.9 0.9 fusion.31
  282.8 0.8 gather_fusion.1
  283.7 2.5 fusion.37
  287.6 2.2 fusion.2
  289.8 1.8 pad_maximum_fusion
  291.6 19.1 %all-to-all-done.5 = bf16[16,16,3584]{2,1,0:T(8,128)(2,1)} async-done(((bf16[16,16,3584]{2,1,0:T(8,128)(2,1)}), bf16[16,16,3584]{2,1,0:T(8,128)(2,1)}, u32[]{:S(2)}, u32[]{:S(2)}) %all-to-all-start.5) | async-done | bytes 1835040 | tf_op jit(solution)/shard_map/all_to_all | solution.py:66
  310.7 2.2 fusion.6
  312.9 1.4 pad_maximum_fusion.1
  (123 shorter events, 16.1 us)
Async XLA Ops:
  2.3 1.5 copy-start
  3.8 1.5 copy-start.2
  5.3 8.6 %copy-start.19 = (s32[2,128,1]{1,2,0:T(1,128)S(1)}, s32[2,128,1]{1,2,0:T(1,128)}, u32[]{:S(2)}) copy-start(s32[2,128,1]{1,2,0:T(1,128)} %param.9) | copy-start | bytes 3076
  5.3 8.6 %copy-start.23 = (bf16[2,128,1,128]{3,1,2,0:T(8,128)(2,1)S(1)}, bf16[2,128,1,128]{3,1,2,0:T(8,128)(2,1)}, u32[]{:S(2)}) copy-start(bf16[2,128,1,128]{3,1,2,0:T(8,128)(2,1)} %param.8) | copy-start | bytes 196612
  5.3 20.3 %copy-start.20 = (f32[2,3584]{1,0:T(2,128)S(1)}, f32[2,3584]{1,0:T(2,128)}, u32[]{:S(2)}) copy-start(f32[2,3584]{1,0:T(2,128)} %param.11) | copy-start | bytes 86020
  9.0 20.7 %collective-permute-start = (bf16[32,3584]{1,0:T(8,128)(2,1)}, bf16[32,3584]{1,0:T(8,128)(2,1)}, u32[]{:S(2)}, u32[]{:S(2)}) collective-permute-start(bf16[32,3584]{1,0:T(8,128)(2,1)} %get-tuple-element.25), channel_id=1, source_target_pairs={{0,1},{1,0},{2,3},{3,2},{4,5},{5,4},{6,7},{7,6},{8,9},{9,8},{10,11... | collective-permute-start | bytes 688136 | tf_op jit(solution)/shard_map/ppermute | solution.py:123
  9.4 23.4 %collective-permute-start.1 = (bf16[32,3584]{1,0:T(8,128)(2,1)S(1)}, bf16[32,3584]{1,0:T(8,128)(2,1)}, u32[]{:S(2)}, u32[]{:S(2)}) collective-permute-start(bf16[32,3584]{1,0:T(8,128)(2,1)S(1)} %get-tuple-element.26), channel_id=1, source_target_pairs={{0,2},{1,3},{2,0},{3,1},{4,6},{5,7},{6,4},{7,5},{8,10},{9,11},{10,... | collective-permute-start | bytes 688136 | tf_op jit(solution)/shard_map/ppermute | solution.py:123
  11.9 24.0 %collective-permute-start.2 = (bf16[32,3584]{1,0:T(8,128)(2,1)S(1)}, bf16[32,3584]{1,0:T(8,128)(2,1)}, u32[]{:S(2)}, u32[]{:S(2)}) collective-permute-start(bf16[32,3584]{1,0:T(8,128)(2,1)S(1)} %get-tuple-element.27), channel_id=1, source_target_pairs={{0,3},{1,2},{2,1},{3,0},{4,7},{5,6},{6,5},{7,4},{8,11},{9,10},{10,... | collective-permute-start | bytes 688136 | tf_op jit(solution)/shard_map/ppermute | solution.py:123
  12.1 26.1 %collective-permute-start.3 = (bf16[32,3584]{1,0:T(8,128)(2,1)S(1)}, bf16[32,3584]{1,0:T(8,128)(2,1)}, u32[]{:S(2)}, u32[]{:S(2)}) collective-permute-start(bf16[32,3584]{1,0:T(8,128)(2,1)S(1)} %get-tuple-element.28), channel_id=1, source_target_pairs={{0,4},{1,5},{2,6},{3,7},{4,0},{5,1},{6,2},{7,3},{8,12},{9,13},{10,... | collective-permute-start | bytes 688136 | tf_op jit(solution)/shard_map/ppermute | solution.py:123
  13.9 0.6 copy-start.17
  15.4 36.3 %all-to-all-start = ((bf16[16,32,128]{2,1,0:T(8,128)(2,1)}), bf16[16,32,128]{2,1,0:T(8,128)(2,1)}, u32[]{:S(2)}, u32[]{:S(2)}) async-start(bf16[16,32,128]{2,1,0:T(8,128)(2,1)} %bitcast.169), calls=%async_computation | async-start | bytes 262144 | tf_op jit(solution)/shard_map/all_to_all | solution.py:66
  20.3 8.2 %collective-permute-start.15 = (s32[2,2,128]{2,1,0:T(2,128)S(1)}, s32[2,2,128]{2,1,0:T(2,128)S(1)}, u32[]{:S(2)}, u32[]{:S(2)}) collective-permute-start(s32[2,2,128]{2,1,0:T(2,128)S(1)} %pad_add_fusion), channel_id=1, source_target_pairs={{0,8},{1,9},{2,10},{3,11},{4,12},{5,13},{6,14},{7,15},{8,0},{9,1},... | collective-permute-start | bytes 6152 | tf_op jit(solution)/shard_map/ppermute | solution.py:77
  25.7 3.9 %copy-start.21 = (pred[2,16,128]{2,1,0:T(8,128)(4,1)S(1)}, pred[2,16,128]{2,1,0:T(8,128)(4,1)}, u32[]{:S(2)}) copy-start(pred[2,16,128]{2,1,0:T(8,128)(4,1)} %iota_compare_fusion.5) | copy-start | bytes 12292
  28.6 13.1 %collective-permute-start.4 = (bf16[32,3584]{1,0:T(8,128)(2,1)S(1)}, bf16[32,3584]{1,0:T(8,128)(2,1)S(1)}, u32[]{:S(2)}, u32[]{:S(2)}) collective-permute-start(bf16[32,3584]{1,0:T(8,128)(2,1)S(1)} %get-tuple-element.29), channel_id=1, source_target_pairs={{0,5},{1,4},{2,7},{3,6},{4,1},{5,0},{6,3},{7,2},{8,13},{9,12},{10,... | collective-permute-start | bytes 688136 | tf_op jit(solution)/shard_map/ppermute | solution.py:123
  29.7 19.4 %collective-permute-start.5 = (bf16[32,3584]{1,0:T(8,128)(2,1)S(1)}, bf16[32,3584]{1,0:T(8,128)(2,1)S(1)}, u32[]{:S(2)}, u32[]{:S(2)}) collective-permute-start(bf16[32,3584]{1,0:T(8,128)(2,1)S(1)} %get-tuple-element.30), channel_id=1, source_target_pairs={{0,6},{1,7},{2,4},{3,5},{4,2},{5,3},{6,0},{7,1},{8,14},{9,15},{10,... | collective-permute-start | bytes 688136 | tf_op jit(solution)/shard_map/ppermute | solution.py:123
  32.9 27.0 %collective-permute-start.6 = (bf16[32,3584]{1,0:T(8,128)(2,1)S(1)}, bf16[32,3584]{1,0:T(8,128)(2,1)S(1)}, u32[]{:S(2)}, u32[]{:S(2)}) collective-permute-start(bf16[32,3584]{1,0:T(8,128)(2,1)S(1)} %get-tuple-element.31), channel_id=1, source_target_pairs={{0,7},{1,6},{2,5},{3,4},{4,3},{5,2},{6,1},{7,0},{8,15},{9,14},{10,... | collective-permute-start | bytes 688136 | tf_op jit(solution)/shard_map/ppermute | solution.py:123
  36.0 26.5 %collective-permute-start.7 = (bf16[32,3584]{1,0:T(8,128)(2,1)S(1)}, bf16[32,3584]{1,0:T(8,128)(2,1)S(1)}, u32[]{:S(2)}, u32[]{:S(2)}) collective-permute-start(bf16[32,3584]{1,0:T(8,128)(2,1)S(1)} %get-tuple-element.32), channel_id=1, source_target_pairs={{0,8},{1,9},{2,10},{3,11},{4,12},{5,13},{6,14},{7,15},{8,0},{9,1},... | collective-permute-start | bytes 688136 | tf_op jit(solution)/shard_map/ppermute | solution.py:123
  38.2 30.3 %collective-permute-start.8 = (bf16[32,3584]{1,0:T(8,128)(2,1)S(1)}, bf16[32,3584]{1,0:T(8,128)(2,1)S(1)}, u32[]{:S(2)}, u32[]{:S(2)}) collective-permute-start(bf16[32,3584]{1,0:T(8,128)(2,1)S(1)} %get-tuple-element.33), channel_id=1, source_target_pairs={{0,9},{1,8},{2,11},{3,10},{4,13},{5,12},{6,15},{7,14},{8,1},{9,0},... | collective-permute-start | bytes 688136 | tf_op jit(solution)/shard_map/ppermute | solution.py:123
  41.6 34.3 %collective-permute-start.9 = (bf16[32,3584]{1,0:T(8,128)(2,1)S(1)}, bf16[32,3584]{1,0:T(8,128)(2,1)S(1)}, u32[]{:S(2)}, u32[]{:S(2)}) collective-permute-start(bf16[32,3584]{1,0:T(8,128)(2,1)S(1)} %get-tuple-element.34), channel_id=1, source_target_pairs={{0,10},{1,11},{2,8},{3,9},{4,14},{5,15},{6,12},{7,13},{8,2},{9,3},... | collective-permute-start | bytes 688136 | tf_op jit(solution)/shard_map/ppermute | solution.py:123
  49.1 77.0 %collective-permute-start.10 = (bf16[32,3584]{1,0:T(8,128)(2,1)S(1)}, bf16[32,3584]{1,0:T(8,128)(2,1)}, u32[]{:S(2)}, u32[]{:S(2)}) collective-permute-start(bf16[32,3584]{1,0:T(8,128)(2,1)S(1)} %get-tuple-element.35), channel_id=1, source_target_pairs={{0,11},{1,10},{2,9},{3,8},{4,15},{5,14},{6,13},{7,12},{8,3},{9,2},... | collective-permute-start | bytes 688136 | tf_op jit(solution)/shard_map/ppermute | solution.py:123
  51.6 1.6 copy-start.4
  52.8 2.3 copy-start.13
  52.8 67.0 %copy-start.15 = (bf16[8,2,16,256]{3,2,1,0:T(8,128)(2,1)}, bf16[8,2,16,256]{3,2,1,0:T(8,128)(2,1)S(1)}, u32[]{:S(2)}) copy-start(bf16[8,2,16,256]{3,2,1,0:T(8,128)(2,1)S(1)} %get-tuple-element.56) | copy-start | bytes 393220
  55.1 61.1 %all-to-all-start.1 = ((bf16[8,32,3584]{2,1,0:T(8,128)(2,1)}), bf16[8,32,3584]{2,1,0:T(8,128)(2,1)}, u32[]{:S(2)}, u32[]{:S(2)}) async-start(bf16[8,32,3584]{2,1,0:T(8,128)(2,1)} %bitcast.162), calls=%async_computation.1 | async-start | bytes 3670016 | tf_op jit(solution)/shard_map/all_to_all | solution.py:69
  59.8 68.1 %collective-permute-start.11 = (bf16[32,3584]{1,0:T(8,128)(2,1)S(1)}, bf16[32,3584]{1,0:T(8,128)(2,1)}, u32[]{:S(2)}, u32[]{:S(2)}) collective-permute-start(bf16[32,3584]{1,0:T(8,128)(2,1)S(1)} %get-tuple-element.36), channel_id=1, source_target_pairs={{0,12},{1,13},{2,14},{3,15},{4,8},{5,9},{6,10},{7,11},{8,4},{9,5},... | collective-permute-start | bytes 688136 | tf_op jit(solution)/shard_map/ppermute | solution.py:123
  62.5 67.1 %collective-permute-start.12 = (bf16[32,3584]{1,0:T(8,128)(2,1)S(1)}, bf16[32,3584]{1,0:T(8,128)(2,1)}, u32[]{:S(2)}, u32[]{:S(2)}) collective-permute-start(bf16[32,3584]{1,0:T(8,128)(2,1)S(1)} %get-tuple-element.37), channel_id=1, source_target_pairs={{0,13},{1,12},{2,15},{3,14},{4,9},{5,8},{6,11},{7,10},{8,5},{9,4},... | collective-permute-start | bytes 688136 | tf_op jit(solution)/shard_map/ppermute | solution.py:123
  68.5 62.7 %collective-permute-start.13 = (bf16[32,3584]{1,0:T(8,128)(2,1)S(1)}, bf16[32,3584]{1,0:T(8,128)(2,1)S(1)}, u32[]{:S(2)}, u32[]{:S(2)}) collective-permute-start(bf16[32,3584]{1,0:T(8,128)(2,1)S(1)} %get-tuple-element.38), channel_id=1, source_target_pairs={{0,14},{1,15},{2,12},{3,13},{4,10},{5,11},{6,8},{7,9},{8,6},{9,7},... | collective-permute-start | bytes 688136 | tf_op jit(solution)/shard_map/ppermute | solution.py:123
  75.9 106.0 %collective-permute-start.14 = (bf16[32,3584]{1,0:T(8,128)(2,1)S(1)}, bf16[32,3584]{1,0:T(8,128)(2,1)}, u32[]{:S(2)}, u32[]{:S(2)}) collective-permute-start(bf16[32,3584]{1,0:T(8,128)(2,1)S(1)} %get-tuple-element.39), channel_id=1, source_target_pairs={{0,15},{1,14},{2,13},{3,12},{4,11},{5,10},{6,9},{7,8},{8,7},{9,6},... | collective-permute-start | bytes 688136 | tf_op jit(solution)/shard_map/ppermute | solution.py:123
  116.2 3.7 %copy-start.5 = (bf16[2,128,3584]{2,1,0:T(8,128)(2,1)S(1)}, bf16[2,128,3584]{2,1,0:T(8,128)(2,1)}, u32[]{:S(2)}) copy-start(bf16[2,128,3584]{2,1,0:T(8,128)(2,1)} %slice.105) | copy-start | bytes 5505028
  121.8 51.3 %all-to-all-start.2 = ((bf16[8,32,3584]{2,1,0:T(8,128)(2,1)}), bf16[8,32,3584]{2,1,0:T(8,128)(2,1)}, u32[]{:S(2)}, u32[]{:S(2)}) async-start(bf16[8,32,3584]{2,1,0:T(8,128)(2,1)} %bitcast.48), calls=%async_computation.2 | async-start | bytes 3670016 | tf_op jit(solution)/shard_map/all_to_all | solution.py:69
  126.1 47.0 %copy-start.3 = (bf16[2,128,3584]{2,1,0:T(8,128)(2,1)S(1)}, bf16[2,128,3584]{2,1,0:T(8,128)(2,1)}, u32[]{:S(2)}) copy-start(bf16[2,128,3584]{2,1,0:T(8,128)(2,1)} %first_ref.1) | copy-start | bytes 5505028
  129.5 43.5 %collective-permute-start.16 = (bf16[128,3584]{1,0:T(8,128)(2,1)}, bf16[128,3584]{1,0:T(8,128)(2,1)}, u32[]{:S(2)}, u32[]{:S(2)}) collective-permute-start(bf16[128,3584]{1,0:T(8,128)(2,1)} %get-tuple-element.64), channel_id=1, source_target_pairs={{0,8},{1,9},{2,10},{3,11},{4,12},{5,13},{6,14},{7,15},{8,0},{9,1},... | collective-permute-start | bytes 2752520 | tf_op jit(solution)/shard_map/ppermute | solution.py:77
  178.4 54.5 %all-to-all-start.3 = ((bf16[8,32,3584]{2,1,0:T(8,128)(2,1)}), bf16[8,32,3584]{2,1,0:T(8,128)(2,1)S(1)}, u32[]{:S(2)}, u32[]{:S(2)}) async-start(bf16[8,32,3584]{2,1,0:T(8,128)(2,1)} %bitcast.163), calls=%async_computation.3 | async-start | bytes 3670016 | tf_op jit(solution)/shard_map/all_to_all | solution.py:69
  183.6 6.3 %copy-start.22 = (pred[16]{0:T(512)(128)(4,1)S(1)}, pred[16]{0:T(512)(128)(4,1)}, u32[]{:S(2)}) copy-start(pred[16]{0:T(512)(128)(4,1)} %compare_and_fusion) | copy-start | bytes 52
  187.8 43.6 %collective-permute-start.17 = (bf16[128,3584]{1,0:T(8,128)(2,1)}, bf16[128,3584]{1,0:T(8,128)(2,1)}, u32[]{:S(2)}, u32[]{:S(2)}) collective-permute-start(bf16[128,3584]{1,0:T(8,128)(2,1)} %get-tuple-element.50), channel_id=1, source_target_pairs={{0,8},{1,9},{2,10},{3,11},{4,12},{5,13},{6,14},{7,15},{8,0},{9,1},... | collective-permute-start | bytes 2752520 | tf_op jit(solution)/shard_map/ppermute | solution.py:77
  190.0 41.4 %copy-start.9 = (f32[128,3584]{1,0:T(8,128)S(1)}, f32[128,3584]{1,0:T(8,128)}, u32[]{:S(2)}) copy-start(f32[128,3584]{1,0:T(8,128)} %get-tuple-element.65) | copy-start | bytes 5505028
  232.8 1.9 copy-start.10
  234.8 5.0 %copy-start.1 = (bf16[2,128,3584]{2,1,0:T(8,128)(2,1)S(1)}, bf16[2,128,3584]{2,1,0:T(8,128)(2,1)}, u32[]{:S(2)}) copy-start(bf16[2,128,3584]{2,1,0:T(8,128)(2,1)} %second_ref.1) | copy-start | bytes 5505028
  234.8 32.6 %all-to-all-start.4 = ((bf16[8,32,3584]{2,1,0:T(8,128)(2,1)}), bf16[8,32,3584]{2,1,0:T(8,128)(2,1)}, u32[]{:S(2)}, u32[]{:S(2)}) async-start(bf16[8,32,3584]{2,1,0:T(8,128)(2,1)} %bitcast.161), calls=%async_computation.4 | async-start | bytes 3670016 | tf_op jit(solution)/shard_map/all_to_all | solution.py:69
  239.3 1.4 collective-permute-start.18
  239.8 27.6 %copy-start.18 = (pred[2,256,128]{2,1,0:T(32,128)(4,1)S(1)}, pred[2,256,128]{2,1,0:T(32,128)(4,1)}, u32[]{:S(2)}) copy-start(pred[2,256,128]{2,1,0:T(32,128)(4,1)} %copy-done.17) | copy-start | bytes 196612
  240.7 21.9 %collective-permute-start.19 = (f32[2,3584]{1,0:T(2,128)S(1)}, f32[2,3584]{1,0:T(2,128)S(1)}, u32[]{:S(2)}, u32[]{:S(2)}) collective-permute-start(f32[2,3584]{1,0:T(2,128)S(1)} %fusion.30), channel_id=1, source_target_pairs={{0,2},{1,3},{2,0},{3,1},{4,6},{5,7},{6,4},{7,5},{8,10},{9,11},{10,... | collective-permute-start | bytes 86024 | tf_op jit(solution)/shard_map/ppermute | solution.py:200
  262.7 4.4 %collective-permute-start.20 = (f32[2,3584]{1,0:T(2,128)S(1)}, f32[2,3584]{1,0:T(2,128)S(1)}, u32[]{:S(2)}, u32[]{:S(2)}) collective-permute-start(f32[2,3584]{1,0:T(2,128)S(1)} %fusion.68), channel_id=1, source_target_pairs={{0,4},{1,5},{2,6},{3,7},{4,0},{5,1},{6,2},{7,3},{8,12},{9,13},{10,... | collective-permute-start | bytes 86024 | tf_op jit(solution)/shard_map/ppermute | solution.py:200
  267.1 7.0 %collective-permute-start.21 = (f32[2,3584]{1,0:T(2,128)S(1)}, f32[2,3584]{1,0:T(2,128)S(1)}, u32[]{:S(2)}, u32[]{:S(2)}) collective-permute-start(f32[2,3584]{1,0:T(2,128)S(1)} %add.108), channel_id=1, source_target_pairs={{0,8},{1,9},{2,10},{3,11},{4,12},{5,13},{6,14},{7,15},{8,0},{9,1},... | collective-permute-start | bytes 86024 | tf_op jit(solution)/shard_map/ppermute | solution.py:200
  269.4 5.4 %copy-start.6 = (bf16[2,128,3584]{2,1,0:T(8,128)(2,1)S(1)}, bf16[2,128,3584]{2,1,0:T(8,128)(2,1)}, u32[]{:S(2)}) copy-start(bf16[2,128,3584]{2,1,0:T(8,128)(2,1)} %slice.105) | copy-start | bytes 5505028
  269.4 41.3 %all-to-all-start.5 = ((bf16[16,16,3584]{2,1,0:T(8,128)(2,1)}), bf16[16,16,3584]{2,1,0:T(8,128)(2,1)}, u32[]{:S(2)}, u32[]{:S(2)}) async-start(bf16[16,16,3584]{2,1,0:T(8,128)(2,1)} %bitcast.160), calls=%async_computation.5 | async-start | bytes 3670016 | tf_op jit(solution)/shard_map/all_to_all | solution.py:66
  274.8 2.3 copy-start.11
  274.8 2.3 copy-start.16
  282.8 4.1 %copy-start.8 = (bf16[16,16,3584]{2,1,0:T(8,128)(2,1)S(1)}, bf16[16,16,3584]{2,1,0:T(8,128)(2,1)}, u32[]{:S(2)}) copy-start(bf16[16,16,3584]{2,1,0:T(8,128)(2,1)} %get-tuple-element.48) | copy-start | bytes 5505028
  283.7 3.8 %copy-start.7 = (f32[256,3584]{1,0:T(8,128)S(1)}, f32[256,3584]{1,0:T(8,128)}, u32[]{:S(2)}) copy-start(f32[256,3584]{1,0:T(8,128)} %fusion.38) | copy-start | bytes 11010052
  286.3 1.3 copy-start.14
  287.6 2.3 copy-start.12

commit v6 on v5

--- a/solution.py
+++ b/solution.py
@@ -116,32 +116,26 @@
     got_pre = everyone(sent_pre.reshape(devices, layers * cap, latents))
     got_pre = got_pre.reshape(devices, layers, cap, latents)
     direct = devices <= 16 and cap % 16 == 0
+    windows = [[8, 9, 10, 11, 12], [1, 2, 4], [3, 5], [6, 7, 13, 14, 15]]
+    arrivals = [None] * devices
     if direct:
+        windows = [[k for k in ks if k < devices] for ks in windows]
         key = ((routes[:1] ^ me) * cap + order[:1]).astype(jnp.int32)
         packed = pack_rows(key, mlp_target, residual, devices, cap)
-        arrivals = [packed[0]] + [
-            lax.ppermute(packed[k], "layer", [(i, i ^ k) for i in range(devices)])
-            for k in range(1, devices)
-        ]
-        windows = [[8, 9, 10], [1, 4, 5], [2, 6], [3, 7, 11, 12, 13, 14, 15]]
-        windows = [[k for k in ks if k < devices] for ks in windows]
+        arrivals[0] = packed[0]
         sender = (me ^ jnp.arange(devices, dtype=jnp.int32)).astype(jnp.int32)
-    else:
-        arrivals = [
-            everyone(
-                jnp.concatenate(
-                    [
-                        mm(place[0], rows[0]).astype(BF).reshape(devices, cap, width)
-                        for rows in (mlp_target, residual)
-                    ],
-                    axis=1,
-                )
-            )
-        ]
-        windows = [[], [], [], [0]]
-
-    def received(window):
-        return [arrivals[k] for k in windows[window]]
+
+    def depart(window, begin):
+        if not direct:
+            return
+        rows = [packed[k] for k in windows[window]]
+        if begin is not None:
+            rows = after(rows, begin)
+        for k, x in zip(windows[window], rows):
+            arrivals[k] = lax.ppermute(x, "layer", [(i, i ^ k) for i in range(devices)])
+
+    def arrived(window):
+        return [arrivals[k] for k in windows[window]] if direct else []
 
     acts = turn(jnp.maximum(got_pre, 0))
     nothing = jnp.zeros((devices, 1, cap, latents), BF)
@@ -157,34 +151,45 @@
     def decode(rows):
         return mm(rows.reshape(-1, 2 * latents), dec1).astype(BF).reshape(half, -1, width)
 
+    depart(0, None)
     pieces_m = within(decode(wide[half:])).reshape(-1, width)
-    sum_m = mm(flat(place_m), pieces_m, ROWS)
-    sum_low_sent = sum_m.astype(BF)
-    sum_low = across(sum_low_sent)
-    pieces_o = within(decode(after(wide[:half], (sum_low_sent, received(0))))).reshape(-1, width)
+    sum_m = mm(flat(place_m), pieces_m, ROWS).astype(BF)
+    sum_low = across(sum_m)
+    depart(1, sum_m)
+    pieces_o = decode(wide[:half])
+    pieces_o = within(after(pieces_o, (sum_m, arrived(0)))).reshape(-1, width)
     sum_o = mm(flat(place_o), pieces_o, ROWS) + decoder_bias[1] - mlp_target[1].astype(F32)
-    sum_high_sent = sum_o.astype(BF)
-    sum_high = across(sum_high_sent)
-
-    error1 = ((sum_o + sum_low.astype(F32)) * scale).astype(BF)
-    error1_m = ((sum_m + sum_high.astype(F32)) * scale).astype(BF)
+    sum_o = sum_o.astype(BF)
+    sum_high = across(sum_o)
+    depart(2, sum_o)
+
+    def add_halves(a, b):
+        return ((a.astype(F32) + b.astype(F32)) * scale).astype(BF)
 
     def send_errors(p, error):
         return within(mm(flat(p), error).astype(BF).reshape(half, layers * cap, width))
 
-    error1 = after(error1, received(1))
+    error1 = after(add_halves(sum_o, sum_low), arrived(1))
     errors_o = send_errors(place_o, error1)
-
-    errors_m = send_errors(place_m, after(error1_m, (errors_o, received(2))))
-    residual1 = after(residual[1], (errors_m, received(3)))
-    resid1 = everyone(mm(place[1], residual1).astype(BF).reshape(devices, cap, width))
-    resid1 = resid1.reshape(slots, width)
+    error1_m = after(add_halves(sum_m, sum_high), (errors_o, arrived(2)))
+    depart(3, error1_m)
+    errors_m = send_errors(place_m, error1_m)
+    resid1 = mm(place[1], residual[1]).astype(BF).reshape(devices, cap, width)
+    resid1 = everyone(after(resid1, (errors_m, arrived(3)))).reshape(slots, width)
 
     if direct:
         layer0 = jnp.stack(arrivals)
         pre0 = jnp.take(got_pre[:, 0], sender, axis=0).reshape(slots, latents)
     else:
-        layer0 = arrivals[0]
+        layer0 = everyone(
+            jnp.concatenate(
+                [
+                    mm(place[0], rows[0]).astype(BF).reshape(devices, cap, width)
+                    for rows in (mlp_target, residual)
+                ],
+                axis=1,
+            )
+        )
         pre0 = got_pre[:, 0].reshape(slots, latents)
     target0 = layer0[:, :cap].reshape(slots, width)
     resid0 = layer0[:, cap:].reshape(slots, width)
@@ -195,10 +200,10 @@
     empties = float(slots * devices - tokens * devices)
 
     def total(x):
-        step = 1
-        while step < devices:
+        step = devices // 2
+        while step >= 1:
             x = x + lax.ppermute(x, "layer", [(i, i ^ step) for i in range(devices)])
-            step *= 2
+            step //= 2
         return x
 
     sums = total(

time: 320 us -> 313 us (0.978)
  waiting for transfers between devices: 173 us -> 129 us
  starting transfers between devices: 52.6 us -> 84.3 us
    ppermute x3, waiting for transfers between devices: 78.4 us -> 41.1 us  [across(): return lax.ppermute(x, 'layer', mirror)]
    ppermute x15, waiting for transfers between devices: 15.6 us -> 45.6 us  [depart(): arrivals[k] = lax.ppermute(x, 'layer', [(i, i ^ k) for i in range(devices)])]
    all_to_all x4, waiting for transfers between devices: 39.5 us -> 12.6 us  [within(): lax.all_to_all(x, 'layer', split_axis=0, concat_axis=0, tiled=True, axis_...]
    ppermute x4, waiting for transfers between devices: 20.7 us -> 1.76 us  [total(): x = x + lax.ppermute(x, 'layer', [(i, i ^ step) for i in range(devices)])]
    ppermute x4, starting transfers between devices: 4.14 us -> 19.4 us  [total(): x = x + lax.ppermute(x, 'layer', [(i, i ^ step) for i in range(devices)])]
    ppermute x15, starting transfers between devices: 18.2 us -> 27.4 us  [depart(): arrivals[k] = lax.ppermute(x, 'layer', [(i, i ^ k) for i in range(devices)])]
    all_to_all x2, waiting for transfers between devices: 19.1 us -> 28 us  [everyone(): return lax.all_to_all(x, 'layer', split_axis=0, concat_axis=0, tiled=True)]
    all_to_all x4, starting transfers between devices: 17.1 us -> 21.3 us  [within(): lax.all_to_all(x, 'layer', split_axis=0, concat_axis=0, tiled=True, axis_...]
  transfers between devices with their start and end apart: 28 -> 28, of which waited for: 9 -> 13; matrix products, arithmetic and copies ran while one was open for 23% -> 24% of each run, Pallas kernels for 0% -> 1%
where the time goes in v6:
time: 313 us; the launch traced here: 307 us
  waiting for transfers between devices  129 us (41%)
  starting transfers between devices  84.3 us (27%)
  matrix products  41.4 us (13%)
  local copies, waits for them, and re-layouts  34.3 us (11%)
  other arithmetic  12.8 us (4%)
  Pallas kernels  4.07 us (1%)
    ppermute x15, waiting for transfers between devices, depart(): arrivals[k] = lax.ppermute(x, 'layer', [(i, i ^ k) for i in range(devices)])  45.6 us
    dot_general x18, matrix products, mm(): return lax.dot_general(a, b, (dims, ((), ())), preferred_element_type=F32)  41.4 us
    ppermute x3, waiting for transfers between devices, across(): return lax.ppermute(x, 'layer', mirror)  41.1 us
    all_to_all x2, waiting for transfers between devices, everyone(): return lax.all_to_all(x, 'layer', split_axis=0, concat_axis=0, tiled=True)  28 us
    ppermute x15, starting transfers between devices, depart(): arrivals[k] = lax.ppermute(x, 'layer', [(i, i ^ k) for i in range(devices)])  27.4 us
    unnamed x81, local copies, waits for them, and re-layouts  23.9 us
    all_to_all x4, starting transfers between devices, within(): lax.all_to_all(x, 'layer', split_axis=0, concat_axis=0, tiled=True, axis_...  21.3 us
    ppermute x4, starting transfers between devices, total(): x = x + lax.ppermute(x, 'layer', [(i, i ^ step) for i in range(devices)])  19.4 us
  transfers between devices with their start and end apart: 28, of which 13 were waited for; matrix products, arithmetic and copies ran while one was open for 24% of the time, Pallas kernels for 1%

profile of v6, /device:TPU:0, one launch (start us, length us, event | category | flops | bytes accessed | tf_op | source)
XLA Modules:
  0.0 307.0 jit_solution(95784963241031449)
XLA Ops:
  0.7 0.9 convert_reduce_fusion.2
  4.8 7.4 %all-to-all-start = ((bf16[16,32,128]{2,1,0:T(8,128)(2,1)}), bf16[16,32,128]{2,1,0:T(8,128)(2,1)S(1)}, u32[]{:S(2)}, u32[]{:S(2)}) async-start(bf16[16,32,128]{2,1,0:T(8,128)(2,1)} %bitcast.9), calls=%async_computation | async-start | bytes 262144 | tf_op jit(solution)/shard_map/all_to_all | solution.py:66
  12.2 1.6 slice.100
  13.8 6.3 %all-to-all-done = bf16[16,32,128]{2,1,0:T(8,128)(2,1)S(1)} async-done(((bf16[16,32,128]{2,1,0:T(8,128)(2,1)}), bf16[16,32,128]{2,1,0:T(8,128)(2,1)S(1)}, u32[]{:S(2)}, u32[]{:S(2)}) %all-to-all-start) | async-done | bytes 131104 | tf_op jit(solution)/shard_map/all_to_all | solution.py:66
  20.9 1.9 convolution_convert_fusion.5
  22.8 4.5 %all-to-all-start.1 = ((bf16[8,32,3584]{2,1,0:T(8,128)(2,1)}), bf16[8,32,3584]{2,1,0:T(8,128)(2,1)}, u32[]{:S(2)}, u32[]{:S(2)}) async-start(bf16[8,32,3584]{2,1,0:T(8,128)(2,1)} %bitcast.157), calls=%async_computation.1 | async-start | bytes 3670016 | tf_op jit(solution)/shard_map/all_to_all | solution.py:69
  28.3 1.5 copy-done.1
  29.8 4.1 %shard_map.93 = (bf16[32,3584]{1,0:T(8,128)(2,1)S(1)}, bf16[32,3584]{1,0:T(8,128)(2,1)S(1)}, bf16[32,3584]{1,0:T(8,128)(2,1)S(1)}, bf16[32,3584]{1,0:T(8,128)(2,...) custom-call(s32[1,128]{1,0:T(1,128)S(1)} %bitcast_add_fusion.key_ref, ...), custom_call_target="tpu_custom_call" | custom-call | flops 469762048 | bytes 5505024 | tf_op jit(solution)/shard_map/pallas_call | solution.py:37
  37.4 2.5 collective-permute-start.3
  39.9 3.4 %collective-permute-start.5 = (bf16[32,3584]{1,0:T(8,128)(2,1)}, bf16[32,3584]{1,0:T(8,128)(2,1)}, u32[]{:S(2)}, u32[]{:S(2)}) collective-permute-start(bf16[32,3584]{1,0:T(8,128)(2,1)} %get-tuple-element.44), channel_id=1, source_target_pairs={{0,10},{1,11},{2,8},{3,9},{4,14},{5,15},{6,12},{7,13},{8,2},{9,3},... | collective-permute-start | bytes 688136 | tf_op jit(solution)/shard_map/ppermute | solution.py:135
  45.1 1.2 slice_reduce_fusion.1
  46.3 1.9 convolution_convert_fusion
  49.0 3.5 %collective-permute-start.7 = (bf16[32,3584]{1,0:T(8,128)(2,1)}, bf16[32,3584]{1,0:T(8,128)(2,1)S(1)}, u32[]{:S(2)}, u32[]{:S(2)}) collective-permute-start(bf16[32,3584]{1,0:T(8,128)(2,1)} %copy-done.8), channel_id=1, source_target_pairs={{0,12},{1,13},{2,14},{3,15},{4,8},{5,9},{6,10},{7,11},{8,4},{9,5},... | collective-permute-start | bytes 688136 | tf_op jit(solution)/shard_map/ppermute | solution.py:135
  53.3 3.5 %convolution_convert_fusion.4 = bf16[256,3584]{1,0:T(8,128)(2,1)} fusion(bf16[256,256]{1,0:T(8,128)(2,1)} %bitcast.165, bf16[256,3584]{1,0:T(8,128)(2,1)} %bitcast.152), kind=kOutput, calls=%fused_computation.10 | convolution fusion | flops 470679552 | bytes 3801088 | tf_op jit(solution)/shard_map/dot_general | solution.py:17
  56.8 2.3 all-to-all-done.1
  59.1 2.9 convolution_convert_fusion.9
  62.0 12.9 %collective-permute-done.4 = bf16[32,3584]{1,0:T(8,128)(2,1)} collective-permute-done((bf16[32,3584]{1,0:T(8,128)(2,1)}, bf16[32,3584]{1,0:T(8,128)(2,1)}, u32[]{:S(2)}, u32[]{:S(2)}) %collective-permute-start.4) | collective-permute-done | bytes 229408 | tf_op jit(solution)/shard_map/ppermute | solution.py:135
  74.9 8.0 %collective-permute-done.5 = bf16[32,3584]{1,0:T(8,128)(2,1)} collective-permute-done((bf16[32,3584]{1,0:T(8,128)(2,1)}, bf16[32,3584]{1,0:T(8,128)(2,1)}, u32[]{:S(2)}, u32[]{:S(2)}) %collective-permute-start.5) | collective-permute-done | bytes 229408 | tf_op jit(solution)/shard_map/ppermute | solution.py:135
  82.8 2.8 collective-permute-done.6
  86.3 8.0 %all-to-all-start.2 = ((bf16[8,32,3584]{2,1,0:T(8,128)(2,1)}), bf16[8,32,3584]{2,1,0:T(8,128)(2,1)}, u32[]{:S(2)}, u32[]{:S(2)}) async-start(bf16[8,32,3584]{2,1,0:T(8,128)(2,1)} %bitcast.158), calls=%async_computation.2 | async-start | bytes 3670016 | tf_op jit(solution)/shard_map/all_to_all | solution.py:69
  97.7 1.4 select_maximum_fusion
  99.1 3.9 %collective-permute-start.12 = (bf16[128,3584]{1,0:T(8,128)(2,1)}, bf16[128,3584]{1,0:T(8,128)(2,1)}, u32[]{:S(2)}, u32[]{:S(2)}) collective-permute-start(bf16[128,3584]{1,0:T(8,128)(2,1)} %convolution_convert_fusion.9), channel_id=1, source_target_pairs={{0,8},{1,9},{2,10},{3,11},{4,12},{5,13},{6,14},{7,15},{8,0},{9,1},... | collective-permute-start | bytes 2752520 | tf_op jit(solution)/shard_map/ppermute | solution.py:77
  102.9 1.7 collective-permute-start.2
  104.6 1.5 collective-permute-start.9
  106.1 1.6 bitcast_dynamic-update-slice_fusion.14
  107.8 9.2 %collective-permute-done.2 = bf16[32,3584]{1,0:T(8,128)(2,1)S(1)} collective-permute-done((bf16[32,3584]{1,0:T(8,128)(2,1)}, bf16[32,3584]{1,0:T(8,128)(2,1)S(1)}, u32[]{:S(2)}, u32[]{:S(2)}) %collective-permute-start.2) | collective-permute-done | bytes 229408 | tf_op jit(solution)/shard_map/ppermute | solution.py:135
  117.7 25.9 %collective-permute-done.12 = bf16[128,3584]{1,0:T(8,128)(2,1)} collective-permute-done((bf16[128,3584]{1,0:T(8,128)(2,1)}, bf16[128,3584]{1,0:T(8,128)(2,1)}, u32[]{:S(2)}, u32[]{:S(2)}) %collective-permute-start.12) | collective-permute-done | bytes 917536 | tf_op jit(solution)/shard_map/ppermute | solution.py:77
  143.6 3.4 %multiply_convert_fusion = (bf16[128,3584]{1,0:T(8,128)(2,1)S(1)}, bf16[128,3584]{1,0:T(8,128)(2,1)}) fusion(bf16[128,3584]{1,0:T(8,128)(2,1)} %collective-permute-done.12, bf16[2,128,3584]{2,1,0:T(8,128)(2,1)S(1)} %copy-done.2, f32[3584]{0:T(1024)S(1)} %get-tuple-element.65, pred[256,128]{1,0:T(8,128)(4,1)} %bitcast.169, bf16[256,3584]{1,0:T(8,128)(2,1)} %bitcast.32), kind=kOutput, calls=%fused_computation.29 | convolution fusion | flops 239009792 | bytes 5552128 | tf_op jit(solution)/shard_map/dot_general | solution.py:17
  147.0 1.4 collective-permute-start.8
  148.4 4.4 %collective-permute-start.10 = (bf16[32,3584]{1,0:T(8,128)(2,1)S(1)}, bf16[32,3584]{1,0:T(8,128)(2,1)}, u32[]{:S(2)}, u32[]{:S(2)}) collective-permute-start(bf16[32,3584]{1,0:T(8,128)(2,1)S(1)} %get-tuple-element.50), channel_id=1, source_target_pairs={{0,5},{1,4},{2,7},{3,6},{4,1},{5,0},{6,3},{7,2},{8,13},{9,12},{10,... | collective-permute-start | bytes 688136 | tf_op jit(solution)/shard_map/ppermute | solution.py:135
  152.8 1.9 convolution_convert_fusion.2
  154.6 4.5 %all-to-all-start.3 = ((bf16[8,32,3584]{2,1,0:T(8,128)(2,1)}), bf16[8,32,3584]{2,1,0:T(8,128)(2,1)}, u32[]{:S(2)}, u32[]{:S(2)}) async-start(bf16[8,32,3584]{2,1,0:T(8,128)(2,1)} %bitcast.159), calls=%async_computation.3 | async-start | bytes 3670016 | tf_op jit(solution)/shard_map/all_to_all | solution.py:69
  159.3 1.7 bitcast_dynamic-update-slice_fusion.12
  161.0 1.6 bitcast_dynamic-update-slice_fusion.11
  162.6 10.3 %collective-permute-done.10 = bf16[32,3584]{1,0:T(8,128)(2,1)} collective-permute-done((bf16[32,3584]{1,0:T(8,128)(2,1)S(1)}, bf16[32,3584]{1,0:T(8,128)(2,1)}, u32[]{:S(2)}, u32[]{:S(2)}) %collective-permute-start.10) | collective-permute-done | bytes 229408 | tf_op jit(solution)/shard_map/ppermute | solution.py:135
  172.9 1.7 bitcast_dynamic-update-slice_fusion.10
  174.6 15.2 %collective-permute-done.11 = bf16[128,3584]{1,0:T(8,128)(2,1)S(1)} collective-permute-done((bf16[128,3584]{1,0:T(8,128)(2,1)}, bf16[128,3584]{1,0:T(8,128)(2,1)S(1)}, u32[]{:S(2)}, u32[]{:S(2)}) %collective-permute-start.11) | collective-permute-done | bytes 917536 | tf_op jit(solution)/shard_map/ppermute | solution.py:77
  190.0 10.2 %all-to-all-done.3 = bf16[8,32,3584]{2,1,0:T(8,128)(2,1)} async-done(((bf16[8,32,3584]{2,1,0:T(8,128)(2,1)}), bf16[8,32,3584]{2,1,0:T(8,128)(2,1)}, u32[]{:S(2)}, u32[]{:S(2)}) %all-to-all-start.3) | async-done | bytes 1835040 | tf_op jit(solution)/shard_map/all_to_all | solution.py:69
  200.2 1.0 collective-permute-start.13
  202.1 1.9 collective-permute-start.15
  204.1 4.2 %collective-permute-start.16 = (bf16[32,3584]{1,0:T(8,128)(2,1)S(1)}, bf16[32,3584]{1,0:T(8,128)(2,1)S(1)}, u32[]{:S(2)}, u32[]{:S(2)}) collective-permute-start(bf16[32,3584]{1,0:T(8,128)(2,1)S(1)} %get-tuple-element.61), channel_id=1, source_target_pairs={{0,14},{1,15},{2,12},{3,13},{4,10},{5,11},{6,8},{7,9},{8,6},{9,7},... | collective-permute-start | bytes 688136 | tf_op jit(solution)/shard_map/ppermute | solution.py:135
  208.2 1.9 convolution_convert_fusion.1
  210.1 4.4 %all-to-all-start.4 = ((bf16[8,32,3584]{2,1,0:T(8,128)(2,1)}), bf16[8,32,3584]{2,1,0:T(8,128)(2,1)}, u32[]{:S(2)}, u32[]{:S(2)}) async-start(bf16[8,32,3584]{2,1,0:T(8,128)(2,1)} %bitcast.51), calls=%async_computation.4 | async-start | bytes 3670016 | tf_op jit(solution)/shard_map/all_to_all | solution.py:69
  215.9 1.6 bitcast_dynamic-update-slice_fusion.7
  217.5 1.7 bitcast_dynamic-update-slice_fusion.6
  219.2 1.6 bitcast_dynamic-update-slice_fusion.5
  220.8 1.7 bitcast_dynamic-update-slice_fusion.4
  224.6 2.5 collective-permute-done.17
  227.8 3.6 %fusion.36 = (bf16[16,16,3584]{2,1,0:T(8,128)(2,1)}, bf16[16,16,3584]{2,1,0:T(8,128)(2,1)S(1)}) fusion(bf16[16,32,3584]{2,1,0:T(8,128)(2,1)} %bitcast_dynamic-update-slice_fusion), kind=kLoop, calls=%fused_computation.118 | loop fusion | bytes 7340032 | tf_op jit(solution)/shard_map/slice | solution.py:195
  231.4 3.4 %convert_reduce_fusion = (f32[3584]{0:T(1024)S(1)}, bf16[256,3584]{1,0:T(8,128)(2,1)}) fusion(bf16[16,16,3584]{2,1,0:T(8,128)(2,1)S(1)} %get-tuple-element.69, f32[3584]{0:T(1024)S(1)} %copy-done.29, bf16[256,128]{1,0:T(8,128)(2,1)S(1)} %bitcast.172, bf16[3,128,3584]{2,1,0:T(8,128)(2,1)} %param.10), kind=kOutput, calls=%fused_computation.25 | convolution fusion | flops 243134976 | bytes 4681728 | tf_op jit(solution)/shard_map/dot_general | solution.py:17
  234.8 15.5 %collective-permute-start.18 = (f32[2,3584]{1,0:T(2,128)S(1)}, f32[2,3584]{1,0:T(2,128)S(1)}, u32[]{:S(2)}, u32[]{:S(2)}) collective-permute-start(f32[2,3584]{1,0:T(2,128)S(1)} %pad_maximum_fusion.4), channel_id=1, source_target_pairs={{0,8},{1,9},{2,10},{3,11},{4,12},{5,13},{6,14},{7,15},{8,0},{9,1},... | collective-permute-start | bytes 86024 | tf_op jit(solution)/shard_map/ppermute | solution.py:205
  250.4 1.7 collective-permute-done.18
  253.1 4.1 %fusion.39 = f32[256,3584]{1,0:T(8,128)} fusion(bf16[256,256]{1,0:T(8,128)(2,1)S(1)} %bitcast.166, bf16[256,3584]{1,0:T(8,128)(2,1)} %bitcast.50), kind=kOutput, calls=%fused_computation.121 | convolution fusion | flops 469762048 | bytes 5636096 | tf_op jit(solution)/shard_map/dot_general | solution.py:17
  257.3 2.9 collective-permute-start.20
  260.1 2.2 fusion.40
  262.4 4.6 %all-to-all-start.5 = ((bf16[16,16,3584]{2,1,0:T(8,128)(2,1)}), bf16[16,16,3584]{2,1,0:T(8,128)(2,1)}, u32[]{:S(2)}, u32[]{:S(2)}) async-start(bf16[16,16,3584]{2,1,0:T(8,128)(2,1)} %bitcast.156), calls=%async_computation.5 | async-start | bytes 3670016 | tf_op jit(solution)/shard_map/all_to_all | solution.py:66
  267.1 2.9 fusion.5
  270.6 2.2 broadcast_select_fusion.1
  273.8 2.5 fusion.38
  277.7 2.2 fusion.2
  279.9 1.8 pad_maximum_fusion
  281.7 21.7 %all-to-all-done.5 = bf16[16,16,3584]{2,1,0:T(8,128)(2,1)} async-done(((bf16[16,16,3584]{2,1,0:T(8,128)(2,1)}), bf16[16,16,3584]{2,1,0:T(8,128)(2,1)}, u32[]{:S(2)}, u32[]{:S(2)}) %all-to-all-start.5) | async-done | bytes 1835040 | tf_op jit(solution)/shard_map/all_to_all | solution.py:66
  303.4 2.2 fusion.7
  305.6 1.4 pad_maximum_fusion.1
  (140 shorter events, 26.3 us)
Async XLA Ops:
  4.8 15.3 %all-to-all-start = ((bf16[16,32,128]{2,1,0:T(8,128)(2,1)}), bf16[16,32,128]{2,1,0:T(8,128)(2,1)S(1)}, u32[]{:S(2)}, u32[]{:S(2)}) async-start(bf16[16,32,128]{2,1,0:T(8,128)(2,1)} %bitcast.9), calls=%async_computation | async-start | bytes 262144 | tf_op jit(solution)/shard_map/all_to_all | solution.py:66
  13.8 9.0 %copy-start.9 = (bf16[2,128,3584]{2,1,0:T(8,128)(2,1)}, bf16[2,128,3584]{2,1,0:T(8,128)(2,1)S(1)}, u32[]{:S(2)}) copy-start(bf16[2,128,3584]{2,1,0:T(8,128)(2,1)S(1)} %slice.100) | copy-start | bytes 5505028
  20.1 2.7 copy-start.19
  20.9 1.9 copy-start.17
  22.8 4.5 %copy-start.27 = (s32[2,128,1]{1,2,0:T(1,128)S(1)}, s32[2,128,1]{1,2,0:T(1,128)}, u32[]{:S(2)}) copy-start(s32[2,128,1]{1,2,0:T(1,128)} %param.9) | copy-start | bytes 3076
  22.8 5.5 %copy-start = (bf16[2,128,3584]{2,1,0:T(8,128)(2,1)S(1)}, bf16[2,128,3584]{2,1,0:T(8,128)(2,1)}, u32[]{:S(2)}) copy-start(bf16[2,128,3584]{2,1,0:T(8,128)(2,1)} %second_ref.1) | copy-start | bytes 5505028
  22.8 36.3 %all-to-all-start.1 = ((bf16[8,32,3584]{2,1,0:T(8,128)(2,1)}), bf16[8,32,3584]{2,1,0:T(8,128)(2,1)}, u32[]{:S(2)}, u32[]{:S(2)}) async-start(bf16[8,32,3584]{2,1,0:T(8,128)(2,1)} %bitcast.157), calls=%async_computation.1 | async-start | bytes 3670016 | tf_op jit(solution)/shard_map/all_to_all | solution.py:69
  27.9 21.1 %collective-permute-start = (s32[2,2,128]{2,1,0:T(2,128)}, s32[2,2,128]{2,1,0:T(2,128)}, u32[]{:S(2)}, u32[]{:S(2)}) collective-permute-start(s32[2,2,128]{2,1,0:T(2,128)} %pad_add_fusion), channel_id=1, source_target_pairs={{0,8},{1,9},{2,10},{3,11},{4,12},{5,13},{6,14},{7,15},{8,0},{9,1},... | collective-permute-start | bytes 6152 | tf_op jit(solution)/shard_map/ppermute | solution.py:77
  28.3 1.5 copy-start.1
  29.8 15.2 %copy-start.28 = (f32[2,3584]{1,0:T(2,128)S(1)}, f32[2,3584]{1,0:T(2,128)}, u32[]{:S(2)}) copy-start(f32[2,3584]{1,0:T(2,128)} %param.11) | copy-start | bytes 86020
  33.9 0.7 copy-start.3
  34.6 0.7 copy-start.5
  35.3 0.7 copy-start.6
  36.0 0.7 copy-start.7
  36.7 0.7 copy-start.8
  37.4 24.6 %collective-permute-start.3 = (bf16[32,3584]{1,0:T(8,128)(2,1)}, bf16[32,3584]{1,0:T(8,128)(2,1)}, u32[]{:S(2)}, u32[]{:S(2)}) collective-permute-start(bf16[32,3584]{1,0:T(8,128)(2,1)} %get-tuple-element.42), channel_id=1, source_target_pairs={{0,8},{1,9},{2,10},{3,11},{4,12},{5,13},{6,14},{7,15},{8,0},{9,1},... | collective-permute-start | bytes 688136 | tf_op jit(solution)/shard_map/ppermute | solution.py:135
  39.9 35.0 %collective-permute-start.4 = (bf16[32,3584]{1,0:T(8,128)(2,1)}, bf16[32,3584]{1,0:T(8,128)(2,1)}, u32[]{:S(2)}, u32[]{:S(2)}) collective-permute-start(bf16[32,3584]{1,0:T(8,128)(2,1)} %get-tuple-element.43), channel_id=1, source_target_pairs={{0,9},{1,8},{2,11},{3,10},{4,13},{5,12},{6,15},{7,14},{8,1},{9,0},... | collective-permute-start | bytes 688136 | tf_op jit(solution)/shard_map/ppermute | solution.py:135
  39.9 43.0 %collective-permute-start.5 = (bf16[32,3584]{1,0:T(8,128)(2,1)}, bf16[32,3584]{1,0:T(8,128)(2,1)}, u32[]{:S(2)}, u32[]{:S(2)}) collective-permute-start(bf16[32,3584]{1,0:T(8,128)(2,1)} %get-tuple-element.44), channel_id=1, source_target_pairs={{0,10},{1,11},{2,8},{3,9},{4,14},{5,15},{6,12},{7,13},{8,2},{9,3},... | collective-permute-start | bytes 688136 | tf_op jit(solution)/shard_map/ppermute | solution.py:135
  43.3 42.3 %collective-permute-start.6 = (bf16[32,3584]{1,0:T(8,128)(2,1)}, bf16[32,3584]{1,0:T(8,128)(2,1)}, u32[]{:S(2)}, u32[]{:S(2)}) collective-permute-start(bf16[32,3584]{1,0:T(8,128)(2,1)} %get-tuple-element.45), channel_id=1, source_target_pairs={{0,11},{1,10},{2,9},{3,8},{4,15},{5,14},{6,13},{7,12},{8,3},{9,2},... | collective-permute-start | bytes 688136 | tf_op jit(solution)/shard_map/ppermute | solution.py:135
  43.9 4.3 %copy-start.32 = (pred[16]{0:T(512)(128)(4,1)}, pred[16]{0:T(512)(128)(4,1)S(1)}, u32[]{:S(2)}) copy-start(pred[16]{0:T(512)(128)(4,1)S(1)} %compare_and_fusion) | copy-start | bytes 52
  49.0 36.7 %collective-permute-start.7 = (bf16[32,3584]{1,0:T(8,128)(2,1)}, bf16[32,3584]{1,0:T(8,128)(2,1)S(1)}, u32[]{:S(2)}, u32[]{:S(2)}) collective-permute-start(bf16[32,3584]{1,0:T(8,128)(2,1)} %copy-done.8), channel_id=1, source_target_pairs={{0,12},{1,13},{2,14},{3,15},{4,8},{5,9},{6,10},{7,11},{8,4},{9,5},... | collective-permute-start | bytes 688136 | tf_op jit(solution)/shard_map/ppermute | solution.py:135
  85.6 0.7 copy-start.23
  86.3 8.7 %copy-start.30 = (pred[2,16,128]{2,1,0:T(8,128)(4,1)S(1)}, pred[2,16,128]{2,1,0:T(8,128)(4,1)}, u32[]{:S(2)}) copy-start(pred[2,16,128]{2,1,0:T(8,128)(4,1)} %iota_compare_fusion.4) | copy-start | bytes 12292
  86.3 57.3 %copy-start.2 = (bf16[2,128,3584]{2,1,0:T(8,128)(2,1)S(1)}, bf16[2,128,3584]{2,1,0:T(8,128)(2,1)}, u32[]{:S(2)}) copy-start(bf16[2,128,3584]{2,1,0:T(8,128)(2,1)} %first_ref.1) | copy-start | bytes 5505028
  86.3 57.3 %all-to-all-start.2 = ((bf16[8,32,3584]{2,1,0:T(8,128)(2,1)}), bf16[8,32,3584]{2,1,0:T(8,128)(2,1)}, u32[]{:S(2)}, u32[]{:S(2)}) async-start(bf16[8,32,3584]{2,1,0:T(8,128)(2,1)} %bitcast.158), calls=%async_computation.2 | async-start | bytes 3670016 | tf_op jit(solution)/shard_map/all_to_all | solution.py:69
  95.6 10.5 %collective-permute-start.1 = (bf16[32,3584]{1,0:T(8,128)(2,1)}, bf16[32,3584]{1,0:T(8,128)(2,1)}, u32[]{:S(2)}, u32[]{:S(2)}) collective-permute-start(bf16[32,3584]{1,0:T(8,128)(2,1)} %copy-done.7), channel_id=1, source_target_pairs={{0,1},{1,0},{2,3},{3,2},{4,5},{5,4},{6,7},{7,6},{8,9},{9,8},{10,11... | collective-permute-start | bytes 688136 | tf_op jit(solution)/shard_map/ppermute | solution.py:135
  99.1 44.5 %collective-permute-start.12 = (bf16[128,3584]{1,0:T(8,128)(2,1)}, bf16[128,3584]{1,0:T(8,128)(2,1)}, u32[]{:S(2)}, u32[]{:S(2)}) collective-permute-start(bf16[128,3584]{1,0:T(8,128)(2,1)} %convolution_convert_fusion.9), channel_id=1, source_target_pairs={{0,8},{1,9},{2,10},{3,11},{4,12},{5,13},{6,14},{7,15},{8,0},{9,1},... | collective-permute-start | bytes 2752520 | tf_op jit(solution)/shard_map/ppermute | solution.py:77
  102.9 14.0 %collective-permute-start.2 = (bf16[32,3584]{1,0:T(8,128)(2,1)}, bf16[32,3584]{1,0:T(8,128)(2,1)S(1)}, u32[]{:S(2)}, u32[]{:S(2)}) collective-permute-start(bf16[32,3584]{1,0:T(8,128)(2,1)} %copy-done.6), channel_id=1, source_target_pairs={{0,2},{1,3},{2,0},{3,1},{4,6},{5,7},{6,4},{7,5},{8,10},{9,11},{10,... | collective-permute-start | bytes 688136 | tf_op jit(solution)/shard_map/ppermute | solution.py:135
  104.6 48.1 %collective-permute-start.9 = (bf16[32,3584]{1,0:T(8,128)(2,1)}, bf16[32,3584]{1,0:T(8,128)(2,1)}, u32[]{:S(2)}, u32[]{:S(2)}) collective-permute-start(bf16[32,3584]{1,0:T(8,128)(2,1)} %copy-done.5), channel_id=1, source_target_pairs={{0,4},{1,5},{2,6},{3,7},{4,0},{5,1},{6,2},{7,3},{8,12},{9,13},{10,... | collective-permute-start | bytes 688136 | tf_op jit(solution)/shard_map/ppermute | solution.py:135
  143.6 3.4 %copy-start.4 = (bf16[32,3584]{1,0:T(8,128)(2,1)S(1)}, bf16[32,3584]{1,0:T(8,128)(2,1)}, u32[]{:S(2)}) copy-start(bf16[32,3584]{1,0:T(8,128)(2,1)} %copy-done.3) | copy-start | bytes 688132
  143.6 9.1 %copy-start.22 = (pred[8,2,16,128]{3,2,1,0:T(8,128)(4,1)S(1)}, pred[8,2,16,128]{3,2,1,0:T(8,128)(4,1)}, u32[]{:S(2)}) copy-start(pred[8,2,16,128]{3,2,1,0:T(8,128)(4,1)} %broadcast_and_fusion) | copy-start | bytes 98308
  147.0 5.8 %copy-start.12 = (bf16[128,3584]{1,0:T(8,128)(2,1)}, bf16[128,3584]{1,0:T(8,128)(2,1)S(1)}, u32[]{:S(2)}) copy-start(bf16[128,3584]{1,0:T(8,128)(2,1)S(1)} %get-tuple-element.56) | copy-start | bytes 2752516
  147.0 42.8 %collective-permute-start.11 = (bf16[128,3584]{1,0:T(8,128)(2,1)}, bf16[128,3584]{1,0:T(8,128)(2,1)S(1)}, u32[]{:S(2)}, u32[]{:S(2)}) collective-permute-start(bf16[128,3584]{1,0:T(8,128)(2,1)} %get-tuple-element.83), channel_id=1, source_target_pairs={{0,8},{1,9},{2,10},{3,11},{4,12},{5,13},{6,14},{7,15},{8,0},{9,1},... | collective-permute-start | bytes 2752520 | tf_op jit(solution)/shard_map/ppermute | solution.py:77
  147.0 12.3 %collective-permute-start.8 = (bf16[32,3584]{1,0:T(8,128)(2,1)S(1)}, bf16[32,3584]{1,0:T(8,128)(2,1)}, u32[]{:S(2)}, u32[]{:S(2)}) collective-permute-start(bf16[32,3584]{1,0:T(8,128)(2,1)S(1)} %copy-done.4), channel_id=1, source_target_pairs={{0,3},{1,2},{2,1},{3,0},{4,7},{5,6},{6,5},{7,4},{8,11},{9,10},{10,... | collective-permute-start | bytes 688136 | tf_op jit(solution)/shard_map/ppermute | solution.py:135
  148.4 24.6 %collective-permute-start.10 = (bf16[32,3584]{1,0:T(8,128)(2,1)S(1)}, bf16[32,3584]{1,0:T(8,128)(2,1)}, u32[]{:S(2)}, u32[]{:S(2)}) collective-permute-start(bf16[32,3584]{1,0:T(8,128)(2,1)S(1)} %get-tuple-element.50), channel_id=1, source_target_pairs={{0,5},{1,4},{2,7},{3,6},{4,1},{5,0},{6,3},{7,2},{8,13},{9,12},{10,... | collective-permute-start | bytes 688136 | tf_op jit(solution)/shard_map/ppermute | solution.py:135
  154.6 4.5 %copy-start.13 = (bf16[128,3584]{1,0:T(8,128)(2,1)S(1)}, bf16[128,3584]{1,0:T(8,128)(2,1)}, u32[]{:S(2)}) copy-start(bf16[128,3584]{1,0:T(8,128)(2,1)} %copy-done.12) | copy-start | bytes 2752516
  154.6 45.6 %all-to-all-start.3 = ((bf16[8,32,3584]{2,1,0:T(8,128)(2,1)}), bf16[8,32,3584]{2,1,0:T(8,128)(2,1)}, u32[]{:S(2)}, u32[]{:S(2)}) async-start(bf16[8,32,3584]{2,1,0:T(8,128)(2,1)} %bitcast.159), calls=%async_computation.3 | async-start | bytes 3670016 | tf_op jit(solution)/shard_map/all_to_all | solution.py:69
  159.1 30.7 %copy-start.16 = (bf16[128,3584]{1,0:T(8,128)(2,1)S(1)}, bf16[128,3584]{1,0:T(8,128)(2,1)}, u32[]{:S(2)}) copy-start(bf16[128,3584]{1,0:T(8,128)(2,1)} %convolution_convert_fusion.9) | copy-start | bytes 2752516
  200.2 14.2 %collective-permute-start.13 = (bf16[32,3584]{1,0:T(8,128)(2,1)S(1)}, bf16[32,3584]{1,0:T(8,128)(2,1)S(1)}, u32[]{:S(2)}, u32[]{:S(2)}) collective-permute-start(bf16[32,3584]{1,0:T(8,128)(2,1)S(1)} %get-tuple-element.58), channel_id=1, source_target_pairs={{0,6},{1,7},{2,4},{3,5},{4,2},{5,3},{6,0},{7,1},{8,14},{9,15},{10,... | collective-permute-start | bytes 688136 | tf_op jit(solution)/shard_map/ppermute | solution.py:135
  201.3 13.9 %collective-permute-start.14 = (bf16[32,3584]{1,0:T(8,128)(2,1)S(1)}, bf16[32,3584]{1,0:T(8,128)(2,1)S(1)}, u32[]{:S(2)}, u32[]{:S(2)}) collective-permute-start(bf16[32,3584]{1,0:T(8,128)(2,1)S(1)} %get-tuple-element.59), channel_id=1, source_target_pairs={{0,7},{1,6},{2,5},{3,4},{4,3},{5,2},{6,1},{7,0},{8,15},{9,14},{10,... | collective-permute-start | bytes 688136 | tf_op jit(solution)/shard_map/ppermute | solution.py:135
  202.1 21.0 %collective-permute-start.15 = (bf16[32,3584]{1,0:T(8,128)(2,1)S(1)}, bf16[32,3584]{1,0:T(8,128)(2,1)S(1)}, u32[]{:S(2)}, u32[]{:S(2)}) collective-permute-start(bf16[32,3584]{1,0:T(8,128)(2,1)S(1)} %get-tuple-element.60), channel_id=1, source_target_pairs={{0,13},{1,12},{2,15},{3,14},{4,9},{5,8},{6,11},{7,10},{8,5},{9,4},... | collective-permute-start | bytes 688136 | tf_op jit(solution)/shard_map/ppermute | solution.py:135
  204.1 19.8 %collective-permute-start.16 = (bf16[32,3584]{1,0:T(8,128)(2,1)S(1)}, bf16[32,3584]{1,0:T(8,128)(2,1)S(1)}, u32[]{:S(2)}, u32[]{:S(2)}) collective-permute-start(bf16[32,3584]{1,0:T(8,128)(2,1)S(1)} %get-tuple-element.61), channel_id=1, source_target_pairs={{0,14},{1,15},{2,12},{3,13},{4,10},{5,11},{6,8},{7,9},{8,6},{9,7},... | collective-permute-start | bytes 688136 | tf_op jit(solution)/shard_map/ppermute | solution.py:135
  208.2 18.9 %collective-permute-start.17 = (bf16[32,3584]{1,0:T(8,128)(2,1)S(1)}, bf16[32,3584]{1,0:T(8,128)(2,1)S(1)}, u32[]{:S(2)}, u32[]{:S(2)}) collective-permute-start(bf16[32,3584]{1,0:T(8,128)(2,1)S(1)} %get-tuple-element.62), channel_id=1, source_target_pairs={{0,15},{1,14},{2,13},{3,12},{4,11},{5,10},{6,9},{7,8},{8,7},{9,6},... | collective-permute-start | bytes 688136 | tf_op jit(solution)/shard_map/ppermute | solution.py:135
  210.1 52.4 %all-to-all-start.4 = ((bf16[8,32,3584]{2,1,0:T(8,128)(2,1)}), bf16[8,32,3584]{2,1,0:T(8,128)(2,1)}, u32[]{:S(2)}, u32[]{:S(2)}) async-start(bf16[8,32,3584]{2,1,0:T(8,128)(2,1)} %bitcast.51), calls=%async_computation.4 | async-start | bytes 3670016 | tf_op jit(solution)/shard_map/all_to_all | solution.py:69
  214.4 8.0 %copy-start.24 = (bf16[32,3584]{1,0:T(8,128)(2,1)S(1)}, bf16[32,3584]{1,0:T(8,128)(2,1)}, u32[]{:S(2)}) copy-start(bf16[32,3584]{1,0:T(8,128)(2,1)} %copy-done.23) | copy-start | bytes 688132
  227.8 3.6 %copy-start.25 = (bf16[16,16,128]{2,1,0:T(8,128)(2,1)S(1)}, bf16[16,16,128]{2,1,0:T(8,128)(2,1)}, u32[]{:S(2)}) copy-start(bf16[16,16,128]{2,1,0:T(8,128)(2,1)} %select_maximum_fusion) | copy-start | bytes 196612
  227.8 3.6 %copy-start.29 = (f32[3584]{0:T(1024)S(1)}, f32[3584]{0:T(1024)}, u32[]{:S(2)}) copy-start(f32[3584]{0:T(1024)} %get-tuple-element.64) | copy-start | bytes 43012
  231.4 18.9 %copy-start.31 = (pred[256]{0:T(512)(128)(4,1)S(1)}, pred[256]{0:T(512)(128)(4,1)}, u32[]{:S(2)}) copy-start(pred[256]{0:T(512)(128)(4,1)} %broadcast_in_dim.49) | copy-start | bytes 772
  231.4 21.8 %copy-start.21 = (bf16[8,2,16,256]{3,2,1,0:T(8,128)(2,1)S(1)}, bf16[8,2,16,256]{3,2,1,0:T(8,128)(2,1)}, u32[]{:S(2)}) copy-start(bf16[8,2,16,256]{3,2,1,0:T(8,128)(2,1)} %get-tuple-element.74) | copy-start | bytes 393220
  234.8 17.3 %collective-permute-start.18 = (f32[2,3584]{1,0:T(2,128)S(1)}, f32[2,3584]{1,0:T(2,128)S(1)}, u32[]{:S(2)}, u32[]{:S(2)}) collective-permute-start(f32[2,3584]{1,0:T(2,128)S(1)} %pad_maximum_fusion.4), channel_id=1, source_target_pairs={{0,8},{1,9},{2,10},{3,11},{4,12},{5,13},{6,14},{7,15},{8,0},{9,1},... | collective-permute-start | bytes 86024 | tf_op jit(solution)/shard_map/ppermute | solution.py:205
  252.2 5.0 %collective-permute-start.19 = (f32[2,3584]{1,0:T(2,128)S(1)}, f32[2,3584]{1,0:T(2,128)S(1)}, u32[]{:S(2)}, u32[]{:S(2)}) collective-permute-start(f32[2,3584]{1,0:T(2,128)S(1)} %fusion.33), channel_id=1, source_target_pairs={{0,4},{1,5},{2,6},{3,7},{4,0},{5,1},{6,2},{7,3},{8,12},{9,13},{10,... | collective-permute-start | bytes 86024 | tf_op jit(solution)/shard_map/ppermute | solution.py:205
  253.1 7.0 %copy-start.10 = (bf16[2,128,3584]{2,1,0:T(8,128)(2,1)S(1)}, bf16[2,128,3584]{2,1,0:T(8,128)(2,1)}, u32[]{:S(2)}) copy-start(bf16[2,128,3584]{2,1,0:T(8,128)(2,1)} %copy-done.9) | copy-start | bytes 5505028
  257.3 5.1 %collective-permute-start.20 = (f32[2,3584]{1,0:T(2,128)S(1)}, f32[2,3584]{1,0:T(2,128)S(1)}, u32[]{:S(2)}, u32[]{:S(2)}) collective-permute-start(f32[2,3584]{1,0:T(2,128)S(1)} %fusion.68), channel_id=1, source_target_pairs={{0,2},{1,3},{2,0},{3,1},{4,6},{5,7},{6,4},{7,5},{8,10},{9,11},{10,... | collective-permute-start | bytes 86024 | tf_op jit(solution)/shard_map/ppermute | solution.py:205
  262.3 7.6 %collective-permute-start.21 = (f32[2,3584]{1,0:T(2,128)S(1)}, f32[2,3584]{1,0:T(2,128)S(1)}, u32[]{:S(2)}, u32[]{:S(2)}) collective-permute-start(f32[2,3584]{1,0:T(2,128)S(1)} %add.108), channel_id=1, source_target_pairs={{0,1},{1,0},{2,3},{3,2},{4,5},{5,4},{6,7},{7,6},{8,9},{9,8},{10,11... | collective-permute-start | bytes 86024 | tf_op jit(solution)/shard_map/ppermute | solution.py:205
  262.4 41.0 %all-to-all-start.5 = ((bf16[16,16,3584]{2,1,0:T(8,128)(2,1)}), bf16[16,16,3584]{2,1,0:T(8,128)(2,1)}, u32[]{:S(2)}, u32[]{:S(2)}) async-start(bf16[16,16,3584]{2,1,0:T(8,128)(2,1)} %bitcast.156), calls=%async_computation.5 | async-start | bytes 3670016 | tf_op jit(solution)/shard_map/all_to_all | solution.py:66
  267.1 2.9 copy-start.26
  270.6 2.2 copy-start.20
  272.9 4.1 %copy-start.14 = (bf16[16,16,3584]{2,1,0:T(8,128)(2,1)S(1)}, bf16[16,16,3584]{2,1,0:T(8,128)(2,1)}, u32[]{:S(2)}) copy-start(bf16[16,16,3584]{2,1,0:T(8,128)(2,1)} %get-tuple-element.68) | copy-start | bytes 5505028
  273.8 3.8 %copy-start.11 = (f32[256,3584]{1,0:T(8,128)S(1)}, f32[256,3584]{1,0:T(8,128)}, u32[]{:S(2)}) copy-start(f32[256,3584]{1,0:T(8,128)} %fusion.39) | copy-start | bytes 11010052
  276.3 1.3 copy-start.18
  277.6 2.3 copy-start.15

commit v7 on v6

--- a/solution.py
+++ b/solution.py
@@ -49,6 +49,115 @@
     )(key, first, second)
 
 
+def layer0_errors(arrivals, act, decoder, bias, scale, cap):
+    groups = len(arrivals)
+    slots, latents = act.shape
+    layers, width = bias.shape
+    step = column_block(width)
+
+    def kernel(act_ref, dec_ref, bias_ref, *refs):
+        rows = refs[:groups]
+        sum_ref, grad_ref, back_ref, target = refs[groups:]
+        for k in range(groups):
+            target[k * cap : (k + 1) * cap, :] = rows[k][:cap, :]
+        piece = mm(act_ref[...], dec_ref[0]).astype(BF).astype(F32)
+        error = (piece + bias_ref[0:1, :] - target[...].astype(F32)) * scale
+        error = error.astype(BF)
+        sum_ref[...] = jnp.sum(error.astype(F32), axis=0, keepdims=True)
+        grad_ref[...] = mm(act_ref[...], error, ROWS).astype(BF)
+
+        @pl.when(pl.program_id(0) == 0)
+        def _():
+            back_ref[...] = jnp.zeros_like(back_ref)
+
+        back_ref[...] += mm(error, dec_ref[0], LAST)
+
+    return pl.pallas_call(
+        kernel,
+        grid=(width // step,),
+        in_specs=[
+            pl.BlockSpec((slots, latents), lambda i: (0, 0)),
+            pl.BlockSpec((1, latents, step), lambda i: (0, 0, i)),
+            pl.BlockSpec((layers, step), lambda i: (0, i)),
+        ]
+        + [pl.BlockSpec((2 * cap, step), lambda i: (0, i))] * groups,
+        out_specs=[
+            pl.BlockSpec((1, step), lambda i: (0, i)),
+            pl.BlockSpec((latents, step), lambda i: (0, i)),
+            pl.BlockSpec((slots, latents), lambda i: (0, 0)),
+        ],
+        out_shape=[
+            jax.ShapeDtypeStruct((1, width), F32),
+            jax.ShapeDtypeStruct((latents, width), BF),
+            jax.ShapeDtypeStruct((slots, latents), F32),
+        ],
+        scratch_shapes=[pltpu.VMEM((slots, step), BF)],
+        compiler_params=pltpu.CompilerParams(vmem_limit_bytes=32 * 2**20),
+        cost_estimate=pl.CostEstimate(
+            flops=6 * slots * latents * width,
+            bytes_accessed=2 * (2 * slots + 2 * latents) * width,
+            transcendentals=0,
+        ),
+    )(act, decoder, bias, *arrivals)
+
+
+def encoder_layer0(arrivals, low, layers, cap):
+    groups = len(arrivals)
+    slots, latents = low.shape
+    width = arrivals[0].shape[1]
+    step = column_block(width)
+
+    def kernel(low_ref, *refs):
+        rows, out_ref, resid = refs[:groups], refs[groups], refs[groups + 1]
+        for k in range(groups):
+            resid[k * cap : (k + 1) * cap, :] = rows[k][cap:, :]
+        out_ref[0] = mm(resid[...], low_ref[...], ROWS).astype(BF)
+
+    return pl.pallas_call(
+        kernel,
+        grid=(width // step,),
+        in_specs=[pl.BlockSpec((slots, latents), lambda i: (0, 0))]
+        + [pl.BlockSpec((2 * cap, step), lambda i: (0, i))] * groups,
+        out_specs=pl.BlockSpec((1, step, latents), lambda i: (0, i, 0)),
+        out_shape=jax.ShapeDtypeStruct((layers, width, latents), BF),
+        scratch_shapes=[pltpu.VMEM((slots, step), BF)],
+        compiler_params=pltpu.CompilerParams(vmem_limit_bytes=32 * 2**20),
+        cost_estimate=pl.CostEstimate(
+            flops=2 * slots * latents * width,
+            bytes_accessed=2 * (2 * slots + latents) * width,
+            transcendentals=0,
+        ),
+    )(low, *arrivals)
+
+
+def encoder_layer1(products, resid, low):
+    slots, latents = low.shape
+    width = resid.shape[1]
+    step = column_block(width)
+
+    def kernel(low_ref, resid_ref, _, out_ref):
+        out_ref[0] = mm(resid_ref[...], low_ref[...], ROWS).astype(BF)
+
+    return pl.pallas_call(
+        kernel,
+        grid=(width // step,),
+        in_specs=[
+            pl.BlockSpec((slots, latents), lambda i: (0, 0)),
+            pl.BlockSpec((slots, step), lambda i: (0, i)),
+            pl.BlockSpec(memory_space=pl.ANY),
+        ],
+        out_specs=pl.BlockSpec((1, step, latents), lambda i: (1, i, 0)),
+        out_shape=jax.ShapeDtypeStruct(products.shape, BF),
+        input_output_aliases={2: 0},
+        compiler_params=pltpu.CompilerParams(vmem_limit_bytes=32 * 2**20),
+        cost_estimate=pl.CostEstimate(
+            flops=2 * slots * latents * width,
+            bytes_accessed=2 * (slots + latents) * width,
+            transcendentals=0,
+        ),
+    )(low, resid, products)
+
+
 def per_device(residual, mlp_target, pre_acts, blocks, decoder, decoder_bias):
     devices = lax.axis_size("layer")
     layers, tokens, width = residual.shape
@@ -116,7 +225,7 @@
     got_pre = everyone(sent_pre.reshape(devices, layers * cap, latents))
     got_pre = got_pre.reshape(devices, layers, cap, latents)
     direct = devices <= 16 and cap % 16 == 0
-    windows = [[8, 9, 10, 11, 12], [1, 2, 4], [3, 5], [6, 7, 13, 14, 15]]
+    windows = [[10, 11, 12], [1, 2, 4], [3, 5], [6, 7, 13, 14, 15], [8, 9]]
     arrivals = [None] * devices
     if direct:
         windows = [[k for k in ks if k < devices] for ks in windows]
@@ -151,13 +260,20 @@
     def decode(rows):
         return mm(rows.reshape(-1, 2 * latents), dec1).astype(BF).reshape(half, -1, width)
 
+    depart(4, None)
     depart(0, None)
-    pieces_m = within(decode(wide[half:])).reshape(-1, width)
+    pieces_m = decode(wide[half:])
+    pieces_m = within(after(pieces_m, arrived(4))).reshape(-1, width)
     sum_m = mm(flat(place_m), pieces_m, ROWS).astype(BF)
     sum_low = across(sum_m)
     depart(1, sum_m)
     pieces_o = decode(wide[:half])
-    pieces_o = within(after(pieces_o, (sum_m, arrived(0)))).reshape(-1, width)
+    if direct:
+        pre0 = jnp.take(got_pre[:, 0], sender, axis=0).reshape(slots, latents)
+    else:
+        pre0 = got_pre[:, 0].reshape(slots, latents)
+    act0 = jnp.maximum(pre0, 0)
+    pieces_o = within(after(pieces_o, (sum_m, act0, arrived(0)))).reshape(-1, width)
     sum_o = mm(flat(place_o), pieces_o, ROWS) + decoder_bias[1] - mlp_target[1].astype(F32)
     sum_o = sum_o.astype(BF)
     sum_high = across(sum_o)
@@ -177,9 +293,10 @@
     resid1 = mm(place[1], residual[1]).astype(BF).reshape(devices, cap, width)
     resid1 = everyone(after(resid1, (errors_m, arrived(3)))).reshape(slots, width)
 
-    if direct:
-        layer0 = jnp.stack(arrivals)
-        pre0 = jnp.take(got_pre[:, 0], sender, axis=0).reshape(slots, latents)
+    empty0 = (decoder_bias[0] * scale).astype(BF).astype(F32)
+    empties = float(slots * devices - tokens * devices)
+    if direct:
+        sum0, dec0, own = layer0_errors(arrivals, act0, decoder, decoder_bias, scale, cap)
     else:
         layer0 = everyone(
             jnp.concatenate(
@@ -190,14 +307,13 @@
                 axis=1,
             )
         )
-        pre0 = got_pre[:, 0].reshape(slots, latents)
-    target0 = layer0[:, :cap].reshape(slots, width)
-    resid0 = layer0[:, cap:].reshape(slots, width)
-    act0 = jnp.maximum(pre0, 0)
-    piece00 = mm(act0, decoder[0]).astype(BF).astype(F32)
-    error0 = ((piece00 + decoder_bias[0] - target0.astype(F32)) * scale).astype(BF)
-    empty0 = (decoder_bias[0] * scale).astype(BF).astype(F32)
-    empties = float(slots * devices - tokens * devices)
+        target0 = layer0[:, :cap].reshape(slots, width)
+        resid0 = layer0[:, cap:].reshape(slots, width)
+        piece00 = mm(act0, decoder[0]).astype(BF).astype(F32)
+        error0 = ((piece00 + decoder_bias[0] - target0.astype(F32)) * scale).astype(BF)
+        sum0 = jnp.sum(error0.astype(F32), axis=0, keepdims=True)
+        dec0 = mm(act0, error0, ROWS).astype(BF)
+        own = mm(error0, decoder[0], LAST)
 
     def total(x):
         step = devices // 2
@@ -207,7 +323,7 @@
         return x
 
     sums = total(
-        jnp.stack([jnp.sum(error0.astype(F32), axis=0), jnp.sum(error1.astype(F32), axis=0)])
+        jnp.concatenate([sum0, jnp.sum(error1.astype(F32), axis=0, keepdims=True)])
     )
     bias_grad = sums - jnp.stack([empties * empty0, jnp.zeros_like(empty0)])
 
@@ -222,19 +338,16 @@
     back0 = back[:, 0, :, :latents]
     if direct:
         back0 = jnp.take(back0, sender, axis=0)
-    grad0 = back0.reshape(slots, latents) + mm(error0, decoder[0], LAST)
+    grad0 = back0.reshape(slots, latents) + own
     grad0 = jnp.where(pre0 > 0, grad0, 0.0)
     grad1 = jnp.where(got_pre[:, 1] > 0, back[:, 1, :, latents:], 0.0).reshape(slots, latents)
     enc_bias = jnp.stack([jnp.sum(grad0, axis=0), jnp.sum(grad1, axis=0)])
-    dec = jnp.concatenate(
-        [mm(act0, error0, ROWS).astype(BF)[None], dec_later.astype(BF).reshape(2, latents, width)]
-    )
-    enc = jnp.stack(
-        [
-            mm(resid0, grad0.astype(BF), ROWS).astype(BF),
-            mm(resid1, grad1.astype(BF), ROWS).astype(BF),
-        ]
-    )
+    dec = jnp.concatenate([dec0[None], dec_later.astype(BF).reshape(2, latents, width)])
+    low0, low1 = grad0.astype(BF), grad1.astype(BF)
+    if direct:
+        enc = encoder_layer1(encoder_layer0(arrivals, low0, layers, cap), resid1, low1)
+    else:
+        enc = jnp.stack([mm(resid0, low0, ROWS).astype(BF), mm(resid1, low1, ROWS).astype(BF)])
     return dec, enc, enc_bias, bias_grad
 
 

time: 313 us -> 330 us (1.054)
  waiting for transfers between devices: 129 us -> 171 us
  starting transfers between devices: 84.3 us -> 58.6 us
  Pallas kernels: 4.07 us -> 19.6 us
  matrix products: 41.4 us -> 31.3 us
  local copies, waits for them, and re-layouts: 34.3 us -> 26.7 us
    ppermute x3, waiting for transfers between devices: 41.1 us -> 88.7 us  [across(): return lax.ppermute(x, 'layer', mirror)]
    all_to_all x2, waiting for transfers between devices: 28 us -> 8.69 us  [everyone(): return lax.all_to_all(x, 'layer', split_axis=0, concat_axis=0, tiled=True)]
    ppermute x4, starting transfers between devices: 19.4 us -> 1.24 us  [total(): x = x + lax.ppermute(x, 'layer', [(i, i ^ step) for i in range(devices)])]
    ppermute x15, waiting for transfers between devices: 45.6 us -> 61.5 us  [depart(): arrivals[k] = lax.ppermute(x, 'layer', [(i, i ^ k) for i in range(devices)])]
    pallas_call x0 -> x3, Pallas kernels: none -> 15.8 us  [the longest x1 6.43 us: layer0_errors(): pl.pallas_call(kernel, grid=(width // step,), in_specs=[pl.BlockSpec((slo...]
    dot_general x18 -> x13, matrix products: 41.4 us -> 31.3 us  [mm(): return lax.dot_general(a, b, (dims, ((), ())), preferred_element_type=F32)]
    all_to_all x4, waiting for transfers between devices: 12.6 us -> 5.46 us  [within(): lax.all_to_all(x, 'layer', split_axis=0, concat_axis=0, tiled=True, axis_...]
    ppermute x4, waiting for transfers between devices: 1.76 us -> 6.7 us  [total(): x = x + lax.ppermute(x, 'layer', [(i, i ^ step) for i in range(devices)])]
  transfers between devices with their start and end apart: 28 -> 28, of which waited for: 13 -> 18; matrix products, arithmetic and copies ran while one was open for 24% -> 13% of each run, Pallas kernels for 1% -> 5%
where the time goes in v7:
time: 330 us; the launch traced here: 323 us
  waiting for transfers between devices  171 us (52%)
  starting transfers between devices  58.6 us (18%)
  matrix products  31.3 us (9%)
  local copies, waits for them, and re-layouts  26.7 us (8%)
  Pallas kernels  19.6 us (6%)
  other arithmetic  15 us (5%)
    ppermute x3, waiting for transfers between devices, across(): return lax.ppermute(x, 'layer', mirror)  88.7 us
    ppermute x15, waiting for transfers between devices, depart(): arrivals[k] = lax.ppermute(x, 'layer', [(i, i ^ k) for i in range(devices)])  61.5 us
    dot_general x13, matrix products, mm(): return lax.dot_general(a, b, (dims, ((), ())), preferred_element_type=F32)  31.3 us
    ppermute x15, starting transfers between devices, depart(): arrivals[k] = lax.ppermute(x, 'layer', [(i, i ^ k) for i in range(devices)])  23.9 us
    unnamed x108, local copies, waits for them, and re-layouts  20.3 us
    all_to_all x4, starting transfers between devices, within(): lax.all_to_all(x, 'layer', split_axis=0, concat_axis=0, tiled=True, axis_...  17.6 us
    all_to_all x2, starting transfers between devices, everyone(): return lax.all_to_all(x, 'layer', split_axis=0, concat_axis=0, tiled=True)  11.6 us
    all_to_all x2, waiting for transfers between devices, everyone(): return lax.all_to_all(x, 'layer', split_axis=0, concat_axis=0, tiled=True)  8.69 us
  transfers between devices with their start and end apart: 28, of which 18 were waited for; matrix products, arithmetic and copies ran while one was open for 13% of the time, Pallas kernels for 5%

profile of v7, /device:TPU:0, one launch (start us, length us, event | category | flops | bytes accessed | tf_op | source)
XLA Modules:
  0.0 323.3 jit_solution(12737361529392472773)
XLA Ops:
  4.9 7.4 %all-to-all-start = ((bf16[16,32,128]{2,1,0:T(8,128)(2,1)}), bf16[16,32,128]{2,1,0:T(8,128)(2,1)}, u32[]{:S(2)}, u32[]{:S(2)}) async-start(bf16[16,32,128]{2,1,0:T(8,128)(2,1)} %bitcast.9), calls=%async_computation | async-start | bytes 262144 | tf_op jit(solution)/shard_map/all_to_all | solution.py:175
  13.0 1.5 copy-done.1
  14.5 1.5 copy-done.2
  16.0 3.9 %shard_map.93 = (bf16[32,3584]{1,0:T(8,128)(2,1)S(1)}, bf16[32,3584]{1,0:T(8,128)(2,1)S(1)}, bf16[32,3584]{1,0:T(8,128)(2,1)S(1)}, bf16[32,3584]{1,0:T(8,128)(2,...) custom-call(s32[1,128]{1,0:T(1,128)S(1)} %bitcast_add_fusion.key_ref, ...), custom_call_target="tpu_custom_call" | custom-call | flops 469762048 | bytes 5505024 | tf_op jit(solution)/shard_map/pallas_call | solution.py:37
  28.9 2.8 collective-permute-start.1
  31.7 1.3 slice.87
  33.0 1.0 broadcast_maximum_fusion
  34.9 1.9 convolution_convert_fusion.4
  36.7 11.5 %collective-permute-done.1.refs_8_ = bf16[32,3584]{1,0:T(8,128)(2,1)S(1)} collective-permute-done((bf16[32,3584]{1,0:T(8,128)(2,1)}, bf16[32,3584]{1,0:T(8,128)(2,1)S(1)}, u32[]{:S(2)}, u32[]{:S(2)}) %collective-permute-start.1) | collective-permute-done | bytes 229408 | tf_op jit(solution)/shard_map/ppermute | solution.py:244
  48.3 3.8 %collective-permute-done.2.refs_9_ = bf16[32,3584]{1,0:T(8,128)(2,1)S(1)} collective-permute-done((bf16[32,3584]{1,0:T(8,128)(2,1)}, bf16[32,3584]{1,0:T(8,128)(2,1)S(1)}, u32[]{:S(2)}, u32[]{:S(2)}) %collective-permute-start.2) | collective-permute-done | bytes 229408 | tf_op jit(solution)/shard_map/ppermute | solution.py:244
  52.1 4.5 %all-to-all-start.1 = ((bf16[8,32,3584]{2,1,0:T(8,128)(2,1)}), bf16[8,32,3584]{2,1,0:T(8,128)(2,1)}, u32[]{:S(2)}, u32[]{:S(2)}) async-start(bf16[8,32,3584]{2,1,0:T(8,128)(2,1)} %bitcast.112), calls=%async_computation.1 | async-start | bytes 3670016 | tf_op jit(solution)/shard_map/all_to_all | solution.py:178
  56.5 2.4 collective-permute-start
  59.0 1.9 collective-permute-start.5
  60.9 1.5 collective-permute-start.6
  62.3 2.0 collective-permute-start.7
  65.1 12.5 %collective-permute-done = s32[2,2,128]{2,1,0:T(2,128)S(1)} collective-permute-done((s32[2,2,128]{2,1,0:T(2,128)S(1)}, s32[2,2,128]{2,1,0:T(2,128)S(1)}, u32[]{:S(2)}, u32[]{:S(2)}) %collective-permute-start) | collective-permute-done | bytes 2080 | tf_op jit(solution)/shard_map/ppermute | solution.py:186
  78.5 1.2 gather_fusion
  79.7 0.9 broadcast_maximum_fusion.1.act_ref
  80.7 3.5 %convolution_convert_fusion.3 = bf16[256,3584]{1,0:T(8,128)(2,1)} fusion(bf16[256,256]{1,0:T(8,128)(2,1)} %bitcast.118, bf16[256,3584]{1,0:T(8,128)(2,1)} %bitcast.106), kind=kOutput, calls=%fused_computation.7 | convolution fusion | flops 470679552 | bytes 3801088 | tf_op jit(solution)/shard_map/dot_general | solution.py:17
  84.1 5.1 %all-to-all-done.1 = bf16[8,32,3584]{2,1,0:T(8,128)(2,1)} async-done(((bf16[8,32,3584]{2,1,0:T(8,128)(2,1)}), bf16[8,32,3584]{2,1,0:T(8,128)(2,1)}, u32[]{:S(2)}, u32[]{:S(2)}) %all-to-all-start.1) | async-done | bytes 1835040 | tf_op jit(solution)/shard_map/all_to_all | solution.py:178
  89.3 2.9 convolution_convert_fusion.5
  92.2 3.9 %collective-permute-done.7.refs_12_ = bf16[32,3584]{1,0:T(8,128)(2,1)} collective-permute-done((bf16[32,3584]{1,0:T(8,128)(2,1)}, bf16[32,3584]{1,0:T(8,128)(2,1)}, u32[]{:S(2)}, u32[]{:S(2)}) %collective-permute-start.7) | collective-permute-done | bytes 229408 | tf_op jit(solution)/shard_map/ppermute | solution.py:244
  96.1 4.4 %all-to-all-start.2 = ((bf16[8,32,3584]{2,1,0:T(8,128)(2,1)}), bf16[8,32,3584]{2,1,0:T(8,128)(2,1)}, u32[]{:S(2)}, u32[]{:S(2)}) async-start(bf16[8,32,3584]{2,1,0:T(8,128)(2,1)} %bitcast.113), calls=%async_computation.2 | async-start | bytes 3670016 | tf_op jit(solution)/shard_map/all_to_all | solution.py:178
  102.8 1.8 collective-permute-start.4
  104.6 1.5 collective-permute-start.9
  106.0 37.2 %collective-permute-done.12 = bf16[128,3584]{1,0:T(8,128)(2,1)} collective-permute-done((bf16[128,3584]{1,0:T(8,128)(2,1)}, bf16[128,3584]{1,0:T(8,128)(2,1)}, u32[]{:S(2)}, u32[]{:S(2)}) %collective-permute-start.12) | collective-permute-done | bytes 917536 | tf_op jit(solution)/shard_map/ppermute | solution.py:186
  143.6 3.6 %multiply_convert_fusion = (bf16[128,3584]{1,0:T(8,128)(2,1)S(1)}, bf16[128,3584]{1,0:T(8,128)(2,1)}) fusion(bf16[128,3584]{1,0:T(8,128)(2,1)} %collective-permute-done.12, bf16[2,128,3584]{2,1,0:T(8,128)(2,1)} %first_ref.1, f32[3584]{0:T(1024)S(1)} %get-tuple-element.84, pred[256,128]{1,0:T(8,128)(4,1)} %bitcast.122, bf16[256,3584]{1,0:T(8,128)(2,1)} %bitcast.27), kind=kOutput, calls=%fused_computation.15 | convolution fusion | flops 239009792 | bytes 5552128 | tf_op jit(solution)/shard_map/dot_general | solution.py:17
  148.1 1.9 convolution_convert_fusion.2
  150.0 4.3 %all-to-all-start.3 = ((bf16[8,32,3584]{2,1,0:T(8,128)(2,1)}), bf16[8,32,3584]{2,1,0:T(8,128)(2,1)}, u32[]{:S(2)}, u32[]{:S(2)}) async-start(bf16[8,32,3584]{2,1,0:T(8,128)(2,1)} %bitcast.114), calls=%async_computation.3 | async-start | bytes 3670016 | tf_op jit(solution)/shard_map/all_to_all | solution.py:178
  154.3 1.2 collective-permute-start.11
  155.5 1.3 collective-permute-start.10
  156.8 1.9 collective-permute-start.8
  158.7 39.0 %collective-permute-done.11 = bf16[128,3584]{1,0:T(8,128)(2,1)S(1)} collective-permute-done((bf16[128,3584]{1,0:T(8,128)(2,1)}, bf16[128,3584]{1,0:T(8,128)(2,1)S(1)}, u32[]{:S(2)}, u32[]{:S(2)}) %collective-permute-start.11) | collective-permute-done | bytes 917536 | tf_op jit(solution)/shard_map/ppermute | solution.py:186
  197.7 2.4 multiply_convert_fusion.1
  200.1 1.1 collective-permute-done.10.refs_5_
  202.6 3.0 convolution_convert_fusion.1
  205.7 4.3 %all-to-all-start.4 = ((bf16[8,32,3584]{2,1,0:T(8,128)(2,1)}), bf16[8,32,3584]{2,1,0:T(8,128)(2,1)}, u32[]{:S(2)}, u32[]{:S(2)}) async-start(bf16[8,32,3584]{2,1,0:T(8,128)(2,1)} %bitcast.111), calls=%async_computation.4 | async-start | bytes 3670016 | tf_op jit(solution)/shard_map/all_to_all | solution.py:178
  210.0 2.8 collective-permute-start.13
  212.8 2.3 collective-permute-start.15
  215.1 2.7 collective-permute-start.16
  217.8 1.2 collective-permute-start.17
  219.0 1.3 convert_reduce_fusion
  220.4 18.7 %collective-permute-done.13.refs_6_ = bf16[32,3584]{1,0:T(8,128)(2,1)S(1)} collective-permute-done((bf16[32,3584]{1,0:T(8,128)(2,1)}, bf16[32,3584]{1,0:T(8,128)(2,1)S(1)}, u32[]{:S(2)}, u32[]{:S(2)}) %collective-permute-start.13) | collective-permute-done | bytes 229408 | tf_op jit(solution)/shard_map/ppermute | solution.py:244
  239.1 4.2 %collective-permute-done.14.refs_7_ = bf16[32,3584]{1,0:T(8,128)(2,1)S(1)} collective-permute-done((bf16[32,3584]{1,0:T(8,128)(2,1)}, bf16[32,3584]{1,0:T(8,128)(2,1)S(1)}, u32[]{:S(2)}, u32[]{:S(2)}) %collective-permute-start.14) | collective-permute-done | bytes 229408 | tf_op jit(solution)/shard_map/ppermute | solution.py:244
  243.3 6.7 %collective-permute-done.15.refs_13_ = bf16[32,3584]{1,0:T(8,128)(2,1)S(1)} collective-permute-done((bf16[32,3584]{1,0:T(8,128)(2,1)}, bf16[32,3584]{1,0:T(8,128)(2,1)S(1)}, u32[]{:S(2)}, u32[]{:S(2)}) %collective-permute-start.15) | collective-permute-done | bytes 229408 | tf_op jit(solution)/shard_map/ppermute | solution.py:244
  250.1 6.8 %collective-permute-done.16.refs_14_ = bf16[32,3584]{1,0:T(8,128)(2,1)S(1)} collective-permute-done((bf16[32,3584]{1,0:T(8,128)(2,1)}, bf16[32,3584]{1,0:T(8,128)(2,1)S(1)}, u32[]{:S(2)}, u32[]{:S(2)}) %collective-permute-start.16) | collective-permute-done | bytes 229408 | tf_op jit(solution)/shard_map/ppermute | solution.py:244
  256.8 4.0 %collective-permute-done.17.refs_15_ = bf16[32,3584]{1,0:T(8,128)(2,1)S(1)} collective-permute-done((bf16[32,3584]{1,0:T(8,128)(2,1)}, bf16[32,3584]{1,0:T(8,128)(2,1)S(1)}, u32[]{:S(2)}, u32[]{:S(2)}) %collective-permute-start.17) | collective-permute-done | bytes 229408 | tf_op jit(solution)/shard_map/ppermute | solution.py:244
  260.8 1.0 copy-done.7
  261.8 0.9 copy-done.10
  262.8 6.4 %shard_map.94 = (f32[1,3584]{1,0:T(1,128)S(1)}, bf16[128,3584]{1,0:T(8,128)(2,1)S(1)}, f32[256,128]{1,0:T(8,128)S(1)}) custom-call(bf16[256,128]{1,0:T(8,128)(2,1)S(1)} %broadcast_maximum_fusion.1.act_ref, bf16[3,128,3584]{2,1,0:T(8,128)(2,1)S(1)} %copy-done, f32[2,3584]{1,0:T(2,128)S(1)} %copy-done.24, bf16[32,3584]{1,0:T(8,128)(2,1)S(1)} %get-tuple-element.38.refs_0_, ...), custom_call_target="tpu_custom_call" | custom-call | flops 704643072 | bytes 5505024 | tf_op jit(solution)/shard_map/pallas_call | solution.py:75
  269.4 4.8 %collective-permute-done.18 = f32[2,3584]{1,0:T(2,128)S(1)} collective-permute-done((f32[2,3584]{1,0:T(2,128)S(1)}, f32[2,3584]{1,0:T(2,128)S(1)}, u32[]{:S(2)}, u32[]{:S(2)}) %collective-permute-start.18) | collective-permute-done | bytes 28704 | tf_op jit(solution)/shard_map/ppermute | solution.py:321
  274.3 1.9 convolution_convert_fusion
  276.2 1.9 collective-permute-done.19
  278.8 4.2 %all-to-all-start.5 = ((bf16[16,16,3584]{2,1,0:T(8,128)(2,1)}), bf16[16,16,3584]{2,1,0:T(8,128)(2,1)S(1)}, u32[]{:S(2)}, u32[]{:S(2)}) async-start(bf16[16,16,3584]{2,1,0:T(8,128)(2,1)} %bitcast.110), calls=%async_computation.5 | async-start | bytes 3670016 | tf_op jit(solution)/shard_map/all_to_all | solution.py:175
  283.0 4.1 %fusion.24 = f32[256,3584]{1,0:T(8,128)} fusion(bf16[256,256]{1,0:T(8,128)(2,1)S(1)} %bitcast.119, bf16[256,3584]{1,0:T(8,128)(2,1)} %bitcast.31), kind=kOutput, calls=%fused_computation.81 | convolution fusion | flops 469762048 | bytes 5636096 | tf_op jit(solution)/shard_map/dot_general | solution.py:17
  287.6 2.2 fusion.25
  290.5 2.2 broadcast_select_fusion.1
  292.7 1.5 fusion.22
  294.3 1.6 gather_fusion.1
  300.7 5.5 %shard_map.95._ = bf16[2,3584,128]{2,1,0:T(8,128)(2,1)} custom-call(bf16[256,128]{1,0:T(8,128)(2,1)S(1)} %get-tuple-element.73.low_ref, bf16[32,3584]{1,0:T(8,128)(2,1)S(1)} %get-tuple-element.38.refs_0_, bf16[32,3584]{1,0:T(8,128)(2,1)} %collective-permute-done.3.refs_1_, bf16[32,3584]{1,0:T(8,128)(2,1)} %collective-permute-done.4.refs_2_, ...), custom_call_target="tpu_custom_call" | custom-call | flops 234881024 | bytes 4587520 | tf_op jit(solution)/shard_map/pallas_call | solution.py:116
  306.8 2.2 fusion
  309.1 1.8 pad_maximum_fusion
  310.9 8.7 %all-to-all-done.5 = bf16[16,16,3584]{2,1,0:T(8,128)(2,1)S(1)} async-done(((bf16[16,16,3584]{2,1,0:T(8,128)(2,1)}), bf16[16,16,3584]{2,1,0:T(8,128)(2,1)S(1)}, u32[]{:S(2)}, u32[]{:S(2)}) %all-to-all-start.5) | async-done | bytes 1835040 | tf_op jit(solution)/shard_map/all_to_all | solution.py:175
  319.5 3.8 %shard_map.96 = bf16[2,3584,128]{2,1,0:T(8,128)(2,1)} custom-call(bf16[256,128]{1,0:T(8,128)(2,1)S(1)} %bitcast.105, bf16[256,3584]{1,0:T(8,128)(2,1)S(1)} %bitcast.103, bf16[2,3584,128]{2,1,0:T(8,128)(2,1)} %shard_map.95._), custom_call_target="tpu_custom_call", output_to_operand_aliasing={{}: (2, {})} | custom-call | flops 234881024 | bytes 2752512 | tf_op jit(solution)/shard_map/pallas_call | solution.py:141
  (160 shorter events, 28.8 us)
Async XLA Ops:
  2.3 10.0 %copy-start.48 = (pred[2,256,128]{2,1,0:T(32,128)(4,1)}, pred[2,256,128]{2,1,0:T(32,128)(4,1)S(1)}, u32[]{:S(2)}) copy-start(pred[2,256,128]{2,1,0:T(32,128)(4,1)S(1)} %iota_compare_fusion.2) | copy-start | bytes 196612
  4.9 28.2 %all-to-all-start = ((bf16[16,32,128]{2,1,0:T(8,128)(2,1)}), bf16[16,32,128]{2,1,0:T(8,128)(2,1)}, u32[]{:S(2)}, u32[]{:S(2)}) async-start(bf16[16,32,128]{2,1,0:T(8,128)(2,1)} %bitcast.9), calls=%async_computation | async-start | bytes 262144 | tf_op jit(solution)/shard_map/all_to_all | solution.py:175
  13.0 1.5 copy-start.1
  14.5 1.5 copy-start.2
  16.0 15.7 %copy-start = (bf16[3,128,3584]{2,1,0:T(8,128)(2,1)S(1)}, bf16[3,128,3584]{2,1,0:T(8,128)(2,1)}, u32[]{:S(2)}) copy-start(bf16[3,128,3584]{2,1,0:T(8,128)(2,1)} %dec_ref.1) | copy-start | bytes 8257540
  28.9 19.4 %collective-permute-start.1 = (bf16[32,3584]{1,0:T(8,128)(2,1)}, bf16[32,3584]{1,0:T(8,128)(2,1)S(1)}, u32[]{:S(2)}, u32[]{:S(2)}) collective-permute-start(bf16[32,3584]{1,0:T(8,128)(2,1)} %get-tuple-element.42), channel_id=1, source_target_pairs={{0,8},{1,9},{2,10},{3,11},{4,12},{5,13},{6,14},{7,15},{8,0},{9,1},... | collective-permute-start | bytes 688136 | tf_op jit(solution)/shard_map/ppermute | solution.py:244
  31.7 20.4 %collective-permute-start.2 = (bf16[32,3584]{1,0:T(8,128)(2,1)}, bf16[32,3584]{1,0:T(8,128)(2,1)S(1)}, u32[]{:S(2)}, u32[]{:S(2)}) collective-permute-start(bf16[32,3584]{1,0:T(8,128)(2,1)} %get-tuple-element.43), channel_id=1, source_target_pairs={{0,9},{1,8},{2,11},{3,10},{4,13},{5,12},{6,15},{7,14},{8,1},{9,0},... | collective-permute-start | bytes 688136 | tf_op jit(solution)/shard_map/ppermute | solution.py:244
  33.0 1.8 copy-start.38
  34.9 1.9 copy-start.42
  52.1 4.5 %copy-start.51 = (s32[2,128,1]{1,2,0:T(1,128)S(1)}, s32[2,128,1]{1,2,0:T(1,128)}, u32[]{:S(2)}) copy-start(s32[2,128,1]{1,2,0:T(1,128)} %param.9) | copy-start | bytes 3076
  52.1 37.2 %all-to-all-start.1 = ((bf16[8,32,3584]{2,1,0:T(8,128)(2,1)}), bf16[8,32,3584]{2,1,0:T(8,128)(2,1)}, u32[]{:S(2)}, u32[]{:S(2)}) async-start(bf16[8,32,3584]{2,1,0:T(8,128)(2,1)} %bitcast.112), calls=%async_computation.1 | async-start | bytes 3670016 | tf_op jit(solution)/shard_map/all_to_all | solution.py:178
  56.5 21.0 %collective-permute-start = (s32[2,2,128]{2,1,0:T(2,128)S(1)}, s32[2,2,128]{2,1,0:T(2,128)S(1)}, u32[]{:S(2)}, u32[]{:S(2)}) collective-permute-start(s32[2,2,128]{2,1,0:T(2,128)S(1)} %pad_add_fusion), channel_id=1, source_target_pairs={{0,8},{1,9},{2,10},{3,11},{4,12},{5,13},{6,14},{7,15},{8,0},{9,1},... | collective-permute-start | bytes 6152 | tf_op jit(solution)/shard_map/ppermute | solution.py:186
  59.0 33.2 %collective-permute-start.5 = (bf16[32,3584]{1,0:T(8,128)(2,1)}, bf16[32,3584]{1,0:T(8,128)(2,1)}, u32[]{:S(2)}, u32[]{:S(2)}) collective-permute-start(bf16[32,3584]{1,0:T(8,128)(2,1)} %copy-done.37), channel_id=1, source_target_pairs={{0,10},{1,11},{2,8},{3,9},{4,14},{5,15},{6,12},{7,13},{8,2},{9,3},... | collective-permute-start | bytes 688136 | tf_op jit(solution)/shard_map/ppermute | solution.py:244
  60.9 31.3 %collective-permute-start.6 = (bf16[32,3584]{1,0:T(8,128)(2,1)}, bf16[32,3584]{1,0:T(8,128)(2,1)}, u32[]{:S(2)}, u32[]{:S(2)}) collective-permute-start(bf16[32,3584]{1,0:T(8,128)(2,1)} %copy-done.36), channel_id=1, source_target_pairs={{0,11},{1,10},{2,9},{3,8},{4,15},{5,14},{6,13},{7,12},{8,3},{9,2},... | collective-permute-start | bytes 688136 | tf_op jit(solution)/shard_map/ppermute | solution.py:244
  62.3 33.8 %collective-permute-start.7 = (bf16[32,3584]{1,0:T(8,128)(2,1)}, bf16[32,3584]{1,0:T(8,128)(2,1)}, u32[]{:S(2)}, u32[]{:S(2)}) collective-permute-start(bf16[32,3584]{1,0:T(8,128)(2,1)} %copy-done.35), channel_id=1, source_target_pairs={{0,12},{1,13},{2,14},{3,15},{4,8},{5,9},{6,10},{7,11},{8,4},{9,5},... | collective-permute-start | bytes 688136 | tf_op jit(solution)/shard_map/ppermute | solution.py:244
  64.4 19.8 %copy-start.52 = (s32[1024]{0:T(1024)}, s32[1024]{0:T(1024)S(1)}, u32[]{:S(2)}) copy-start(s32[1024]{0:T(1024)S(1)} %pad_clamp_fusion) | copy-start | bytes 12292
  77.7 11.6 %copy-start.46 = (pred[8,2,16,128]{3,2,1,0:T(8,128)(4,1)}, pred[8,2,16,128]{3,2,1,0:T(8,128)(4,1)S(1)}, u32[]{:S(2)}) copy-start(pred[8,2,16,128]{3,2,1,0:T(8,128)(4,1)S(1)} %broadcast_and_fusion.1) | copy-start | bytes 98308
  96.1 5.2 %copy-start.24 = (f32[2,3584]{1,0:T(2,128)S(1)}, f32[2,3584]{1,0:T(2,128)}, u32[]{:S(2)}) copy-start(f32[2,3584]{1,0:T(2,128)} %bias_ref.1) | copy-start | bytes 86020
  96.1 47.5 %all-to-all-start.2 = ((bf16[8,32,3584]{2,1,0:T(8,128)(2,1)}), bf16[8,32,3584]{2,1,0:T(8,128)(2,1)}, u32[]{:S(2)}, u32[]{:S(2)}) async-start(bf16[8,32,3584]{2,1,0:T(8,128)(2,1)} %bitcast.113), calls=%async_computation.2 | async-start | bytes 3670016 | tf_op jit(solution)/shard_map/all_to_all | solution.py:178
  100.6 42.7 %collective-permute-start.12 = (bf16[128,3584]{1,0:T(8,128)(2,1)}, bf16[128,3584]{1,0:T(8,128)(2,1)}, u32[]{:S(2)}, u32[]{:S(2)}) collective-permute-start(bf16[128,3584]{1,0:T(8,128)(2,1)} %convolution_convert_fusion.5), channel_id=1, source_target_pairs={{0,8},{1,9},{2,10},{3,11},{4,12},{5,13},{6,14},{7,15},{8,0},{9,1},... | collective-permute-start | bytes 2752520 | tf_op jit(solution)/shard_map/ppermute | solution.py:186
  102.6 44.6 %collective-permute-start.3 = (bf16[32,3584]{1,0:T(8,128)(2,1)}, bf16[32,3584]{1,0:T(8,128)(2,1)}, u32[]{:S(2)}, u32[]{:S(2)}) collective-permute-start(bf16[32,3584]{1,0:T(8,128)(2,1)} %copy-done.34), channel_id=1, source_target_pairs={{0,1},{1,0},{2,3},{3,2},{4,5},{5,4},{6,7},{7,6},{8,9},{9,8},{10,11... | collective-permute-start | bytes 688136 | tf_op jit(solution)/shard_map/ppermute | solution.py:244
  102.8 44.4 %collective-permute-start.4 = (bf16[32,3584]{1,0:T(8,128)(2,1)}, bf16[32,3584]{1,0:T(8,128)(2,1)}, u32[]{:S(2)}, u32[]{:S(2)}) collective-permute-start(bf16[32,3584]{1,0:T(8,128)(2,1)} %copy-done.33), channel_id=1, source_target_pairs={{0,2},{1,3},{2,0},{3,1},{4,6},{5,7},{6,4},{7,5},{8,10},{9,11},{10,... | collective-permute-start | bytes 688136 | tf_op jit(solution)/shard_map/ppermute | solution.py:244
  104.6 43.4 %collective-permute-start.9 = (bf16[32,3584]{1,0:T(8,128)(2,1)}, bf16[32,3584]{1,0:T(8,128)(2,1)}, u32[]{:S(2)}, u32[]{:S(2)}) collective-permute-start(bf16[32,3584]{1,0:T(8,128)(2,1)} %copy-done.32), channel_id=1, source_target_pairs={{0,4},{1,5},{2,6},{3,7},{4,0},{5,1},{6,2},{7,3},{8,12},{9,13},{10,... | collective-permute-start | bytes 688136 | tf_op jit(solution)/shard_map/ppermute | solution.py:244
  143.6 4.6 %copy-start.47 = (pred[8,2,16,128]{3,2,1,0:T(8,128)(4,1)S(1)}, pred[8,2,16,128]{3,2,1,0:T(8,128)(4,1)}, u32[]{:S(2)}) copy-start(pred[8,2,16,128]{3,2,1,0:T(8,128)(4,1)} %broadcast_and_fusion) | copy-start | bytes 98308
  150.0 52.6 %all-to-all-start.3 = ((bf16[8,32,3584]{2,1,0:T(8,128)(2,1)}), bf16[8,32,3584]{2,1,0:T(8,128)(2,1)}, u32[]{:S(2)}, u32[]{:S(2)}) async-start(bf16[8,32,3584]{2,1,0:T(8,128)(2,1)} %bitcast.114), calls=%async_computation.3 | async-start | bytes 3670016 | tf_op jit(solution)/shard_map/all_to_all | solution.py:178
  154.3 43.4 %collective-permute-start.11 = (bf16[128,3584]{1,0:T(8,128)(2,1)}, bf16[128,3584]{1,0:T(8,128)(2,1)S(1)}, u32[]{:S(2)}, u32[]{:S(2)}) collective-permute-start(bf16[128,3584]{1,0:T(8,128)(2,1)} %get-tuple-element.90), channel_id=1, source_target_pairs={{0,8},{1,9},{2,10},{3,11},{4,12},{5,13},{6,14},{7,15},{8,0},{9,1},... | collective-permute-start | bytes 2752520 | tf_op jit(solution)/shard_map/ppermute | solution.py:186
  155.5 45.7 %collective-permute-start.10 = (bf16[32,3584]{1,0:T(8,128)(2,1)}, bf16[32,3584]{1,0:T(8,128)(2,1)S(1)}, u32[]{:S(2)}, u32[]{:S(2)}) collective-permute-start(bf16[32,3584]{1,0:T(8,128)(2,1)} %copy-done.31), channel_id=1, source_target_pairs={{0,5},{1,4},{2,7},{3,6},{4,1},{5,0},{6,3},{7,2},{8,13},{9,12},{10,... | collective-permute-start | bytes 688136 | tf_op jit(solution)/shard_map/ppermute | solution.py:244
  156.8 45.1 %collective-permute-start.8 = (bf16[32,3584]{1,0:T(8,128)(2,1)}, bf16[32,3584]{1,0:T(8,128)(2,1)S(1)}, u32[]{:S(2)}, u32[]{:S(2)}) collective-permute-start(bf16[32,3584]{1,0:T(8,128)(2,1)} %copy-done.30), channel_id=1, source_target_pairs={{0,3},{1,2},{2,1},{3,0},{4,7},{5,6},{6,5},{7,4},{8,11},{9,10},{10,... | collective-permute-start | bytes 688136 | tf_op jit(solution)/shard_map/ppermute | solution.py:244
  205.7 73.2 %all-to-all-start.4 = ((bf16[8,32,3584]{2,1,0:T(8,128)(2,1)}), bf16[8,32,3584]{2,1,0:T(8,128)(2,1)}, u32[]{:S(2)}, u32[]{:S(2)}) async-start(bf16[8,32,3584]{2,1,0:T(8,128)(2,1)} %bitcast.111), calls=%async_computation.4 | async-start | bytes 3670016 | tf_op jit(solution)/shard_map/all_to_all | solution.py:178
  210.0 29.1 %collective-permute-start.13 = (bf16[32,3584]{1,0:T(8,128)(2,1)}, bf16[32,3584]{1,0:T(8,128)(2,1)S(1)}, u32[]{:S(2)}, u32[]{:S(2)}) collective-permute-start(bf16[32,3584]{1,0:T(8,128)(2,1)} %copy-done.29), channel_id=1, source_target_pairs={{0,6},{1,7},{2,4},{3,5},{4,2},{5,3},{6,0},{7,1},{8,14},{9,15},{10,... | collective-permute-start | bytes 688136 | tf_op jit(solution)/shard_map/ppermute | solution.py:244
  212.8 30.5 %collective-permute-start.14 = (bf16[32,3584]{1,0:T(8,128)(2,1)}, bf16[32,3584]{1,0:T(8,128)(2,1)S(1)}, u32[]{:S(2)}, u32[]{:S(2)}) collective-permute-start(bf16[32,3584]{1,0:T(8,128)(2,1)} %copy-done.28), channel_id=1, source_target_pairs={{0,7},{1,6},{2,5},{3,4},{4,3},{5,2},{6,1},{7,0},{8,15},{9,14},{10,... | collective-permute-start | bytes 688136 | tf_op jit(solution)/shard_map/ppermute | solution.py:244
  212.8 37.2 %collective-permute-start.15 = (bf16[32,3584]{1,0:T(8,128)(2,1)}, bf16[32,3584]{1,0:T(8,128)(2,1)S(1)}, u32[]{:S(2)}, u32[]{:S(2)}) collective-permute-start(bf16[32,3584]{1,0:T(8,128)(2,1)} %copy-done.27), channel_id=1, source_target_pairs={{0,13},{1,12},{2,15},{3,14},{4,9},{5,8},{6,11},{7,10},{8,5},{9,4},... | collective-permute-start | bytes 688136 | tf_op jit(solution)/shard_map/ppermute | solution.py:244
  215.1 41.7 %collective-permute-start.16 = (bf16[32,3584]{1,0:T(8,128)(2,1)}, bf16[32,3584]{1,0:T(8,128)(2,1)S(1)}, u32[]{:S(2)}, u32[]{:S(2)}) collective-permute-start(bf16[32,3584]{1,0:T(8,128)(2,1)} %copy-done.26), channel_id=1, source_target_pairs={{0,14},{1,15},{2,12},{3,13},{4,10},{5,11},{6,8},{7,9},{8,6},{9,7},... | collective-permute-start | bytes 688136 | tf_op jit(solution)/shard_map/ppermute | solution.py:244
  217.8 43.0 %collective-permute-start.17 = (bf16[32,3584]{1,0:T(8,128)(2,1)}, bf16[32,3584]{1,0:T(8,128)(2,1)S(1)}, u32[]{:S(2)}, u32[]{:S(2)}) collective-permute-start(bf16[32,3584]{1,0:T(8,128)(2,1)} %copy-done.25), channel_id=1, source_target_pairs={{0,15},{1,14},{2,13},{3,12},{4,11},{5,10},{6,9},{7,8},{8,7},{9,6},... | collective-permute-start | bytes 688136 | tf_op jit(solution)/shard_map/ppermute | solution.py:244
  239.1 30.1 %copy-start.12 = (bf16[32,3584]{1,0:T(8,128)(2,1)}, bf16[32,3584]{1,0:T(8,128)(2,1)S(1)}, u32[]{:S(2)}) copy-start(bf16[32,3584]{1,0:T(8,128)(2,1)S(1)} %collective-permute-done.13.refs_6_) | copy-start | bytes 688132
  243.3 25.9 %copy-start.14 = (bf16[32,3584]{1,0:T(8,128)(2,1)}, bf16[32,3584]{1,0:T(8,128)(2,1)S(1)}, u32[]{:S(2)}) copy-start(bf16[32,3584]{1,0:T(8,128)(2,1)S(1)} %collective-permute-done.14.refs_7_) | copy-start | bytes 688132
  250.1 19.2 %copy-start.16 = (bf16[32,3584]{1,0:T(8,128)(2,1)}, bf16[32,3584]{1,0:T(8,128)(2,1)S(1)}, u32[]{:S(2)}) copy-start(bf16[32,3584]{1,0:T(8,128)(2,1)S(1)} %collective-permute-done.15.refs_13_) | copy-start | bytes 688132
  256.8 12.4 %copy-start.18 = (bf16[32,3584]{1,0:T(8,128)(2,1)}, bf16[32,3584]{1,0:T(8,128)(2,1)S(1)}, u32[]{:S(2)}) copy-start(bf16[32,3584]{1,0:T(8,128)(2,1)S(1)} %collective-permute-done.16.refs_14_) | copy-start | bytes 688132
  260.8 8.5 %copy-start.20 = (bf16[32,3584]{1,0:T(8,128)(2,1)}, bf16[32,3584]{1,0:T(8,128)(2,1)S(1)}, u32[]{:S(2)}) copy-start(bf16[32,3584]{1,0:T(8,128)(2,1)S(1)} %collective-permute-done.17.refs_15_) | copy-start | bytes 688132
  260.8 1.0 copy-start.7
  261.8 0.9 copy-start.10
  262.8 11.5 %copy-start.3 = (bf16[2,128,3584]{2,1,0:T(8,128)(2,1)S(1)}, bf16[2,128,3584]{2,1,0:T(8,128)(2,1)}, u32[]{:S(2)}) copy-start(bf16[2,128,3584]{2,1,0:T(8,128)(2,1)} %second_ref.1) | copy-start | bytes 5505028
  262.8 11.5 %copy-start.49 = (pred[2,256,128]{2,1,0:T(32,128)(4,1)S(1)}, pred[2,256,128]{2,1,0:T(32,128)(4,1)}, u32[]{:S(2)}) copy-start(pred[2,256,128]{2,1,0:T(32,128)(4,1)} %copy-done.48) | copy-start | bytes 196612
  269.3 6.9 %copy-start.4 = (bf16[128,3584]{1,0:T(8,128)(2,1)}, bf16[128,3584]{1,0:T(8,128)(2,1)S(1)}, u32[]{:S(2)}) copy-start(bf16[128,3584]{1,0:T(8,128)(2,1)S(1)} %get-tuple-element.68) | copy-start | bytes 2752516
  269.3 8.9 %copy-start.22 = (f32[256,128]{1,0:T(8,128)}, f32[256,128]{1,0:T(8,128)S(1)}, u32[]{:S(2)}) copy-start(f32[256,128]{1,0:T(8,128)S(1)} %get-tuple-element.70) | copy-start | bytes 393220
  269.3 4.8 %collective-permute-start.18 = (f32[2,3584]{1,0:T(2,128)S(1)}, f32[2,3584]{1,0:T(2,128)S(1)}, u32[]{:S(2)}, u32[]{:S(2)}) collective-permute-start(f32[2,3584]{1,0:T(2,128)S(1)} %pad_maximum_fusion.3), channel_id=1, source_target_pairs={{0,8},{1,9},{2,10},{3,11},{4,12},{5,13},{6,14},{7,15},{8,0},{9,1},... | collective-permute-start | bytes 86024 | tf_op jit(solution)/shard_map/ppermute | solution.py:321
  274.2 3.9 %collective-permute-start.19 = (f32[2,3584]{1,0:T(2,128)S(1)}, f32[2,3584]{1,0:T(2,128)S(1)}, u32[]{:S(2)}, u32[]{:S(2)}) collective-permute-start(f32[2,3584]{1,0:T(2,128)S(1)} %fusion.19), channel_id=1, source_target_pairs={{0,4},{1,5},{2,6},{3,7},{4,0},{5,1},{6,2},{7,3},{8,12},{9,13},{10,... | collective-permute-start | bytes 86024 | tf_op jit(solution)/shard_map/ppermute | solution.py:321
  278.2 9.0 %collective-permute-start.20 = (f32[2,3584]{1,0:T(2,128)S(1)}, f32[2,3584]{1,0:T(2,128)S(1)}, u32[]{:S(2)}, u32[]{:S(2)}) collective-permute-start(f32[2,3584]{1,0:T(2,128)S(1)} %fusion.46), channel_id=1, source_target_pairs={{0,2},{1,3},{2,0},{3,1},{4,6},{5,7},{6,4},{7,5},{8,10},{9,11},{10,... | collective-permute-start | bytes 86024 | tf_op jit(solution)/shard_map/ppermute | solution.py:321
  278.8 4.2 %copy-start.44 = (bf16[8,2,16,256]{3,2,1,0:T(8,128)(2,1)S(1)}, bf16[8,2,16,256]{3,2,1,0:T(8,128)(2,1)}, u32[]{:S(2)}) copy-start(bf16[8,2,16,256]{3,2,1,0:T(8,128)(2,1)} %get-tuple-element.80) | copy-start | bytes 393220
  278.8 40.7 %all-to-all-start.5 = ((bf16[16,16,3584]{2,1,0:T(8,128)(2,1)}), bf16[16,16,3584]{2,1,0:T(8,128)(2,1)S(1)}, u32[]{:S(2)}, u32[]{:S(2)}) async-start(bf16[16,16,3584]{2,1,0:T(8,128)(2,1)} %bitcast.110), calls=%async_computation.5 | async-start | bytes 3670016 | tf_op jit(solution)/shard_map/all_to_all | solution.py:175
  283.0 4.6 %copy-start.39 = (bf16[2,128,3584]{2,1,0:T(8,128)(2,1)S(1)}, bf16[2,128,3584]{2,1,0:T(8,128)(2,1)}, u32[]{:S(2)}) copy-start(bf16[2,128,3584]{2,1,0:T(8,128)(2,1)} %slice.87) | copy-start | bytes 5505028
  287.2 2.7 collective-permute-start.21
  287.6 2.2 copy-start.50
  290.5 5.4 %copy-start.23 = (f32[256,128]{1,0:T(8,128)S(1)}, f32[256,128]{1,0:T(8,128)}, u32[]{:S(2)}) copy-start(f32[256,128]{1,0:T(8,128)} %copy-done.22) | copy-start | bytes 393220
  290.5 5.4 %copy-start.45 = (bf16[16,16,128]{2,1,0:T(8,128)(2,1)S(1)}, bf16[16,16,128]{2,1,0:T(8,128)(2,1)}, u32[]{:S(2)}) copy-start(bf16[16,16,128]{2,1,0:T(8,128)(2,1)} %gather_fusion) | copy-start | bytes 196612
  290.5 5.4 %copy-start.53 = (pred[256]{0:T(512)(128)(4,1)S(1)}, pred[256]{0:T(512)(128)(4,1)}, u32[]{:S(2)}) copy-start(pred[256]{0:T(512)(128)(4,1)} %broadcast_in_dim.48) | copy-start | bytes 772
  290.5 5.5 %copy-start.8 = (bf16[32,3584]{1,0:T(8,128)(2,1)S(1)}, bf16[32,3584]{1,0:T(8,128)(2,1)}, u32[]{:S(2)}) copy-start(bf16[32,3584]{1,0:T(8,128)(2,1)} %copy-done.6) | copy-start | bytes 688132
  290.5 5.5 %copy-start.11 = (bf16[32,3584]{1,0:T(8,128)(2,1)S(1)}, bf16[32,3584]{1,0:T(8,128)(2,1)}, u32[]{:S(2)}) copy-start(bf16[32,3584]{1,0:T(8,128)(2,1)} %copy-done.9) | copy-start | bytes 688132
  296.0 0.9 copy-start.13
  297.0 0.9 copy-start.15
  297.9 0.9 copy-start.17
  300.7 6.1 %copy-start.40 = (f32[256,3584]{1,0:T(8,128)S(1)}, f32[256,3584]{1,0:T(8,128)}, u32[]{:S(2)}) copy-start(f32[256,3584]{1,0:T(8,128)} %fusion.24) | copy-start | bytes 11010052
  300.7 6.1 %copy-start.43 = (bf16[8,2,16,256]{3,2,1,0:T(8,128)(2,1)S(1)}, bf16[8,2,16,256]{3,2,1,0:T(8,128)(2,1)}, u32[]{:S(2)}) copy-start(bf16[8,2,16,256]{3,2,1,0:T(8,128)(2,1)} %copy-done.42) | copy-start | bytes 393220
  306.8 2.3 copy-start.5
  (18 other events, 13.3 us)

commit v8 on v7

--- a/solution.py
+++ b/solution.py
@@ -11,6 +11,8 @@
 F32 = jnp.float32
 ROWS = ((0,), (0,))
 LAST = ((1,), (1,))
+SMALL = pl.CostEstimate(flops=1, bytes_accessed=1, transcendentals=0)
+PARAMS = pltpu.CompilerParams(vmem_limit_bytes=56 * 2**20)
 
 
 def mm(a, b, dims=((1,), (0,))):
@@ -40,12 +42,8 @@
         in_specs=[pl.BlockSpec((1, tokens), lambda i: (0, 0)), rows_spec, rows_spec],
         out_specs=[pl.BlockSpec((2 * cap, step), lambda i: (0, i))] * groups,
         out_shape=[jax.ShapeDtypeStruct((2 * cap, width), BF)] * groups,
-        compiler_params=pltpu.CompilerParams(vmem_limit_bytes=32 * 2**20),
-        cost_estimate=pl.CostEstimate(
-            flops=4 * groups * cap * tokens * width,
-            bytes_accessed=4 * (tokens + groups * cap) * width,
-            transcendentals=0,
-        ),
+        compiler_params=PARAMS,
+        cost_estimate=SMALL,
     )(key, first, second)
 
 
@@ -92,12 +90,8 @@
             jax.ShapeDtypeStruct((slots, latents), F32),
         ],
         scratch_shapes=[pltpu.VMEM((slots, step), BF)],
-        compiler_params=pltpu.CompilerParams(vmem_limit_bytes=32 * 2**20),
-        cost_estimate=pl.CostEstimate(
-            flops=6 * slots * latents * width,
-            bytes_accessed=2 * (2 * slots + 2 * latents) * width,
-            transcendentals=0,
-        ),
+        compiler_params=PARAMS,
+        cost_estimate=SMALL,
     )(act, decoder, bias, *arrivals)
 
 
@@ -121,12 +115,8 @@
         out_specs=pl.BlockSpec((1, step, latents), lambda i: (0, i, 0)),
         out_shape=jax.ShapeDtypeStruct((layers, width, latents), BF),
         scratch_shapes=[pltpu.VMEM((slots, step), BF)],
-        compiler_params=pltpu.CompilerParams(vmem_limit_bytes=32 * 2**20),
-        cost_estimate=pl.CostEstimate(
-            flops=2 * slots * latents * width,
-            bytes_accessed=2 * (2 * slots + latents) * width,
-            transcendentals=0,
-        ),
+        compiler_params=PARAMS,
+        cost_estimate=SMALL,
     )(low, *arrivals)
 
 
@@ -149,13 +139,84 @@
         out_specs=pl.BlockSpec((1, step, latents), lambda i: (1, i, 0)),
         out_shape=jax.ShapeDtypeStruct(products.shape, BF),
         input_output_aliases={2: 0},
-        compiler_params=pltpu.CompilerParams(vmem_limit_bytes=32 * 2**20),
-        cost_estimate=pl.CostEstimate(
-            flops=2 * slots * latents * width,
-            bytes_accessed=2 * (slots + latents) * width,
-            transcendentals=0,
-        ),
+        compiler_params=PARAMS,
+        cost_estimate=SMALL,
     )(low, resid, products)
+
+
+def gradients(me, errors, wide, decoder, pres, own, dec0, cap):
+    devices = pres.shape[0]
+    half = devices // 2
+    pairs, latents, width = decoder.shape
+    slots = devices * cap
+    step = column_block(width)
+    steps = width // step
+
+    def kernel(me_ref, eo_ref, em_ref, wo_ref, wm_ref, dec1_ref, dec2_ref, pre_ref, own_ref, dec0_ref, dec_ref, low_ref, bias_ref, back):
+        at = pl.program_id(0)
+        grad = mm(wo_ref[...], eo_ref[...], ROWS) + mm(wm_ref[...], em_ref[...], ROWS)
+        dec_ref[0] = dec0_ref[...]
+        dec_ref[1] = grad[:latents].astype(BF)
+        dec_ref[2] = grad[latents:].astype(BF)
+
+        @pl.when(at == 0)
+        def _():
+            back[...] = jnp.zeros_like(back)
+
+        both = jnp.concatenate([dec1_ref[0], dec2_ref[0]], axis=0)
+        back[0] += mm(eo_ref[...], both, LAST)
+        back[1] += mm(em_ref[...], both, LAST)
+
+        @pl.when(at == steps - 1)
+        def _():
+            my = me_ref[0]
+            sums = [jnp.zeros((1, latents), F32) for _ in range(2)]
+            for k in range(devices):
+                group = (my ^ k) % half
+                sender = my ^ k
+                for l in range(2):
+                    at_row = pl.multiple_of(group * 2 * cap + l * cap, cap)
+                    part = back[k // half, pl.ds(at_row, cap), l * latents : (l + 1) * latents]
+                    if l == 0:
+                        part = part + own_ref[k * cap : (k + 1) * cap, :]
+                        place = k * cap
+                    else:
+                        place = pl.multiple_of(sender * cap, cap)
+                    pre = pre_ref[(k // half) * half + group, l * cap : (l + 1) * cap, :]
+                    part = jnp.where(pre.astype(F32) > 0, part, 0.0)
+                    sums[l] = sums[l] + jnp.sum(part, axis=0, keepdims=True)
+                    low_ref[l, pl.ds(place, cap), :] = part.astype(BF)
+            for l in range(2):
+                bias_ref[l : l + 1, :] = sums[l]
+
+    whole = lambda shape: pl.BlockSpec(shape, lambda i: (0,) * len(shape))
+    return pl.pallas_call(
+        kernel,
+        grid=(steps,),
+        in_specs=[pl.BlockSpec(memory_space=pltpu.SMEM)]
+        + [pl.BlockSpec((half * 2 * cap, step), lambda i: (0, i))] * 2
+        + [whole((half * 2 * cap, 2 * latents))] * 2
+        + [
+            pl.BlockSpec((1, latents, step), lambda i: (1, 0, i)),
+            pl.BlockSpec((1, latents, step), lambda i: (2, 0, i)),
+            whole((devices, 2 * cap, latents)),
+            whole((slots, latents)),
+            pl.BlockSpec((latents, step), lambda i: (0, i)),
+        ],
+        out_specs=[
+            pl.BlockSpec((pairs, latents, step), lambda i: (0, 0, i)),
+            whole((2, slots, latents)),
+            whole((2, latents)),
+        ],
+        out_shape=[
+            jax.ShapeDtypeStruct((pairs, latents, width), BF),
+            jax.ShapeDtypeStruct((2, slots, latents), BF),
+            jax.ShapeDtypeStruct((2, latents), F32),
+        ],
+        scratch_shapes=[pltpu.VMEM((2, half * 2 * cap, 2 * latents), F32)],
+        compiler_params=PARAMS,
+        cost_estimate=SMALL,
+    )(me, *errors, *wide, decoder, decoder, pres, own, dec0)
 
 
 def per_device(residual, mlp_target, pre_acts, blocks, decoder, decoder_bias):
@@ -225,7 +286,7 @@
     got_pre = everyone(sent_pre.reshape(devices, layers * cap, latents))
     got_pre = got_pre.reshape(devices, layers, cap, latents)
     direct = devices <= 16 and cap % 16 == 0
-    windows = [[10, 11, 12], [1, 2, 4], [3, 5], [6, 7, 13, 14, 15], [8, 9]]
+    windows = [[8, 9, 10], [1, 2, 4], [3, 5], [6, 7, 11, 12, 13, 14, 15]]
     arrivals = [None] * devices
     if direct:
         windows = [[k for k in ks if k < devices] for ks in windows]
@@ -260,10 +321,10 @@
     def decode(rows):
         return mm(rows.reshape(-1, 2 * latents), dec1).astype(BF).reshape(half, -1, width)
 
-    depart(4, None)
     depart(0, None)
     pieces_m = decode(wide[half:])
-    pieces_m = within(after(pieces_m, arrived(4))).reshape(-1, width)
+    pieces_m = after(pieces_m, packed) if direct else pieces_m
+    pieces_m = within(pieces_m).reshape(-1, width)
     sum_m = mm(flat(place_m), pieces_m, ROWS).astype(BF)
     sum_low = across(sum_m)
     depart(1, sum_m)
@@ -331,23 +392,31 @@
     wide_m = wide[half:].reshape(-1, 2 * latents)
     errors_o = errors_o.reshape(-1, width)
     errors_m = errors_m.reshape(-1, width)
-    dec_later = mm(wide_o, errors_o, ROWS) + mm(wide_m, errors_m, ROWS)
-    back = jnp.concatenate([mm(errors_o, dec1, LAST), mm(errors_m, dec1, LAST)], axis=0)
-    back = back.reshape(devices, layers, cap, 2 * latents)
-    back = turn(back)
-    back0 = back[:, 0, :, :latents]
     if direct:
-        back0 = jnp.take(back0, sender, axis=0)
-    grad0 = back0.reshape(slots, latents) + own
-    grad0 = jnp.where(pre0 > 0, grad0, 0.0)
-    grad1 = jnp.where(got_pre[:, 1] > 0, back[:, 1, :, latents:], 0.0).reshape(slots, latents)
-    enc_bias = jnp.stack([jnp.sum(grad0, axis=0), jnp.sum(grad1, axis=0)])
-    dec = jnp.concatenate([dec0[None], dec_later.astype(BF).reshape(2, latents, width)])
-    low0, low1 = grad0.astype(BF), grad1.astype(BF)
-    if direct:
-        enc = encoder_layer1(encoder_layer0(arrivals, low0, layers, cap), resid1, low1)
+        pres = turn(got_pre).reshape(devices, layers * cap, latents)
+        dec, low, enc_bias = gradients(
+            me.astype(jnp.int32).reshape(1),
+            (errors_o, errors_m),
+            (wide_o, wide_m),
+            decoder,
+            pres,
+            own,
+            dec0,
+            cap,
+        )
+        enc = encoder_layer1(encoder_layer0(arrivals, low[0], layers, cap), resid1, low[1])
     else:
-        enc = jnp.stack([mm(resid0, low0, ROWS).astype(BF), mm(resid1, low1, ROWS).astype(BF)])
+        dec_later = mm(wide_o, errors_o, ROWS) + mm(wide_m, errors_m, ROWS)
+        dec = jnp.concatenate([dec0[None], dec_later.astype(BF).reshape(2, latents, width)])
+        back = jnp.concatenate([mm(errors_o, dec1, LAST), mm(errors_m, dec1, LAST)], axis=0)
+        back = turn(back.reshape(devices, layers, cap, 2 * latents))
+        own = own.reshape(devices, cap, latents)
+        grads = jnp.stack([back[:, 0, :, :latents] + own, back[:, 1, :, latents:]])
+        grads = jnp.where(jnp.swapaxes(got_pre, 0, 1) > 0, grads, 0.0)
+        grads = grads.reshape(layers, slots, latents)
+        enc_bias = jnp.sum(grads, axis=1)
+        low = grads.astype(BF)
+        enc = jnp.stack([mm(resid0, low[0], ROWS).astype(BF), mm(resid1, low[1], ROWS).astype(BF)])
     return dec, enc, enc_bias, bias_grad
 
 

time: 330 us -> 346 us (1.048); the launches traced: 323 us -> 343 us
  waiting for transfers between devices: 171 us -> 205 us
  local copies, waits for them, and re-layouts: 26.7 us -> 7.99 us
  Pallas kernels: 19.6 us -> 35 us
  matrix products: 31.3 us -> 19.3 us
  starting transfers between devices: 58.6 us -> 66.4 us
  other arithmetic: 15 us -> 8.56 us
    ppermute x4, waiting for transfers between devices: 6.7 us -> 48.4 us  [total(): x = x + lax.ppermute(x, 'layer', [(i, i ^ step) for i in range(devices)])]
    ppermute x3, waiting for transfers between devices: 88.7 us -> 108 us  [across(): return lax.ppermute(x, 'layer', mirror)]
    unnamed x108 -> x56, local copies, waits for them, and re-layouts: 20.3 us -> 4.33 us
    ppermute x15, waiting for transfers between devices: 61.5 us -> 48.3 us  [depart(): arrivals[k] = lax.ppermute(x, 'layer', [(i, i ^ k) for i in range(devices)])]
    dot_general x13 -> x9, matrix products: 31.3 us -> 19.3 us  [mm(): return lax.dot_general(a, b, (dims, ((), ())), preferred_element_type=F32)]
    pallas_call x0 -> x1, Pallas kernels: none -> 9.04 us  [gradients(): pl.pallas_call(kernel, grid=(steps,), in_specs=[pl.BlockSpec(memory_space...]
    all_to_all x2, waiting for transfers between devices: 8.69 us -> 0.01 us  [everyone(): return lax.all_to_all(x, 'layer', split_axis=0, concat_axis=0, tiled=True)]
    all_to_all x2, starting transfers between devices: 11.6 us -> 20.3 us  [everyone(): return lax.all_to_all(x, 'layer', split_axis=0, concat_axis=0, tiled=True)]
  transfers between devices with their start and end apart: 28 -> 28, of which waited for: 18 -> 15; matrix products, arithmetic and copies ran while one was open for 13% -> 6% of each run, Pallas kernels for 5% -> 9%
where the time goes in v8:
time: 346 us; the launch traced here: 343 us
  waiting for transfers between devices  205 us (59%)
  starting transfers between devices  66.4 us (19%)
  Pallas kernels  35 us (10%)
  matrix products  19.3 us (6%)
  other arithmetic  8.56 us (2%)
  local copies, waits for them, and re-layouts  7.99 us (2%)
    ppermute x3, waiting for transfers between devices, across(): return lax.ppermute(x, 'layer', mirror)  108 us
    ppermute x4, waiting for transfers between devices, total(): x = x + lax.ppermute(x, 'layer', [(i, i ^ step) for i in range(devices)])  48.4 us
    ppermute x15, waiting for transfers between devices, depart(): arrivals[k] = lax.ppermute(x, 'layer', [(i, i ^ k) for i in range(devices)])  48.3 us
    ppermute x15, starting transfers between devices, depart(): arrivals[k] = lax.ppermute(x, 'layer', [(i, i ^ k) for i in range(devices)])  21.2 us
    all_to_all x2, starting transfers between devices, everyone(): return lax.all_to_all(x, 'layer', split_axis=0, concat_axis=0, tiled=True)  20.3 us
    all_to_all x4, starting transfers between devices, within(): lax.all_to_all(x, 'layer', split_axis=0, concat_axis=0, tiled=True, axis_...  19.7 us
    dot_general x9, matrix products, mm(): return lax.dot_general(a, b, (dims, ((), ())), preferred_element_type=F32)  19.3 us
    pallas_call x1, Pallas kernels, gradients(): pl.pallas_call(kernel, grid=(steps,), in_specs=[pl.BlockSpec(memory_space...  9.04 us
  transfers between devices with their start and end apart: 28, of which 15 were waited for; matrix products, arithmetic and copies ran while one was open for 6% of the time, Pallas kernels for 9%

profile of v8, /device:TPU:0, one launch (start us, length us, event | category | flops | bytes accessed | tf_op | source)
XLA Modules:
  0.0 343.5 jit_solution(13186074272648246168)
XLA Ops:
  0.7 0.9 convert_reduce_fusion.1
  1.6 0.7 multiply_add_fusion
  2.3 0.9 convolution_convert_fusion.6
  3.3 0.9 convolution_convert_fusion.7
  4.2 0.7 pad_maximum_fusion
  4.9 7.4 %all-to-all-start = ((bf16[16,32,128]{2,1,0:T(8,128)(2,1)}), bf16[16,32,128]{2,1,0:T(8,128)(2,1)S(1)}, u32[]{:S(2)}, u32[]{:S(2)}) async-start(bf16[16,32,128]{2,1,0:T(8,128)(2,1)} %bitcast.11), calls=%async_computation | async-start | bytes 262144 | tf_op jit(solution)/shard_map/all_to_all | solution.py:236
  12.2 1.2 bitcast_add_fusion.key_ref
  13.4 6.4 %shard_map.93 = (bf16[32,3584]{1,0:T(8,128)(2,1)}, bf16[32,3584]{1,0:T(8,128)(2,1)}, bf16[32,3584]{1,0:T(8,128)(2,1)}, bf16[32,3584]{1,0:T(8,128)(2,1)}, bf16[32...) custom-call(s32[1,128]{1,0:T(1,128)} %bitcast_add_fusion.key_ref, ...), custom_call_target="tpu_custom_call" | custom-call | flops 1 | bytes 1 | tf_op jit(solution)/shard_map/pallas_call | solution.py:39
  19.8 1.3 slice.85
  21.3 1.4 copy-done.1
  22.7 1.9 convolution_convert_fusion.3
  24.6 4.5 %all-to-all-start.1 = ((bf16[8,32,3584]{2,1,0:T(8,128)(2,1)}), bf16[8,32,3584]{2,1,0:T(8,128)(2,1)}, u32[]{:S(2)}, u32[]{:S(2)}) async-start(bf16[8,32,3584]{2,1,0:T(8,128)(2,1)} %bitcast.78), calls=%async_computation.1 | async-start | bytes 3670016 | tf_op jit(solution)/shard_map/all_to_all | solution.py:239
  29.1 2.9 collective-permute-start.1
  32.0 3.6 %collective-permute-start.3 = (bf16[32,3584]{1,0:T(8,128)(2,1)S(1)}, bf16[32,3584]{1,0:T(8,128)(2,1)S(1)}, u32[]{:S(2)}, u32[]{:S(2)}) collective-permute-start(bf16[32,3584]{1,0:T(8,128)(2,1)S(1)} %copy-done.26), channel_id=1, source_target_pairs={{0,10},{1,11},{2,8},{3,9},{4,14},{5,15},{6,12},{7,13},{8,2},{9,3},... | collective-permute-start | bytes 688136 | tf_op jit(solution)/shard_map/ppermute | solution.py:305
  35.7 0.6 collective-permute-start
  36.5 28.1 %collective-permute-done = s32[2,2,128]{2,1,0:T(2,128)S(1)} collective-permute-done((s32[2,2,128]{2,1,0:T(2,128)S(1)}, s32[2,2,128]{2,1,0:T(2,128)S(1)}, u32[]{:S(2)}, u32[]{:S(2)}) %collective-permute-start) | collective-permute-done | bytes 2080 | tf_op jit(solution)/shard_map/ppermute | solution.py:247
  64.7 0.6 gather_fusion
  65.3 0.7 fusion.10.act_ref
  66.0 1.9 convolution_convert_fusion.4
  67.9 1.9 convolution_convert_fusion.5
  69.9 0.8 copy-done.9
  70.8 7.1 %all-to-all-start.2 = ((bf16[8,32,3584]{2,1,0:T(8,128)(2,1)}), bf16[8,32,3584]{2,1,0:T(8,128)(2,1)S(1)}, u32[]{:S(2)}, u32[]{:S(2)}) async-start(bf16[8,32,3584]{2,1,0:T(8,128)(2,1)} %bitcast.15), calls=%async_computation.2 | async-start | bytes 3670016 | tf_op jit(solution)/shard_map/all_to_all | solution.py:239
  78.0 0.6 collective-permute-start.5
  78.6 1.7 collective-permute-start.6
  80.3 1.5 collective-permute-start.7
  81.7 39.7 %collective-permute-done.4 = bf16[128,3584]{1,0:T(8,128)(2,1)} collective-permute-done((bf16[128,3584]{1,0:T(8,128)(2,1)S(1)}, bf16[128,3584]{1,0:T(8,128)(2,1)}, u32[]{:S(2)}, u32[]{:S(2)}) %collective-permute-start.4) | collective-permute-done | bytes 917536 | tf_op jit(solution)/shard_map/ppermute | solution.py:247
  121.5 3.0 multiply_convert_fusion.1
  124.5 0.9 collective-permute-done.7.refs_4_
  125.5 1.9 convolution_convert_fusion.2
  127.3 3.6 %all-to-all-start.3 = ((bf16[8,32,3584]{2,1,0:T(8,128)(2,1)}), bf16[8,32,3584]{2,1,0:T(8,128)(2,1)S(1)}, u32[]{:S(2)}, u32[]{:S(2)}) async-start(bf16[8,32,3584]{2,1,0:T(8,128)(2,1)} %bitcast.30), calls=%async_computation.3 | async-start | bytes 3670016 | tf_op jit(solution)/shard_map/all_to_all | solution.py:239
  131.0 1.6 collective-permute-start.10
  132.6 1.4 collective-permute-start.9
  134.1 40.4 %collective-permute-done.8 = bf16[128,3584]{1,0:T(8,128)(2,1)S(1)} collective-permute-done((bf16[128,3584]{1,0:T(8,128)(2,1)}, bf16[128,3584]{1,0:T(8,128)(2,1)S(1)}, u32[]{:S(2)}, u32[]{:S(2)}) %collective-permute-start.8) | collective-permute-done | bytes 917536 | tf_op jit(solution)/shard_map/ppermute | solution.py:247
  174.5 2.4 multiply_convert_fusion
  176.9 0.9 collective-permute-done.10.refs_5_
  177.9 3.7 %convolution_convert_fusion.1 = bf16[256,3584]{1,0:T(8,128)(2,1)} fusion(pred[256,128]{1,0:T(8,128)(4,1)S(1)} %bitcast.89, bf16[128,3584]{1,0:T(8,128)(2,1)} %multiply_convert_fusion), kind=kOutput, calls=%fused_computation.2 | convolution fusion | flops 235798528 | bytes 2785280 | tf_op jit(solution)/shard_map/dot_general | solution.py:19
  181.6 4.5 %all-to-all-start.4 = ((bf16[8,32,3584]{2,1,0:T(8,128)(2,1)}), bf16[8,32,3584]{2,1,0:T(8,128)(2,1)}, u32[]{:S(2)}, u32[]{:S(2)}) async-start(bf16[8,32,3584]{2,1,0:T(8,128)(2,1)} %bitcast.32), calls=%async_computation.4 | async-start | bytes 3670016 | tf_op jit(solution)/shard_map/all_to_all | solution.py:239
  186.1 2.8 collective-permute-start.11
  188.9 1.0 collective-permute-start.13
  189.9 4.0 %collective-permute-start.14 = (bf16[32,3584]{1,0:T(8,128)(2,1)}, bf16[32,3584]{1,0:T(8,128)(2,1)S(1)}, u32[]{:S(2)}, u32[]{:S(2)}) collective-permute-start(bf16[32,3584]{1,0:T(8,128)(2,1)} %get-tuple-element.71), channel_id=1, source_target_pairs={{0,12},{1,13},{2,14},{3,15},{4,8},{5,9},{6,10},{7,11},{8,4},{9,5},... | collective-permute-start | bytes 688136 | tf_op jit(solution)/shard_map/ppermute | solution.py:305
  193.9 26.2 %collective-permute-done.11.refs_6_ = bf16[32,3584]{1,0:T(8,128)(2,1)S(1)} collective-permute-done((bf16[32,3584]{1,0:T(8,128)(2,1)}, bf16[32,3584]{1,0:T(8,128)(2,1)S(1)}, u32[]{:S(2)}, u32[]{:S(2)}) %collective-permute-start.11) | collective-permute-done | bytes 229408 | tf_op jit(solution)/shard_map/ppermute | solution.py:305
  220.1 4.0 %collective-permute-done.12.refs_7_ = bf16[32,3584]{1,0:T(8,128)(2,1)S(1)} collective-permute-done((bf16[32,3584]{1,0:T(8,128)(2,1)}, bf16[32,3584]{1,0:T(8,128)(2,1)S(1)}, u32[]{:S(2)}, u32[]{:S(2)}) %collective-permute-start.12) | collective-permute-done | bytes 229408 | tf_op jit(solution)/shard_map/ppermute | solution.py:305
  224.1 3.1 convolution_convert_fusion
  227.2 0.1 convert_reduce_fusion
  227.4 1.6 collective-permute-done.14.refs_12_
  229.0 4.0 %collective-permute-done.15.refs_13_ = bf16[32,3584]{1,0:T(8,128)(2,1)S(1)} collective-permute-done((bf16[32,3584]{1,0:T(8,128)(2,1)}, bf16[32,3584]{1,0:T(8,128)(2,1)S(1)}, u32[]{:S(2)}, u32[]{:S(2)}) %collective-permute-start.15) | collective-permute-done | bytes 229408 | tf_op jit(solution)/shard_map/ppermute | solution.py:305
  233.0 6.8 %collective-permute-done.16.refs_14_ = bf16[32,3584]{1,0:T(8,128)(2,1)S(1)} collective-permute-done((bf16[32,3584]{1,0:T(8,128)(2,1)}, bf16[32,3584]{1,0:T(8,128)(2,1)S(1)}, u32[]{:S(2)}, u32[]{:S(2)}) %collective-permute-start.16) | collective-permute-done | bytes 229408 | tf_op jit(solution)/shard_map/ppermute | solution.py:305
  239.8 4.0 %collective-permute-done.17.refs_15_ = bf16[32,3584]{1,0:T(8,128)(2,1)S(1)} collective-permute-done((bf16[32,3584]{1,0:T(8,128)(2,1)}, bf16[32,3584]{1,0:T(8,128)(2,1)S(1)}, u32[]{:S(2)}, u32[]{:S(2)}) %collective-permute-start.17) | collective-permute-done | bytes 229408 | tf_op jit(solution)/shard_map/ppermute | solution.py:305
  243.8 0.7 copy-done.20
  244.5 7.9 %shard_map.94 = (f32[1,3584]{1,0:T(1,128)}, bf16[128,3584]{1,0:T(8,128)(2,1)}, f32[256,128]{1,0:T(8,128)}) custom-call(bf16[256,128]{1,0:T(8,128)(2,1)} %fusion.10.act_ref, bf16[3,128,3584]{2,1,0:T(8,128)(2,1)} %dec2_ref.1, f32[2,3584]{1,0:T(2,128)} %bias_ref.1, bf16[32,3584]{1,0:T(8,128)(2,1)} %get-tuple-element.43.refs_0_, bf16[32,3584]{1,0:T(8,128)(2,1)} %copy-done.10, ...), custom_call_target="tpu_custom_call" | custom-call | flops 1 | bytes 1 | tf_op jit(solution)/shard_map/pallas_call | solution.py:73
  252.4 12.9 %all-to-all-start.5 = ((bf16[16,16,3584]{2,1,0:T(8,128)(2,1)}), bf16[16,16,3584]{2,1,0:T(8,128)(2,1)S(1)}, u32[]{:S(2)}, u32[]{:S(2)}) async-start(bf16[16,16,3584]{2,1,0:T(8,128)(2,1)} %bitcast.36), calls=%async_computation.5 | async-start | bytes 3670016 | tf_op jit(solution)/shard_map/all_to_all | solution.py:236
  265.3 2.9 collective-permute-start.18
  268.2 41.7 %collective-permute-done.18 = f32[2,3584]{1,0:T(2,128)S(1)} collective-permute-done((f32[2,3584]{1,0:T(2,128)S(1)}, f32[2,3584]{1,0:T(2,128)S(1)}, u32[]{:S(2)}, u32[]{:S(2)}) %collective-permute-start.18) | collective-permute-done | bytes 28704 | tf_op jit(solution)/shard_map/ppermute | solution.py:382
  310.1 3.9 %collective-permute-done.19 = f32[2,3584]{1,0:T(2,128)S(1)} collective-permute-done((f32[2,3584]{1,0:T(2,128)S(1)}, f32[2,3584]{1,0:T(2,128)S(1)}, u32[]{:S(2)}, u32[]{:S(2)}) %collective-permute-start.19) | collective-permute-done | bytes 28704 | tf_op jit(solution)/shard_map/ppermute | solution.py:382
  314.0 1.6 collective-permute-start.20
  315.6 2.3 collective-permute-done.20
  318.0 0.7 pad_maximum_fusion.1.pre_ref
  318.7 0.5 collective-permute-done.21
  319.2 0.6 pad_subtract_fusion
  319.8 9.0 %shard_map.95 = (bf16[3,128,3584]{2,1,0:T(8,128)(2,1)}, bf16[2,256,128]{2,1,0:T(8,128)(2,1)}, f32[2,128]{1,0:T(2,128)}) custom-call(s32[1]{0:T(128)} %bitcast.me_ref, bf16[256,3584]{1,0:T(8,128)(2,1)} %bitcast.79, bf16[256,3584]{1,0:T(8,128)(2,1)} %bitcast.33.em_ref, bf16[256,256]{1,0:T(8,128)(2,1)} %bitcast.85, bf16[256,256]{1,0:T(8,128)(2,1)} %bitcast.87, ...), custom_call_target="tpu_custom_call" | custom-call | flops 1 | bytes 1 | tf_op jit(solution)/shard_map/pallas_call | solution.py:193
  328.9 1.5 slice_bitcast_fusion.6
  330.4 6.1 %shard_map.96._ = bf16[2,3584,128]{2,1,0:T(8,128)(2,1)} custom-call(bf16[256,128]{1,0:T(8,128)(2,1)} %get-tuple-element.84.low_ref, bf16[32,3584]{1,0:T(8,128)(2,1)} %get-tuple-element.43.refs_0_, bf16[32,3584]{1,0:T(8,128)(2,1)} %copy-done.10, bf16[32,3584]{1,0:T(8,128)(2,1)} %copy-done.11, bf16[32,3584]{1,0:T(8,128)(2,1)} %copy-done.13, ...), custom_call_target="tpu_custom_call" | custom-call | flops 1 | bytes 1 | tf_op jit(solution)/shard_map/pallas_call | solution.py:110
  336.5 1.2 copy-done.3
  337.7 5.7 %shard_map.97 = bf16[2,3584,128]{2,1,0:T(8,128)(2,1)} custom-call(bf16[256,128]{1,0:T(8,128)(2,1)} %get-tuple-element.85.low_ref, bf16[256,3584]{1,0:T(8,128)(2,1)} %bitcast.80, bf16[2,3584,128]{2,1,0:T(8,128)(2,1)} %shard_map.96._), custom_call_target="tpu_custom_call", output_to_operand_aliasing={{}: (2, {})} | custom-call | flops 1 | bytes 1 | tf_op jit(solution)/shard_map/pallas_call | solution.py:131
  (103 shorter events, 1.1 us)
Async XLA Ops:
  2.3 0.9 copy-start.21
  4.9 16.3 %all-to-all-start = ((bf16[16,32,128]{2,1,0:T(8,128)(2,1)}), bf16[16,32,128]{2,1,0:T(8,128)(2,1)S(1)}, u32[]{:S(2)}, u32[]{:S(2)}) async-start(bf16[16,32,128]{2,1,0:T(8,128)(2,1)} %bitcast.11), calls=%async_computation | async-start | bytes 262144 | tf_op jit(solution)/shard_map/all_to_all | solution.py:236
  13.4 6.4 %copy-start = (bf16[3,128,3584]{2,1,0:T(8,128)(2,1)S(1)}, bf16[3,128,3584]{2,1,0:T(8,128)(2,1)}, u32[]{:S(2)}) copy-start(bf16[3,128,3584]{2,1,0:T(8,128)(2,1)} %dec2_ref.1) | copy-start | bytes 8257540
  21.1 1.6 copy-start.1
  21.3 3.3 copy-start.6
  21.3 44.7 %copy-start.5 = (bf16[8,2,16,256]{3,2,1,0:T(8,128)(2,1)}, bf16[8,2,16,256]{3,2,1,0:T(8,128)(2,1)S(1)}, u32[]{:S(2)}) copy-start(bf16[8,2,16,256]{3,2,1,0:T(8,128)(2,1)S(1)} %get-tuple-element.82) | copy-start | bytes 393220
  24.6 7.4 %copy-start.27 = (bf16[32,3584]{1,0:T(8,128)(2,1)S(1)}, bf16[32,3584]{1,0:T(8,128)(2,1)}, u32[]{:S(2)}) copy-start(bf16[32,3584]{1,0:T(8,128)(2,1)} %get-tuple-element.52) | copy-start | bytes 688132
  24.6 7.4 %copy-start.26 = (bf16[32,3584]{1,0:T(8,128)(2,1)S(1)}, bf16[32,3584]{1,0:T(8,128)(2,1)}, u32[]{:S(2)}) copy-start(bf16[32,3584]{1,0:T(8,128)(2,1)} %get-tuple-element.53) | copy-start | bytes 688132
  24.6 11.1 %copy-start.25 = (s32[2,128,1]{1,2,0:T(1,128)S(1)}, s32[2,128,1]{1,2,0:T(1,128)}, u32[]{:S(2)}) copy-start(s32[2,128,1]{1,2,0:T(1,128)} %param.9) | copy-start | bytes 3076
  24.6 43.3 %all-to-all-start.1 = ((bf16[8,32,3584]{2,1,0:T(8,128)(2,1)}), bf16[8,32,3584]{2,1,0:T(8,128)(2,1)}, u32[]{:S(2)}, u32[]{:S(2)}) async-start(bf16[8,32,3584]{2,1,0:T(8,128)(2,1)} %bitcast.78), calls=%async_computation.1 | async-start | bytes 3670016 | tf_op jit(solution)/shard_map/all_to_all | solution.py:239
  29.1 40.8 %collective-permute-start.1 = (bf16[32,3584]{1,0:T(8,128)(2,1)}, bf16[32,3584]{1,0:T(8,128)(2,1)S(1)}, u32[]{:S(2)}, u32[]{:S(2)}) collective-permute-start(bf16[32,3584]{1,0:T(8,128)(2,1)} %get-tuple-element.51), channel_id=1, source_target_pairs={{0,8},{1,9},{2,10},{3,11},{4,12},{5,13},{6,14},{7,15},{8,0},{9,1},... | collective-permute-start | bytes 688136 | tf_op jit(solution)/shard_map/ppermute | solution.py:305
  32.0 37.9 %collective-permute-start.2 = (bf16[32,3584]{1,0:T(8,128)(2,1)S(1)}, bf16[32,3584]{1,0:T(8,128)(2,1)S(1)}, u32[]{:S(2)}, u32[]{:S(2)}) collective-permute-start(bf16[32,3584]{1,0:T(8,128)(2,1)S(1)} %copy-done.27), channel_id=1, source_target_pairs={{0,9},{1,8},{2,11},{3,10},{4,13},{5,12},{6,15},{7,14},{8,1},{9,0},... | collective-permute-start | bytes 688136 | tf_op jit(solution)/shard_map/ppermute | solution.py:305
  32.0 37.9 %collective-permute-start.3 = (bf16[32,3584]{1,0:T(8,128)(2,1)S(1)}, bf16[32,3584]{1,0:T(8,128)(2,1)S(1)}, u32[]{:S(2)}, u32[]{:S(2)}) collective-permute-start(bf16[32,3584]{1,0:T(8,128)(2,1)S(1)} %copy-done.26), channel_id=1, source_target_pairs={{0,10},{1,11},{2,8},{3,9},{4,14},{5,15},{6,12},{7,13},{8,2},{9,3},... | collective-permute-start | bytes 688136 | tf_op jit(solution)/shard_map/ppermute | solution.py:305
  35.7 28.9 %collective-permute-start = (s32[2,2,128]{2,1,0:T(2,128)S(1)}, s32[2,2,128]{2,1,0:T(2,128)S(1)}, u32[]{:S(2)}, u32[]{:S(2)}) collective-permute-start(s32[2,2,128]{2,1,0:T(2,128)S(1)} %pad_add_fusion), channel_id=1, source_target_pairs={{0,8},{1,9},{2,10},{3,11},{4,12},{5,13},{6,14},{7,15},{8,0},{9,1},... | collective-permute-start | bytes 6152 | tf_op jit(solution)/shard_map/ppermute | solution.py:247
  69.9 51.6 %copy-start.4 = (bf16[128,3584]{1,0:T(8,128)(2,1)}, bf16[128,3584]{1,0:T(8,128)(2,1)S(1)}, u32[]{:S(2)}) copy-start(bf16[128,3584]{1,0:T(8,128)(2,1)S(1)} %convolution_convert_fusion.5) | copy-start | bytes 2752516
  69.9 0.8 copy-start.7
  69.9 0.9 copy-start.8
  69.9 0.8 copy-start.9
  69.9 8.0 %copy-start.24 = (f32[2,3584]{1,0:T(2,128)S(1)}, f32[2,3584]{1,0:T(2,128)}, u32[]{:S(2)}) copy-start(f32[2,3584]{1,0:T(2,128)} %bias_ref.1) | copy-start | bytes 86020
  70.8 50.7 %all-to-all-start.2 = ((bf16[8,32,3584]{2,1,0:T(8,128)(2,1)}), bf16[8,32,3584]{2,1,0:T(8,128)(2,1)S(1)}, u32[]{:S(2)}, u32[]{:S(2)}) async-start(bf16[8,32,3584]{2,1,0:T(8,128)(2,1)} %bitcast.15), calls=%async_computation.2 | async-start | bytes 3670016 | tf_op jit(solution)/shard_map/all_to_all | solution.py:239
  77.9 43.6 %collective-permute-start.4 = (bf16[128,3584]{1,0:T(8,128)(2,1)S(1)}, bf16[128,3584]{1,0:T(8,128)(2,1)}, u32[]{:S(2)}, u32[]{:S(2)}) collective-permute-start(bf16[128,3584]{1,0:T(8,128)(2,1)S(1)} %convolution_convert_fusion.5), channel_id=1, source_target_pairs={{0,8},{1,9},{2,10},{3,11},{4,12},{5,13},{6,14},{7,15},{8,0},{9,1},... | collective-permute-start | bytes 2752520 | tf_op jit(solution)/shard_map/ppermute | solution.py:247
  78.0 46.5 %collective-permute-start.5 = (bf16[32,3584]{1,0:T(8,128)(2,1)}, bf16[32,3584]{1,0:T(8,128)(2,1)S(1)}, u32[]{:S(2)}, u32[]{:S(2)}) collective-permute-start(bf16[32,3584]{1,0:T(8,128)(2,1)} %get-tuple-element.61), channel_id=1, source_target_pairs={{0,1},{1,0},{2,3},{3,2},{4,5},{5,4},{6,7},{7,6},{8,9},{9,8},{10,11... | collective-permute-start | bytes 688136 | tf_op jit(solution)/shard_map/ppermute | solution.py:305
  78.6 45.9 %collective-permute-start.6 = (bf16[32,3584]{1,0:T(8,128)(2,1)}, bf16[32,3584]{1,0:T(8,128)(2,1)S(1)}, u32[]{:S(2)}, u32[]{:S(2)}) collective-permute-start(bf16[32,3584]{1,0:T(8,128)(2,1)} %get-tuple-element.62), channel_id=1, source_target_pairs={{0,2},{1,3},{2,0},{3,1},{4,6},{5,7},{6,4},{7,5},{8,10},{9,11},{10,... | collective-permute-start | bytes 688136 | tf_op jit(solution)/shard_map/ppermute | solution.py:305
  80.3 45.2 %collective-permute-start.7 = (bf16[32,3584]{1,0:T(8,128)(2,1)}, bf16[32,3584]{1,0:T(8,128)(2,1)}, u32[]{:S(2)}, u32[]{:S(2)}) collective-permute-start(bf16[32,3584]{1,0:T(8,128)(2,1)} %get-tuple-element.63), channel_id=1, source_target_pairs={{0,4},{1,5},{2,6},{3,7},{4,0},{5,1},{6,2},{7,3},{8,12},{9,13},{10,... | collective-permute-start | bytes 688136 | tf_op jit(solution)/shard_map/ppermute | solution.py:305
  124.5 2.8 copy-start.10
  124.5 2.8 copy-start.11
  127.3 50.5 %all-to-all-start.3 = ((bf16[8,32,3584]{2,1,0:T(8,128)(2,1)}), bf16[8,32,3584]{2,1,0:T(8,128)(2,1)S(1)}, u32[]{:S(2)}, u32[]{:S(2)}) async-start(bf16[8,32,3584]{2,1,0:T(8,128)(2,1)} %bitcast.30), calls=%async_computation.3 | async-start | bytes 3670016 | tf_op jit(solution)/shard_map/all_to_all | solution.py:239
  130.9 43.6 %collective-permute-start.8 = (bf16[128,3584]{1,0:T(8,128)(2,1)}, bf16[128,3584]{1,0:T(8,128)(2,1)S(1)}, u32[]{:S(2)}, u32[]{:S(2)}) collective-permute-start(bf16[128,3584]{1,0:T(8,128)(2,1)} %get-tuple-element.97), channel_id=1, source_target_pairs={{0,8},{1,9},{2,10},{3,11},{4,12},{5,13},{6,14},{7,15},{8,0},{9,1},... | collective-permute-start | bytes 2752520 | tf_op jit(solution)/shard_map/ppermute | solution.py:247
  131.0 46.8 %collective-permute-start.10 = (bf16[32,3584]{1,0:T(8,128)(2,1)}, bf16[32,3584]{1,0:T(8,128)(2,1)S(1)}, u32[]{:S(2)}, u32[]{:S(2)}) collective-permute-start(bf16[32,3584]{1,0:T(8,128)(2,1)} %get-tuple-element.66), channel_id=1, source_target_pairs={{0,5},{1,4},{2,7},{3,6},{4,1},{5,0},{6,3},{7,2},{8,13},{9,12},{10,... | collective-permute-start | bytes 688136 | tf_op jit(solution)/shard_map/ppermute | solution.py:305
  132.6 45.2 %collective-permute-start.9 = (bf16[32,3584]{1,0:T(8,128)(2,1)}, bf16[32,3584]{1,0:T(8,128)(2,1)S(1)}, u32[]{:S(2)}, u32[]{:S(2)}) collective-permute-start(bf16[32,3584]{1,0:T(8,128)(2,1)} %get-tuple-element.65), channel_id=1, source_target_pairs={{0,3},{1,2},{2,1},{3,0},{4,7},{5,6},{6,5},{7,4},{8,11},{9,10},{10,... | collective-permute-start | bytes 688136 | tf_op jit(solution)/shard_map/ppermute | solution.py:305
  177.8 3.8 %copy-start.12 = (bf16[32,3584]{1,0:T(8,128)(2,1)}, bf16[32,3584]{1,0:T(8,128)(2,1)S(1)}, u32[]{:S(2)}) copy-start(bf16[32,3584]{1,0:T(8,128)(2,1)S(1)} %collective-permute-done.10.refs_5_) | copy-start | bytes 688132
  177.8 3.8 %copy-start.13 = (bf16[32,3584]{1,0:T(8,128)(2,1)}, bf16[32,3584]{1,0:T(8,128)(2,1)S(1)}, u32[]{:S(2)}) copy-start(bf16[32,3584]{1,0:T(8,128)(2,1)S(1)} %collective-permute-done.9.refs_3_) | copy-start | bytes 688132
  177.9 3.8 %copy-start.2 = (bf16[8,32,3584]{2,1,0:T(8,128)(2,1)}, bf16[8,32,3584]{2,1,0:T(8,128)(2,1)S(1)}, u32[]{:S(2)}) copy-start(bf16[8,32,3584]{2,1,0:T(8,128)(2,1)S(1)} %all-to-all-done.3) | copy-start | bytes 5505028
  181.6 42.5 %copy-start.22 = (pred[2,256,128]{2,1,0:T(32,128)(4,1)S(1)}, pred[2,256,128]{2,1,0:T(32,128)(4,1)}, u32[]{:S(2)}) copy-start(pred[2,256,128]{2,1,0:T(32,128)(4,1)} %copy-done.21) | copy-start | bytes 196612
  181.6 70.8 %all-to-all-start.4 = ((bf16[8,32,3584]{2,1,0:T(8,128)(2,1)}), bf16[8,32,3584]{2,1,0:T(8,128)(2,1)}, u32[]{:S(2)}, u32[]{:S(2)}) async-start(bf16[8,32,3584]{2,1,0:T(8,128)(2,1)} %bitcast.32), calls=%async_computation.4 | async-start | bytes 3670016 | tf_op jit(solution)/shard_map/all_to_all | solution.py:239
  186.1 34.0 %collective-permute-start.11 = (bf16[32,3584]{1,0:T(8,128)(2,1)}, bf16[32,3584]{1,0:T(8,128)(2,1)S(1)}, u32[]{:S(2)}, u32[]{:S(2)}) collective-permute-start(bf16[32,3584]{1,0:T(8,128)(2,1)} %get-tuple-element.68), channel_id=1, source_target_pairs={{0,6},{1,7},{2,4},{3,5},{4,2},{5,3},{6,0},{7,1},{8,14},{9,15},{10,... | collective-permute-start | bytes 688136 | tf_op jit(solution)/shard_map/ppermute | solution.py:305
  188.9 35.1 %collective-permute-start.12 = (bf16[32,3584]{1,0:T(8,128)(2,1)}, bf16[32,3584]{1,0:T(8,128)(2,1)S(1)}, u32[]{:S(2)}, u32[]{:S(2)}) collective-permute-start(bf16[32,3584]{1,0:T(8,128)(2,1)} %get-tuple-element.69), channel_id=1, source_target_pairs={{0,7},{1,6},{2,5},{3,4},{4,3},{5,2},{6,1},{7,0},{8,15},{9,14},{10,... | collective-permute-start | bytes 688136 | tf_op jit(solution)/shard_map/ppermute | solution.py:305
  188.9 38.5 %collective-permute-start.13 = (bf16[32,3584]{1,0:T(8,128)(2,1)}, bf16[32,3584]{1,0:T(8,128)(2,1)S(1)}, u32[]{:S(2)}, u32[]{:S(2)}) collective-permute-start(bf16[32,3584]{1,0:T(8,128)(2,1)} %get-tuple-element.70), channel_id=1, source_target_pairs={{0,11},{1,10},{2,9},{3,8},{4,15},{5,14},{6,13},{7,12},{8,3},{9,2},... | collective-permute-start | bytes 688136 | tf_op jit(solution)/shard_map/ppermute | solution.py:305
  189.9 39.1 %collective-permute-start.14 = (bf16[32,3584]{1,0:T(8,128)(2,1)}, bf16[32,3584]{1,0:T(8,128)(2,1)S(1)}, u32[]{:S(2)}, u32[]{:S(2)}) collective-permute-start(bf16[32,3584]{1,0:T(8,128)(2,1)} %get-tuple-element.71), channel_id=1, source_target_pairs={{0,12},{1,13},{2,14},{3,15},{4,8},{5,9},{6,10},{7,11},{8,4},{9,5},... | collective-permute-start | bytes 688136 | tf_op jit(solution)/shard_map/ppermute | solution.py:305
  193.9 39.0 %collective-permute-start.15 = (bf16[32,3584]{1,0:T(8,128)(2,1)}, bf16[32,3584]{1,0:T(8,128)(2,1)S(1)}, u32[]{:S(2)}, u32[]{:S(2)}) collective-permute-start(bf16[32,3584]{1,0:T(8,128)(2,1)} %get-tuple-element.72), channel_id=1, source_target_pairs={{0,13},{1,12},{2,15},{3,14},{4,9},{5,8},{6,11},{7,10},{8,5},{9,4},... | collective-permute-start | bytes 688136 | tf_op jit(solution)/shard_map/ppermute | solution.py:305
  220.1 7.3 %copy-start.14 = (bf16[32,3584]{1,0:T(8,128)(2,1)}, bf16[32,3584]{1,0:T(8,128)(2,1)S(1)}, u32[]{:S(2)}) copy-start(bf16[32,3584]{1,0:T(8,128)(2,1)S(1)} %collective-permute-done.11.refs_6_) | copy-start | bytes 688132
  220.1 19.7 %collective-permute-start.16 = (bf16[32,3584]{1,0:T(8,128)(2,1)}, bf16[32,3584]{1,0:T(8,128)(2,1)S(1)}, u32[]{:S(2)}, u32[]{:S(2)}) collective-permute-start(bf16[32,3584]{1,0:T(8,128)(2,1)} %get-tuple-element.73), channel_id=1, source_target_pairs={{0,14},{1,15},{2,12},{3,13},{4,10},{5,11},{6,8},{7,9},{8,6},{9,7},... | collective-permute-start | bytes 688136 | tf_op jit(solution)/shard_map/ppermute | solution.py:305
  224.1 3.3 copy-start.15
  224.1 19.7 %collective-permute-start.17 = (bf16[32,3584]{1,0:T(8,128)(2,1)}, bf16[32,3584]{1,0:T(8,128)(2,1)S(1)}, u32[]{:S(2)}, u32[]{:S(2)}) collective-permute-start(bf16[32,3584]{1,0:T(8,128)(2,1)} %get-tuple-element.74), channel_id=1, source_target_pairs={{0,15},{1,14},{2,13},{3,12},{4,11},{5,10},{6,9},{7,8},{8,7},{9,6},... | collective-permute-start | bytes 688136 | tf_op jit(solution)/shard_map/ppermute | solution.py:305
  227.4 16.4 %copy-start.16 = (bf16[32,3584]{1,0:T(8,128)(2,1)}, bf16[32,3584]{1,0:T(8,128)(2,1)S(1)}, u32[]{:S(2)}) copy-start(bf16[32,3584]{1,0:T(8,128)(2,1)S(1)} %collective-permute-done.13.refs_11_) | copy-start | bytes 688132
  229.0 14.8 %copy-start.17 = (bf16[32,3584]{1,0:T(8,128)(2,1)}, bf16[32,3584]{1,0:T(8,128)(2,1)S(1)}, u32[]{:S(2)}) copy-start(bf16[32,3584]{1,0:T(8,128)(2,1)S(1)} %collective-permute-done.14.refs_12_) | copy-start | bytes 688132
  233.0 10.8 %copy-start.18 = (bf16[32,3584]{1,0:T(8,128)(2,1)}, bf16[32,3584]{1,0:T(8,128)(2,1)S(1)}, u32[]{:S(2)}) copy-start(bf16[32,3584]{1,0:T(8,128)(2,1)S(1)} %collective-permute-done.15.refs_13_) | copy-start | bytes 688132
  239.8 4.0 %copy-start.19 = (bf16[32,3584]{1,0:T(8,128)(2,1)}, bf16[32,3584]{1,0:T(8,128)(2,1)S(1)}, u32[]{:S(2)}) copy-start(bf16[32,3584]{1,0:T(8,128)(2,1)S(1)} %collective-permute-done.16.refs_14_) | copy-start | bytes 688132
  243.8 0.7 copy-start.20
  252.4 12.9 %copy-start.23 = (f32[1,3584]{1,0:T(1,128)S(1)}, f32[1,3584]{1,0:T(1,128)}, u32[]{:S(2)}) copy-start(f32[1,3584]{1,0:T(1,128)} %get-tuple-element.81) | copy-start | bytes 43012
  252.4 84.1 %all-to-all-start.5 = ((bf16[16,16,3584]{2,1,0:T(8,128)(2,1)}), bf16[16,16,3584]{2,1,0:T(8,128)(2,1)S(1)}, u32[]{:S(2)}, u32[]{:S(2)}) async-start(bf16[16,16,3584]{2,1,0:T(8,128)(2,1)} %bitcast.36), calls=%async_computation.5 | async-start | bytes 3670016 | tf_op jit(solution)/shard_map/all_to_all | solution.py:236
  265.3 44.6 %collective-permute-start.18 = (f32[2,3584]{1,0:T(2,128)S(1)}, f32[2,3584]{1,0:T(2,128)S(1)}, u32[]{:S(2)}, u32[]{:S(2)}) collective-permute-start(f32[2,3584]{1,0:T(2,128)S(1)} %pad_maximum_fusion.2), channel_id=1, source_target_pairs={{0,8},{1,9},{2,10},{3,11},{4,12},{5,13},{6,14},{7,15},{8,0},{9,1},... | collective-permute-start | bytes 86024 | tf_op jit(solution)/shard_map/ppermute | solution.py:382
  310.0 3.9 %collective-permute-start.19 = (f32[2,3584]{1,0:T(2,128)S(1)}, f32[2,3584]{1,0:T(2,128)S(1)}, u32[]{:S(2)}, u32[]{:S(2)}) collective-permute-start(f32[2,3584]{1,0:T(2,128)S(1)} %fusion.16), channel_id=1, source_target_pairs={{0,4},{1,5},{2,6},{3,7},{4,0},{5,1},{6,2},{7,3},{8,12},{9,13},{10,... | collective-permute-start | bytes 86024 | tf_op jit(solution)/shard_map/ppermute | solution.py:382
  314.0 3.9 %collective-permute-start.20 = (f32[2,3584]{1,0:T(2,128)S(1)}, f32[2,3584]{1,0:T(2,128)S(1)}, u32[]{:S(2)}, u32[]{:S(2)}) collective-permute-start(f32[2,3584]{1,0:T(2,128)S(1)} %fusion.30), channel_id=1, source_target_pairs={{0,2},{1,3},{2,0},{3,1},{4,6},{5,7},{6,4},{7,5},{8,10},{9,11},{10,... | collective-permute-start | bytes 86024 | tf_op jit(solution)/shard_map/ppermute | solution.py:382
  317.9 1.3 collective-permute-start.21
  336.5 1.3 copy-start.3

commit v9 on v8

v9 whole, which is shorter than its diff:
```python
import math

import jax
import jax.numpy as jnp
from jax import lax
from jax.experimental import pallas as pl
from jax.experimental.pallas import tpu as pltpu
from jax.sharding import PartitionSpec as P

BF = jnp.bfloat16
F32 = jnp.float32
ROWS = ((0,), (0,))
LAST = ((1,), (1,))
SMALL = pl.CostEstimate(flops=1, bytes_accessed=1, transcendentals=0)
PARAMS = pltpu.CompilerParams(vmem_limit_bytes=56 * 2**20)


def mm(a, b, dims=((1,), (0,))):
    return lax.dot_general(a, b, (dims, ((), ())), preferred_element_type=F32)


def column_block(width):
    return next((b for b in (896, 512, 256, 128) if width % b == 0), width)


def first_rows(routes, target, pre, groups, cap):
    layers, tokens, width = target.shape
    latents = pre.shape[2]
    slots = groups * cap
    step = column_block(width)

    def kernel(routes_ref, target_ref, pre_ref, out_ref, order_ref):
        at = lax.broadcasted_iota(jnp.int32, (tokens, tokens), 0)
        earlier = at < lax.broadcasted_iota(jnp.int32, (tokens, tokens), 1)
        slot = lax.broadcasted_iota(jnp.int32, (slots, tokens), 0)
        hot = []
        for l in range(layers):
            named = routes_ref[l : l + 1, :]
            other = jnp.broadcast_to(named.astype(F32), (tokens, tokens)).T
            same = earlier & (other == named.astype(F32))
            order = jnp.sum(same.astype(F32), axis=0, keepdims=True).astype(jnp.int32)
            order_ref[l : l + 1, :] = order
            hot.append((named * cap + order == slot).astype(F32).astype(BF))
        for i in range(width // step):
            cols = slice(i * step, (i + 1) * step)
            out_ref[:, cols] = mm(hot[0], target_ref[0, :, cols]).astype(BF)
        for l in range(layers):
            cols = slice(width + l * latents, width + (l + 1) * latents)
            out_ref[:, cols] = mm(hot[l], pre_ref[l]).astype(BF)

    whole = lambda shape: pl.BlockSpec(shape, lambda i: (0,) * len(shape))
    return pl.pallas_call(
        kernel,
        grid=(1,),
        in_specs=[
            whole((layers, tokens)),
            whole((1, tokens, width)),
            whole((layers, tokens, latents)),
        ],
        out_specs=[whole((slots, width + layers * latents)), whole((layers, tokens))],
        out_shape=[
            jax.ShapeDtypeStruct((slots, width + layers * latents), BF),
            jax.ShapeDtypeStruct((layers, tokens), jnp.int32),
        ],
        compiler_params=PARAMS,
        cost_estimate=SMALL,
    )(routes, target, pre)


def decoded_pieces(base, first, decoder, half, cap):
    _, latents, width = decoder.shape
    slots = first.shape[0]
    rows = half * cap
    step = column_block(width)

    def kernel(base_ref, pre_ref, dec1_ref, dec2_ref, far_ref, near_ref):
        for at, out_ref in enumerate((near_ref, far_ref)):
            begin = pl.multiple_of(base_ref[at], rows)
            for l, dec_ref in enumerate((dec1_ref, dec2_ref)):
                pre = pre_ref[pl.ds(begin, rows), l * latents : (l + 1) * latents]
                act = jnp.maximum(pre.astype(F32), 0).astype(BF)
                piece = mm(act, dec_ref[0]).astype(BF)
                for j in range(half):
                    place = (2 * j + l) * cap
                    out_ref[place : place + cap, :] = piece[j * cap : (j + 1) * cap]

    return pl.pallas_call(
        kernel,
        grid=(width // step,),
        in_specs=[
            pl.BlockSpec(memory_space=pltpu.SMEM),
            pl.BlockSpec((slots, 2 * latents), lambda i: (0, width // (2 * latents))),
            pl.BlockSpec((1, latents, step), lambda i: (1, 0, i)),
            pl.BlockSpec((1, latents, step), lambda i: (2, 0, i)),
        ],
        out_specs=[pl.BlockSpec((2 * rows, step), lambda i: (0, i))] * 2,
        out_shape=[jax.ShapeDtypeStruct((2 * rows, width), BF)] * 2,
        compiler_params=PARAMS,
        cost_estimate=SMALL,
    )(base, first, decoder, decoder)


def pack_rows(keys, rows, groups, cap):
    layers, tokens, width = rows.shape
    step = column_block(width)

    def kernel(keys_ref, rows_ref, *outs):
        slot = lax.broadcasted_iota(jnp.int32, (groups * cap, tokens), 0)
        for l in range(layers):
            hot = (keys_ref[l : l + 1, :] == slot).astype(F32).astype(BF)
            placed = mm(hot, rows_ref[l]).astype(BF)
            for k in range(groups):
                outs[k][l * cap : (l + 1) * cap, :] = placed[k * cap : (k + 1) * cap]

    return pl.pallas_call(
        kernel,
        grid=(width // step,),
        in_specs=[
            pl.BlockSpec((layers, tokens), lambda i: (0, 0)),
            pl.BlockSpec((layers, tokens, step), lambda i: (0, 0, i)),
        ],
        out_specs=[pl.BlockSpec((layers * cap, step), lambda i: (0, i))] * groups,
        out_shape=[jax.ShapeDtypeStruct((layers * cap, width), BF)] * groups,
        compiler_params=PARAMS,
        cost_estimate=SMALL,
    )(keys, rows)


def layer0_errors(first, act, decoder, bias, scale):
    slots, latents = act.shape
    layers, width = bias.shape
    step = column_block(width)

    def kernel(act_ref, dec_ref, bias_ref, target_ref, sum_ref, grad_ref, back_ref):
        piece = mm(act_ref[...], dec_ref[0]).astype(BF).astype(F32)
        error = (piece + bias_ref[0:1, :] - target_ref[...].astype(F32)) * scale
        error = error.astype(BF)
        sum_ref[...] = jnp.sum(error.astype(F32), axis=0, keepdims=True)
        grad_ref[...] = mm(act_ref[...], error, ROWS).astype(BF)

        @pl.when(pl.program_id(0) == 0)
        def _():
            back_ref[...] = jnp.zeros_like(back_ref)

        back_ref[...] += mm(error, dec_ref[0], LAST)

    return pl.pallas_call(
        kernel,
        grid=(width // step,),
        in_specs=[
            pl.BlockSpec((slots, latents), lambda i: (0, 0)),
            pl.BlockSpec((1, latents, step), lambda i: (0, 0, i)),
            pl.BlockSpec((layers, step), lambda i: (0, i)),
            pl.BlockSpec((slots, step), lambda i: (0, i)),
        ],
        out_specs=[
            pl.BlockSpec((1, step), lambda i: (0, i)),
            pl.BlockSpec((latents, step), lambda i: (0, i)),
            pl.BlockSpec((slots, latents), lambda i: (0, 0)),
        ],
        out_shape=[
            jax.ShapeDtypeStruct((1, width), F32),
            jax.ShapeDtypeStruct((latents, width), BF),
            jax.ShapeDtypeStruct((slots, latents), F32),
        ],
        compiler_params=PARAMS,
        cost_estimate=SMALL,
    )(act, decoder, bias, first)


def gradients(me, errors, wide, decoder, pres, own, dec0, cap):
    devices = pres.shape[0]
    half = devices // 2
    pairs, latents, width = decoder.shape
    slots = devices * cap
    step = 2 * column_block(width)
    step = step if width % step == 0 else width
    steps = width // step

    def kernel(me_ref, eo_ref, em_ref, wo_ref, wm_ref, dec1_ref, dec2_ref, pre_ref, own_ref, dec0_ref, dec_ref, low_ref, bias_ref, back):
        at = pl.program_id(0)
        grad = mm(wo_ref[...], eo_ref[...], ROWS) + mm(wm_ref[...], em_ref[...], ROWS)
        dec_ref[0] = dec0_ref[...]
        dec_ref[1] = grad[:latents].astype(BF)
        dec_ref[2] = grad[latents:].astype(BF)

        @pl.when(at == 0)
        def _():
            back[...] = jnp.zeros_like(back)

        both = jnp.concatenate([dec1_ref[0], dec2_ref[0]], axis=0)
        back[0] += mm(eo_ref[...], both, LAST)
        back[1] += mm(em_ref[...], both, LAST)

        @pl.when(at == steps - 1)
        def _():
            my = me_ref[0]
            sums = [jnp.zeros((1, latents), F32) for _ in range(2)]
            for k in range(devices):
                group = (my ^ k) % half
                sender = my ^ k
                for l in range(2):
                    at_row = pl.multiple_of(group * 2 * cap + l * cap, cap)
                    part = back[k // half, pl.ds(at_row, cap), l * latents : (l + 1) * latents]
                    if l == 0:
                        part = part + own_ref[pl.ds(pl.multiple_of(sender * cap, cap), cap), :]
                    pre = pre_ref[(k // half) * half + group, l * cap : (l + 1) * cap, :]
                    part = jnp.where(pre.astype(F32) > 0, part, 0.0)
                    sums[l] = sums[l] + jnp.sum(part, axis=0, keepdims=True)
                    low_ref[l, k * cap : (k + 1) * cap, :] = part.astype(BF)
            for l in range(2):
                bias_ref[l : l + 1, :] = sums[l]

    whole = lambda shape: pl.BlockSpec(shape, lambda i: (0,) * len(shape))
    return pl.pallas_call(
        kernel,
        grid=(steps,),
        in_specs=[pl.BlockSpec(memory_space=pltpu.SMEM)]
        + [pl.BlockSpec((half * 2 * cap, step), lambda i: (0, i))] * 2
        + [whole((half * 2 * cap, 2 * latents))] * 2
        + [
            pl.BlockSpec((1, latents, step), lambda i: (1, 0, i)),
            pl.BlockSpec((1, latents, step), lambda i: (2, 0, i)),
            whole((devices, 2 * cap, latents)),
            whole((slots, latents)),
            pl.BlockSpec((latents, step), lambda i: (0, i)),
        ],
        out_specs=[
            pl.BlockSpec((pairs, latents, step), lambda i: (0, 0, i)),
            whole((2, slots, latents)),
            whole((2, latents)),
        ],
        out_shape=[
            jax.ShapeDtypeStruct((pairs, latents, width), BF),
            jax.ShapeDtypeStruct((2, slots, latents), BF),
            jax.ShapeDtypeStruct((2, latents), F32),
        ],
        scratch_shapes=[pltpu.VMEM((2, half * 2 * cap, 2 * latents), F32)],
        compiler_params=PARAMS,
        cost_estimate=SMALL,
    )(me, *errors, *wide, decoder, decoder, pres, own, dec0)


def encoder_products(resid, low, cap):
    devices = len(resid)
    _, slots, latents = low.shape
    width = resid[0].shape[1]
    step = column_block(width)

    def kernel(low_ref, *refs):
        rows, enc_ref, all_rows = refs[:devices], refs[devices], refs[devices + 1]
        for l in range(2):
            for k in range(devices):
                all_rows[l, k * cap : (k + 1) * cap, :] = rows[k][l * cap : (l + 1) * cap, :]
            enc_ref[l] = mm(all_rows[l], low_ref[l], ROWS).astype(BF)

    return pl.pallas_call(
        kernel,
        grid=(width // step,),
        in_specs=[pl.BlockSpec((2, slots, latents), lambda i: (0, 0, 0))]
        + [pl.BlockSpec((2 * cap, step), lambda i: (0, i))] * devices,
        out_specs=pl.BlockSpec((2, step, latents), lambda i: (0, i, 0)),
        out_shape=jax.ShapeDtypeStruct((2, width, latents), BF),
        scratch_shapes=[pltpu.VMEM((2, slots, step), BF)],
        compiler_params=PARAMS,
        cost_estimate=SMALL,
    )(low, *resid)


def per_device(residual, mlp_target, pre_acts, blocks, decoder, decoder_bias):
    devices = lax.axis_size("layer")
    layers, tokens, width = residual.shape
    latents = pre_acts.shape[3]
    cap = max(2, 2 * tokens // devices)
    slots = devices * cap
    half = devices // 2
    scale = 1.0 / math.sqrt(tokens)
    me = lax.axis_index("layer")
    upper = me >= half
    mirror = [(i, (i + half) % devices) for i in range(devices)]
    halves = [list(range(half)), list(range(half, devices))]

    def everyone(x):
        return lax.all_to_all(x, "layer", split_axis=0, concat_axis=0, tiled=True)

    def within(x):
        return lax.all_to_all(
            x, "layer", split_axis=0, concat_axis=0, tiled=True, axis_index_groups=halves
        )

    def after(x, done):
        return lax.optimization_barrier((x, done))[0]

    def across(x):
        return lax.ppermute(x, "layer", mirror)

    def turn(x):
        first, second = x[: x.shape[0] // 2], x[x.shape[0] // 2 :]
        return jnp.concatenate(
            [jnp.where(upper, second, first), jnp.where(upper, first, second)], axis=0
        )

    routes = blocks.reshape(layers, tokens)
    pre = pre_acts.reshape(layers, tokens, latents)
    direct = devices == 16 and cap % 16 == 0
    if direct:
        first, order = first_rows(routes, mlp_target, pre, devices, cap)
    else:
        earlier = jnp.arange(tokens)[:, None] > jnp.arange(tokens)[None, :]
        same = routes[:, :, None] == routes[:, None, :]
        order = jnp.sum((same & earlier).astype(jnp.int32), axis=2)
        slot_of = (routes * cap + order)[:, None, :]
        place = (slot_of == jnp.arange(slots, dtype=jnp.int32)[None, :, None]).astype(BF)
        first = jnp.concatenate(
            [
                mm(place[0], mlp_target[0]).astype(BF),
                mm(place[0], pre[0]).astype(BF),
                mm(place[1], pre[1]).astype(BF),
            ],
            axis=1,
        )
    routes_m, order_m = across(jnp.stack([routes, order]))

    def pair_places(named, order, base):
        block = base + jnp.arange(half, dtype=jnp.int32)[:, None, None, None]
        slot = jnp.arange(cap, dtype=jnp.int32)[None, None, :, None]
        hit = (named[None, :, None, :] == block) & (order[None, :, None, :] == slot)
        return hit.astype(BF).reshape(half, layers, cap, tokens)

    base = jnp.where(upper, half, 0).astype(jnp.int32)
    place_o = pair_places(routes, order, base)
    place_m = pair_places(routes_m, order_m, base)

    def flat(p):
        return p.reshape(-1, p.shape[-1])

    first = everyone(first.reshape(devices, cap, -1)).reshape(slots, -1)
    pre0 = first[:, width : width + latents]
    pre1 = first[:, width + latents :]
    act0 = jnp.maximum(pre0, 0)
    got_pre = jnp.stack(
        [pre0.reshape(devices, cap, latents), pre1.reshape(devices, cap, latents)], axis=1
    )

    later = half + half // 2
    windows = [
        list(range(1, half - 2)),
        list(range(half, later)),
        [half - 2],
        [half - 1],
        list(range(later, devices)),
    ]
    arrivals = [None] * devices
    if direct:
        packed = pack_rows((routes ^ me) * cap + order, residual, devices, cap)
        arrivals[0] = packed[0]

    def depart(window, begin):
        if not direct:
            return
        rows = [packed[k] for k in windows[window]]
        if begin is not None:
            rows = after(rows, begin)
        for k, x in zip(windows[window], rows):
            arrivals[k] = lax.ppermute(x, "layer", [(i, i ^ k) for i in range(devices)])

    def arrived(window):
        return [arrivals[k] for k in windows[window]] if direct else []

    acts = turn(jnp.maximum(got_pre, 0))
    nothing = jnp.zeros((devices, 1, cap, latents), BF)
    wide = jnp.concatenate(
        [
            jnp.concatenate([acts[:, 0:1], nothing], axis=3),
            jnp.concatenate([nothing, acts[:, 1:2]], axis=3),
        ],
        axis=1,
    ).reshape(devices, layers * cap, 2 * latents)
    dec1 = decoder[1:3].reshape(2 * latents, width)

    def decode(rows):
        return mm(rows.reshape(-1, 2 * latents), dec1).astype(BF).reshape(half, -1, width)

    depart(0, None)
    depart(1, got_pre)
    if direct:
        bases = jnp.stack([base * cap, (half - base) * cap]).astype(jnp.int32)
        pieces_m, pieces_o = (
            x.reshape(half, -1, width) for x in decoded_pieces(bases, first, decoder, half, cap)
        )
    else:
        pieces_m, pieces_o = decode(wide[half:]), decode(wide[:half])
    pieces_m = within(after(pieces_m, (arrived(0), routes_m))).reshape(-1, width)
    sum_m = mm(flat(place_m), pieces_m, ROWS).astype(BF)
    sum_low = across(sum_m)
    depart(2, sum_m)
    pieces_o = within(after(pieces_o, (sum_m, arrived(1)))).reshape(-1, width)
    sum0, dec0, own = layer0_errors(
        after(first, sum_m), act0, decoder, decoder_bias, scale
    )
    empty0 = (decoder_bias[0] * scale).astype(BF).astype(F32)
    empties = float(slots * devices - tokens * devices)

    pieces_o = after(pieces_o, sum0)
    sum_o = mm(flat(place_o), pieces_o, ROWS) + decoder_bias[1] - mlp_target[1].astype(F32)
    sum_o = lax.optimization_barrier(sum_o.astype(BF))
    head = 16 if direct else tokens // 2
    sum_high_head = across(sum_o[:head])
    depart(3, sum_o)

    def add_halves(a, b):
        return ((a.astype(F32) + b.astype(F32)) * scale).astype(BF)

    def sent(x, step):
        return lax.ppermute(x, "layer", [(i, i ^ step) for i in range(devices)])

    error1 = add_halves(sum_o, sum_low)
    sums = jnp.concatenate([sum0, jnp.sum(error1.astype(F32), axis=0, keepdims=True)])
    sent_o = mm(flat(place_o), error1).astype(BF).reshape(half, layers * cap, width)
    sent_o, rest = after((sent_o, sum_o[head:]), (sum_high_head, arrived(2)))
    errors_o = within(sent_o).reshape(-1, width)
    sum_high = jnp.concatenate([sum_high_head, across(rest)])
    sums = after(sums, errors_o)
    step = devices // 2
    while step > 2:
        if direct and step == 8:
            sums = (sums + sent(sums, 4)) + (sent(sums, 8) + sent(sums, 12))
            step = 2
        else:
            sums = sums + sent(sums, step)
            step //= 2
    error1_m = after(add_halves(sum_m, sum_high), (errors_o, arrived(3)))
    sent_errors = mm(flat(place_m), error1_m).astype(BF).reshape(half, layers * cap, width)
    sent_errors = after(sent_errors, sums)
    depart(4, sent_errors)
    errors_m = within(sent_errors).reshape(-1, width)
    if devices > 1:
        sums = sums + sent(after(sums, sent_errors), 1)
    errors_m = after(errors_m, sums)
    if devices > 2:
        sums = sums + sent(sums, 2)
    bias_grad = sums - jnp.stack([empties * empty0, jnp.zeros_like(empty0)])

    wide_o = wide[:half].reshape(-1, 2 * latents)
    wide_m = wide[half:].reshape(-1, 2 * latents)
    if direct:
        pres = turn(got_pre).reshape(devices, layers * cap, latents)
        dec, low, enc_bias = gradients(
            me.astype(jnp.int32).reshape(1),
            (errors_o, errors_m),
            (wide_o, wide_m),
            decoder,
            pres,
            own,
            dec0,
            cap,
        )
        enc = encoder_products(after(arrivals, low), low, cap)
    else:
        resid = everyone(
            jnp.stack(
                [
                    mm(place[l], residual[l]).astype(BF).reshape(devices, cap, width)
                    for l in range(layers)
                ],
                axis=1,
            ).reshape(devices, layers * cap, width)
        ).reshape(devices, layers, cap, width)
        dec_later = mm(wide_o, errors_o, ROWS) + mm(wide_m, errors_m, ROWS)
        dec = jnp.concatenate([dec0[None], dec_later.astype(BF).reshape(2, latents, width)])
        back = jnp.concatenate([mm(errors_o, dec1, LAST), mm(errors_m, dec1, LAST)], axis=0)
        back = turn(back.reshape(devices, layers, cap, 2 * latents))
        own = own.reshape(devices, cap, latents)
        grads = jnp.stack([back[:, 0, :, :latents] + own, back[:, 1, :, latents:]])
        grads = jnp.where(jnp.swapaxes(got_pre, 0, 1) > 0, grads, 0.0)
        grads = grads.reshape(layers, slots, latents)
        enc_bias = jnp.sum(grads, axis=1)
        resid = jnp.swapaxes(resid, 0, 1).reshape(layers, slots, width)
        enc = jnp.stack([mm(resid[l], grads[l].astype(BF), ROWS).astype(BF) for l in range(layers)])
    return dec, enc, enc_bias, bias_grad


def solution(mesh):
    return jax.shard_map(
        per_device,
        mesh=mesh,
        in_specs=(
            P(None, ("grp", "layer"), None),
            P(None, ("grp", "layer"), None),
            P(None, ("grp", "layer"), None, None),
            P(None, ("grp", "layer"), None),
            P(None, "layer", None),
            P(),
        ),
        out_specs=(
            P("grp", "layer", None),
            P("grp", None, "layer"),
            P("grp", "layer"),
            P("grp", None),
        ),
        check_vma=False,
    )
```

time: 346 us -> 282 us (0.82)
  waiting for transfers between devices: 205 us -> 165 us
  matrix products: 19.3 us -> 8.7 us
  Pallas kernels: 35 us -> 29.9 us
  starting transfers between devices: 66.4 us -> 62.1 us
    all_to_all x4, waiting for transfers between devices: 0.01 us -> 69.6 us  [within(): lax.all_to_all(x, 'layer', split_axis=0, concat_axis=0, tiled=True, axis_...]
    ppermute x3 -> x4, waiting for transfers between devices: 108 us -> 48.3 us  [across(): return lax.ppermute(x, 'layer', mirror)]
    ppermute x15, waiting for transfers between devices: 48.3 us -> 5.79 us  [depart(): arrivals[k] = lax.ppermute(x, 'layer', [(i, i ^ k) for i in range(devices)])]
    ppermute x4 -> x5, waiting for transfers between devices: 48.4 us -> 12.2 us  [sent(): return lax.ppermute(x, 'layer', [(i, i ^ step) for i in range(devices)])]
    all_to_all x2 -> x1, waiting for transfers between devices: 0.01 us -> 29.1 us  [everyone(): return lax.all_to_all(x, 'layer', split_axis=0, concat_axis=0, tiled=True)]
    all_to_all x2 -> x1, starting transfers between devices: 20.3 us -> 7.48 us  [everyone(): return lax.all_to_all(x, 'layer', split_axis=0, concat_axis=0, tiled=True)]
    dot_general x9 -> x4, matrix products: 19.3 us -> 8.7 us  [mm(): return lax.dot_general(a, b, (dims, ((), ())), preferred_element_type=F32)]
    pallas_call x3 -> x4, Pallas kernels: 18.2 us -> 17.7 us  [the longest x1 4.98 us: encoder_products(): pl.pallas_call(kernel, grid=(width // step,), in_specs=[pl.BlockSpec((2,...]
  transfers between devices with their start and end apart: 28 -> 29, of which waited for: 15 -> 15; matrix products, arithmetic and copies ran while one was open for 6% -> 6% of each run, Pallas kernels for 9% -> 8%
where the time goes in v9:
time: 282 us; the launch traced here: 281 us
  waiting for transfers between devices  165 us (59%)
  starting transfers between devices  62.1 us (22%)
  Pallas kernels  29.9 us (11%)
  matrix products  8.7 us (3%)
  other arithmetic  8.54 us (3%)
  local copies, waits for them, and re-layouts  5.28 us (2%)
    all_to_all x4, waiting for transfers between devices, within(): lax.all_to_all(x, 'layer', split_axis=0, concat_axis=0, tiled=True, axis_...  69.6 us
    ppermute x4, waiting for transfers between devices, across(): return lax.ppermute(x, 'layer', mirror)  48.3 us
    all_to_all x1, waiting for transfers between devices, everyone(): return lax.all_to_all(x, 'layer', split_axis=0, concat_axis=0, tiled=True)  29.1 us
    ppermute x15, starting transfers between devices, depart(): arrivals[k] = lax.ppermute(x, 'layer', [(i, i ^ k) for i in range(devices)])  23.4 us
    all_to_all x4, starting transfers between devices, within(): lax.all_to_all(x, 'layer', split_axis=0, concat_axis=0, tiled=True, axis_...  21.4 us
    ppermute x5, waiting for transfers between devices, sent(): return lax.ppermute(x, 'layer', [(i, i ^ step) for i in range(devices)])  12.2 us
    dot_general x4, matrix products, mm(): return lax.dot_general(a, b, (dims, ((), ())), preferred_element_type=F32)  8.7 us
    all_to_all x1, starting transfers between devices, everyone(): return lax.all_to_all(x, 'layer', split_axis=0, concat_axis=0, tiled=True)  7.48 us
  transfers between devices with their start and end apart: 29, of which 15 were waited for; matrix products, arithmetic and copies ran while one was open for 6% of the time, Pallas kernels for 8%

profile of v9, /device:TPU:0, one launch (start us, length us, event | category | flops | bytes accessed | tf_op | source)
XLA Modules:
  0.0 280.6 jit_solution(12320659119621752212)
XLA Ops:
  0.6 3.2 %shard_map.93 = (bf16[256,3840]{1,0:T(8,128)(2,1)}, s32[2,128]{1,0:T(2,128)}) custom-call(s32[2,128]{1,0:T(2,128)} %bitcast.63, bf16[2,128,3584]{2,1,0:T(8,128)(2,1)} %target_ref.1, bf16[2,128,128]{2,1,0:T(8,128)(2,1)} %bitcast.62), custom_call_target="tpu_custom_call" | custom-call | flops 1 | bytes 1 | tf_op jit(solution)/shard_map/pallas_call | solution.py:52
  3.8 7.5 %all-to-all-start = ((bf16[16,16,3840]{2,1,0:T(8,128)(2,1)}), bf16[16,16,3840]{2,1,0:T(8,128)(2,1)S(1)}, u32[]{:S(2)}, u32[]{:S(2)}) async-start(bf16[16,16,3840]{2,1,0:T(8,128)(2,1)} %bitcast.48), calls=%async_computation | async-start | bytes 3932160 | tf_op jit(solution)/shard_map/all_to_all | solution.py:284
  11.4 0.6 multiply_add_fusion.keys_ref
  11.9 4.8 %shard_map.95 = (bf16[32,3584]{1,0:T(8,128)(2,1)}, bf16[32,3584]{1,0:T(8,128)(2,1)}, bf16[32,3584]{1,0:T(8,128)(2,1)}, bf16[32,3584]{1,0:T(8,128)(2,1)}, bf16[32...) custom-call(s32[2,128]{1,0:T(2,128)} %multiply_add_fusion.keys_ref, ...), custom_call_target="tpu_custom_call" | custom-call | flops 1 | bytes 1 | tf_op jit(solution)/shard_map/pallas_call | solution.py:115
  16.7 0.5 collective-permute-start.1
  17.2 1.7 collective-permute-start.2
  18.9 1.7 collective-permute-start.4
  20.7 0.6 pad_add_fusion.1.base_ref
  21.3 29.1 %all-to-all-done = bf16[16,16,3840]{2,1,0:T(8,128)(2,1)S(1)} async-done(((bf16[16,16,3840]{2,1,0:T(8,128)(2,1)}), bf16[16,16,3840]{2,1,0:T(8,128)(2,1)S(1)}, u32[]{:S(2)}, u32[]{:S(2)}) %all-to-all-start) | async-done | bytes 1966112 | tf_op jit(solution)/shard_map/all_to_all | solution.py:284
  50.4 1.3 copy-done
  51.6 4.7 %shard_map.94 = (bf16[256,3584]{1,0:T(8,128)(2,1)}, bf16[256,3584]{1,0:T(8,128)(2,1)}) custom-call(s32[2]{0:T(128)} %pad_add_fusion.1.base_ref, bf16[256,3840]{1,0:T(8,128)(2,1)} %bitcast.42, bf16[3,128,3584]{2,1,0:T(8,128)(2,1)} %dec2_ref.3, bf16[3,128,3584]{2,1,0:T(8,128)(2,1)} %dec2_ref.3), custom_call_target="tpu_custom_call" | custom-call | flops 1 | bytes 1 | tf_op jit(solution)/shard_map/pallas_call | solution.py:87
  56.4 0.6 copy-done.5
  57.4 9.7 %all-to-all-start.1 = ((bf16[8,32,3584]{2,1,0:T(8,128)(2,1)}), bf16[8,32,3584]{2,1,0:T(8,128)(2,1)S(1)}, u32[]{:S(2)}, u32[]{:S(2)}) async-start(bf16[8,32,3584]{2,1,0:T(8,128)(2,1)} %bitcast.50), calls=%async_computation.1 | async-start | bytes 3670016 | tf_op jit(solution)/shard_map/all_to_all | solution.py:287
  67.1 2.7 collective-permute-start
  69.7 0.3 collective-permute-start.6
  70.1 2.0 collective-permute-start.7
  72.0 1.9 collective-permute-start.8
  74.0 2.0 collective-permute-start.9
  75.9 12.2 %collective-permute-done = s32[2,2,128]{2,1,0:T(2,128)S(1)} collective-permute-done((s32[2,2,128]{2,1,0:T(2,128)S(1)}, s32[2,2,128]{2,1,0:T(2,128)S(1)}, u32[]{:S(2)}, u32[]{:S(2)}) %collective-permute-start) | collective-permute-done | bytes 2080 | tf_op jit(solution)/shard_map/ppermute | solution.py:295
  88.3 20.2 %all-to-all-done.1 = bf16[8,32,3584]{2,1,0:T(8,128)(2,1)S(1)} async-done(((bf16[8,32,3584]{2,1,0:T(8,128)(2,1)}), bf16[8,32,3584]{2,1,0:T(8,128)(2,1)S(1)}, u32[]{:S(2)}, u32[]{:S(2)}) %all-to-all-start.1) | async-done | bytes 1835040 | tf_op jit(solution)/shard_map/all_to_all | solution.py:287
  108.5 1.4 convolution_convert_fusion.2
  109.9 3.1 %collective-permute-done.9.refs_11_ = bf16[32,3584]{1,0:T(8,128)(2,1)S(1)} collective-permute-done((bf16[32,3584]{1,0:T(8,128)(2,1)S(1)}, bf16[32,3584]{1,0:T(8,128)(2,1)S(1)}, u32[]{:S(2)}, u32[]{:S(2)}) %collective-permute-start.9) | collective-permute-done | bytes 229408 | tf_op jit(solution)/shard_map/ppermute | solution.py:365
  113.0 0.7 copy-done.13
  113.6 3.6 %all-to-all-start.2 = ((bf16[8,32,3584]{2,1,0:T(8,128)(2,1)}), bf16[8,32,3584]{2,1,0:T(8,128)(2,1)S(1)}, u32[]{:S(2)}, u32[]{:S(2)}) async-start(bf16[8,32,3584]{2,1,0:T(8,128)(2,1)} %bitcast.49), calls=%async_computation.2 | async-start | bytes 3670016 | tf_op jit(solution)/shard_map/all_to_all | solution.py:287
  117.3 0.6 convert_multiply_fusion
  117.9 1.6 fusion.11
  119.5 2.9 %collective-permute-start.12 = (bf16[32,3584]{1,0:T(8,128)(2,1)}, bf16[32,3584]{1,0:T(8,128)(2,1)}, u32[]{:S(2)}, u32[]{:S(2)}) collective-permute-start(bf16[32,3584]{1,0:T(8,128)(2,1)} %get-tuple-element.90), channel_id=1, source_target_pairs={{0,6},{1,7},{2,4},{3,5},{4,2},{5,3},{6,0},{7,1},{8,14},{9,15},{10,... | collective-permute-start | bytes 688136 | tf_op jit(solution)/shard_map/ppermute | solution.py:365
  122.4 5.8 %shard_map.96 = (f32[1,3584]{1,0:T(1,128)}, bf16[128,3584]{1,0:T(8,128)(2,1)}, f32[256,128]{1,0:T(8,128)}) custom-call(bf16[256,128]{1,0:T(8,128)(2,1)} %get-tuple-element.131.act_ref, bf16[3,128,3584]{2,1,0:T(8,128)(2,1)} %dec2_ref.3, f32[2,3584]{1,0:T(2,128)} %bias_ref.1, bf16[256,3840]{1,0:T(8,128)(2,1)} %bitcast.44), custom_call_target="tpu_custom_call" | custom-call | flops 1 | bytes 1 | tf_op jit(solution)/shard_map/pallas_call | solution.py:147
  128.2 30.0 %all-to-all-done.2 = bf16[8,32,3584]{2,1,0:T(8,128)(2,1)S(1)} async-done(((bf16[8,32,3584]{2,1,0:T(8,128)(2,1)}), bf16[8,32,3584]{2,1,0:T(8,128)(2,1)S(1)}, u32[]{:S(2)}, u32[]{:S(2)}) %all-to-all-start.2) | async-done | bytes 1835040 | tf_op jit(solution)/shard_map/all_to_all | solution.py:287
  158.2 1.6 fusion.1
  160.0 2.0 collective-permute-done.10
  162.0 3.1 %convolution_convert_fusion.1 = bf16[256,3584]{1,0:T(8,128)(2,1)} fusion(pred[256,128]{1,0:T(8,128)(4,1)S(1)} %bitcast.61, bf16[128,3584]{1,0:T(8,128)(2,1)} %collective-permute-done.10, bf16[128,3584]{1,0:T(8,128)(2,1)S(1)} %fusion.1), kind=kOutput, calls=%fused_computation.1 | convolution fusion | flops 238092288 | bytes 3702784 | tf_op jit(solution)/shard_map/dot_general | solution.py:19
  165.1 2.1 collective-permute-done.12.refs_6_
  167.2 0.9 collective-permute-done.11
  168.1 0.6 copy-done.19
  168.8 3.6 %all-to-all-start.3 = ((bf16[8,32,3584]{2,1,0:T(8,128)(2,1)}), bf16[8,32,3584]{2,1,0:T(8,128)(2,1)S(1)}, u32[]{:S(2)}, u32[]{:S(2)}) async-start(bf16[8,32,3584]{2,1,0:T(8,128)(2,1)} %bitcast.22), calls=%async_computation.3 | async-start | bytes 3670016 | tf_op jit(solution)/shard_map/all_to_all | solution.py:287
  172.4 0.4 collective-permute-start.13
  172.8 1.5 convert_reduce_fusion
  174.3 2.3 collective-permute-start.14
  176.7 0.6 pad_maximum_fusion.2
  177.3 33.2 %collective-permute-done.13 = bf16[112,3584]{1,0:T(8,128)(2,1)S(1)} collective-permute-done((bf16[112,3584]{1,0:T(8,128)(2,1)S(1)}, bf16[112,3584]{1,0:T(8,128)(2,1)S(1)}, u32[]{:S(2)}, u32[]{:S(2)}) %collective-permute-start.13) | collective-permute-done | bytes 802848 | tf_op jit(solution)/shard_map/ppermute | solution.py:295
  210.5 1.5 multiply_convert_fusion
  212.0 0.9 all-to-all-done.3
  212.8 1.9 collective-permute-start.15
  214.7 0.8 collective-permute-start.16
  215.5 1.7 collective-permute-start.17
  217.2 0.6 collective-permute-done.14.refs_7_
  217.8 2.6 convolution_convert_fusion
  220.4 0.8 collective-permute-done.17
  221.3 4.5 %all-to-all-start.4 = ((bf16[8,32,3584]{2,1,0:T(8,128)(2,1)}), bf16[8,32,3584]{2,1,0:T(8,128)(2,1)}, u32[]{:S(2)}, u32[]{:S(2)}) async-start(bf16[8,32,3584]{2,1,0:T(8,128)(2,1)} %bitcast.24), calls=%async_computation.4 | async-start | bytes 3670016 | tf_op jit(solution)/shard_map/all_to_all | solution.py:287
  225.9 0.4 collective-permute-start.18
  226.4 0.7 fusion.12
  227.2 1.9 collective-permute-start.23
  229.2 0.7 pad_maximum_fusion.1
  229.8 1.3 collective-permute-start.19
  231.2 1.7 collective-permute-start.20
  232.9 1.3 collective-permute-start.21
  234.2 3.7 %collective-permute-start.22 = (bf16[32,3584]{1,0:T(8,128)(2,1)S(1)}, bf16[32,3584]{1,0:T(8,128)(2,1)S(1)}, u32[]{:S(2)}, u32[]{:S(2)}) collective-permute-start(bf16[32,3584]{1,0:T(8,128)(2,1)S(1)} %copy-done.26), channel_id=1, source_target_pairs={{0,15},{1,14},{2,13},{3,12},{4,11},{5,10},{6,9},{7,8},{8,7},{9,6},... | collective-permute-start | bytes 688136 | tf_op jit(solution)/shard_map/ppermute | solution.py:365
  237.8 11.3 %collective-permute-done.23 = f32[2,3584]{1,0:T(2,128)S(1)} collective-permute-done((f32[2,3584]{1,0:T(2,128)S(1)}, f32[2,3584]{1,0:T(2,128)S(1)}, u32[]{:S(2)}, u32[]{:S(2)}) %collective-permute-start.23) | collective-permute-done | bytes 28704 | tf_op jit(solution)/shard_map/ppermute | solution.py:415
  249.1 0.6 pad_subtract_fusion
  249.8 18.5 %all-to-all-done.4 = bf16[8,32,3584]{2,1,0:T(8,128)(2,1)} async-done(((bf16[8,32,3584]{2,1,0:T(8,128)(2,1)}), bf16[8,32,3584]{2,1,0:T(8,128)(2,1)}, u32[]{:S(2)}, u32[]{:S(2)}) %all-to-all-start.4) | async-done | bytes 1835040 | tf_op jit(solution)/shard_map/all_to_all | solution.py:287
  268.3 6.4 %shard_map.97 = (bf16[3,128,3584]{2,1,0:T(8,128)(2,1)}, bf16[2,256,128]{2,1,0:T(8,128)(2,1)}, f32[2,128]{1,0:T(2,128)}) custom-call(s32[1]{0:T(128)} %bitcast.me_ref, bf16[256,3584]{1,0:T(8,128)(2,1)} %bitcast.47, bf16[256,3584]{1,0:T(8,128)(2,1)} %bitcast.25.em_ref, bf16[256,256]{1,0:T(8,128)(2,1)} %bitcast.57, bf16[256,256]{1,0:T(8,128)(2,1)} %bitcast.56, ...), custom_call_target="tpu_custom_call" | custom-call | flops 1 | bytes 1 | tf_op jit(solution)/shard_map/pallas_call | solution.py:215
  274.8 0.6 copy-done.14
  275.7 5.0 %shard_map.98 = bf16[2,3584,128]{2,1,0:T(8,128)(2,1)} custom-call(bf16[2,256,128]{2,1,0:T(8,128)(2,1)} %get-tuple-element.103.low_ref, bf16[32,3584]{1,0:T(8,128)(2,1)} %get-tuple-element.113.refs_0_, bf16[32,3584]{1,0:T(8,128)(2,1)} %copy-done.5, bf16[32,3584]{1,0:T(8,128)(2,1)} %copy-done.6, bf16[32,3584]{1,0:T(8,128)(2,1)} %copy-done.7, ...), custom_call_target="tpu_custom_call" | custom-call | flops 1 | bytes 1 | tf_op jit(solution)/shard_map/pallas_call | solution.py:257
  (94 shorter events, 1.4 us)
Async XLA Ops:
  3.8 7.5 %copy-start.23 = (s32[2,128,1]{1,2,0:T(1,128)S(1)}, s32[2,128,1]{1,2,0:T(1,128)}, u32[]{:S(2)}) copy-start(s32[2,128,1]{1,2,0:T(1,128)} %param.9) | copy-start | bytes 3076
  3.8 7.5 %copy-start.25 = (s32[2,128]{1,0:T(2,128)S(1)}, s32[2,128]{1,0:T(2,128)}, u32[]{:S(2)}) copy-start(s32[2,128]{1,0:T(2,128)} %get-tuple-element.67) | copy-start | bytes 3076
  3.8 46.5 %all-to-all-start = ((bf16[16,16,3840]{2,1,0:T(8,128)(2,1)}), bf16[16,16,3840]{2,1,0:T(8,128)(2,1)S(1)}, u32[]{:S(2)}, u32[]{:S(2)}) async-start(bf16[16,16,3840]{2,1,0:T(8,128)(2,1)} %bitcast.48), calls=%async_computation | async-start | bytes 3932160 | tf_op jit(solution)/shard_map/all_to_all | solution.py:284
  16.7 39.6 %collective-permute-start.1 = (bf16[32,3584]{1,0:T(8,128)(2,1)}, bf16[32,3584]{1,0:T(8,128)(2,1)S(1)}, u32[]{:S(2)}, u32[]{:S(2)}) collective-permute-start(bf16[32,3584]{1,0:T(8,128)(2,1)} %get-tuple-element.71), channel_id=1, source_target_pairs={{0,1},{1,0},{2,3},{3,2},{4,5},{5,4},{6,7},{7,6},{8,9},{9,8},{10,11... | collective-permute-start | bytes 688136 | tf_op jit(solution)/shard_map/ppermute | solution.py:365
  17.2 39.2 %collective-permute-start.2 = (bf16[32,3584]{1,0:T(8,128)(2,1)}, bf16[32,3584]{1,0:T(8,128)(2,1)S(1)}, u32[]{:S(2)}, u32[]{:S(2)}) collective-permute-start(bf16[32,3584]{1,0:T(8,128)(2,1)} %get-tuple-element.72), channel_id=1, source_target_pairs={{0,2},{1,3},{2,0},{3,1},{4,6},{5,7},{6,4},{7,5},{8,10},{9,11},{10,... | collective-permute-start | bytes 688136 | tf_op jit(solution)/shard_map/ppermute | solution.py:365
  18.9 37.5 %collective-permute-start.3 = (bf16[32,3584]{1,0:T(8,128)(2,1)}, bf16[32,3584]{1,0:T(8,128)(2,1)S(1)}, u32[]{:S(2)}, u32[]{:S(2)}) collective-permute-start(bf16[32,3584]{1,0:T(8,128)(2,1)} %get-tuple-element.73), channel_id=1, source_target_pairs={{0,3},{1,2},{2,1},{3,0},{4,7},{5,6},{6,5},{7,4},{8,11},{9,10},{10,... | collective-permute-start | bytes 688136 | tf_op jit(solution)/shard_map/ppermute | solution.py:365
  18.9 37.5 %collective-permute-start.4 = (bf16[32,3584]{1,0:T(8,128)(2,1)}, bf16[32,3584]{1,0:T(8,128)(2,1)S(1)}, u32[]{:S(2)}, u32[]{:S(2)}) collective-permute-start(bf16[32,3584]{1,0:T(8,128)(2,1)} %get-tuple-element.74), channel_id=1, source_target_pairs={{0,4},{1,5},{2,6},{3,7},{4,0},{5,1},{6,2},{7,3},{8,12},{9,13},{10,... | collective-permute-start | bytes 688136 | tf_op jit(solution)/shard_map/ppermute | solution.py:365
  20.6 35.8 %collective-permute-start.5 = (bf16[32,3584]{1,0:T(8,128)(2,1)}, bf16[32,3584]{1,0:T(8,128)(2,1)S(1)}, u32[]{:S(2)}, u32[]{:S(2)}) collective-permute-start(bf16[32,3584]{1,0:T(8,128)(2,1)} %get-tuple-element.75), channel_id=1, source_target_pairs={{0,5},{1,4},{2,7},{3,6},{4,1},{5,0},{6,3},{7,2},{8,13},{9,12},{10,... | collective-permute-start | bytes 688136 | tf_op jit(solution)/shard_map/ppermute | solution.py:365
  50.4 1.3 copy-start
  56.3 0.7 copy-start.5
  56.4 0.7 copy-start.6
  56.4 0.8 copy-start.7
  56.4 0.9 copy-start.8
  56.4 0.9 copy-start.9
  56.4 17.5 %copy-start.30 = (bf16[32,3584]{1,0:T(8,128)(2,1)S(1)}, bf16[32,3584]{1,0:T(8,128)(2,1)}, u32[]{:S(2)}) copy-start(bf16[32,3584]{1,0:T(8,128)(2,1)} %get-tuple-element.84) | copy-start | bytes 688132
  57.4 51.1 %all-to-all-start.1 = ((bf16[8,32,3584]{2,1,0:T(8,128)(2,1)}), bf16[8,32,3584]{2,1,0:T(8,128)(2,1)S(1)}, u32[]{:S(2)}, u32[]{:S(2)}) async-start(bf16[8,32,3584]{2,1,0:T(8,128)(2,1)} %bitcast.50), calls=%async_computation.1 | async-start | bytes 3670016 | tf_op jit(solution)/shard_map/all_to_all | solution.py:287
  67.1 21.1 %collective-permute-start = (s32[2,2,128]{2,1,0:T(2,128)S(1)}, s32[2,2,128]{2,1,0:T(2,128)S(1)}, u32[]{:S(2)}, u32[]{:S(2)}) collective-permute-start(s32[2,2,128]{2,1,0:T(2,128)S(1)} %pad_add_fusion), channel_id=1, source_target_pairs={{0,8},{1,9},{2,10},{3,11},{4,12},{5,13},{6,14},{7,15},{8,0},{9,1},... | collective-permute-start | bytes 6152 | tf_op jit(solution)/shard_map/ppermute | solution.py:295
  69.7 40.1 %collective-permute-start.6 = (bf16[32,3584]{1,0:T(8,128)(2,1)}, bf16[32,3584]{1,0:T(8,128)(2,1)S(1)}, u32[]{:S(2)}, u32[]{:S(2)}) collective-permute-start(bf16[32,3584]{1,0:T(8,128)(2,1)} %get-tuple-element.81), channel_id=1, source_target_pairs={{0,8},{1,9},{2,10},{3,11},{4,12},{5,13},{6,14},{7,15},{8,0},{9,1},... | collective-permute-start | bytes 688136 | tf_op jit(solution)/shard_map/ppermute | solution.py:365
  70.1 39.8 %collective-permute-start.7 = (bf16[32,3584]{1,0:T(8,128)(2,1)}, bf16[32,3584]{1,0:T(8,128)(2,1)S(1)}, u32[]{:S(2)}, u32[]{:S(2)}) collective-permute-start(bf16[32,3584]{1,0:T(8,128)(2,1)} %get-tuple-element.82), channel_id=1, source_target_pairs={{0,9},{1,8},{2,11},{3,10},{4,13},{5,12},{6,15},{7,14},{8,1},{9,0},... | collective-permute-start | bytes 688136 | tf_op jit(solution)/shard_map/ppermute | solution.py:365
  72.0 37.8 %collective-permute-start.8 = (bf16[32,3584]{1,0:T(8,128)(2,1)}, bf16[32,3584]{1,0:T(8,128)(2,1)S(1)}, u32[]{:S(2)}, u32[]{:S(2)}) collective-permute-start(bf16[32,3584]{1,0:T(8,128)(2,1)} %get-tuple-element.83), channel_id=1, source_target_pairs={{0,10},{1,11},{2,8},{3,9},{4,14},{5,15},{6,12},{7,13},{8,2},{9,3},... | collective-permute-start | bytes 688136 | tf_op jit(solution)/shard_map/ppermute | solution.py:365
  74.0 39.0 %collective-permute-start.9 = (bf16[32,3584]{1,0:T(8,128)(2,1)S(1)}, bf16[32,3584]{1,0:T(8,128)(2,1)S(1)}, u32[]{:S(2)}, u32[]{:S(2)}) collective-permute-start(bf16[32,3584]{1,0:T(8,128)(2,1)S(1)} %copy-done.30), channel_id=1, source_target_pairs={{0,11},{1,10},{2,9},{3,8},{4,15},{5,14},{6,13},{7,12},{8,3},{9,2},... | collective-permute-start | bytes 688136 | tf_op jit(solution)/shard_map/ppermute | solution.py:365
  88.3 24.7 %copy-start.4 = (pred[8,2,16,128]{3,2,1,0:T(8,128)(4,1)}, pred[8,2,16,128]{3,2,1,0:T(8,128)(4,1)S(1)}, u32[]{:S(2)}) copy-start(pred[8,2,16,128]{3,2,1,0:T(8,128)(4,1)S(1)} %broadcast_and_fusion) | copy-start | bytes 98308
  109.8 3.1 %copy-start.10 = (bf16[32,3584]{1,0:T(8,128)(2,1)}, bf16[32,3584]{1,0:T(8,128)(2,1)S(1)}, u32[]{:S(2)}) copy-start(bf16[32,3584]{1,0:T(8,128)(2,1)S(1)} %collective-permute-done.6.refs_8_) | copy-start | bytes 688132
  109.9 3.1 %copy-start.11 = (bf16[32,3584]{1,0:T(8,128)(2,1)}, bf16[32,3584]{1,0:T(8,128)(2,1)S(1)}, u32[]{:S(2)}) copy-start(bf16[32,3584]{1,0:T(8,128)(2,1)S(1)} %collective-permute-done.7.refs_9_) | copy-start | bytes 688132
  109.9 3.1 %copy-start.12 = (bf16[32,3584]{1,0:T(8,128)(2,1)}, bf16[32,3584]{1,0:T(8,128)(2,1)S(1)}, u32[]{:S(2)}) copy-start(bf16[32,3584]{1,0:T(8,128)(2,1)S(1)} %collective-permute-done.8.refs_10_) | copy-start | bytes 688132
  113.0 0.7 copy-start.13
  113.0 4.3 %copy-start.21 = (f32[2,3584]{1,0:T(2,128)S(1)}, f32[2,3584]{1,0:T(2,128)}, u32[]{:S(2)}) copy-start(f32[2,3584]{1,0:T(2,128)} %bias_ref.1) | copy-start | bytes 86020
  113.6 44.6 %all-to-all-start.2 = ((bf16[8,32,3584]{2,1,0:T(8,128)(2,1)}), bf16[8,32,3584]{2,1,0:T(8,128)(2,1)S(1)}, u32[]{:S(2)}, u32[]{:S(2)}) async-start(bf16[8,32,3584]{2,1,0:T(8,128)(2,1)} %bitcast.49), calls=%async_computation.2 | async-start | bytes 3670016 | tf_op jit(solution)/shard_map/all_to_all | solution.py:287
  117.9 44.1 %collective-permute-start.10 = (bf16[128,3584]{1,0:T(8,128)(2,1)}, bf16[128,3584]{1,0:T(8,128)(2,1)}, u32[]{:S(2)}, u32[]{:S(2)}) collective-permute-start(bf16[128,3584]{1,0:T(8,128)(2,1)} %convolution_convert_fusion.2), channel_id=1, source_target_pairs={{0,8},{1,9},{2,10},{3,11},{4,12},{5,13},{6,14},{7,15},{8,0},{9,1},... | collective-permute-start | bytes 2752520 | tf_op jit(solution)/shard_map/ppermute | solution.py:295
  119.5 47.7 %collective-permute-start.12 = (bf16[32,3584]{1,0:T(8,128)(2,1)}, bf16[32,3584]{1,0:T(8,128)(2,1)}, u32[]{:S(2)}, u32[]{:S(2)}) collective-permute-start(bf16[32,3584]{1,0:T(8,128)(2,1)} %get-tuple-element.90), channel_id=1, source_target_pairs={{0,6},{1,7},{2,4},{3,5},{4,2},{5,3},{6,0},{7,1},{8,14},{9,15},{10,... | collective-permute-start | bytes 688136 | tf_op jit(solution)/shard_map/ppermute | solution.py:365
  159.9 8.2 %collective-permute-start.11 = (bf16[16,3584]{1,0:T(8,128)(2,1)S(1)}, bf16[16,3584]{1,0:T(8,128)(2,1)S(1)}, u32[]{:S(2)}, u32[]{:S(2)}) collective-permute-start(bf16[16,3584]{1,0:T(8,128)(2,1)S(1)} %slice.65), channel_id=1, source_target_pairs={{0,8},{1,9},{2,10},{3,11},{4,12},{5,13},{6,14},{7,15},{8,0},{9,1},... | collective-permute-start | bytes 344072 | tf_op jit(solution)/shard_map/ppermute | solution.py:295
  168.1 0.6 copy-start.19
  168.8 44.1 %all-to-all-start.3 = ((bf16[8,32,3584]{2,1,0:T(8,128)(2,1)}), bf16[8,32,3584]{2,1,0:T(8,128)(2,1)S(1)}, u32[]{:S(2)}, u32[]{:S(2)}) async-start(bf16[8,32,3584]{2,1,0:T(8,128)(2,1)} %bitcast.22), calls=%async_computation.3 | async-start | bytes 3670016 | tf_op jit(solution)/shard_map/all_to_all | solution.py:287
  172.4 4.3 %copy-start.24 = (f32[1,3584]{1,0:T(1,128)S(1)}, f32[1,3584]{1,0:T(1,128)}, u32[]{:S(2)}) copy-start(f32[1,3584]{1,0:T(1,128)} %get-tuple-element.87) | copy-start | bytes 43012
  172.4 38.1 %copy-start.20 = (bf16[16,3584]{1,0:T(8,128)(2,1)S(1)}, bf16[16,3584]{1,0:T(8,128)(2,1)}, u32[]{:S(2)}) copy-start(bf16[16,3584]{1,0:T(8,128)(2,1)} %copy-done.19) | copy-start | bytes 344068
  172.4 38.1 %collective-permute-start.13 = (bf16[112,3584]{1,0:T(8,128)(2,1)S(1)}, bf16[112,3584]{1,0:T(8,128)(2,1)S(1)}, u32[]{:S(2)}, u32[]{:S(2)}) collective-permute-start(bf16[112,3584]{1,0:T(8,128)(2,1)S(1)} %slice.64), channel_id=1, source_target_pairs={{0,8},{1,9},{2,10},{3,11},{4,12},{5,13},{6,14},{7,15},{8,0},{9,1},... | collective-permute-start | bytes 2408456 | tf_op jit(solution)/shard_map/ppermute | solution.py:295
  174.3 43.5 %collective-permute-start.14 = (bf16[32,3584]{1,0:T(8,128)(2,1)}, bf16[32,3584]{1,0:T(8,128)(2,1)}, u32[]{:S(2)}, u32[]{:S(2)}) collective-permute-start(bf16[32,3584]{1,0:T(8,128)(2,1)} %get-tuple-element.94), channel_id=1, source_target_pairs={{0,7},{1,6},{2,5},{3,4},{4,3},{5,2},{6,1},{7,0},{8,15},{9,14},{10,... | collective-permute-start | bytes 688136 | tf_op jit(solution)/shard_map/ppermute | solution.py:365
  210.5 2.3 copy-start.18
  212.8 8.4 %copy-start.1 = (bf16[8,32,3584]{2,1,0:T(8,128)(2,1)}, bf16[8,32,3584]{2,1,0:T(8,128)(2,1)S(1)}, u32[]{:S(2)}) copy-start(bf16[8,32,3584]{2,1,0:T(8,128)(2,1)S(1)} %all-to-all-done.3) | copy-start | bytes 5505028
  212.8 7.6 %collective-permute-start.15 = (f32[2,3584]{1,0:T(2,128)S(1)}, f32[2,3584]{1,0:T(2,128)S(1)}, u32[]{:S(2)}, u32[]{:S(2)}) collective-permute-start(f32[2,3584]{1,0:T(2,128)S(1)} %copy-done.18), channel_id=1, source_target_pairs={{0,4},{1,5},{2,6},{3,7},{4,0},{5,1},{6,2},{7,3},{8,12},{9,13},{10,... | collective-permute-start | bytes 86024 | tf_op jit(solution)/shard_map/ppermute | solution.py:415
  214.7 5.7 %collective-permute-start.16 = (f32[2,3584]{1,0:T(2,128)S(1)}, f32[2,3584]{1,0:T(2,128)S(1)}, u32[]{:S(2)}, u32[]{:S(2)}) collective-permute-start(f32[2,3584]{1,0:T(2,128)S(1)} %copy-done.18), channel_id=1, source_target_pairs={{0,8},{1,9},{2,10},{3,11},{4,12},{5,13},{6,14},{7,15},{8,0},{9,1},... | collective-permute-start | bytes 86024 | tf_op jit(solution)/shard_map/ppermute | solution.py:415
  215.5 5.7 %collective-permute-start.17 = (f32[2,3584]{1,0:T(2,128)S(1)}, f32[2,3584]{1,0:T(2,128)S(1)}, u32[]{:S(2)}, u32[]{:S(2)}) collective-permute-start(f32[2,3584]{1,0:T(2,128)S(1)} %copy-done.18), channel_id=1, source_target_pairs={{0,12},{1,13},{2,14},{3,15},{4,8},{5,9},{6,10},{7,11},{8,4},{9,5},... | collective-permute-start | bytes 86024 | tf_op jit(solution)/shard_map/ppermute | solution.py:415
  221.2 4.6 %copy-start.2 = (bf16[256,128]{1,0:T(8,128)(2,1)S(1)}, bf16[256,128]{1,0:T(8,128)(2,1)}, u32[]{:S(2)}) copy-start(bf16[256,128]{1,0:T(8,128)(2,1)} %get-tuple-element.130) | copy-start | bytes 196612
  221.2 4.6 %copy-start.3 = (bf16[256,128]{1,0:T(8,128)(2,1)S(1)}, bf16[256,128]{1,0:T(8,128)(2,1)}, u32[]{:S(2)}) copy-start(bf16[256,128]{1,0:T(8,128)(2,1)} %get-tuple-element.132) | copy-start | bytes 196612
  221.3 47.0 %all-to-all-start.4 = ((bf16[8,32,3584]{2,1,0:T(8,128)(2,1)}), bf16[8,32,3584]{2,1,0:T(8,128)(2,1)}, u32[]{:S(2)}, u32[]{:S(2)}) async-start(bf16[8,32,3584]{2,1,0:T(8,128)(2,1)} %bitcast.24), calls=%async_computation.4 | async-start | bytes 3670016 | tf_op jit(solution)/shard_map/all_to_all | solution.py:287
  225.7 4.1 %copy-start.29 = (bf16[32,3584]{1,0:T(8,128)(2,1)S(1)}, bf16[32,3584]{1,0:T(8,128)(2,1)}, u32[]{:S(2)}) copy-start(bf16[32,3584]{1,0:T(8,128)(2,1)} %get-tuple-element.109) | copy-start | bytes 688132
  225.7 5.4 %copy-start.28 = (bf16[32,3584]{1,0:T(8,128)(2,1)S(1)}, bf16[32,3584]{1,0:T(8,128)(2,1)}, u32[]{:S(2)}) copy-start(bf16[32,3584]{1,0:T(8,128)(2,1)} %get-tuple-element.110) | copy-start | bytes 688132
  225.8 7.1 %copy-start.27 = (bf16[32,3584]{1,0:T(8,128)(2,1)S(1)}, bf16[32,3584]{1,0:T(8,128)(2,1)}, u32[]{:S(2)}) copy-start(bf16[32,3584]{1,0:T(8,128)(2,1)} %get-tuple-element.111) | copy-start | bytes 688132
  225.8 8.4 %copy-start.26 = (bf16[32,3584]{1,0:T(8,128)(2,1)S(1)}, bf16[32,3584]{1,0:T(8,128)(2,1)}, u32[]{:S(2)}) copy-start(bf16[32,3584]{1,0:T(8,128)(2,1)} %get-tuple-element.112) | copy-start | bytes 688132
  225.8 23.3 %copy-start.22 = (f32[1,3584]{1,0:T(1,128)S(1)}, f32[1,3584]{1,0:T(1,128)}, u32[]{:S(2)}) copy-start(f32[1,3584]{1,0:T(1,128)} %get-tuple-element.139) | copy-start | bytes 43012
  225.9 1.3 collective-permute-start.18
  227.2 21.9 %collective-permute-start.23 = (f32[2,3584]{1,0:T(2,128)S(1)}, f32[2,3584]{1,0:T(2,128)S(1)}, u32[]{:S(2)}, u32[]{:S(2)}) collective-permute-start(f32[2,3584]{1,0:T(2,128)S(1)} %add.64), channel_id=1, source_target_pairs={{0,2},{1,3},{2,0},{3,1},{4,6},{5,7},{6,4},{7,5},{8,10},{9,11},{10,... | collective-permute-start | bytes 86024 | tf_op jit(solution)/shard_map/ppermute | solution.py:415
  229.8 44.9 %collective-permute-start.19 = (bf16[32,3584]{1,0:T(8,128)(2,1)S(1)}, bf16[32,3584]{1,0:T(8,128)(2,1)S(1)}, u32[]{:S(2)}, u32[]{:S(2)}) collective-permute-start(bf16[32,3584]{1,0:T(8,128)(2,1)S(1)} %copy-done.29), channel_id=1, source_target_pairs={{0,12},{1,13},{2,14},{3,15},{4,8},{5,9},{6,10},{7,11},{8,4},{9,5},... | collective-permute-start | bytes 688136 | tf_op jit(solution)/shard_map/ppermute | solution.py:365
  231.2 43.6 %collective-permute-start.20 = (bf16[32,3584]{1,0:T(8,128)(2,1)S(1)}, bf16[32,3584]{1,0:T(8,128)(2,1)S(1)}, u32[]{:S(2)}, u32[]{:S(2)}) collective-permute-start(bf16[32,3584]{1,0:T(8,128)(2,1)S(1)} %copy-done.28), channel_id=1, source_target_pairs={{0,13},{1,12},{2,15},{3,14},{4,9},{5,8},{6,11},{7,10},{8,5},{9,4},... | collective-permute-start | bytes 688136 | tf_op jit(solution)/shard_map/ppermute | solution.py:365
  232.9 41.9 %collective-permute-start.21 = (bf16[32,3584]{1,0:T(8,128)(2,1)S(1)}, bf16[32,3584]{1,0:T(8,128)(2,1)S(1)}, u32[]{:S(2)}, u32[]{:S(2)}) collective-permute-start(bf16[32,3584]{1,0:T(8,128)(2,1)S(1)} %copy-done.27), channel_id=1, source_target_pairs={{0,14},{1,15},{2,12},{3,13},{4,10},{5,11},{6,8},{7,9},{8,6},{9,7},... | collective-permute-start | bytes 688136 | tf_op jit(solution)/shard_map/ppermute | solution.py:365
  234.2 40.6 %collective-permute-start.22 = (bf16[32,3584]{1,0:T(8,128)(2,1)S(1)}, bf16[32,3584]{1,0:T(8,128)(2,1)S(1)}, u32[]{:S(2)}, u32[]{:S(2)}) collective-permute-start(bf16[32,3584]{1,0:T(8,128)(2,1)S(1)} %copy-done.26), channel_id=1, source_target_pairs={{0,15},{1,14},{2,13},{3,12},{4,11},{5,10},{6,9},{7,8},{8,7},{9,6},... | collective-permute-start | bytes 688136 | tf_op jit(solution)/shard_map/ppermute | solution.py:365
  274.7 0.7 copy-start.14
  274.7 0.8 copy-start.15
  274.8 0.8 copy-start.16
  274.8 0.9 copy-start.17
